TPU v7x, 32 devices: a whole 2x2x4 slice. The times are simulated.
32 devices in a mesh: groups: 2 (over x), region: 16 (over z, y, core).
Axes of the slice: x: 2, y: 2, z: 4, core: 2. Of those that a mesh axis runs over, the one named last changes fastest.
Arguments:
- patch_tiles: bfloat16 [512, 2, 4, 14336], P(('groups', 'region')), parts along dimension 0, may hold values from -6 to 6
- slot_lists: int32 [512, 2, 3], P(('groups', 'region')), parts along dimension 0, may hold values from -1 to 448, as said below
- blend_table: float32 [14, 14336], replicated, may hold values from 0.2 to 2
- smoothing: float32 [512, 896], P('region'), may hold values from 0.02 to 0.2
- analysis: bfloat16 [4, 1024, 896], P(None, 'groups', 'region'), parts along dimension 1, may hold values from -6 to 6
Outputs:
- crps_score: bfloat16 [4, 1024, 896], P(None, 'groups', 'region'), parts along dimension 1
- spread_skill: bfloat16 [2, 4, 1024, 896], P(None, None, 'groups', 'region'), parts along dimension 2
There are 2 independent parts, one for each index of `groups`. A program takes and returns all parts, laid end to end along the dimension named above; an argument that names none is the same for every part. Nothing has to cross between parts.
Inputs may be any that keep to these rules, and one draw needn't show every extreme that they name: `slot_lists`: row p * 16 + r lists device p's slots for region r: sample (-1 marks an empty slot), first column, blend_table row. Device p lists only tiles of sample p // 2. In a region every sample has tiles at the same columns with the same table rows; a quarter of the regions, drawn, hold 4 tiles a sample and the others 2; in each region one tile starts at column 0 and one at 448. Slot 0 of every row is live; slot 1 is live exactly in the regions with 4 tiles.
All inputs are finite; a program needn't handle non-finite values.
Results may differ from a plain program's by a relative error of at most 0.0022.
The roundings to bfloat16 on the way count: a program that leaves them out, or rounds other values in their place, can miss the bound.
Values may be sent and summed in bfloat16 or wider, within the bound.
No kernel may reach another device: no remote copies, remote signals or barrier semaphores. Data moves between devices by JAX's collectives and lax.ppermute only.
A program may use at most 192 MiB of HBM per device.

v0:
```python
import functools

import jax
import jax.numpy as jnp
from jax import lax
from jax.experimental import pallas as pl
from jax.experimental.pallas import tpu as pltpu
from jax.sharding import PartitionSpec as P

SAMPLES = 8
FIELDS = 4
PATCH = 448
CAP = 2
ROWS = 32
COLS = 896
PAIRS = ROWS // 2
FLAT = ROWS * PATCH
LANES = 128
TILES = COLS // LANES
QUAD = LANES // ROWS
MID = 0.11
VMEM = 40 * 1024 * 1024


def round_up(value, step):
    return -(-value // step) * step


class Sizes:
    def __init__(self, regions):
        self.regions = regions
        self.makers = regions // SAMPLES
        self.block = regions // self.makers
        self.quads = self.block // QUAD
        self.width = COLS // regions
        self.span = round_up(self.width, 8)
        self.rows = regions * ROWS
        self.main = round_up(FIELDS * self.span, 16)
        self.sent = self.main + 16


def stage(staged, load):
    for k in range(PAIRS):
        for t in range(TILES):
            at = COLS * k + LANES * t
            staged[t, FIELDS * k : FIELDS * (k + 1), :] = load(at).astype(jnp.float32)


def staged_field(staged, field):
    return jnp.concatenate([staged[t, pl.ds(field, PAIRS, stride=FIELDS), :] for t in range(TILES)], 1)


def lane_index():
    return lax.broadcasted_iota(jnp.int32, (PAIRS, COLS), 1)


def place_side(pairs, column):
    left = (lane_index() < PATCH) & (column == 0)
    right = (lane_index() >= PATCH) & (column != 0)
    turned = pltpu.roll(pairs, PATCH, 1)
    even = jnp.where(left, pairs, jnp.where(right, turned, 0.0))
    odd = jnp.where(left, turned, jnp.where(right, pairs, 0.0))
    return even, odd


def place_any(pairs, column):
    inside = (lane_index() >= column) & (lane_index() < column + PATCH)
    turned = pltpu.roll(pairs, column, 1)
    return jnp.where(inside, turned, 0.0), jnp.where(inside, pltpu.roll(turned, PATCH, 1), 0.0)


def either_kind(z, heavy, body):
    @pl.when(heavy)
    def _():
        body(place_any, range(CAP))

    @pl.when(jnp.logical_not(heavy))
    def _():
        body(place_side if z.makers == 2 else place_any, range(1))


def own_kernel(z, place, *refs):
    lists, (tiles, table, half, inverse) = refs[: z.makers], refs[z.makers : z.makers + 4]
    landed, staged, weights, sems = refs[z.makers + 4 :]
    first = lax.rem(place[0], z.makers) * z.block

    def fetch(j):
        return pltpu.make_async_copy(tiles.at[first + j], landed.at[j], sems.at[j])

    for j in range(z.block):
        fetch(j).start()
    kinds = table.shape[0]
    for k in range(PAIRS):
        for t in range(TILES):
            at = COLS * k + LANES * t
            for low in range(0, kinds, 8):
                count = min(8, kinds - low)
                weights[t, pl.ds(PAIRS * low + k, count, stride=PAIRS), :] = table[
                    low : low + count, at : at + LANES
                ]

    def weight(kind):
        at = pl.multiple_of(kind * PAIRS, PAIRS)
        return jnp.concatenate([weights[t, pl.ds(at, PAIRS), :] for t in range(TILES)], 1)

    def region(j, carry):
        fetch(j).wait()

        def body(place_tile, slots):
            even, odd = 0.0, 0.0
            for maker in range(z.makers):
                for slot in slots:
                    column, kind = (lists[maker][field, slot, first + j] for field in (1, 2))
                    a, b = place_tile(weight(kind), column)
                    even, odd = even + a, odd + b
            inverse[j, 0] = 1.0 / even
            inverse[j, 1] = 1.0 / odd
            for slot in slots:
                stage(staged.at[slot], lambda at, slot=slot: landed[j, slot, :, at : at + LANES])

            def one_field(field, carry):
                even, odd = 0.0, 0.0
                for slot in slots:
                    column, kind = (lists[0][entry, slot, first + j] for entry in (1, 2))
                    a, b = place_tile(staged_field(staged.at[slot], field) * weight(kind), column)
                    even, odd = even + a, odd + b
                half[j, field, 0] = even * inverse[j, 0]
                half[j, field, 1] = odd * inverse[j, 1]
                return carry

            lax.fori_loop(0, FIELDS, one_field, 0)

        either_kind(z, lists[0][0, 1, first + j] >= 0, body)
        return carry

    lax.fori_loop(0, z.block, region, 0)


def own_share(z, place, lists, tiles, table):
    smem = pl.BlockSpec(memory_space=pltpu.SMEM)
    kinds = round_up(table.shape[0], 8)
    return pl.pallas_call(
        functools.partial(own_kernel, z),
        out_shape=[
            jax.ShapeDtypeStruct((z.block, FIELDS, 2, PAIRS, COLS), jnp.float32),
            jax.ShapeDtypeStruct((z.block, 2, PAIRS, COLS), jnp.float32),
        ],
        in_specs=[smem] * (1 + z.makers)
        + [pl.BlockSpec(memory_space=pltpu.HBM), pl.BlockSpec(memory_space=pltpu.VMEM)],
        out_specs=[pl.BlockSpec(memory_space=pltpu.VMEM)] * 2,
        scratch_shapes=[
            pltpu.VMEM((z.block, CAP, FIELDS, FLAT), jnp.bfloat16),
            pltpu.VMEM((CAP, TILES, PAIRS * FIELDS, LANES), jnp.float32),
            pltpu.VMEM((TILES, kinds * PAIRS, LANES), jnp.float32),
            pltpu.SemaphoreType.DMA((z.block,)),
        ],
        compiler_params=pltpu.CompilerParams(vmem_limit_bytes=VMEM),
        cost_estimate=pl.CostEstimate(flops=5_000_000, bytes_accessed=8_000_000, transcendentals=0),
        name="own_share",
    )(place, *lists, tiles, table)


def join_kernel(z, *refs):
    place, lists, refs = refs[0], refs[1 : 1 + z.makers], refs[1 + z.makers :]
    received, (half, inverse, table, smoothing, out) = refs[: z.makers - 1], refs[z.makers - 1 : z.makers + 4]
    staged, lines, turned, strength, blocks, sems = refs[z.makers + 4 :]
    first = lax.rem(place[0], z.makers) * z.block

    turned_strength = jnp.transpose(smoothing[...] - MID)
    for dest in range(z.regions):
        for g in range(z.span // 8):
            top = z.width * dest + 8 * g
            count, at = min(8, COLS - top), ROWS * (g % QUAD)
            strength[dest, g // QUAD, 0:count, at : at + ROWS] = turned_strength[top : top + count]

    def send(quad):
        return pltpu.make_async_copy(blocks.at[:, quad], out.at[:, quad], sems.at[quad])

    for quad in range(z.quads):

        def region(i, carry):
            j = quad * QUAD + i

            def body(place_tile, slots):
                entries = []
                for maker in range(1, z.makers):
                    for slot in slots:
                        index = (maker - 1) * CAP + slot
                        stage(
                            staged.at[index],
                            lambda at, maker=maker, slot=slot: received[maker - 1][j, slot, :, at : at + LANES],
                        )
                        column, kind = (lists[maker][field, slot, first + j] for field in (1, 2))
                        entries.append((index, column, kind))

                def one_field(field, carry):
                    even, odd = 0.0, 0.0
                    for index, column, kind in entries:
                        a, b = place_tile(staged_field(staged.at[index], field) * table[kind], column)
                        even, odd = even + a, odd + b
                    even = even * inverse[j, 0] + half[j, field, 0]
                    odd = odd * inverse[j, 1] + half[j, field, 1]
                    for t in range(TILES):
                        here = slice(LANES * t, LANES * (t + 1))
                        lines[field, t, pl.ds(ROWS * i, PAIRS, stride=2), :] = even[:, here]
                        lines[field, t, pl.ds(ROWS * i + 1, PAIRS, stride=2), :] = odd[:, here]
                    return carry

                lax.fori_loop(0, FIELDS, one_field, 0)

            either_kind(z, lists[0][0, 1, first + j] >= 0, body)
            return carry

        lax.fori_loop(0, QUAD, region, 0)
        for field in range(FIELDS):
            for t in range(TILES):
                turned[field, LANES * t : LANES * (t + 1), :] = jnp.transpose(lines[field, t])
        for dest in range(z.regions):
            top = z.width * dest
            for low in range(0, FIELDS, 2):
                block = [turned[field, top : top + z.span, :] for field in (low, low + 1)]
                blocks[dest, quad, low * z.span : (low + 2) * z.span, :] = jnp.concatenate(block, 0).astype(
                    jnp.bfloat16
                )
            ends = (max(top - 1, 0), min(top + z.width, COLS - 1))
            edge = [turned[field, end : end + 1, :] for field in range(FIELDS) for end in ends]
            edge.append(strength[dest, quad])
            blocks[dest, quad, z.main : z.sent, :] = jnp.concatenate(edge, 0).astype(jnp.bfloat16)
        send(quad).start()
    for quad in range(z.quads):
        send(quad).wait()


def join(z, place, lists, received, half, inverse, table, smoothing):
    smem = pl.BlockSpec(memory_space=pltpu.SMEM)
    vmem = pl.BlockSpec(memory_space=pltpu.VMEM)
    shape = (z.regions, z.quads, z.sent, LANES)
    return pl.pallas_call(
        functools.partial(join_kernel, z),
        out_shape=pltpu.HBM(shape, jnp.bfloat16),
        in_specs=[smem] * (1 + z.makers) + [vmem] * (z.makers + 3),
        out_specs=pl.BlockSpec(memory_space=pltpu.HBM),
        scratch_shapes=[
            pltpu.VMEM((CAP * (z.makers - 1), TILES, PAIRS * FIELDS, LANES), jnp.float32),
            pltpu.VMEM((FIELDS, TILES, LANES, LANES), jnp.float32),
            pltpu.VMEM((FIELDS, COLS + 8, LANES), jnp.float32),
            pltpu.VMEM((z.regions, z.quads, 8, LANES), jnp.float32),
            pltpu.VMEM(shape, jnp.bfloat16),
            pltpu.SemaphoreType.DMA((z.quads,)),
        ],
        compiler_params=pltpu.CompilerParams(vmem_limit_bytes=VMEM),
        cost_estimate=pl.CostEstimate(flops=5_000_000, bytes_accessed=8_000_000, transcendentals=0),
        name="join",
    )(place, *lists, *received, half, inverse, table, smoothing)


SORT_STEPS = (
    ((0, 1), (2, 3), (4, 5), (6, 7)),
    ((0, 2), (1, 3), (4, 6), (5, 7)),
    ((1, 2), (5, 6)),
    ((0, 4), (1, 5), (2, 6), (3, 7)),
    ((2, 4), (3, 5)),
    ((1, 2), (3, 4), (5, 6)),
)
STEP_FIELDS = 2


def score_kernel(z, blocks, analysis, crps, spread, strength, edges, padded):
    step = pl.program_id(0)
    rows = z.rows
    sources = [(source, quad) for source in range(z.regions) for quad in range(z.quads)]

    @pl.when(step == 0)
    def _():
        slot = lax.broadcasted_iota(jnp.int32, (8, LANES), 1) // ROWS
        for low in range(0, z.regions, QUAD):
            for quad in range(z.quads):
                tails = [
                    blocks[source, quad, z.main : z.sent, :].astype(jnp.float32)
                    for source in range(low, low + QUAD)
                ]
                for i, tail in enumerate(tails):
                    at = ((low + i) % z.makers * z.quads + quad) * LANES
                    edges[(low + i) // z.makers, :, at : at + LANES] = tail[0:8]
                for g in range(quad * QUAD, min((quad + 1) * QUAD, z.span // 8)):
                    joined = jnp.zeros((8, LANES), jnp.float32)
                    for i, tail in enumerate(tails):
                        near = pltpu.roll(tail[8:16], (i - g) % QUAD * ROWS, 1)
                        joined = jnp.where(slot == i, near, joined)
                    at = low // QUAD * LANES
                    strength[8 * g : 8 * (g + 1), at : at + LANES] = joined + MID

    top = pl.multiple_of(step * STEP_FIELDS * z.span, 16)
    for source, quad in sources:
        at = (source % z.makers * z.quads + quad) * LANES
        values = blocks[source, quad, pl.ds(top, STEP_FIELDS * z.span), :].astype(jnp.float32)
        for f in range(STEP_FIELDS):
            padded[source // z.makers, f, 8 : 8 + z.span, at : at + LANES] = values[f * z.span : (f + 1) * z.span]
    for sample in range(SAMPLES):
        for f in range(STEP_FIELDS):
            low = 2 * (step * STEP_FIELDS + f)
            padded[sample, f, 7:8, :] = edges[sample, pl.ds(low, 1), :]
            padded[sample, f, 8 + z.width : 9 + z.width, :] = edges[sample, pl.ds(low + 1, 1), :]
    for f in range(STEP_FIELDS):
        target_field = analysis[f].astype(jnp.float32)
        for low in range(0, z.width, 16):
            high = min(low + 16, z.width)
            shape = (high - low, rows)
            lane = lax.broadcasted_iota(jnp.int32, shape, 1)
            strong = strength[low:high, :]
            members = []
            for sample in range(SAMPLES):
                here = padded[sample, f, 8 + low : 8 + high, :]
                sides = padded[sample, f, 7 + low : 7 + high, :] + padded[sample, f, 9 + low : 9 + high, :]
                above = jnp.where(lane == 0, here, pltpu.roll(here, 1, 1))
                below = jnp.where(lane == rows - 1, here, pltpu.roll(here, rows - 1, 1))
                smooth = here + strong * (above + below + sides - 4.0 * here)
                members.append(smooth.astype(jnp.bfloat16))
            values = [member.astype(jnp.float32) for member in members]
            target = target_field[low:high]
            error = sum(jnp.abs(value - target) for value in values) * (1.0 / SAMPLES)
            average = sum(values) * (1.0 / SAMPLES)
            variance = sum((value - average) ** 2 for value in values) * (1.0 / (SAMPLES - 1.0))
            ranked = list(members)
            for pairs in SORT_STEPS:
                for a, b in pairs:
                    ranked[a], ranked[b] = jnp.minimum(ranked[a], ranked[b]), jnp.maximum(ranked[a], ranked[b])
            ranked = [member.astype(jnp.float32) for member in ranked]
            pairs = sum(
                (2 * k - SAMPLES + 1.0) * (ranked[k] - ranked[SAMPLES - 1 - k])
                for k in range(SAMPLES // 2, SAMPLES)
            )
            crps[f, low:high, :] = (error - pairs * (1.0 / (SAMPLES * SAMPLES))).astype(jnp.bfloat16)
            spread[0, f, low:high, :] = variance.astype(jnp.bfloat16)
            spread[1, f, low:high, :] = ((average - target) ** 2).astype(jnp.bfloat16)


def score(z, blocks, analysis):
    width, rows = z.width, z.rows
    return pl.pallas_call(
        functools.partial(score_kernel, z),
        out_shape=[
            jax.ShapeDtypeStruct((FIELDS, width, rows), jnp.bfloat16),
            jax.ShapeDtypeStruct((2, FIELDS, width, rows), jnp.bfloat16),
        ],
        grid=(FIELDS // STEP_FIELDS,),
        in_specs=[
            pl.BlockSpec(blocks.shape, lambda i: (0, 0, 0, 0)),
            pl.BlockSpec((STEP_FIELDS, width, rows), lambda i: (i, 0, 0)),
        ],
        out_specs=[
            pl.BlockSpec((STEP_FIELDS, width, rows), lambda i: (i, 0, 0)),
            pl.BlockSpec((2, STEP_FIELDS, width, rows), lambda i: (0, i, 0, 0)),
        ],
        scratch_shapes=[
            pltpu.VMEM((z.span, rows), jnp.float32),
            pltpu.VMEM((SAMPLES, 8, rows), jnp.float32),
            pltpu.VMEM((SAMPLES, STEP_FIELDS, z.span + 16, rows), jnp.float32),
        ],
        compiler_params=pltpu.CompilerParams(vmem_limit_bytes=VMEM),
        name="score",
    )(blocks, analysis)


def shards(patch_tiles, slot_lists, blend_table, smoothing, analysis):
    z = Sizes(lax.axis_size("region"))
    place = lax.axis_index("region")
    part = lax.rem(place, z.makers)
    place = place.reshape(1)
    turns = [
        [(i, i - i % z.makers + (i + k) % z.makers) for i in range(z.regions)] for k in range(1, z.makers)
    ]
    lists = jnp.transpose(slot_lists, (2, 1, 0))
    lists = [lists] + [lax.ppermute(lists, "region", turn) for turn in turns]
    received = []
    for k, turn in enumerate(turns, 1):
        first = lax.rem(part + k, z.makers) * z.block
        received.append(
            lax.ppermute(lax.dynamic_slice_in_dim(patch_tiles, first, z.block, 0), "region", turn)
        )
    half, inverse = own_share(z, place, lists, patch_tiles, blend_table)
    table = blend_table.reshape(blend_table.shape[0], PAIRS, COLS)
    blocks = join(z, place, lists, received, half, inverse, table, smoothing)
    moved = lax.all_to_all(blocks, "region", split_axis=0, concat_axis=0, tiled=True)
    outs = score(z, moved, jnp.swapaxes(analysis, 1, 2))
    return tuple(jnp.swapaxes(item, -1, -2) for item in outs)


def solution(mesh):
    return jax.shard_map(
        shards,
        mesh=mesh,
        in_specs=(
            P(("groups", "region"), None, None, None),
            P(("groups", "region"), None, None),
            P(),
            P("region", None),
            P(None, "groups", "region"),
        ),
        out_specs=(P(None, "groups", "region"), P(None, None, "groups", "region")),
        check_vma=False,
    )
```

profile of v0, /device:TPU:1, one launch (start us, length us, event | category | flops | bytes accessed | tf_op | source)
XLA Modules:
  0.0 80.6 jit_solution(11405840930432496781)
XLA Ops:
  0.6 0.0 copy-start.4
  0.6 0.0 copy-start.1
  0.7 0.0 copy-start
  0.7 2.3 %constant_dynamic-slice_fusion = bf16[8,2,4,14336]{3,2,1,0:T(4,128)(2,1)S(1)} fusion(bf16[16,2,4,14336]{3,2,1,0:T(4,128)(2,1)} %refs_2_.1, s32[]{:T(128)S(6)} %select_n.3), kind=kLoop, calls=%fused_computation | loop fusion | bytes 3670020 | tf_op jit(solution)/shard_map/dynamic_slice | solution.py:379
  3.0 0.1 collective-permute-start.1
  3.1 0.0 copy-done.4
  3.1 0.5 collective-permute-start
  3.6 0.0 copy-done.1
  3.6 0.2 copy.7
  3.8 0.1 slice.refs_6_
  3.8 3.0 %collective-permute-done.refs_1_.refs_2_ = s32[3,2,16]{2,1,0:T(2,128)S(1)} collective-permute-done((s32[3,2,16]{2,1,0:T(2,128)S(1)}, s32[3,2,16]{2,1,0:T(2,128)S(1)}, u32[]{:S(2)}, u32[]{:S(2)}) %collective-permute-start) | collective-permute-done | bytes 416 | tf_op jit(solution)/shard_map/ppermute | solution.py:374
  6.9 0.0 copy-done
  6.9 0.0 copy-start.3
  6.9 8.5 %own_share.1 = (f32[8,4,2,16,896]{4,3,2,1,0:T(8,128)S(1)}, f32[8,2,16,896]{3,2,1,0:T(8,128)S(1)}) custom-call(s32[1]{0:T(128)} %bitcast.place.refs_0_, s32[3,2,16]{2,1,0:T(2,128)S(1)} %bitcast.11, s32[3,2,16]{2,1,0:T(2,128)S(1)} %collective-permute-done.refs_1_.refs_2_, bf16[16,2,4,14336]{3,2,1,0:T(4,128)(2,1)S(1)} %copy-done, f32[14,14336]{1,0:T(8,128)S(1)} %copy-done.1), custom_call_target="tpu_custom_call" | custom-call | flops 5000000 | bytes 8000000 | tf_op jit(solution)/shard_map/own_share/pallas_call | solution.py:142
  15.4 0.0 collective-permute-done.1.refs_3_
  15.4 0.0 copy-done.3
  15.4 7.1 %join.1 = bf16[16,2,240,128]{3,2,1,0:T(8,128)(2,1)} custom-call(s32[1]{0:T(128)} %bitcast.place.refs_0_, s32[3,2,16]{2,1,0:T(2,128)S(1)} %bitcast.12, s32[3,2,16]{2,1,0:T(2,128)S(1)} %collective-permute-done.refs_1_.refs_2_, bf16[8,2,4,14336]{3,2,1,0:T(4,128)(2,1)S(1)} %collective-permute-done.1.refs_3_, f32[8,4,2,16,896]{4,3,2,1,0:T(8,128)S(1)} %get-tuple-element.6.refs_4_, ...), custom_call_target="tpu_custom_call" | custom-call | flops 5000000 | bytes 8000000 | tf_op jit(solution)/shard_map/join/pallas_call | solution.py:238
  22.5 0.0 copy-start.2
  22.6 52.9 %all_to_all.5.blocks = bf16[16,2,240,128]{3,2,1,0:T(8,128)(2,1)S(1)} all-to-all(bf16[16,2,240,128]{3,2,1,0:T(8,128)(2,1)} %join.1), channel_id=1, replica_groups=mesh['groups'=2,'region'=16] {'region'}, dimensions={0} | all-to-all | bytes 3932160 | tf_op jit(solution)/shard_map/all_to_all | solution.py:384
  75.4 0.0 copy-done.2
  75.4 5.2 %score.1 = (bf16[4,56,512]{2,1,0:T(8,128)(2,1)}, bf16[2,4,56,512]{3,2,1,0:T(8,128)(2,1)}) custom-call(bf16[16,2,240,128]{3,2,1,0:T(8,128)(2,1)S(1)} %all_to_all.5.blocks, bf16[4,56,512]{2,1,0:T(8,128)(2,1)S(1)} %bitcast.9), custom_call_target="tpu_custom_call" | custom-call | tf_op jit(solution)/shard_map/score/pallas_call | solution.py:340
Async XLA Ops:
  0.6 2.5 %copy-start.4 = (s32[16,2,3]{0,1,2:T(2,128)S(1)}, s32[16,2,3]{0,1,2:T(2,128)}, u32[]{:S(2)}) copy-start(s32[16,2,3]{0,1,2:T(2,128)} %param.6) | copy-start | bytes 1156
  0.6 2.9 %copy-start.1 = (f32[14,14336]{1,0:T(8,128)S(1)}, f32[14,14336]{1,0:T(8,128)}, u32[]{:S(2)}) copy-start(f32[14,14336]{1,0:T(8,128)} %refs_3_.1) | copy-start | bytes 2408452
  0.7 6.2 %copy-start = (bf16[16,2,4,14336]{3,2,1,0:T(4,128)(2,1)S(1)}, bf16[16,2,4,14336]{3,2,1,0:T(4,128)(2,1)}, u32[]{:S(2)}) copy-start(bf16[16,2,4,14336]{3,2,1,0:T(4,128)(2,1)} %refs_2_.1) | copy-start | bytes 11010052
  3.0 12.4 %collective-permute-start.1 = (bf16[8,2,4,14336]{3,2,1,0:T(4,128)(2,1)S(1)}, bf16[8,2,4,14336]{3,2,1,0:T(4,128)(2,1)S(1)}, u32[]{:S(2)}, u32[]{:S(2)}) collective-permute-start(bf16[8,2,4,14336]{3,2,1,0:T(4,128)(2,1)S(1)} %constant_dynamic-slice_fusion), channel_id=1, source_target_pairs={{0,1},{1,0},{2,3},{3,2},{4,5},{5,4},{6,7},{7,6},{8,9},{9,8},{10,11... | collective-permute-start | bytes 5505032 | tf_op jit(solution)/shard_map/ppermute | solution.py:379
  3.1 3.7 %collective-permute-start = (s32[3,2,16]{2,1,0:T(2,128)S(1)}, s32[3,2,16]{2,1,0:T(2,128)S(1)}, u32[]{:S(2)}, u32[]{:S(2)}) collective-permute-start(s32[3,2,16]{2,1,0:T(2,128)S(1)} %bitcast.10), channel_id=1, source_target_pairs={{0,1},{1,0},{2,3},{3,2},{4,5},{5,4},{6,7},{7,6},{8,9},{9,8},{10,11... | collective-permute-start | bytes 1160 | tf_op jit(solution)/shard_map/ppermute | solution.py:374
  6.9 8.5 %copy-start.3 = (f32[32,896]{1,0:T(8,128)S(1)}, f32[32,896]{1,0:T(8,128)}, u32[]{:S(2)}) copy-start(f32[32,896]{1,0:T(8,128)} %refs_7_.1) | copy-start | bytes 344068
  22.5 52.9 %copy-start.2 = (bf16[4,512,56]{1,2,0:T(8,128)(2,1)S(1)}, bf16[4,512,56]{1,2,0:T(8,128)(2,1)}, u32[]{:S(2)}) copy-start(bf16[4,512,56]{1,2,0:T(8,128)(2,1)} %param.9) | copy-start | bytes 688132
where the time goes:
time: 81.7 us; the launch traced here: 80.6 us
  blocking collectives  52.9 us (65%)
  Pallas kernels  20.8 us (25%)
  waiting for transfers between devices  3.03 us (4%)
  local copies, waits for them, and re-layouts  2.58 us (3%)
    all_to_all x1, blocking collectives, shards(): lax.all_to_all(blocks, 'region', split_axis=0, concat_axis=0, tiled=True)  52.9 us
    pallas_call x1, Pallas kernels, own_share(): pl.pallas_call(functools.partial(own_kernel, z), out_shape=[jax.ShapeDtyp...  8.53 us
    pallas_call x1, Pallas kernels, join(): pl.pallas_call(functools.partial(join_kernel, z), out_shape=pltpu.HBM(sha...  7.12 us
    pallas_call x1, Pallas kernels, score(): pl.pallas_call(functools.partial(score_kernel, z), out_shape=[jax.ShapeDt...  5.15 us
    ppermute x1, waiting for transfers between devices, shards(): lists = [lists] + [lax.ppermute(lists, 'region', turn) for turn in turns]  3.03 us
    dynamic_slice x1, local copies, waits for them, and re-layouts, shards(): lax.dynamic_slice_in_dim(patch_tiles, first, z.block, 0)  2.32 us
  transfers between devices with their start and end apart: 2, of which 1 were waited for; matrix products, arithmetic and copies ran while one was open for 0% of the time, Pallas kernels for 11%

commit v1 on v0

--- a/solution.py
+++ b/solution.py
@@ -14,12 +14,13 @@
 ROWS = 32
 COLS = 896
 PAIRS = ROWS // 2
-FLAT = ROWS * PATCH
+LINES = FIELDS * ROWS * PATCH // 128
 LANES = 128
 TILES = COLS // LANES
 QUAD = LANES // ROWS
 MID = 0.11
 VMEM = 40 * 1024 * 1024
+MOST_VMEM = 52 * 1024 * 1024
 
 
 def round_up(value, step):
@@ -39,15 +40,19 @@
         self.sent = self.main + 16
 
 
-def stage(staged, load):
-    for k in range(PAIRS):
-        for t in range(TILES):
-            at = COLS * k + LANES * t
-            staged[t, FIELDS * k : FIELDS * (k + 1), :] = load(at).astype(jnp.float32)
+def stage(staged, tile):
+    staged[...] = tile.astype(jnp.float32)
 
 
 def staged_field(staged, field):
-    return jnp.concatenate([staged[t, pl.ds(field, PAIRS, stride=FIELDS), :] for t in range(TILES)], 1)
+    return jnp.concatenate(
+        [staged[pl.ds(FIELDS * t + field, PAIRS, stride=FIELDS * TILES), :] for t in range(TILES)], 1
+    )
+
+
+def weight_of(weights, kind):
+    at = pl.multiple_of(kind * PAIRS, PAIRS)
+    return jnp.concatenate([weights[t, pl.ds(at, PAIRS), :] for t in range(TILES)], 1)
 
 
 def lane_index():
@@ -79,9 +84,7 @@
         body(place_side if z.makers == 2 else place_any, range(1))
 
 
-def own_kernel(z, place, *refs):
-    lists, (tiles, table, half, inverse) = refs[: z.makers], refs[z.makers : z.makers + 4]
-    landed, staged, weights, sems = refs[z.makers + 4 :]
+def own_kernel(z, place, lists, tiles, table, half, total, weights, landed, staged, sems):
     first = lax.rem(place[0], z.makers) * z.block
 
     def fetch(j):
@@ -99,38 +102,28 @@
                     low : low + count, at : at + LANES
                 ]
 
-    def weight(kind):
-        at = pl.multiple_of(kind * PAIRS, PAIRS)
-        return jnp.concatenate([weights[t, pl.ds(at, PAIRS), :] for t in range(TILES)], 1)
-
     def region(j, carry):
         fetch(j).wait()
 
         def body(place_tile, slots):
+            entries = []
+            for slot in slots:
+                stage(staged.at[slot], landed[j, slot])
+                column, kind = (lists[field, slot, first + j] for field in (1, 2))
+                entries.append((slot, column, weight_of(weights, kind)))
             even, odd = 0.0, 0.0
-            for maker in range(z.makers):
-                for slot in slots:
-                    column, kind = (lists[maker][field, slot, first + j] for field in (1, 2))
-                    a, b = place_tile(weight(kind), column)
+            for _, column, weight in entries:
+                a, b = place_tile(weight, column)
+                even, odd = even + a, odd + b
+            total[j, 0], total[j, 1] = even, odd
+            for field in range(FIELDS):
+                even, odd = 0.0, 0.0
+                for slot, column, weight in entries:
+                    a, b = place_tile(staged_field(staged.at[slot], field) * weight, column)
                     even, odd = even + a, odd + b
-            inverse[j, 0] = 1.0 / even
-            inverse[j, 1] = 1.0 / odd
-            for slot in slots:
-                stage(staged.at[slot], lambda at, slot=slot: landed[j, slot, :, at : at + LANES])
-
-            def one_field(field, carry):
-                even, odd = 0.0, 0.0
-                for slot in slots:
-                    column, kind = (lists[0][entry, slot, first + j] for entry in (1, 2))
-                    a, b = place_tile(staged_field(staged.at[slot], field) * weight(kind), column)
-                    even, odd = even + a, odd + b
-                half[j, field, 0] = even * inverse[j, 0]
-                half[j, field, 1] = odd * inverse[j, 1]
-                return carry
-
-            lax.fori_loop(0, FIELDS, one_field, 0)
-
-        either_kind(z, lists[0][0, 1, first + j] >= 0, body)
+                half[j, field, 0], half[j, field, 1] = even, odd
+
+        either_kind(z, lists[0, 1, first + j] >= 0, body)
         return carry
 
     lax.fori_loop(0, z.block, region, 0)
@@ -138,32 +131,32 @@
 
 def own_share(z, place, lists, tiles, table):
     smem = pl.BlockSpec(memory_space=pltpu.SMEM)
+    vmem = pl.BlockSpec(memory_space=pltpu.VMEM)
     kinds = round_up(table.shape[0], 8)
     return pl.pallas_call(
         functools.partial(own_kernel, z),
         out_shape=[
             jax.ShapeDtypeStruct((z.block, FIELDS, 2, PAIRS, COLS), jnp.float32),
             jax.ShapeDtypeStruct((z.block, 2, PAIRS, COLS), jnp.float32),
-        ],
-        in_specs=[smem] * (1 + z.makers)
-        + [pl.BlockSpec(memory_space=pltpu.HBM), pl.BlockSpec(memory_space=pltpu.VMEM)],
-        out_specs=[pl.BlockSpec(memory_space=pltpu.VMEM)] * 2,
+            jax.ShapeDtypeStruct((TILES, kinds * PAIRS, LANES), jnp.float32),
+        ],
+        in_specs=[smem, smem, pl.BlockSpec(memory_space=pltpu.HBM), vmem],
+        out_specs=[vmem] * 3,
         scratch_shapes=[
-            pltpu.VMEM((z.block, CAP, FIELDS, FLAT), jnp.bfloat16),
-            pltpu.VMEM((CAP, TILES, PAIRS * FIELDS, LANES), jnp.float32),
-            pltpu.VMEM((TILES, kinds * PAIRS, LANES), jnp.float32),
+            pltpu.VMEM((z.block, CAP, LINES, LANES), jnp.bfloat16),
+            pltpu.VMEM((CAP, LINES, LANES), jnp.float32),
             pltpu.SemaphoreType.DMA((z.block,)),
         ],
-        compiler_params=pltpu.CompilerParams(vmem_limit_bytes=VMEM),
+        compiler_params=pltpu.CompilerParams(vmem_limit_bytes=MOST_VMEM),
         cost_estimate=pl.CostEstimate(flops=5_000_000, bytes_accessed=8_000_000, transcendentals=0),
         name="own_share",
-    )(place, *lists, tiles, table)
+    )(place, lists, tiles, table)
 
 
 def join_kernel(z, *refs):
     place, lists, refs = refs[0], refs[1 : 1 + z.makers], refs[1 + z.makers :]
-    received, (half, inverse, table, smoothing, out) = refs[: z.makers - 1], refs[z.makers - 1 : z.makers + 4]
-    staged, lines, turned, strength, blocks, sems = refs[z.makers + 4 :]
+    received, refs = refs[: z.makers - 1], refs[z.makers - 1 :]
+    half, total, weights, smoothing, out, staged, lines, turned, strength, blocks, sems = refs
     first = lax.rem(place[0], z.makers) * z.block
 
     turned_strength = jnp.transpose(smoothing[...] - MID)
@@ -186,27 +179,24 @@
                 for maker in range(1, z.makers):
                     for slot in slots:
                         index = (maker - 1) * CAP + slot
-                        stage(
-                            staged.at[index],
-                            lambda at, maker=maker, slot=slot: received[maker - 1][j, slot, :, at : at + LANES],
-                        )
+                        stage(staged.at[index], received[maker - 1][first + j, slot])
                         column, kind = (lists[maker][field, slot, first + j] for field in (1, 2))
-                        entries.append((index, column, kind))
-
-                def one_field(field, carry):
-                    even, odd = 0.0, 0.0
-                    for index, column, kind in entries:
-                        a, b = place_tile(staged_field(staged.at[index], field) * table[kind], column)
+                        entries.append((index, column, weight_of(weights, kind)))
+                even, odd = total[j, 0], total[j, 1]
+                for _, column, weight in entries:
+                    a, b = place_tile(weight, column)
+                    even, odd = even + a, odd + b
+                even_inverse, odd_inverse = 1.0 / even, 1.0 / odd
+                for field in range(FIELDS):
+                    even, odd = half[j, field, 0], half[j, field, 1]
+                    for index, column, weight in entries:
+                        a, b = place_tile(staged_field(staged.at[index], field) * weight, column)
                         even, odd = even + a, odd + b
-                    even = even * inverse[j, 0] + half[j, field, 0]
-                    odd = odd * inverse[j, 1] + half[j, field, 1]
+                    even, odd = even * even_inverse, odd * odd_inverse
                     for t in range(TILES):
                         here = slice(LANES * t, LANES * (t + 1))
                         lines[field, t, pl.ds(ROWS * i, PAIRS, stride=2), :] = even[:, here]
                         lines[field, t, pl.ds(ROWS * i + 1, PAIRS, stride=2), :] = odd[:, here]
-                    return carry
-
-                lax.fori_loop(0, FIELDS, one_field, 0)
 
             either_kind(z, lists[0][0, 1, first + j] >= 0, body)
             return carry
@@ -231,7 +221,7 @@
         send(quad).wait()
 
 
-def join(z, place, lists, received, half, inverse, table, smoothing):
+def join(z, place, lists, received, half, total, weights, smoothing):
     smem = pl.BlockSpec(memory_space=pltpu.SMEM)
     vmem = pl.BlockSpec(memory_space=pltpu.VMEM)
     shape = (z.regions, z.quads, z.sent, LANES)
@@ -241,7 +231,7 @@
         in_specs=[smem] * (1 + z.makers) + [vmem] * (z.makers + 3),
         out_specs=pl.BlockSpec(memory_space=pltpu.HBM),
         scratch_shapes=[
-            pltpu.VMEM((CAP * (z.makers - 1), TILES, PAIRS * FIELDS, LANES), jnp.float32),
+            pltpu.VMEM((CAP * (z.makers - 1), LINES, LANES), jnp.float32),
             pltpu.VMEM((FIELDS, TILES, LANES, LANES), jnp.float32),
             pltpu.VMEM((FIELDS, COLS + 8, LANES), jnp.float32),
             pltpu.VMEM((z.regions, z.quads, 8, LANES), jnp.float32),
@@ -251,7 +241,7 @@
         compiler_params=pltpu.CompilerParams(vmem_limit_bytes=VMEM),
         cost_estimate=pl.CostEstimate(flops=5_000_000, bytes_accessed=8_000_000, transcendentals=0),
         name="join",
-    )(place, *lists, *received, half, inverse, table, smoothing)
+    )(place, *lists, *received, half, total, weights, smoothing)
 
 
 SORT_STEPS = (
@@ -364,23 +354,17 @@
 
 def shards(patch_tiles, slot_lists, blend_table, smoothing, analysis):
     z = Sizes(lax.axis_size("region"))
-    place = lax.axis_index("region")
-    part = lax.rem(place, z.makers)
-    place = place.reshape(1)
+    place = lax.axis_index("region").reshape(1)
     turns = [
         [(i, i - i % z.makers + (i + k) % z.makers) for i in range(z.regions)] for k in range(1, z.makers)
     ]
+    tiles = patch_tiles.reshape(z.regions, CAP, FIELDS, PAIRS * TILES, LANES)
+    tiles = jnp.swapaxes(tiles, 2, 3).reshape(z.regions, CAP, LINES, LANES)
     lists = jnp.transpose(slot_lists, (2, 1, 0))
+    received = [lax.ppermute(tiles, "region", turn) for turn in turns]
     lists = [lists] + [lax.ppermute(lists, "region", turn) for turn in turns]
-    received = []
-    for k, turn in enumerate(turns, 1):
-        first = lax.rem(part + k, z.makers) * z.block
-        received.append(
-            lax.ppermute(lax.dynamic_slice_in_dim(patch_tiles, first, z.block, 0), "region", turn)
-        )
-    half, inverse = own_share(z, place, lists, patch_tiles, blend_table)
-    table = blend_table.reshape(blend_table.shape[0], PAIRS, COLS)
-    blocks = join(z, place, lists, received, half, inverse, table, smoothing)
+    shares = own_share(z, place, lists[0], tiles, blend_table)
+    blocks = join(z, place, lists, received, *shares, smoothing)
     moved = lax.all_to_all(blocks, "region", split_axis=0, concat_axis=0, tiled=True)
     outs = score(z, moved, jnp.swapaxes(analysis, 1, 2))
     return tuple(jnp.swapaxes(item, -1, -2) for item in outs)

time: 81.7 us -> 76.7 us (0.939)
  waiting for transfers between devices: 3.03 us -> 0.01 us
  Pallas kernels: 20.8 us -> 18.9 us
    ppermute x1, waiting for transfers between devices: 3.03 us -> 0.01 us  [shards(): lists = [lists] + [lax.ppermute(lists, 'region', turn) for turn in turns]]
    unnamed x11 -> x8, local copies, waits for them, and re-layouts: 0.2 us -> 2.73 us
    dynamic_slice x1 -> x0, local copies, waits for them, and re-layouts: 2.32 us -> none  [shards(): lax.dynamic_slice_in_dim(patch_tiles, first, z.block, 0)]
    pallas_call x1, Pallas kernels: 8.53 us -> 6.72 us  [own_share(): pl.pallas_call(functools.partial(own_kernel, z), out_shape=[jax.ShapeDtyp...]
  transfers between devices with their start and end apart: 2 -> 2, of which waited for: 1 -> 0; matrix products, arithmetic and copies ran while one was open for 0% -> 0% of each run, Pallas kernels for 11% -> 9%
where the time goes in v1:
time: 76.7 us; the launch traced here: 75.8 us
  blocking collectives  52.9 us (69%)
  Pallas kernels  18.9 us (25%)
  local copies, waits for them, and re-layouts  2.73 us (4%)
    all_to_all x1, blocking collectives, shards(): lax.all_to_all(blocks, 'region', split_axis=0, concat_axis=0, tiled=True)  52.9 us
    pallas_call x1, Pallas kernels, join(): pl.pallas_call(functools.partial(join_kernel, z), out_shape=pltpu.HBM(sha...  7.05 us
    pallas_call x1, Pallas kernels, own_share(): pl.pallas_call(functools.partial(own_kernel, z), out_shape=[jax.ShapeDtyp...  6.72 us
    pallas_call x1, Pallas kernels, score(): pl.pallas_call(functools.partial(score_kernel, z), out_shape=[jax.ShapeDt...  5.16 us
    unnamed x8, local copies, waits for them, and re-layouts  2.73 us
  transfers between devices with their start and end apart: 2, of which 0 were waited for; matrix products, arithmetic and copies ran while one was open for 0% of the time, Pallas kernels for 9%

profile of v1, /device:TPU:1, one launch (start us, length us, event | category | flops | bytes accessed | tf_op | source)
XLA Modules:
  0.0 75.8 jit_solution(15710781099035628937)
XLA Ops:
  0.6 0.0 copy-start.2
  0.6 0.1 collective-permute-start.1
  0.8 0.5 collective-permute-start
  1.2 0.0 copy-start.3
  1.2 0.7 copy-done.3
  1.9 6.7 %own_share.1 = (f32[8,4,2,16,896]{4,3,2,1,0:T(8,128)}, f32[8,2,16,896]{3,2,1,0:T(8,128)S(1)}, f32[7,256,128]{2,1,0:T(8,128)S(1)}) custom-call(s32[1]{0:T(128)} %bitcast.place.refs_0_, s32[3,2,16]{2,1,0:T(2,128)S(1)} %bitcast.12, bf16[16,2,448,128]{3,2,1,0:T(8,128)(2,1)} %bitcast.15, f32[14,14336]{1,0:T(8,128)} %table.1), custom_call_target="tpu_custom_call" | custom-call | flops 5000000 | bytes 8000000 | tf_op jit(solution)/shard_map/own_share/pallas_call | solution.py:136
  8.6 0.0 collective-permute-done.refs_2_
  8.6 0.0 collective-permute-done.1.refs_3_
  8.6 0.0 copy-done.2
  8.7 0.0 copy-start
  8.7 2.0 %copy-done = f32[8,4,2,16,896]{4,3,2,1,0:T(8,128)S(1)} copy-done((f32[8,4,2,16,896]{4,3,2,1,0:T(8,128)S(1)}, f32[8,4,2,16,896]{4,3,2,1,0:T(8,128)}, u32[]{:S(2)}) %copy-start) | copy-done | bytes 3670040
  10.7 7.1 %join.1 = bf16[16,2,240,128]{3,2,1,0:T(8,128)(2,1)} custom-call(s32[1]{0:T(128)} %bitcast.place.refs_0_, s32[3,2,16]{2,1,0:T(2,128)S(1)} %bitcast.13, s32[3,2,16]{2,1,0:T(2,128)S(1)} %collective-permute-done.refs_2_, bf16[16,2,448,128]{3,2,1,0:T(8,128)(2,1)} %collective-permute-done.1.refs_3_, f32[8,4,2,16,896]{4,3,2,1,0:T(8,128)S(1)} %copy-done, ...), custom_call_target="tpu_custom_call" | custom-call | flops 5000000 | bytes 8000000 | tf_op jit(solution)/shard_map/join/pallas_call | solution.py:228
  17.8 0.0 copy-start.1
  17.8 52.9 %all_to_all.5.blocks = bf16[16,2,240,128]{3,2,1,0:T(8,128)(2,1)S(1)} all-to-all(bf16[16,2,240,128]{3,2,1,0:T(8,128)(2,1)} %join.1), channel_id=1, replica_groups=mesh['groups'=2,'region'=16] {'region'}, dimensions={0} | all-to-all | bytes 3932160 | tf_op jit(solution)/shard_map/all_to_all | solution.py:368
  70.6 0.0 copy-done.1
  70.6 5.2 %score.1 = (bf16[4,56,512]{2,1,0:T(8,128)(2,1)}, bf16[2,4,56,512]{3,2,1,0:T(8,128)(2,1)}) custom-call(bf16[16,2,240,128]{3,2,1,0:T(8,128)(2,1)S(1)} %all_to_all.5.blocks, bf16[4,56,512]{2,1,0:T(8,128)(2,1)S(1)} %bitcast.10), custom_call_target="tpu_custom_call" | custom-call | tf_op jit(solution)/shard_map/score/pallas_call | solution.py:330
Async XLA Ops:
  0.6 8.0 %copy-start.2 = (f32[32,896]{1,0:T(8,128)S(1)}, f32[32,896]{1,0:T(8,128)}, u32[]{:S(2)}) copy-start(f32[32,896]{1,0:T(8,128)} %refs_7_.1) | copy-start | bytes 344068
  0.6 8.0 %collective-permute-start.1 = (bf16[16,2,448,128]{3,2,1,0:T(8,128)(2,1)}, bf16[16,2,448,128]{3,2,1,0:T(8,128)(2,1)}, u32[]{:S(2)}, u32[]{:S(2)}) collective-permute-start(bf16[16,2,448,128]{3,2,1,0:T(8,128)(2,1)} %bitcast.14), channel_id=1, source_target_pairs={{0,1},{1,0},{2,3},{3,2},{4,5},{5,4},{6,7},{7,6},{8,9},{9,8},{10,11... | collective-permute-start | bytes 11010056 | tf_op jit(solution)/shard_map/ppermute | solution.py:364
  0.8 7.9 %collective-permute-start = (s32[3,2,16]{2,1,0:T(2,128)}, s32[3,2,16]{2,1,0:T(2,128)S(1)}, u32[]{:S(2)}, u32[]{:S(2)}) collective-permute-start(s32[3,2,16]{2,1,0:T(2,128)} %bitcast.11), channel_id=1, source_target_pairs={{0,1},{1,0},{2,3},{3,2},{4,5},{5,4},{6,7},{7,6},{8,9},{9,8},{10,11... | collective-permute-start | bytes 1160 | tf_op jit(solution)/shard_map/ppermute | solution.py:365
  1.2 0.7 copy-start.3
  8.7 2.0 %copy-start = (f32[8,4,2,16,896]{4,3,2,1,0:T(8,128)S(1)}, f32[8,4,2,16,896]{4,3,2,1,0:T(8,128)}, u32[]{:S(2)}) copy-start(f32[8,4,2,16,896]{4,3,2,1,0:T(8,128)} %get-tuple-element.7.refs_4_) | copy-start | bytes 11010052
  17.8 52.9 %copy-start.1 = (bf16[4,512,56]{1,2,0:T(8,128)(2,1)S(1)}, bf16[4,512,56]{1,2,0:T(8,128)(2,1)}, u32[]{:S(2)}) copy-start(bf16[4,512,56]{1,2,0:T(8,128)(2,1)} %param.9) | copy-start | bytes 688132

commit v2 on v1

--- a/solution.py
+++ b/solution.py
@@ -20,7 +20,7 @@
 QUAD = LANES // ROWS
 MID = 0.11
 VMEM = 40 * 1024 * 1024
-MOST_VMEM = 52 * 1024 * 1024
+MOST_VMEM = 48 * 1024 * 1024
 
 
 def round_up(value, step):
@@ -84,14 +84,24 @@
         body(place_side if z.makers == 2 else place_any, range(1))
 
 
-def own_kernel(z, place, lists, tiles, table, half, total, weights, landed, staged, sems):
+def own_kernel(z, place, lists, tiles, table_hbm, smoothing, *refs):
+    half, (total, weights, strength, landed, staged, table, sems) = refs[:FIELDS], refs[FIELDS:]
     first = lax.rem(place[0], z.makers) * z.block
 
     def fetch(j):
         return pltpu.make_async_copy(tiles.at[first + j], landed.at[j], sems.at[j])
 
+    fetch_table = pltpu.make_async_copy(table_hbm, table, sems.at[z.block])
+    fetch_table.start()
     for j in range(z.block):
         fetch(j).start()
+    turned_strength = jnp.transpose(smoothing[...] - MID)
+    for dest in range(z.regions):
+        for g in range(z.span // 8):
+            top = z.width * dest + 8 * g
+            count, at = min(8, COLS - top), ROWS * (g % QUAD)
+            strength[dest, g // QUAD, 0:count, at : at + ROWS] = turned_strength[top : top + count]
+    fetch_table.wait()
     kinds = table.shape[0]
     for k in range(PAIRS):
         for t in range(TILES):
@@ -121,7 +131,7 @@
                 for slot, column, weight in entries:
                     a, b = place_tile(staged_field(staged.at[slot], field) * weight, column)
                     even, odd = even + a, odd + b
-                half[j, field, 0], half[j, field, 1] = even, odd
+                half[field][j, 0], half[field][j, 1] = even, odd
 
         either_kind(z, lists[0, 1, first + j] >= 0, body)
         return carry
@@ -129,42 +139,37 @@
     lax.fori_loop(0, z.block, region, 0)
 
 
-def own_share(z, place, lists, tiles, table):
+def own_share(z, place, lists, tiles, table, smoothing):
     smem = pl.BlockSpec(memory_space=pltpu.SMEM)
     vmem = pl.BlockSpec(memory_space=pltpu.VMEM)
+    hbm = pl.BlockSpec(memory_space=pltpu.HBM)
     kinds = round_up(table.shape[0], 8)
     return pl.pallas_call(
         functools.partial(own_kernel, z),
         out_shape=[
-            jax.ShapeDtypeStruct((z.block, FIELDS, 2, PAIRS, COLS), jnp.float32),
-            jax.ShapeDtypeStruct((z.block, 2, PAIRS, COLS), jnp.float32),
+            *[jax.ShapeDtypeStruct((z.block, 2, PAIRS, COLS), jnp.float32)] * (FIELDS + 1),
             jax.ShapeDtypeStruct((TILES, kinds * PAIRS, LANES), jnp.float32),
-        ],
-        in_specs=[smem, smem, pl.BlockSpec(memory_space=pltpu.HBM), vmem],
-        out_specs=[vmem] * 3,
+            jax.ShapeDtypeStruct((z.regions, z.quads, 8, LANES), jnp.float32),
+        ],
+        in_specs=[smem, smem, hbm, hbm, vmem],
+        out_specs=[vmem] * (FIELDS + 3),
         scratch_shapes=[
             pltpu.VMEM((z.block, CAP, LINES, LANES), jnp.bfloat16),
             pltpu.VMEM((CAP, LINES, LANES), jnp.float32),
-            pltpu.SemaphoreType.DMA((z.block,)),
+            pltpu.VMEM(table.shape, jnp.float32),
+            pltpu.SemaphoreType.DMA((z.block + 1,)),
         ],
         compiler_params=pltpu.CompilerParams(vmem_limit_bytes=MOST_VMEM),
         cost_estimate=pl.CostEstimate(flops=5_000_000, bytes_accessed=8_000_000, transcendentals=0),
         name="own_share",
-    )(place, lists, tiles, table)
+    )(place, lists, tiles, table, smoothing)
 
 
 def join_kernel(z, *refs):
     place, lists, refs = refs[0], refs[1 : 1 + z.makers], refs[1 + z.makers :]
     received, refs = refs[: z.makers - 1], refs[z.makers - 1 :]
-    half, total, weights, smoothing, out, staged, lines, turned, strength, blocks, sems = refs
+    half, (total, weights, strength, out, staged, lines, turned, blocks, sems) = refs[:FIELDS], refs[FIELDS:]
     first = lax.rem(place[0], z.makers) * z.block
-
-    turned_strength = jnp.transpose(smoothing[...] - MID)
-    for dest in range(z.regions):
-        for g in range(z.span // 8):
-            top = z.width * dest + 8 * g
-            count, at = min(8, COLS - top), ROWS * (g % QUAD)
-            strength[dest, g // QUAD, 0:count, at : at + ROWS] = turned_strength[top : top + count]
 
     def send(quad):
         return pltpu.make_async_copy(blocks.at[:, quad], out.at[:, quad], sems.at[quad])
@@ -188,7 +193,7 @@
                     even, odd = even + a, odd + b
                 even_inverse, odd_inverse = 1.0 / even, 1.0 / odd
                 for field in range(FIELDS):
-                    even, odd = half[j, field, 0], half[j, field, 1]
+                    even, odd = half[field][j, 0], half[field][j, 1]
                     for index, column, weight in entries:
                         a, b = place_tile(staged_field(staged.at[index], field) * weight, column)
                         even, odd = even + a, odd + b
@@ -221,27 +226,26 @@
         send(quad).wait()
 
 
-def join(z, place, lists, received, half, total, weights, smoothing):
+def join(z, place, lists, received, shares):
     smem = pl.BlockSpec(memory_space=pltpu.SMEM)
     vmem = pl.BlockSpec(memory_space=pltpu.VMEM)
     shape = (z.regions, z.quads, z.sent, LANES)
     return pl.pallas_call(
         functools.partial(join_kernel, z),
         out_shape=pltpu.HBM(shape, jnp.bfloat16),
-        in_specs=[smem] * (1 + z.makers) + [vmem] * (z.makers + 3),
+        in_specs=[smem] * (1 + z.makers) + [vmem] * (z.makers - 1 + len(shares)),
         out_specs=pl.BlockSpec(memory_space=pltpu.HBM),
         scratch_shapes=[
             pltpu.VMEM((CAP * (z.makers - 1), LINES, LANES), jnp.float32),
             pltpu.VMEM((FIELDS, TILES, LANES, LANES), jnp.float32),
             pltpu.VMEM((FIELDS, COLS + 8, LANES), jnp.float32),
-            pltpu.VMEM((z.regions, z.quads, 8, LANES), jnp.float32),
             pltpu.VMEM(shape, jnp.bfloat16),
             pltpu.SemaphoreType.DMA((z.quads,)),
         ],
         compiler_params=pltpu.CompilerParams(vmem_limit_bytes=VMEM),
         cost_estimate=pl.CostEstimate(flops=5_000_000, bytes_accessed=8_000_000, transcendentals=0),
         name="join",
-    )(place, *lists, *received, half, total, weights, smoothing)
+    )(place, *lists, *received, *shares)
 
 
 SORT_STEPS = (
@@ -363,8 +367,8 @@
     lists = jnp.transpose(slot_lists, (2, 1, 0))
     received = [lax.ppermute(tiles, "region", turn) for turn in turns]
     lists = [lists] + [lax.ppermute(lists, "region", turn) for turn in turns]
-    shares = own_share(z, place, lists[0], tiles, blend_table)
-    blocks = join(z, place, lists, received, *shares, smoothing)
+    shares = own_share(z, place, lists[0], tiles, blend_table, smoothing)
+    blocks = join(z, place, lists, received, shares)
     moved = lax.all_to_all(blocks, "region", split_axis=0, concat_axis=0, tiled=True)
     outs = score(z, moved, jnp.swapaxes(analysis, 1, 2))
     return tuple(jnp.swapaxes(item, -1, -2) for item in outs)

time: 76.7 us -> 74.4 us (0.970)
  Pallas kernels: 18.9 us -> 15.8 us
  blocking collectives: 52.9 us -> 55.3 us
  local copies, waits for them, and re-layouts: 2.73 us -> 1.59 us
    all_to_all x1, blocking collectives: 52.9 us -> 55.3 us  [shards(): lax.all_to_all(blocks, 'region', split_axis=0, concat_axis=0, tiled=True)]
    pallas_call x1, Pallas kernels: 6.72 us -> 4.45 us  [own_share(): pl.pallas_call(functools.partial(own_kernel, z), out_shape=[*[jax.ShapeDt...]
    unnamed x8, local copies, waits for them, and re-layouts: 2.73 us -> 1.59 us
    pallas_call x1, Pallas kernels: 7.05 us -> 6.16 us  [join(): pl.pallas_call(functools.partial(join_kernel, z), out_shape=pltpu.HBM(sha...]
  transfers between devices with their start and end apart: 2 -> 2, of which waited for: 0 -> 1; matrix products, arithmetic and copies ran while one was open for 0% -> 0% of each run, Pallas kernels for 9% -> 6%
where the time goes in v2:
time: 74.4 us; the launch traced here: 74.1 us
  blocking collectives  55.3 us (74%)
  Pallas kernels  15.8 us (21%)
  local copies, waits for them, and re-layouts  1.59 us (2%)
    all_to_all x1, blocking collectives, shards(): lax.all_to_all(blocks, 'region', split_axis=0, concat_axis=0, tiled=True)  55.3 us
    pallas_call x1, Pallas kernels, join(): pl.pallas_call(functools.partial(join_kernel, z), out_shape=pltpu.HBM(sha...  6.16 us
    pallas_call x1, Pallas kernels, score(): pl.pallas_call(functools.partial(score_kernel, z), out_shape=[jax.ShapeDt...  5.18 us
    pallas_call x1, Pallas kernels, own_share(): pl.pallas_call(functools.partial(own_kernel, z), out_shape=[*[jax.ShapeDt...  4.45 us
    unnamed x8, local copies, waits for them, and re-layouts  1.59 us
  transfers between devices with their start and end apart: 2, of which 1 were waited for; matrix products, arithmetic and copies ran while one was open for 0% of the time, Pallas kernels for 6%

profile of v2, /device:TPU:1, one launch (start us, length us, event | category | flops | bytes accessed | tf_op | source)
XLA Modules:
  0.0 74.1 jit_solution(1819550226359392258)
XLA Ops:
  0.6 0.0 copy-start.3
  0.6 0.1 collective-permute-start.1
  0.8 0.5 collective-permute-start
  1.2 0.0 copy-start.1
  1.2 0.9 %copy-done.1 = f32[32,896]{1,0:T(8,128)S(1)} copy-done((f32[32,896]{1,0:T(8,128)S(1)}, f32[32,896]{1,0:T(8,128)}, u32[]{:S(2)}) %copy-start.1) | copy-done | bytes 114712
  2.1 0.0 copy-start.2
  2.1 0.7 copy-done.2
  2.8 4.4 %own_share.1 = (f32[8,2,16,896]{3,2,1,0:T(8,128)S(1)}, f32[8,2,16,896]{3,2,1,0:T(8,128)S(1)}, f32[8,2,16,896]{3,2,1,0:T(8,128)S(1)}, f32[8,2,16,896]{3,2,1,0:T(8...) custom-call(s32[1]{0:T(128)} %bitcast.place.refs_0_, ...), custom_call_target="tpu_custom_call" | custom-call | flops 5000000 | bytes 8000000 | tf_op jit(solution)/shard_map/own_share/pallas_call | solution.py:147
  7.3 0.0 collective-permute-done.refs_2_
  7.3 0.2 collective-permute-done.1.refs_3_
  7.5 0.0 copy-done.3
  7.5 6.2 %join.1 = bf16[16,2,240,128]{3,2,1,0:T(8,128)(2,1)} custom-call(s32[1]{0:T(128)} %bitcast.place.refs_0_, s32[3,2,16]{2,1,0:T(2,128)S(1)} %bitcast.13, s32[3,2,16]{2,1,0:T(2,128)S(1)} %collective-permute-done.refs_2_, bf16[16,2,448,128]{3,2,1,0:T(8,128)(2,1)} %collective-permute-done.1.refs_3_, f32[8,2,16,896]{3,2,1,0:T(8,128)S(1)} %get-tuple-element.11.refs_4_, ...), custom_call_target="tpu_custom_call" | custom-call | flops 5000000 | bytes 8000000 | tf_op jit(solution)/shard_map/join/pallas_call | solution.py:233
  13.6 0.0 copy-start
  13.6 55.3 %all_to_all.5.blocks = bf16[16,2,240,128]{3,2,1,0:T(8,128)(2,1)S(1)} all-to-all(bf16[16,2,240,128]{3,2,1,0:T(8,128)(2,1)} %join.1), channel_id=1, replica_groups=mesh['groups'=2,'region'=16] {'region'}, dimensions={0} | all-to-all | bytes 3932160 | tf_op jit(solution)/shard_map/all_to_all | solution.py:372
  68.9 0.0 copy-done
  68.9 5.2 %score.1 = (bf16[4,56,512]{2,1,0:T(8,128)(2,1)}, bf16[2,4,56,512]{3,2,1,0:T(8,128)(2,1)}) custom-call(bf16[16,2,240,128]{3,2,1,0:T(8,128)(2,1)S(1)} %all_to_all.5.blocks, bf16[4,56,512]{2,1,0:T(8,128)(2,1)S(1)} %bitcast.10), custom_call_target="tpu_custom_call" | custom-call | tf_op jit(solution)/shard_map/score/pallas_call | solution.py:334
Async XLA Ops:
  0.6 6.8 %copy-start.3 = (s32[16,2,3]{0,1,2:T(2,128)S(1)}, s32[16,2,3]{0,1,2:T(2,128)}, u32[]{:S(2)}) copy-start(s32[16,2,3]{0,1,2:T(2,128)} %param.6) | copy-start | bytes 1156
  0.6 6.8 %collective-permute-start.1 = (bf16[16,2,448,128]{3,2,1,0:T(8,128)(2,1)}, bf16[16,2,448,128]{3,2,1,0:T(8,128)(2,1)}, u32[]{:S(2)}, u32[]{:S(2)}) collective-permute-start(bf16[16,2,448,128]{3,2,1,0:T(8,128)(2,1)} %bitcast.14), channel_id=1, source_target_pairs={{0,1},{1,0},{2,3},{3,2},{4,5},{5,4},{6,7},{7,6},{8,9},{9,8},{10,11... | collective-permute-start | bytes 11010056 | tf_op jit(solution)/shard_map/ppermute | solution.py:368
  0.8 6.5 %collective-permute-start = (s32[3,2,16]{2,1,0:T(2,128)}, s32[3,2,16]{2,1,0:T(2,128)S(1)}, u32[]{:S(2)}, u32[]{:S(2)}) collective-permute-start(s32[3,2,16]{2,1,0:T(2,128)} %bitcast.11), channel_id=1, source_target_pairs={{0,1},{1,0},{2,3},{3,2},{4,5},{5,4},{6,7},{7,6},{8,9},{9,8},{10,11... | collective-permute-start | bytes 1160 | tf_op jit(solution)/shard_map/ppermute | solution.py:369
  1.2 0.9 %copy-start.1 = (f32[32,896]{1,0:T(8,128)S(1)}, f32[32,896]{1,0:T(8,128)}, u32[]{:S(2)}) copy-start(f32[32,896]{1,0:T(8,128)} %smoothing.1) | copy-start | bytes 344068
  2.1 0.7 copy-start.2
  13.6 55.3 %copy-start = (bf16[4,512,56]{1,2,0:T(8,128)(2,1)S(1)}, bf16[4,512,56]{1,2,0:T(8,128)(2,1)}, u32[]{:S(2)}) copy-start(bf16[4,512,56]{1,2,0:T(8,128)(2,1)} %param.9) | copy-start | bytes 688132

commit v3 on v2

--- a/solution.py
+++ b/solution.py
@@ -27,6 +27,12 @@
     return -(-value // step) * step
 
 
+def swap_order(regions):
+    far, near = list(range(regions // 2, regions)), list(range(1, regions // 2))
+    near = near[regions // 4 - 1 :] + near[: regions // 4 - 1]
+    return [0] + [item for pair in zip(far, near + [None]) for item in pair if item is not None]
+
+
 class Sizes:
     def __init__(self, regions):
         self.regions = regions
@@ -37,6 +43,7 @@
         self.span = round_up(self.width, 8)
         self.rows = regions * ROWS
         self.main = round_up(FIELDS * self.span, 16)
+        self.offsets = swap_order(regions)
         self.sent = self.main + 16
 
 
@@ -168,11 +175,13 @@
 def join_kernel(z, *refs):
     place, lists, refs = refs[0], refs[1 : 1 + z.makers], refs[1 + z.makers :]
     received, refs = refs[: z.makers - 1], refs[z.makers - 1 :]
-    half, (total, weights, strength, out, staged, lines, turned, blocks, sems) = refs[:FIELDS], refs[FIELDS:]
-    first = lax.rem(place[0], z.makers) * z.block
-
-    def send(quad):
-        return pltpu.make_async_copy(blocks.at[:, quad], out.at[:, quad], sems.at[quad])
+    half, (total, weights, strength), outs = refs[:FIELDS], refs[FIELDS : FIELDS + 3], refs[FIELDS + 3 : -5]
+    staged, lines, turned, blocks, sems = refs[-5:]
+    me = place[0]
+    first = lax.rem(me, z.makers) * z.block
+
+    def send(i, quad):
+        return pltpu.make_async_copy(blocks.at[i, quad], outs[i].at[quad], sems.at[i, quad])
 
     for quad in range(z.quads):
 
@@ -210,37 +219,41 @@
         for field in range(FIELDS):
             for t in range(TILES):
                 turned[field, LANES * t : LANES * (t + 1), :] = jnp.transpose(lines[field, t])
-        for dest in range(z.regions):
-            top = z.width * dest
+        for i, offset in enumerate(z.offsets):
+            dest = me ^ offset
+            top = dest * z.width
+            if z.width % 8 == 0:
+                top = pl.multiple_of(top, 8)
             for low in range(0, FIELDS, 2):
-                block = [turned[field, top : top + z.span, :] for field in (low, low + 1)]
-                blocks[dest, quad, low * z.span : (low + 2) * z.span, :] = jnp.concatenate(block, 0).astype(
+                block = [turned[field, pl.ds(top, z.span), :] for field in (low, low + 1)]
+                blocks[i, quad, low * z.span : (low + 2) * z.span, :] = jnp.concatenate(block, 0).astype(
                     jnp.bfloat16
                 )
-            ends = (max(top - 1, 0), min(top + z.width, COLS - 1))
-            edge = [turned[field, end : end + 1, :] for field in range(FIELDS) for end in ends]
+            ends = (jnp.maximum(top - 1, 0), jnp.minimum(top + z.width, COLS - 1))
+            edge = [turned[field, pl.ds(end, 1), :] for field in range(FIELDS) for end in ends]
             edge.append(strength[dest, quad])
-            blocks[dest, quad, z.main : z.sent, :] = jnp.concatenate(edge, 0).astype(jnp.bfloat16)
-        send(quad).start()
+            blocks[i, quad, z.main : z.sent, :] = jnp.concatenate(edge, 0).astype(jnp.bfloat16)
+            send(i, quad).start()
     for quad in range(z.quads):
-        send(quad).wait()
+        for i in range(z.regions):
+            send(i, quad).wait()
 
 
 def join(z, place, lists, received, shares):
     smem = pl.BlockSpec(memory_space=pltpu.SMEM)
     vmem = pl.BlockSpec(memory_space=pltpu.VMEM)
-    shape = (z.regions, z.quads, z.sent, LANES)
+    shape = (z.quads, z.sent, LANES)
     return pl.pallas_call(
         functools.partial(join_kernel, z),
-        out_shape=pltpu.HBM(shape, jnp.bfloat16),
+        out_shape=[pltpu.HBM(shape, jnp.bfloat16)] * z.regions,
         in_specs=[smem] * (1 + z.makers) + [vmem] * (z.makers - 1 + len(shares)),
-        out_specs=pl.BlockSpec(memory_space=pltpu.HBM),
+        out_specs=[pl.BlockSpec(memory_space=pltpu.HBM)] * z.regions,
         scratch_shapes=[
             pltpu.VMEM((CAP * (z.makers - 1), LINES, LANES), jnp.float32),
             pltpu.VMEM((FIELDS, TILES, LANES, LANES), jnp.float32),
             pltpu.VMEM((FIELDS, COLS + 8, LANES), jnp.float32),
-            pltpu.VMEM(shape, jnp.bfloat16),
-            pltpu.SemaphoreType.DMA((z.quads,)),
+            pltpu.VMEM((z.regions, *shape), jnp.bfloat16),
+            pltpu.SemaphoreType.DMA((z.regions, z.quads)),
         ],
         compiler_params=pltpu.CompilerParams(vmem_limit_bytes=VMEM),
         cost_estimate=pl.CostEstimate(flops=5_000_000, bytes_accessed=8_000_000, transcendentals=0),
@@ -259,37 +272,43 @@
 STEP_FIELDS = 2
 
 
-def score_kernel(z, blocks, analysis, crps, spread, strength, edges, padded):
+def score_kernel(z, place, *refs):
+    blocks = dict(zip(z.offsets, refs))
+    analysis, crps, spread, strength, edges, padded = refs[z.regions :]
+    me = place[0]
     step = pl.program_id(0)
     rows = z.rows
-    sources = [(source, quad) for source in range(z.regions) for quad in range(z.quads)]
+
+    def lanes_of(offset, quad):
+        at = (lax.rem(me ^ offset, z.makers) * z.quads + quad) * LANES
+        return pl.ds(pl.multiple_of(at, LANES), LANES)
 
     @pl.when(step == 0)
     def _():
         slot = lax.broadcasted_iota(jnp.int32, (8, LANES), 1) // ROWS
         for low in range(0, z.regions, QUAD):
+            offsets = range(low, low + QUAD)
+            slots = [lax.rem(me ^ offset, QUAD) for offset in offsets]
+            at = pl.multiple_of(lax.div(me ^ low, QUAD) * LANES, LANES)
             for quad in range(z.quads):
-                tails = [
-                    blocks[source, quad, z.main : z.sent, :].astype(jnp.float32)
-                    for source in range(low, low + QUAD)
-                ]
-                for i, tail in enumerate(tails):
-                    at = ((low + i) % z.makers * z.quads + quad) * LANES
-                    edges[(low + i) // z.makers, :, at : at + LANES] = tail[0:8]
+                tails = [blocks[offset][quad, z.main : z.sent, :].astype(jnp.float32) for offset in offsets]
+                for offset, tail in zip(offsets, tails):
+                    edges[offset // z.makers, :, lanes_of(offset, quad)] = tail[0:8]
                 for g in range(quad * QUAD, min((quad + 1) * QUAD, z.span // 8)):
                     joined = jnp.zeros((8, LANES), jnp.float32)
-                    for i, tail in enumerate(tails):
-                        near = pltpu.roll(tail[8:16], (i - g) % QUAD * ROWS, 1)
+                    for i, tail in zip(slots, tails):
+                        near = pltpu.roll(tail[8:16], lax.rem(i + QUAD - g % QUAD, QUAD) * ROWS, 1)
                         joined = jnp.where(slot == i, near, joined)
-                    at = low // QUAD * LANES
-                    strength[8 * g : 8 * (g + 1), at : at + LANES] = joined + MID
+                    strength[8 * g : 8 * (g + 1), pl.ds(at, LANES)] = joined + MID
 
     top = pl.multiple_of(step * STEP_FIELDS * z.span, 16)
-    for source, quad in sources:
-        at = (source % z.makers * z.quads + quad) * LANES
-        values = blocks[source, quad, pl.ds(top, STEP_FIELDS * z.span), :].astype(jnp.float32)
-        for f in range(STEP_FIELDS):
-            padded[source // z.makers, f, 8 : 8 + z.span, at : at + LANES] = values[f * z.span : (f + 1) * z.span]
+    for offset in range(z.regions):
+        for quad in range(z.quads):
+            values = blocks[offset][quad, pl.ds(top, STEP_FIELDS * z.span), :].astype(jnp.float32)
+            for f in range(STEP_FIELDS):
+                padded[offset // z.makers, f, 8 : 8 + z.span, lanes_of(offset, quad)] = values[
+                    f * z.span : (f + 1) * z.span
+                ]
     for sample in range(SAMPLES):
         for f in range(STEP_FIELDS):
             low = 2 * (step * STEP_FIELDS + f)
@@ -329,7 +348,7 @@
             spread[1, f, low:high, :] = ((average - target) ** 2).astype(jnp.bfloat16)
 
 
-def score(z, blocks, analysis):
+def score(z, place, blocks, analysis):
     width, rows = z.width, z.rows
     return pl.pallas_call(
         functools.partial(score_kernel, z),
@@ -338,10 +357,9 @@
             jax.ShapeDtypeStruct((2, FIELDS, width, rows), jnp.bfloat16),
         ],
         grid=(FIELDS // STEP_FIELDS,),
-        in_specs=[
-            pl.BlockSpec(blocks.shape, lambda i: (0, 0, 0, 0)),
-            pl.BlockSpec((STEP_FIELDS, width, rows), lambda i: (i, 0, 0)),
-        ],
+        in_specs=[pl.BlockSpec(memory_space=pltpu.SMEM)]
+        + [pl.BlockSpec(blocks[0].shape, lambda i: (0, 0, 0))] * z.regions
+        + [pl.BlockSpec((STEP_FIELDS, width, rows), lambda i: (i, 0, 0))],
         out_specs=[
             pl.BlockSpec((STEP_FIELDS, width, rows), lambda i: (i, 0, 0)),
             pl.BlockSpec((2, STEP_FIELDS, width, rows), lambda i: (0, i, 0, 0)),
@@ -353,7 +371,7 @@
         ],
         compiler_params=pltpu.CompilerParams(vmem_limit_bytes=VMEM),
         name="score",
-    )(blocks, analysis)
+    )(place, *blocks, analysis)
 
 
 def shards(patch_tiles, slot_lists, blend_table, smoothing, analysis):
@@ -369,8 +387,11 @@
     lists = [lists] + [lax.ppermute(lists, "region", turn) for turn in turns]
     shares = own_share(z, place, lists[0], tiles, blend_table, smoothing)
     blocks = join(z, place, lists, received, shares)
-    moved = lax.all_to_all(blocks, "region", split_axis=0, concat_axis=0, tiled=True)
-    outs = score(z, moved, jnp.swapaxes(analysis, 1, 2))
+    moved = [blocks[0]] + [
+        lax.ppermute(block, "region", [(i, i ^ offset) for i in range(z.regions)])
+        for block, offset in zip(blocks[1:], z.offsets[1:])
+    ]
+    outs = score(z, place, moved, jnp.swapaxes(analysis, 1, 2))
     return tuple(jnp.swapaxes(item, -1, -2) for item in outs)
 
 

time: 74.4 us -> 69.2 us (0.930)
  the two profiles are of different devices: /device:TPU:1 before, /device:TPU:17 now
where the time goes in v3:
time: 69.2 us; the launch traced here: 68.9 us
  starting transfers between devices  26.8 us (39%)
  waiting for transfers between devices  20.9 us (30%)
  Pallas kernels  18 us (26%)
  local copies, waits for them, and re-layouts  2.49 us (4%)
  between operations  0.72 us (1%)
    ppermute x15, starting transfers between devices, shards(): lax.ppermute(block, 'region', [(i, i ^ offset) for i in range(z.regions)])  25.9 us
    ppermute x15, waiting for transfers between devices, shards(): lax.ppermute(block, 'region', [(i, i ^ offset) for i in range(z.regions)])  20.9 us
    pallas_call x1, Pallas kernels, join(): pl.pallas_call(functools.partial(join_kernel, z), out_shape=[pltpu.HBM(sh...  7.22 us
    pallas_call x1, Pallas kernels, score(): pl.pallas_call(functools.partial(score_kernel, z), out_shape=[jax.ShapeDt...  5.69 us
    pallas_call x1, Pallas kernels, own_share(): pl.pallas_call(functools.partial(own_kernel, z), out_shape=[*[jax.ShapeDt...  5.12 us
    unnamed x10, local copies, waits for them, and re-layouts  2.49 us
  transfers between devices with their start and end apart: 17, of which 6 were waited for; matrix products, arithmetic and copies ran while one was open for 0% of the time, Pallas kernels for 7%

profile of v3, /device:TPU:17, one launch (start us, length us, event | category | flops | bytes accessed | tf_op | source)
XLA Modules:
  0.0 68.9 jit_solution(13688153418386204440)
XLA Ops:
  0.6 0.7 %collective-permute-start.1 = (bf16[16,2,448,128]{3,2,1,0:T(8,128)(2,1)}, bf16[16,2,448,128]{3,2,1,0:T(8,128)(2,1)}, u32[]{:S(2)}, u32[]{:S(2)}) collective-permute-start(bf16[16,2,448,128]{3,2,1,0:T(8,128)(2,1)} %bitcast.14), channel_id=1, source_target_pairs={{0,1},{1,0},{2,3},{3,2},{4,5},{5,4},{6,7},{7,6},{8,9},{9,8},{10,11... | collective-permute-start | bytes 11010056 | tf_op jit(solution)/shard_map/ppermute | solution.py:386
  1.5 0.9 %copy-done.2 = f32[32,896]{1,0:T(8,128)S(1)} copy-done((f32[32,896]{1,0:T(8,128)S(1)}, f32[32,896]{1,0:T(8,128)}, u32[]{:S(2)}) %copy-start.2) | copy-done | bytes 114712
  2.4 0.7 copy-done.3
  3.0 5.1 %own_share.1 = (f32[8,2,16,896]{3,2,1,0:T(8,128)S(1)}, f32[8,2,16,896]{3,2,1,0:T(8,128)S(1)}, f32[8,2,16,896]{3,2,1,0:T(8,128)S(1)}, f32[8,2,16,896]{3,2,1,0:T(8...) custom-call(s32[1]{0:T(128)} %bitcast.place.refs_0_, ...), custom_call_target="tpu_custom_call" | custom-call | flops 5000000 | bytes 8000000 | tf_op jit(solution)/shard_map/own_share/pallas_call | solution.py:154
  8.2 7.2 %join.1 = (bf16[2,240,128]{2,1,0:T(8,128)(2,1)}, bf16[2,240,128]{2,1,0:T(8,128)(2,1)}, bf16[2,240,128]{2,1,0:T(8,128)(2,1)}, bf16[2,240,128]{2,1,0:T(8,128)(2,1)...) custom-call(s32[1]{0:T(128)} %bitcast.place.refs_0_, ...), custom_call_target="tpu_custom_call" | custom-call | flops 5000000 | bytes 8000000 | tf_op jit(solution)/shard_map/join/pallas_call | solution.py:246
  15.5 1.4 %collective-permute-start.3 = (bf16[2,240,128]{2,1,0:T(8,128)(2,1)}, bf16[2,240,128]{2,1,0:T(8,128)(2,1)S(1)}, u32[]{:S(2)}, u32[]{:S(2)}) collective-permute-start(bf16[2,240,128]{2,1,0:T(8,128)(2,1)} %get-tuple-element.36), channel_id=1, source_target_pairs={{0,4},{1,5},{2,6},{3,7},{4,0},{5,1},{6,2},{7,3},{8,12},{9,13},{10,... | collective-permute-start | bytes 368648 | tf_op jit(solution)/shard_map/ppermute | solution.py:391
  16.9 3.2 %collective-permute-start.4 = (bf16[2,240,128]{2,1,0:T(8,128)(2,1)}, bf16[2,240,128]{2,1,0:T(8,128)(2,1)S(1)}, u32[]{:S(2)}, u32[]{:S(2)}) collective-permute-start(bf16[2,240,128]{2,1,0:T(8,128)(2,1)} %get-tuple-element.37), channel_id=1, source_target_pairs={{0,9},{1,8},{2,11},{3,10},{4,13},{5,12},{6,15},{7,14},{8,1},{9,0},... | collective-permute-start | bytes 368648 | tf_op jit(solution)/shard_map/ppermute | solution.py:391
  20.1 1.1 %collective-permute-start.6 = (bf16[2,240,128]{2,1,0:T(8,128)(2,1)}, bf16[2,240,128]{2,1,0:T(8,128)(2,1)S(1)}, u32[]{:S(2)}, u32[]{:S(2)}) collective-permute-start(bf16[2,240,128]{2,1,0:T(8,128)(2,1)} %get-tuple-element.39), channel_id=1, source_target_pairs={{0,10},{1,11},{2,8},{3,9},{4,14},{5,15},{6,12},{7,13},{8,2},{9,3},... | collective-permute-start | bytes 368648 | tf_op jit(solution)/shard_map/ppermute | solution.py:391
  21.2 6.2 %collective-permute-start.7 = (bf16[2,240,128]{2,1,0:T(8,128)(2,1)}, bf16[2,240,128]{2,1,0:T(8,128)(2,1)S(1)}, u32[]{:S(2)}, u32[]{:S(2)}) collective-permute-start(bf16[2,240,128]{2,1,0:T(8,128)(2,1)} %get-tuple-element.40), channel_id=1, source_target_pairs={{0,6},{1,7},{2,4},{3,5},{4,2},{5,3},{6,0},{7,1},{8,14},{9,15},{10,... | collective-permute-start | bytes 368648 | tf_op jit(solution)/shard_map/ppermute | solution.py:391
  27.4 0.7 %collective-permute-start.8 = (bf16[2,240,128]{2,1,0:T(8,128)(2,1)}, bf16[2,240,128]{2,1,0:T(8,128)(2,1)S(1)}, u32[]{:S(2)}, u32[]{:S(2)}) collective-permute-start(bf16[2,240,128]{2,1,0:T(8,128)(2,1)} %get-tuple-element.41), channel_id=1, source_target_pairs={{0,11},{1,10},{2,9},{3,8},{4,15},{5,14},{6,13},{7,12},{8,3},{9,2},... | collective-permute-start | bytes 368648 | tf_op jit(solution)/shard_map/ppermute | solution.py:391
  28.1 4.8 %collective-permute-start.9 = (bf16[2,240,128]{2,1,0:T(8,128)(2,1)}, bf16[2,240,128]{2,1,0:T(8,128)(2,1)S(1)}, u32[]{:S(2)}, u32[]{:S(2)}) collective-permute-start(bf16[2,240,128]{2,1,0:T(8,128)(2,1)} %get-tuple-element.42), channel_id=1, source_target_pairs={{0,7},{1,6},{2,5},{3,4},{4,3},{5,2},{6,1},{7,0},{8,15},{9,14},{10,... | collective-permute-start | bytes 368648 | tf_op jit(solution)/shard_map/ppermute | solution.py:391
  33.0 2.5 %collective-permute-start.11 = (bf16[2,240,128]{2,1,0:T(8,128)(2,1)}, bf16[2,240,128]{2,1,0:T(8,128)(2,1)S(1)}, u32[]{:S(2)}, u32[]{:S(2)}) collective-permute-start(bf16[2,240,128]{2,1,0:T(8,128)(2,1)} %get-tuple-element.44), channel_id=1, source_target_pairs={{0,1},{1,0},{2,3},{3,2},{4,5},{5,4},{6,7},{7,6},{8,9},{9,8},{10,11... | collective-permute-start | bytes 368648 | tf_op jit(solution)/shard_map/ppermute | solution.py:391
  35.5 2.1 %collective-permute-start.12 = (bf16[2,240,128]{2,1,0:T(8,128)(2,1)}, bf16[2,240,128]{2,1,0:T(8,128)(2,1)S(1)}, u32[]{:S(2)}, u32[]{:S(2)}) collective-permute-start(bf16[2,240,128]{2,1,0:T(8,128)(2,1)} %get-tuple-element.45), channel_id=1, source_target_pairs={{0,13},{1,12},{2,15},{3,14},{4,9},{5,8},{6,11},{7,10},{8,5},{9,4},... | collective-permute-start | bytes 368648 | tf_op jit(solution)/shard_map/ppermute | solution.py:391
  37.5 2.5 %collective-permute-done.8.refs_7_ = bf16[2,240,128]{2,1,0:T(8,128)(2,1)S(1)} collective-permute-done((bf16[2,240,128]{2,1,0:T(8,128)(2,1)}, bf16[2,240,128]{2,1,0:T(8,128)(2,1)S(1)}, u32[]{:S(2)}, u32[]{:S(2)}) %collective-permute-start.8) | collective-permute-done | bytes 122912 | tf_op jit(solution)/shard_map/ppermute | solution.py:391
  40.0 0.2 collective-permute-start.13
  40.3 1.3 %collective-permute-done.9.refs_8_ = bf16[2,240,128]{2,1,0:T(8,128)(2,1)S(1)} collective-permute-done((bf16[2,240,128]{2,1,0:T(8,128)(2,1)}, bf16[2,240,128]{2,1,0:T(8,128)(2,1)S(1)}, u32[]{:S(2)}, u32[]{:S(2)}) %collective-permute-start.9) | collective-permute-done | bytes 122912 | tf_op jit(solution)/shard_map/ppermute | solution.py:391
  41.6 0.7 collective-permute-start.14
  42.3 6.0 %collective-permute-done.10.refs_9_ = bf16[2,240,128]{2,1,0:T(8,128)(2,1)S(1)} collective-permute-done((bf16[2,240,128]{2,1,0:T(8,128)(2,1)}, bf16[2,240,128]{2,1,0:T(8,128)(2,1)S(1)}, u32[]{:S(2)}, u32[]{:S(2)}) %collective-permute-start.10) | collective-permute-done | bytes 122912 | tf_op jit(solution)/shard_map/ppermute | solution.py:391
  48.2 3.0 %collective-permute-start.15 = (bf16[2,240,128]{2,1,0:T(8,128)(2,1)}, bf16[2,240,128]{2,1,0:T(8,128)(2,1)S(1)}, u32[]{:S(2)}, u32[]{:S(2)}) collective-permute-start(bf16[2,240,128]{2,1,0:T(8,128)(2,1)} %get-tuple-element.48), channel_id=1, source_target_pairs={{0,3},{1,2},{2,1},{3,0},{4,7},{5,6},{6,5},{7,4},{8,11},{9,10},{10,... | collective-permute-start | bytes 368648 | tf_op jit(solution)/shard_map/ppermute | solution.py:391
  51.2 4.9 %collective-permute-done.12.refs_11_ = bf16[2,240,128]{2,1,0:T(8,128)(2,1)S(1)} collective-permute-done((bf16[2,240,128]{2,1,0:T(8,128)(2,1)}, bf16[2,240,128]{2,1,0:T(8,128)(2,1)S(1)}, u32[]{:S(2)}, u32[]{:S(2)}) %collective-permute-start.12) | collective-permute-done | bytes 122912 | tf_op jit(solution)/shard_map/ppermute | solution.py:391
  56.1 3.5 %collective-permute-done.14.refs_13_ = bf16[2,240,128]{2,1,0:T(8,128)(2,1)S(1)} collective-permute-done((bf16[2,240,128]{2,1,0:T(8,128)(2,1)}, bf16[2,240,128]{2,1,0:T(8,128)(2,1)S(1)}, u32[]{:S(2)}, u32[]{:S(2)}) %collective-permute-start.14) | collective-permute-done | bytes 122912 | tf_op jit(solution)/shard_map/ppermute | solution.py:391
  59.7 2.6 %collective-permute-done.16.refs_15_ = bf16[2,240,128]{2,1,0:T(8,128)(2,1)S(1)} collective-permute-done((bf16[2,240,128]{2,1,0:T(8,128)(2,1)}, bf16[2,240,128]{2,1,0:T(8,128)(2,1)S(1)}, u32[]{:S(2)}, u32[]{:S(2)}) %collective-permute-start.16) | collective-permute-done | bytes 122912 | tf_op jit(solution)/shard_map/ppermute | solution.py:391
  62.3 0.9 %copy-done.1 = bf16[2,240,128]{2,1,0:T(8,128)(2,1)S(1)} copy-done((bf16[2,240,128]{2,1,0:T(8,128)(2,1)S(1)}, bf16[2,240,128]{2,1,0:T(8,128)(2,1)}, u32[]{:S(2)}) %copy-start.1) | copy-done | bytes 122904
  63.2 5.7 %score.1 = (bf16[4,56,512]{2,1,0:T(8,128)(2,1)}, bf16[2,4,56,512]{3,2,1,0:T(8,128)(2,1)}) custom-call(s32[1]{0:T(128)} %bitcast.place.refs_0_, bf16[2,240,128]{2,1,0:T(8,128)(2,1)S(1)} %copy-done.1, bf16[2,240,128]{2,1,0:T(8,128)(2,1)S(1)} %collective-permute-done.2.refs_1_, bf16[2,240,128]{2,1,0:T(8,128)(2,1)S(1)} %collective-permute-done.3.refs_2_, ...), custom_call_target="tpu_custom_call" | custom-call | tf_op jit(solution)/shard_map/score/pallas_call | solution.py:353
  (23 shorter events, 0.2 us)
Async XLA Ops:
  0.6 7.6 %copy-start.4 = (s32[16,2,3]{0,1,2:T(2,128)S(1)}, s32[16,2,3]{0,1,2:T(2,128)}, u32[]{:S(2)}) copy-start(s32[16,2,3]{0,1,2:T(2,128)} %param.6) | copy-start | bytes 1156
  0.6 7.5 %collective-permute-start.1 = (bf16[16,2,448,128]{3,2,1,0:T(8,128)(2,1)}, bf16[16,2,448,128]{3,2,1,0:T(8,128)(2,1)}, u32[]{:S(2)}, u32[]{:S(2)}) collective-permute-start(bf16[16,2,448,128]{3,2,1,0:T(8,128)(2,1)} %bitcast.14), channel_id=1, source_target_pairs={{0,1},{1,0},{2,3},{3,2},{4,5},{5,4},{6,7},{7,6},{8,9},{9,8},{10,11... | collective-permute-start | bytes 11010056 | tf_op jit(solution)/shard_map/ppermute | solution.py:386
  1.4 6.8 %collective-permute-start = (s32[3,2,16]{2,1,0:T(2,128)}, s32[3,2,16]{2,1,0:T(2,128)S(1)}, u32[]{:S(2)}, u32[]{:S(2)}) collective-permute-start(s32[3,2,16]{2,1,0:T(2,128)} %bitcast.11), channel_id=1, source_target_pairs={{0,1},{1,0},{2,3},{3,2},{4,5},{5,4},{6,7},{7,6},{8,9},{9,8},{10,11... | collective-permute-start | bytes 1160 | tf_op jit(solution)/shard_map/ppermute | solution.py:387
  1.5 0.9 %copy-start.2 = (f32[32,896]{1,0:T(8,128)S(1)}, f32[32,896]{1,0:T(8,128)}, u32[]{:S(2)}) copy-start(f32[32,896]{1,0:T(8,128)} %smoothing.1) | copy-start | bytes 344068
  2.4 0.7 copy-start.3
  8.2 54.1 %copy-start = (bf16[4,512,56]{1,2,0:T(8,128)(2,1)S(1)}, bf16[4,512,56]{1,2,0:T(8,128)(2,1)}, u32[]{:S(2)}) copy-start(bf16[4,512,56]{1,2,0:T(8,128)(2,1)} %param.9) | copy-start | bytes 688132
  15.4 5.7 %collective-permute-start.2 = (bf16[2,240,128]{2,1,0:T(8,128)(2,1)}, bf16[2,240,128]{2,1,0:T(8,128)(2,1)S(1)}, u32[]{:S(2)}, u32[]{:S(2)}) collective-permute-start(bf16[2,240,128]{2,1,0:T(8,128)(2,1)} %get-tuple-element.35), channel_id=1, source_target_pairs={{0,8},{1,9},{2,10},{3,11},{4,12},{5,13},{6,14},{7,15},{8,0},{9,1},... | collective-permute-start | bytes 368648 | tf_op jit(solution)/shard_map/ppermute | solution.py:391
  15.5 11.9 %collective-permute-start.3 = (bf16[2,240,128]{2,1,0:T(8,128)(2,1)}, bf16[2,240,128]{2,1,0:T(8,128)(2,1)S(1)}, u32[]{:S(2)}, u32[]{:S(2)}) collective-permute-start(bf16[2,240,128]{2,1,0:T(8,128)(2,1)} %get-tuple-element.36), channel_id=1, source_target_pairs={{0,4},{1,5},{2,6},{3,7},{4,0},{5,1},{6,2},{7,3},{8,12},{9,13},{10,... | collective-permute-start | bytes 368648 | tf_op jit(solution)/shard_map/ppermute | solution.py:391
  16.9 11.2 %collective-permute-start.4 = (bf16[2,240,128]{2,1,0:T(8,128)(2,1)}, bf16[2,240,128]{2,1,0:T(8,128)(2,1)S(1)}, u32[]{:S(2)}, u32[]{:S(2)}) collective-permute-start(bf16[2,240,128]{2,1,0:T(8,128)(2,1)} %get-tuple-element.37), channel_id=1, source_target_pairs={{0,9},{1,8},{2,11},{3,10},{4,13},{5,12},{6,15},{7,14},{8,1},{9,0},... | collective-permute-start | bytes 368648 | tf_op jit(solution)/shard_map/ppermute | solution.py:391
  20.0 12.9 %collective-permute-start.5 = (bf16[2,240,128]{2,1,0:T(8,128)(2,1)}, bf16[2,240,128]{2,1,0:T(8,128)(2,1)S(1)}, u32[]{:S(2)}, u32[]{:S(2)}) collective-permute-start(bf16[2,240,128]{2,1,0:T(8,128)(2,1)} %get-tuple-element.38), channel_id=1, source_target_pairs={{0,5},{1,4},{2,7},{3,6},{4,1},{5,0},{6,3},{7,2},{8,13},{9,12},{10,... | collective-permute-start | bytes 368648 | tf_op jit(solution)/shard_map/ppermute | solution.py:391
  20.1 12.9 %collective-permute-start.6 = (bf16[2,240,128]{2,1,0:T(8,128)(2,1)}, bf16[2,240,128]{2,1,0:T(8,128)(2,1)S(1)}, u32[]{:S(2)}, u32[]{:S(2)}) collective-permute-start(bf16[2,240,128]{2,1,0:T(8,128)(2,1)} %get-tuple-element.39), channel_id=1, source_target_pairs={{0,10},{1,11},{2,8},{3,9},{4,14},{5,15},{6,12},{7,13},{8,2},{9,3},... | collective-permute-start | bytes 368648 | tf_op jit(solution)/shard_map/ppermute | solution.py:391
  21.2 14.3 %collective-permute-start.7 = (bf16[2,240,128]{2,1,0:T(8,128)(2,1)}, bf16[2,240,128]{2,1,0:T(8,128)(2,1)S(1)}, u32[]{:S(2)}, u32[]{:S(2)}) collective-permute-start(bf16[2,240,128]{2,1,0:T(8,128)(2,1)} %get-tuple-element.40), channel_id=1, source_target_pairs={{0,6},{1,7},{2,4},{3,5},{4,2},{5,3},{6,0},{7,1},{8,14},{9,15},{10,... | collective-permute-start | bytes 368648 | tf_op jit(solution)/shard_map/ppermute | solution.py:391
  27.4 12.6 %collective-permute-start.8 = (bf16[2,240,128]{2,1,0:T(8,128)(2,1)}, bf16[2,240,128]{2,1,0:T(8,128)(2,1)S(1)}, u32[]{:S(2)}, u32[]{:S(2)}) collective-permute-start(bf16[2,240,128]{2,1,0:T(8,128)(2,1)} %get-tuple-element.41), channel_id=1, source_target_pairs={{0,11},{1,10},{2,9},{3,8},{4,15},{5,14},{6,13},{7,12},{8,3},{9,2},... | collective-permute-start | bytes 368648 | tf_op jit(solution)/shard_map/ppermute | solution.py:391
  28.1 13.5 %collective-permute-start.9 = (bf16[2,240,128]{2,1,0:T(8,128)(2,1)}, bf16[2,240,128]{2,1,0:T(8,128)(2,1)S(1)}, u32[]{:S(2)}, u32[]{:S(2)}) collective-permute-start(bf16[2,240,128]{2,1,0:T(8,128)(2,1)} %get-tuple-element.42), channel_id=1, source_target_pairs={{0,7},{1,6},{2,5},{3,4},{4,3},{5,2},{6,1},{7,0},{8,15},{9,14},{10,... | collective-permute-start | bytes 368648 | tf_op jit(solution)/shard_map/ppermute | solution.py:391
  33.0 15.3 %collective-permute-start.10 = (bf16[2,240,128]{2,1,0:T(8,128)(2,1)}, bf16[2,240,128]{2,1,0:T(8,128)(2,1)S(1)}, u32[]{:S(2)}, u32[]{:S(2)}) collective-permute-start(bf16[2,240,128]{2,1,0:T(8,128)(2,1)} %get-tuple-element.43), channel_id=1, source_target_pairs={{0,12},{1,13},{2,14},{3,15},{4,8},{5,9},{6,10},{7,11},{8,4},{9,5},... | collective-permute-start | bytes 368648 | tf_op jit(solution)/shard_map/ppermute | solution.py:391
  33.0 18.2 %collective-permute-start.11 = (bf16[2,240,128]{2,1,0:T(8,128)(2,1)}, bf16[2,240,128]{2,1,0:T(8,128)(2,1)S(1)}, u32[]{:S(2)}, u32[]{:S(2)}) collective-permute-start(bf16[2,240,128]{2,1,0:T(8,128)(2,1)} %get-tuple-element.44), channel_id=1, source_target_pairs={{0,1},{1,0},{2,3},{3,2},{4,5},{5,4},{6,7},{7,6},{8,9},{9,8},{10,11... | collective-permute-start | bytes 368648 | tf_op jit(solution)/shard_map/ppermute | solution.py:391
  35.5 20.7 %collective-permute-start.12 = (bf16[2,240,128]{2,1,0:T(8,128)(2,1)}, bf16[2,240,128]{2,1,0:T(8,128)(2,1)S(1)}, u32[]{:S(2)}, u32[]{:S(2)}) collective-permute-start(bf16[2,240,128]{2,1,0:T(8,128)(2,1)} %get-tuple-element.45), channel_id=1, source_target_pairs={{0,13},{1,12},{2,15},{3,14},{4,9},{5,8},{6,11},{7,10},{8,5},{9,4},... | collective-permute-start | bytes 368648 | tf_op jit(solution)/shard_map/ppermute | solution.py:391
  40.0 16.1 %collective-permute-start.13 = (bf16[2,240,128]{2,1,0:T(8,128)(2,1)}, bf16[2,240,128]{2,1,0:T(8,128)(2,1)S(1)}, u32[]{:S(2)}, u32[]{:S(2)}) collective-permute-start(bf16[2,240,128]{2,1,0:T(8,128)(2,1)} %get-tuple-element.46), channel_id=1, source_target_pairs={{0,2},{1,3},{2,0},{3,1},{4,6},{5,7},{6,4},{7,5},{8,10},{9,11},{10,... | collective-permute-start | bytes 368648 | tf_op jit(solution)/shard_map/ppermute | solution.py:391
  41.6 18.1 %collective-permute-start.14 = (bf16[2,240,128]{2,1,0:T(8,128)(2,1)}, bf16[2,240,128]{2,1,0:T(8,128)(2,1)S(1)}, u32[]{:S(2)}, u32[]{:S(2)}) collective-permute-start(bf16[2,240,128]{2,1,0:T(8,128)(2,1)} %get-tuple-element.47), channel_id=1, source_target_pairs={{0,14},{1,15},{2,12},{3,13},{4,10},{5,11},{6,8},{7,9},{8,6},{9,7},... | collective-permute-start | bytes 368648 | tf_op jit(solution)/shard_map/ppermute | solution.py:391
  48.2 11.4 %collective-permute-start.15 = (bf16[2,240,128]{2,1,0:T(8,128)(2,1)}, bf16[2,240,128]{2,1,0:T(8,128)(2,1)S(1)}, u32[]{:S(2)}, u32[]{:S(2)}) collective-permute-start(bf16[2,240,128]{2,1,0:T(8,128)(2,1)} %get-tuple-element.48), channel_id=1, source_target_pairs={{0,3},{1,2},{2,1},{3,0},{4,7},{5,6},{6,5},{7,4},{8,11},{9,10},{10,... | collective-permute-start | bytes 368648 | tf_op jit(solution)/shard_map/ppermute | solution.py:391
  51.2 11.1 %collective-permute-start.16 = (bf16[2,240,128]{2,1,0:T(8,128)(2,1)}, bf16[2,240,128]{2,1,0:T(8,128)(2,1)S(1)}, u32[]{:S(2)}, u32[]{:S(2)}) collective-permute-start(bf16[2,240,128]{2,1,0:T(8,128)(2,1)} %get-tuple-element.49), channel_id=1, source_target_pairs={{0,15},{1,14},{2,13},{3,12},{4,11},{5,10},{6,9},{7,8},{8,7},{9,6},... | collective-permute-start | bytes 368648 | tf_op jit(solution)/shard_map/ppermute | solution.py:391
  62.3 0.9 %copy-start.1 = (bf16[2,240,128]{2,1,0:T(8,128)(2,1)S(1)}, bf16[2,240,128]{2,1,0:T(8,128)(2,1)}, u32[]{:S(2)}) copy-start(bf16[2,240,128]{2,1,0:T(8,128)(2,1)} %get-tuple-element.34.refs_0_) | copy-start | bytes 368644

commit v4 on v3

--- a/solution.py
+++ b/solution.py
@@ -20,7 +20,7 @@
 QUAD = LANES // ROWS
 MID = 0.11
 VMEM = 40 * 1024 * 1024
-MOST_VMEM = 48 * 1024 * 1024
+MOST_VMEM = 46 * 1024 * 1024
 
 
 def round_up(value, step):
@@ -51,48 +51,75 @@
     staged[...] = tile.astype(jnp.float32)
 
 
-def staged_field(staged, field):
-    return jnp.concatenate(
-        [staged[pl.ds(FIELDS * t + field, PAIRS, stride=FIELDS * TILES), :] for t in range(TILES)], 1
+def staged_tile(staged, field, t):
+    return staged[pl.ds(FIELDS * t + field, PAIRS, stride=FIELDS * TILES), :]
+
+
+def weight_tile(weights, kind, t):
+    return weights[t, pl.ds(pl.multiple_of(kind * PAIRS, PAIRS), PAIRS), :]
+
+
+SLOTS = TILES + 2
+
+
+def zero(sums):
+    for parity in range(2):
+        for t in range(SLOTS):
+            sums[parity, t] = jnp.zeros((PAIRS, LANES), jnp.float32)
+
+
+def add_side(sums, tile, column, fresh):
+    pairs = jnp.concatenate([tile(t) for t in range(TILES)], 1)
+    turned = pltpu.roll(pairs, PATCH, 1)
+    lane = lax.broadcasted_iota(jnp.int32, pairs.shape, 1)
+    left = (lane < PATCH) & (column == 0)
+    right = (lane >= PATCH) & (column != 0)
+    placed = (
+        jnp.where(left, pairs, jnp.where(right, turned, 0.0)),
+        jnp.where(left, turned, jnp.where(right, pairs, 0.0)),
     )
-
-
-def weight_of(weights, kind):
-    at = pl.multiple_of(kind * PAIRS, PAIRS)
-    return jnp.concatenate([weights[t, pl.ds(at, PAIRS), :] for t in range(TILES)], 1)
-
-
-def lane_index():
-    return lax.broadcasted_iota(jnp.int32, (PAIRS, COLS), 1)
-
-
-def place_side(pairs, column):
-    left = (lane_index() < PATCH) & (column == 0)
-    right = (lane_index() >= PATCH) & (column != 0)
-    turned = pltpu.roll(pairs, PATCH, 1)
-    even = jnp.where(left, pairs, jnp.where(right, turned, 0.0))
-    odd = jnp.where(left, turned, jnp.where(right, pairs, 0.0))
-    return even, odd
-
-
-def place_any(pairs, column):
-    inside = (lane_index() >= column) & (lane_index() < column + PATCH)
-    turned = pltpu.roll(pairs, column, 1)
-    return jnp.where(inside, turned, 0.0), jnp.where(inside, pltpu.roll(turned, PATCH, 1), 0.0)
+    for parity in range(2):
+        for t in range(TILES):
+            piece = placed[parity][:, LANES * t : LANES * (t + 1)]
+            sums[parity, t + 1] = piece if fresh else sums[parity, t + 1] + piece
+
+
+def add_any(sums, tile, column, fresh):
+    if fresh:
+        zero(sums)
+    lane = lax.broadcasted_iota(jnp.int32, (PAIRS, LANES), 1)
+    middle = PATCH // LANES
+    split = PATCH % LANES
+    for parity in range(2):
+        first = middle * parity
+        start = column if parity == 0 else column + COLS - PATCH
+        shift = lax.rem(start, LANES)
+        at = lax.div(start, LANES) + first + 1 - (TILES if parity else 0)
+        turned = []
+        for t in range(first, first + middle + 1):
+            piece = tile(t)
+            if t == middle:
+                piece = jnp.where((lane >= split) if parity else (lane < split), piece, 0.0)
+            turned.append(pltpu.roll(piece, shift, 1))
+        none = jnp.zeros((PAIRS, LANES), jnp.float32)
+        for v in range(middle + 2):
+            low = turned[v - 1] if v else none
+            high = turned[v] if v <= middle else none
+            sums[parity, at + v] = sums[parity, at + v] + jnp.where(lane < shift, low, high)
 
 
 def either_kind(z, heavy, body):
     @pl.when(heavy)
     def _():
-        body(place_any, range(CAP))
+        body(add_any, range(CAP))
 
     @pl.when(jnp.logical_not(heavy))
     def _():
-        body(place_side if z.makers == 2 else place_any, range(1))
-
-
-def own_kernel(z, place, lists, tiles, table_hbm, smoothing, *refs):
-    half, (total, weights, strength, landed, staged, table, sems) = refs[:FIELDS], refs[FIELDS:]
+        body(add_side if z.makers == 2 else add_any, range(1))
+
+
+def own_kernel(z, place, lists, tiles, table_hbm, *refs):
+    half, (total, weights, landed, staged, table, sems) = refs[:FIELDS], refs[FIELDS:]
     first = lax.rem(place[0], z.makers) * z.block
 
     def fetch(j):
@@ -102,12 +129,6 @@
     fetch_table.start()
     for j in range(z.block):
         fetch(j).start()
-    turned_strength = jnp.transpose(smoothing[...] - MID)
-    for dest in range(z.regions):
-        for g in range(z.span // 8):
-            top = z.width * dest + 8 * g
-            count, at = min(8, COLS - top), ROWS * (g % QUAD)
-            strength[dest, g // QUAD, 0:count, at : at + ROWS] = turned_strength[top : top + count]
     fetch_table.wait()
     kinds = table.shape[0]
     for k in range(PAIRS):
@@ -122,23 +143,19 @@
     def region(j, carry):
         fetch(j).wait()
 
-        def body(place_tile, slots):
-            entries = []
+        def body(add, slots):
             for slot in slots:
                 stage(staged.at[slot], landed[j, slot])
-                column, kind = (lists[field, slot, first + j] for field in (1, 2))
-                entries.append((slot, column, weight_of(weights, kind)))
-            even, odd = 0.0, 0.0
-            for _, column, weight in entries:
-                a, b = place_tile(weight, column)
-                even, odd = even + a, odd + b
-            total[j, 0], total[j, 1] = even, odd
+            entries = [(slot, *(lists[entry, slot, first + j] for entry in (1, 2))) for slot in slots]
+            for i, (_, column, kind) in enumerate(entries):
+                add(total.at[j], functools.partial(weight_tile, weights, kind), column, i == 0)
             for field in range(FIELDS):
-                even, odd = 0.0, 0.0
-                for slot, column, weight in entries:
-                    a, b = place_tile(staged_field(staged.at[slot], field) * weight, column)
-                    even, odd = even + a, odd + b
-                half[field][j, 0], half[field][j, 1] = even, odd
+                for i, (slot, column, kind) in enumerate(entries):
+
+                    def tile(t):
+                        return staged_tile(staged.at[slot], field, t) * weight_tile(weights, kind, t)
+
+                    add(half[field].at[j], tile, column, i == 0)
 
         either_kind(z, lists[0, 1, first + j] >= 0, body)
         return carry
@@ -146,7 +163,7 @@
     lax.fori_loop(0, z.block, region, 0)
 
 
-def own_share(z, place, lists, tiles, table, smoothing):
+def own_share(z, place, lists, tiles, table):
     smem = pl.BlockSpec(memory_space=pltpu.SMEM)
     vmem = pl.BlockSpec(memory_space=pltpu.VMEM)
     hbm = pl.BlockSpec(memory_space=pltpu.HBM)
@@ -154,12 +171,11 @@
     return pl.pallas_call(
         functools.partial(own_kernel, z),
         out_shape=[
-            *[jax.ShapeDtypeStruct((z.block, 2, PAIRS, COLS), jnp.float32)] * (FIELDS + 1),
+            *[jax.ShapeDtypeStruct((z.block, 2, SLOTS, PAIRS, LANES), jnp.float32)] * (FIELDS + 1),
             jax.ShapeDtypeStruct((TILES, kinds * PAIRS, LANES), jnp.float32),
-            jax.ShapeDtypeStruct((z.regions, z.quads, 8, LANES), jnp.float32),
-        ],
-        in_specs=[smem, smem, hbm, hbm, vmem],
-        out_specs=[vmem] * (FIELDS + 3),
+        ],
+        in_specs=[smem, smem, hbm, hbm],
+        out_specs=[vmem] * (FIELDS + 2),
         scratch_shapes=[
             pltpu.VMEM((z.block, CAP, LINES, LANES), jnp.bfloat16),
             pltpu.VMEM((CAP, LINES, LANES), jnp.float32),
@@ -169,16 +185,38 @@
         compiler_params=pltpu.CompilerParams(vmem_limit_bytes=MOST_VMEM),
         cost_estimate=pl.CostEstimate(flops=5_000_000, bytes_accessed=8_000_000, transcendentals=0),
         name="own_share",
-    )(place, lists, tiles, table, smoothing)
+    )(place, lists, tiles, table)
+
+
+def strength_kernel(z, smoothing, _, strength):
+    turned_strength = jnp.transpose(smoothing[...] - MID)
+    for dest in range(z.regions):
+        for g in range(z.span // 8):
+            top = z.width * dest + 8 * g
+            count, at = min(8, COLS - top), ROWS * (g % QUAD)
+            strength[dest, g // QUAD, 0:count, at : at + ROWS] = turned_strength[top : top + count]
+
+
+def strength_blocks(z, smoothing, before):
+    return pl.pallas_call(
+        functools.partial(strength_kernel, z),
+        out_shape=jax.ShapeDtypeStruct((z.regions, z.quads, 8, LANES), jnp.float32),
+        in_specs=[pl.BlockSpec(memory_space=pltpu.VMEM), pl.BlockSpec(memory_space=pl.ANY)],
+        out_specs=pl.BlockSpec(memory_space=pltpu.VMEM),
+        compiler_params=pltpu.CompilerParams(vmem_limit_bytes=VMEM),
+        name="strength_blocks",
+    )(smoothing, before)
 
 
 def join_kernel(z, *refs):
     place, lists, refs = refs[0], refs[1 : 1 + z.makers], refs[1 + z.makers :]
     received, refs = refs[: z.makers - 1], refs[z.makers - 1 :]
-    half, (total, weights, strength), outs = refs[:FIELDS], refs[FIELDS : FIELDS + 3], refs[FIELDS + 3 : -5]
-    staged, lines, turned, blocks, sems = refs[-5:]
+    half, (total, weights, strength), outs = refs[:FIELDS], refs[FIELDS : FIELDS + 3], refs[FIELDS + 3 : -6]
+    staged, sums, lines, turned, blocks, sems = refs[-6:]
     me = place[0]
     first = lax.rem(me, z.makers) * z.block
+    row, column = (lax.broadcasted_iota(jnp.int32, (LANES, LANES), axis) for axis in (0, 1))
+    identity = (row == column).astype(jnp.bfloat16)
 
     def send(i, quad):
         return pltpu.make_async_copy(blocks.at[i, quad], outs[i].at[quad], sems.at[i, quad])
@@ -188,29 +226,36 @@
         def region(i, carry):
             j = quad * QUAD + i
 
-            def body(place_tile, slots):
+            def body(add, slots):
                 entries = []
                 for maker in range(1, z.makers):
                     for slot in slots:
                         index = (maker - 1) * CAP + slot
                         stage(staged.at[index], received[maker - 1][first + j, slot])
-                        column, kind = (lists[maker][field, slot, first + j] for field in (1, 2))
-                        entries.append((index, column, weight_of(weights, kind)))
-                even, odd = total[j, 0], total[j, 1]
-                for _, column, weight in entries:
-                    a, b = place_tile(weight, column)
-                    even, odd = even + a, odd + b
-                even_inverse, odd_inverse = 1.0 / even, 1.0 / odd
+                        entries.append((index, *(lists[maker][entry, slot, first + j] for entry in (1, 2))))
+
+                def begin(index, own):
+                    for parity in range(2):
+                        for t in range(SLOTS):
+                            sums[index, parity, t] = own[j, parity, t]
+
+                begin(FIELDS, total)
+                for _, column, kind in entries:
+                    add(sums.at[FIELDS], functools.partial(weight_tile, weights, kind), column, False)
+                inverse = [[1.0 / sums[FIELDS, parity, t + 1] for t in range(TILES)] for parity in range(2)]
                 for field in range(FIELDS):
-                    even, odd = half[field][j, 0], half[field][j, 1]
-                    for index, column, weight in entries:
-                        a, b = place_tile(staged_field(staged.at[index], field) * weight, column)
-                        even, odd = even + a, odd + b
-                    even, odd = even * even_inverse, odd * odd_inverse
-                    for t in range(TILES):
-                        here = slice(LANES * t, LANES * (t + 1))
-                        lines[field, t, pl.ds(ROWS * i, PAIRS, stride=2), :] = even[:, here]
-                        lines[field, t, pl.ds(ROWS * i + 1, PAIRS, stride=2), :] = odd[:, here]
+                    begin(field, half[field])
+                    for index, column, kind in entries:
+
+                        def tile(t):
+                            return staged_tile(staged.at[index], field, t) * weight_tile(weights, kind, t)
+
+                        add(sums.at[field], tile, column, False)
+                    for parity in range(2):
+                        for t in range(TILES):
+                            lines[field, t, pl.ds(ROWS * i + parity, PAIRS, stride=2), :] = (
+                                sums[field, parity, t + 1] * inverse[parity][t]
+                            )
 
             either_kind(z, lists[0][0, 1, first + j] >= 0, body)
             return carry
@@ -218,38 +263,46 @@
         lax.fori_loop(0, QUAD, region, 0)
         for field in range(FIELDS):
             for t in range(TILES):
-                turned[field, LANES * t : LANES * (t + 1), :] = jnp.transpose(lines[field, t])
+                turned[field, LANES * t : LANES * (t + 1), :] = lax.dot_general(
+                    identity,
+                    lines[field, t].astype(jnp.bfloat16),
+                    (((1,), (1,)), ((), ())),
+                    preferred_element_type=jnp.float32,
+                )
         for i, offset in enumerate(z.offsets):
+            target = blocks.at[i, quad] if i else outs[0].at[quad]
             dest = me ^ offset
             top = dest * z.width
             if z.width % 8 == 0:
                 top = pl.multiple_of(top, 8)
             for low in range(0, FIELDS, 2):
                 block = [turned[field, pl.ds(top, z.span), :] for field in (low, low + 1)]
-                blocks[i, quad, low * z.span : (low + 2) * z.span, :] = jnp.concatenate(block, 0).astype(
-                    jnp.bfloat16
-                )
+                target[low * z.span : (low + 2) * z.span, :] = jnp.concatenate(block, 0).astype(jnp.bfloat16)
             ends = (jnp.maximum(top - 1, 0), jnp.minimum(top + z.width, COLS - 1))
             edge = [turned[field, pl.ds(end, 1), :] for field in range(FIELDS) for end in ends]
             edge.append(strength[dest, quad])
-            blocks[i, quad, z.main : z.sent, :] = jnp.concatenate(edge, 0).astype(jnp.bfloat16)
-            send(i, quad).start()
+            target[z.main : z.sent, :] = jnp.concatenate(edge, 0).astype(jnp.bfloat16)
+            if i:
+                send(i, quad).start()
     for quad in range(z.quads):
-        for i in range(z.regions):
+        for i in range(1, z.regions):
             send(i, quad).wait()
 
 
 def join(z, place, lists, received, shares):
     smem = pl.BlockSpec(memory_space=pltpu.SMEM)
     vmem = pl.BlockSpec(memory_space=pltpu.VMEM)
+    hbm = pl.BlockSpec(memory_space=pltpu.HBM)
     shape = (z.quads, z.sent, LANES)
     return pl.pallas_call(
         functools.partial(join_kernel, z),
-        out_shape=[pltpu.HBM(shape, jnp.bfloat16)] * z.regions,
+        out_shape=[jax.ShapeDtypeStruct(shape, jnp.bfloat16)]
+        + [pltpu.HBM(shape, jnp.bfloat16)] * (z.regions - 1),
         in_specs=[smem] * (1 + z.makers) + [vmem] * (z.makers - 1 + len(shares)),
-        out_specs=[pl.BlockSpec(memory_space=pltpu.HBM)] * z.regions,
+        out_specs=[vmem] + [hbm] * (z.regions - 1),
         scratch_shapes=[
             pltpu.VMEM((CAP * (z.makers - 1), LINES, LANES), jnp.float32),
+            pltpu.VMEM((FIELDS + 1, 2, SLOTS, PAIRS, LANES), jnp.float32),
             pltpu.VMEM((FIELDS, TILES, LANES, LANES), jnp.float32),
             pltpu.VMEM((FIELDS, COLS + 8, LANES), jnp.float32),
             pltpu.VMEM((z.regions, *shape), jnp.bfloat16),
@@ -318,16 +371,19 @@
         target_field = analysis[f].astype(jnp.float32)
         for low in range(0, z.width, 16):
             high = min(low + 16, z.width)
-            shape = (high - low, rows)
-            lane = lax.broadcasted_iota(jnp.int32, shape, 1)
+            lane = lax.broadcasted_iota(jnp.int32, (high - low, LANES), 1)
             strong = strength[low:high, :]
             members = []
             for sample in range(SAMPLES):
                 here = padded[sample, f, 8 + low : 8 + high, :]
                 sides = padded[sample, f, 7 + low : 7 + high, :] + padded[sample, f, 9 + low : 9 + high, :]
-                above = jnp.where(lane == 0, here, pltpu.roll(here, 1, 1))
-                below = jnp.where(lane == rows - 1, here, pltpu.roll(here, rows - 1, 1))
-                smooth = here + strong * (above + below + sides - 4.0 * here)
+                pieces = [here[:, at : at + LANES] for at in range(0, rows, LANES)]
+                later = [pltpu.roll(piece, 1, 1) for piece in pieces]
+                sooner = [pltpu.roll(piece, LANES - 1, 1) for piece in pieces]
+                above = [jnp.where(lane == 0, a, b) for a, b in zip([pieces[0]] + later[:-1], later)]
+                below = [jnp.where(lane == LANES - 1, a, b) for a, b in zip(sooner[1:] + [pieces[-1]], sooner)]
+                along = jnp.concatenate([a + b for a, b in zip(above, below)], 1)
+                smooth = here + strong * (along + sides - 4.0 * here)
                 members.append(smooth.astype(jnp.bfloat16))
             values = [member.astype(jnp.float32) for member in members]
             target = target_field[low:high]
@@ -358,7 +414,7 @@
         ],
         grid=(FIELDS // STEP_FIELDS,),
         in_specs=[pl.BlockSpec(memory_space=pltpu.SMEM)]
-        + [pl.BlockSpec(blocks[0].shape, lambda i: (0, 0, 0))] * z.regions
+        + [pl.BlockSpec(memory_space=pltpu.VMEM)] * z.regions
         + [pl.BlockSpec((STEP_FIELDS, width, rows), lambda i: (i, 0, 0))],
         out_specs=[
             pl.BlockSpec((STEP_FIELDS, width, rows), lambda i: (i, 0, 0)),
@@ -385,7 +441,8 @@
     lists = jnp.transpose(slot_lists, (2, 1, 0))
     received = [lax.ppermute(tiles, "region", turn) for turn in turns]
     lists = [lists] + [lax.ppermute(lists, "region", turn) for turn in turns]
-    shares = own_share(z, place, lists[0], tiles, blend_table, smoothing)
+    shares = own_share(z, place, lists[0], tiles, blend_table)
+    shares = [*shares, strength_blocks(z, smoothing, shares[-1])]
     blocks = join(z, place, lists, received, shares)
     moved = [blocks[0]] + [
         lax.ppermute(block, "region", [(i, i ^ offset) for i in range(z.regions)])

time: 69.2 us -> 68.3 us (0.987); the launches traced: 68.9 us -> 69.4 us
  waiting for transfers between devices: 20.9 us -> 25.3 us
  Pallas kernels: 18 us -> 16.1 us
  starting transfers between devices: 26.8 us -> 25.4 us
    ppermute x15, waiting for transfers between devices: 20.9 us -> 24.6 us  [shards(): lax.ppermute(block, 'region', [(i, i ^ offset) for i in range(z.regions)])]
    pallas_call x1, Pallas kernels: 5.12 us -> 3.42 us  [own_share(): pl.pallas_call(functools.partial(own_kernel, z), out_shape=[*[jax.ShapeDt...]
    ppermute x15, starting transfers between devices: 25.9 us -> 24.6 us  [shards(): lax.ppermute(block, 'region', [(i, i ^ offset) for i in range(z.regions)])]
    unnamed x10 -> x8, local copies, waits for them, and re-layouts: 2.49 us -> 1.87 us
    pallas_call x1 -> x2, Pallas kernels: 7.22 us -> 7 us  [the longest x1 6.71 us: join(): pl.pallas_call(functools.partial(join_kernel, z), out_shape=[jax.ShapeDty...]
  transfers between devices with their start and end apart: 17 -> 17, of which waited for: 6 -> 8; matrix products, arithmetic and copies ran while one was open for 0% -> 0% of each run, Pallas kernels for 7% -> 5%
where the time goes in v4:
time: 68.3 us; the launch traced here: 69.4 us
  starting transfers between devices  25.4 us (37%)
  waiting for transfers between devices  25.3 us (37%)
  Pallas kernels  16.1 us (24%)
  local copies, waits for them, and re-layouts  1.87 us (3%)
  between operations  0.69 us (1%)
    ppermute x15, starting transfers between devices, shards(): lax.ppermute(block, 'region', [(i, i ^ offset) for i in range(z.regions)])  24.6 us
    ppermute x15, waiting for transfers between devices, shards(): lax.ppermute(block, 'region', [(i, i ^ offset) for i in range(z.regions)])  24.6 us
    pallas_call x1, Pallas kernels, join(): pl.pallas_call(functools.partial(join_kernel, z), out_shape=[jax.ShapeDty...  6.71 us
    pallas_call x1, Pallas kernels, score(): pl.pallas_call(functools.partial(score_kernel, z), out_shape=[jax.ShapeDt...  5.69 us
    pallas_call x1, Pallas kernels, own_share(): pl.pallas_call(functools.partial(own_kernel, z), out_shape=[*[jax.ShapeDt...  3.42 us
    unnamed x8, local copies, waits for them, and re-layouts  1.87 us
  transfers between devices with their start and end apart: 17, of which 8 were waited for; matrix products, arithmetic and copies ran while one was open for 0% of the time, Pallas kernels for 5%

profile of v4, /device:TPU:17, one launch (start us, length us, event | category | flops | bytes accessed | tf_op | source)
XLA Modules:
  0.0 69.4 jit_solution(2689432319953514940)
XLA Ops:
  0.6 0.7 %collective-permute-start.1 = (bf16[16,2,448,128]{3,2,1,0:T(8,128)(2,1)}, bf16[16,2,448,128]{3,2,1,0:T(8,128)(2,1)}, u32[]{:S(2)}, u32[]{:S(2)}) collective-permute-start(bf16[16,2,448,128]{3,2,1,0:T(8,128)(2,1)} %bitcast.14), channel_id=1, source_target_pairs={{0,1},{1,0},{2,3},{3,2},{4,5},{5,4},{6,7},{7,6},{8,9},{9,8},{10,11... | collective-permute-start | bytes 11010056 | tf_op jit(solution)/shard_map/ppermute | solution.py:442
  1.5 1.2 %copy-done = f32[14,14336]{1,0:T(8,128)S(1)} copy-done((f32[14,14336]{1,0:T(8,128)S(1)}, f32[14,14336]{1,0:T(8,128)}, u32[]{:S(2)}) %copy-start) | copy-done | bytes 802840
  2.6 0.7 copy-done.3
  3.3 3.4 %own_share.1 = (f32[8,2,9,16,128]{4,3,2,1,0:T(8,128)S(1)}, f32[8,2,9,16,128]{4,3,2,1,0:T(8,128)S(1)}, f32[8,2,9,16,128]{4,3,2,1,0:T(8,128)S(1)}, f32[8,2,9,16,12...) custom-call(s32[1]{0:T(128)} %bitcast.place.refs_0_, s32[3,2,16]{2,1,0:T(2,128)S(1)} %bitcast.12, ...), custom_call_target="tpu_custom_call" | custom-call | flops 5000000 | bytes 8000000 | tf_op jit(solution)/shard_map/own_share/pallas_call | solution.py:171
  6.8 0.3 strength_blocks.1.refs_10_
  7.3 0.5 collective-permute-done.1.refs_3_
  7.8 6.7 %join.1 = (bf16[2,240,128]{2,1,0:T(8,128)(2,1)S(1)}, bf16[2,240,128]{2,1,0:T(8,128)(2,1)}, bf16[2,240,128]{2,1,0:T(8,128)(2,1)}, bf16[2,240,128]{2,1,0:T(8,128)(...) custom-call(s32[1]{0:T(128)} %bitcast.place.refs_0_, ...), custom_call_target="tpu_custom_call" | custom-call | flops 5000000 | bytes 8000000 | tf_op jit(solution)/shard_map/join/pallas_call | solution.py:297
  14.6 1.4 %collective-permute-start.3 = (bf16[2,240,128]{2,1,0:T(8,128)(2,1)}, bf16[2,240,128]{2,1,0:T(8,128)(2,1)S(1)}, u32[]{:S(2)}, u32[]{:S(2)}) collective-permute-start(bf16[2,240,128]{2,1,0:T(8,128)(2,1)} %get-tuple-element.34), channel_id=1, source_target_pairs={{0,4},{1,5},{2,6},{3,7},{4,0},{5,1},{6,2},{7,3},{8,12},{9,13},{10,... | collective-permute-start | bytes 368648 | tf_op jit(solution)/shard_map/ppermute | solution.py:448
  15.9 3.1 %collective-permute-start.4 = (bf16[2,240,128]{2,1,0:T(8,128)(2,1)}, bf16[2,240,128]{2,1,0:T(8,128)(2,1)S(1)}, u32[]{:S(2)}, u32[]{:S(2)}) collective-permute-start(bf16[2,240,128]{2,1,0:T(8,128)(2,1)} %get-tuple-element.35), channel_id=1, source_target_pairs={{0,9},{1,8},{2,11},{3,10},{4,13},{5,12},{6,15},{7,14},{8,1},{9,0},... | collective-permute-start | bytes 368648 | tf_op jit(solution)/shard_map/ppermute | solution.py:448
  19.0 1.1 %collective-permute-start.6 = (bf16[2,240,128]{2,1,0:T(8,128)(2,1)}, bf16[2,240,128]{2,1,0:T(8,128)(2,1)S(1)}, u32[]{:S(2)}, u32[]{:S(2)}) collective-permute-start(bf16[2,240,128]{2,1,0:T(8,128)(2,1)} %get-tuple-element.37), channel_id=1, source_target_pairs={{0,10},{1,11},{2,8},{3,9},{4,14},{5,15},{6,12},{7,13},{8,2},{9,3},... | collective-permute-start | bytes 368648 | tf_op jit(solution)/shard_map/ppermute | solution.py:448
  20.2 6.3 %collective-permute-start.7 = (bf16[2,240,128]{2,1,0:T(8,128)(2,1)}, bf16[2,240,128]{2,1,0:T(8,128)(2,1)S(1)}, u32[]{:S(2)}, u32[]{:S(2)}) collective-permute-start(bf16[2,240,128]{2,1,0:T(8,128)(2,1)} %get-tuple-element.38), channel_id=1, source_target_pairs={{0,6},{1,7},{2,4},{3,5},{4,2},{5,3},{6,0},{7,1},{8,14},{9,15},{10,... | collective-permute-start | bytes 368648 | tf_op jit(solution)/shard_map/ppermute | solution.py:448
  26.5 0.6 collective-permute-start.8
  27.0 5.0 %collective-permute-start.9 = (bf16[2,240,128]{2,1,0:T(8,128)(2,1)}, bf16[2,240,128]{2,1,0:T(8,128)(2,1)S(1)}, u32[]{:S(2)}, u32[]{:S(2)}) collective-permute-start(bf16[2,240,128]{2,1,0:T(8,128)(2,1)} %get-tuple-element.40), channel_id=1, source_target_pairs={{0,7},{1,6},{2,5},{3,4},{4,3},{5,2},{6,1},{7,0},{8,15},{9,14},{10,... | collective-permute-start | bytes 368648 | tf_op jit(solution)/shard_map/ppermute | solution.py:448
  32.0 2.5 %collective-permute-start.11 = (bf16[2,240,128]{2,1,0:T(8,128)(2,1)}, bf16[2,240,128]{2,1,0:T(8,128)(2,1)S(1)}, u32[]{:S(2)}, u32[]{:S(2)}) collective-permute-start(bf16[2,240,128]{2,1,0:T(8,128)(2,1)} %get-tuple-element.42), channel_id=1, source_target_pairs={{0,1},{1,0},{2,3},{3,2},{4,5},{5,4},{6,7},{7,6},{8,9},{9,8},{10,11... | collective-permute-start | bytes 368648 | tf_op jit(solution)/shard_map/ppermute | solution.py:448
  34.5 2.0 %collective-permute-start.12 = (bf16[2,240,128]{2,1,0:T(8,128)(2,1)}, bf16[2,240,128]{2,1,0:T(8,128)(2,1)S(1)}, u32[]{:S(2)}, u32[]{:S(2)}) collective-permute-start(bf16[2,240,128]{2,1,0:T(8,128)(2,1)} %get-tuple-element.43), channel_id=1, source_target_pairs={{0,13},{1,12},{2,15},{3,14},{4,9},{5,8},{6,11},{7,10},{8,5},{9,4},... | collective-permute-start | bytes 368648 | tf_op jit(solution)/shard_map/ppermute | solution.py:448
  36.6 2.4 %collective-permute-done.8.refs_7_ = bf16[2,240,128]{2,1,0:T(8,128)(2,1)S(1)} collective-permute-done((bf16[2,240,128]{2,1,0:T(8,128)(2,1)}, bf16[2,240,128]{2,1,0:T(8,128)(2,1)S(1)}, u32[]{:S(2)}, u32[]{:S(2)}) %collective-permute-start.8) | collective-permute-done | bytes 122912 | tf_op jit(solution)/shard_map/ppermute | solution.py:448
  39.3 1.5 %collective-permute-done.9.refs_8_ = bf16[2,240,128]{2,1,0:T(8,128)(2,1)S(1)} collective-permute-done((bf16[2,240,128]{2,1,0:T(8,128)(2,1)}, bf16[2,240,128]{2,1,0:T(8,128)(2,1)S(1)}, u32[]{:S(2)}, u32[]{:S(2)}) %collective-permute-start.9) | collective-permute-done | bytes 122912 | tf_op jit(solution)/shard_map/ppermute | solution.py:448
  40.7 0.7 %collective-permute-start.14 = (bf16[2,240,128]{2,1,0:T(8,128)(2,1)}, bf16[2,240,128]{2,1,0:T(8,128)(2,1)S(1)}, u32[]{:S(2)}, u32[]{:S(2)}) collective-permute-start(bf16[2,240,128]{2,1,0:T(8,128)(2,1)} %get-tuple-element.45), channel_id=1, source_target_pairs={{0,14},{1,15},{2,12},{3,13},{4,10},{5,11},{6,8},{7,9},{8,6},{9,7},... | collective-permute-start | bytes 368648 | tf_op jit(solution)/shard_map/ppermute | solution.py:448
  41.4 11.1 %collective-permute-done.10.refs_9_ = bf16[2,240,128]{2,1,0:T(8,128)(2,1)S(1)} collective-permute-done((bf16[2,240,128]{2,1,0:T(8,128)(2,1)}, bf16[2,240,128]{2,1,0:T(8,128)(2,1)S(1)}, u32[]{:S(2)}, u32[]{:S(2)}) %collective-permute-start.10) | collective-permute-done | bytes 122912 | tf_op jit(solution)/shard_map/ppermute | solution.py:448
  52.6 1.6 %collective-permute-start.15 = (bf16[2,240,128]{2,1,0:T(8,128)(2,1)}, bf16[2,240,128]{2,1,0:T(8,128)(2,1)S(1)}, u32[]{:S(2)}, u32[]{:S(2)}) collective-permute-start(bf16[2,240,128]{2,1,0:T(8,128)(2,1)} %get-tuple-element.46), channel_id=1, source_target_pairs={{0,3},{1,2},{2,1},{3,0},{4,7},{5,6},{6,5},{7,4},{8,11},{9,10},{10,... | collective-permute-start | bytes 368648 | tf_op jit(solution)/shard_map/ppermute | solution.py:448
  54.2 1.0 %collective-permute-done.12.refs_11_ = bf16[2,240,128]{2,1,0:T(8,128)(2,1)S(1)} collective-permute-done((bf16[2,240,128]{2,1,0:T(8,128)(2,1)}, bf16[2,240,128]{2,1,0:T(8,128)(2,1)S(1)}, u32[]{:S(2)}, u32[]{:S(2)}) %collective-permute-start.12) | collective-permute-done | bytes 122912 | tf_op jit(solution)/shard_map/ppermute | solution.py:448
  55.2 3.6 %collective-permute-done.14.refs_13_ = bf16[2,240,128]{2,1,0:T(8,128)(2,1)S(1)} collective-permute-done((bf16[2,240,128]{2,1,0:T(8,128)(2,1)}, bf16[2,240,128]{2,1,0:T(8,128)(2,1)S(1)}, u32[]{:S(2)}, u32[]{:S(2)}) %collective-permute-start.14) | collective-permute-done | bytes 122912 | tf_op jit(solution)/shard_map/ppermute | solution.py:448
  58.8 4.9 %collective-permute-done.15.refs_14_ = bf16[2,240,128]{2,1,0:T(8,128)(2,1)S(1)} collective-permute-done((bf16[2,240,128]{2,1,0:T(8,128)(2,1)}, bf16[2,240,128]{2,1,0:T(8,128)(2,1)S(1)}, u32[]{:S(2)}, u32[]{:S(2)}) %collective-permute-start.15) | collective-permute-done | bytes 122912 | tf_op jit(solution)/shard_map/ppermute | solution.py:448
  63.7 5.7 %score.1 = (bf16[4,56,512]{2,1,0:T(8,128)(2,1)}, bf16[2,4,56,512]{3,2,1,0:T(8,128)(2,1)}) custom-call(s32[1]{0:T(128)} %bitcast.place.refs_0_, bf16[2,240,128]{2,1,0:T(8,128)(2,1)S(1)} %get-tuple-element.32.refs_0_, bf16[2,240,128]{2,1,0:T(8,128)(2,1)S(1)} %collective-permute-done.2.refs_1_, bf16[2,240,128]{2,1,0:T(8,128)(2,1)S(1)} %collective-permute-done.3.refs_2_, ...), custom_call_target="tpu_custom_call" | custom-call | tf_op jit(solution)/shard_map/score/pallas_call | solution.py:409
  (22 shorter events, 0.8 us)
Async XLA Ops:
  0.6 7.1 %collective-permute-start.1 = (bf16[16,2,448,128]{3,2,1,0:T(8,128)(2,1)}, bf16[16,2,448,128]{3,2,1,0:T(8,128)(2,1)}, u32[]{:S(2)}, u32[]{:S(2)}) collective-permute-start(bf16[16,2,448,128]{3,2,1,0:T(8,128)(2,1)} %bitcast.14), channel_id=1, source_target_pairs={{0,1},{1,0},{2,3},{3,2},{4,5},{5,4},{6,7},{7,6},{8,9},{9,8},{10,11... | collective-permute-start | bytes 11010056 | tf_op jit(solution)/shard_map/ppermute | solution.py:442
  1.4 5.9 %collective-permute-start = (s32[3,2,16]{2,1,0:T(2,128)}, s32[3,2,16]{2,1,0:T(2,128)S(1)}, u32[]{:S(2)}, u32[]{:S(2)}) collective-permute-start(s32[3,2,16]{2,1,0:T(2,128)} %bitcast.11), channel_id=1, source_target_pairs={{0,1},{1,0},{2,3},{3,2},{4,5},{5,4},{6,7},{7,6},{8,9},{9,8},{10,11... | collective-permute-start | bytes 1160 | tf_op jit(solution)/shard_map/ppermute | solution.py:443
  1.5 1.2 %copy-start = (f32[14,14336]{1,0:T(8,128)S(1)}, f32[14,14336]{1,0:T(8,128)}, u32[]{:S(2)}) copy-start(f32[14,14336]{1,0:T(8,128)} %table_hbm.1) | copy-start | bytes 2408452
  2.6 0.7 copy-start.3
  3.3 3.4 %copy-start.2 = (f32[32,896]{1,0:T(8,128)S(1)}, f32[32,896]{1,0:T(8,128)}, u32[]{:S(2)}) copy-start(f32[32,896]{1,0:T(8,128)} %smoothing.1) | copy-start | bytes 344068
  7.8 56.0 %copy-start.1 = (bf16[4,512,56]{1,2,0:T(8,128)(2,1)S(1)}, bf16[4,512,56]{1,2,0:T(8,128)(2,1)}, u32[]{:S(2)}) copy-start(bf16[4,512,56]{1,2,0:T(8,128)(2,1)} %param.9) | copy-start | bytes 688132
  14.5 5.7 %collective-permute-start.2 = (bf16[2,240,128]{2,1,0:T(8,128)(2,1)}, bf16[2,240,128]{2,1,0:T(8,128)(2,1)S(1)}, u32[]{:S(2)}, u32[]{:S(2)}) collective-permute-start(bf16[2,240,128]{2,1,0:T(8,128)(2,1)} %get-tuple-element.33), channel_id=1, source_target_pairs={{0,8},{1,9},{2,10},{3,11},{4,12},{5,13},{6,14},{7,15},{8,0},{9,1},... | collective-permute-start | bytes 368648 | tf_op jit(solution)/shard_map/ppermute | solution.py:448
  14.6 11.9 %collective-permute-start.3 = (bf16[2,240,128]{2,1,0:T(8,128)(2,1)}, bf16[2,240,128]{2,1,0:T(8,128)(2,1)S(1)}, u32[]{:S(2)}, u32[]{:S(2)}) collective-permute-start(bf16[2,240,128]{2,1,0:T(8,128)(2,1)} %get-tuple-element.34), channel_id=1, source_target_pairs={{0,4},{1,5},{2,6},{3,7},{4,0},{5,1},{6,2},{7,3},{8,12},{9,13},{10,... | collective-permute-start | bytes 368648 | tf_op jit(solution)/shard_map/ppermute | solution.py:448
  15.9 11.1 %collective-permute-start.4 = (bf16[2,240,128]{2,1,0:T(8,128)(2,1)}, bf16[2,240,128]{2,1,0:T(8,128)(2,1)S(1)}, u32[]{:S(2)}, u32[]{:S(2)}) collective-permute-start(bf16[2,240,128]{2,1,0:T(8,128)(2,1)} %get-tuple-element.35), channel_id=1, source_target_pairs={{0,9},{1,8},{2,11},{3,10},{4,13},{5,12},{6,15},{7,14},{8,1},{9,0},... | collective-permute-start | bytes 368648 | tf_op jit(solution)/shard_map/ppermute | solution.py:448
  19.0 13.0 %collective-permute-start.5 = (bf16[2,240,128]{2,1,0:T(8,128)(2,1)}, bf16[2,240,128]{2,1,0:T(8,128)(2,1)S(1)}, u32[]{:S(2)}, u32[]{:S(2)}) collective-permute-start(bf16[2,240,128]{2,1,0:T(8,128)(2,1)} %get-tuple-element.36), channel_id=1, source_target_pairs={{0,5},{1,4},{2,7},{3,6},{4,1},{5,0},{6,3},{7,2},{8,13},{9,12},{10,... | collective-permute-start | bytes 368648 | tf_op jit(solution)/shard_map/ppermute | solution.py:448
  19.0 13.0 %collective-permute-start.6 = (bf16[2,240,128]{2,1,0:T(8,128)(2,1)}, bf16[2,240,128]{2,1,0:T(8,128)(2,1)S(1)}, u32[]{:S(2)}, u32[]{:S(2)}) collective-permute-start(bf16[2,240,128]{2,1,0:T(8,128)(2,1)} %get-tuple-element.37), channel_id=1, source_target_pairs={{0,10},{1,11},{2,8},{3,9},{4,14},{5,15},{6,12},{7,13},{8,2},{9,3},... | collective-permute-start | bytes 368648 | tf_op jit(solution)/shard_map/ppermute | solution.py:448
  20.2 14.3 %collective-permute-start.7 = (bf16[2,240,128]{2,1,0:T(8,128)(2,1)}, bf16[2,240,128]{2,1,0:T(8,128)(2,1)S(1)}, u32[]{:S(2)}, u32[]{:S(2)}) collective-permute-start(bf16[2,240,128]{2,1,0:T(8,128)(2,1)} %get-tuple-element.38), channel_id=1, source_target_pairs={{0,6},{1,7},{2,4},{3,5},{4,2},{5,3},{6,0},{7,1},{8,14},{9,15},{10,... | collective-permute-start | bytes 368648 | tf_op jit(solution)/shard_map/ppermute | solution.py:448
  26.5 12.5 %collective-permute-start.8 = (bf16[2,240,128]{2,1,0:T(8,128)(2,1)}, bf16[2,240,128]{2,1,0:T(8,128)(2,1)S(1)}, u32[]{:S(2)}, u32[]{:S(2)}) collective-permute-start(bf16[2,240,128]{2,1,0:T(8,128)(2,1)} %get-tuple-element.39), channel_id=1, source_target_pairs={{0,11},{1,10},{2,9},{3,8},{4,15},{5,14},{6,13},{7,12},{8,3},{9,2},... | collective-permute-start | bytes 368648 | tf_op jit(solution)/shard_map/ppermute | solution.py:448
  27.0 13.7 %collective-permute-start.9 = (bf16[2,240,128]{2,1,0:T(8,128)(2,1)}, bf16[2,240,128]{2,1,0:T(8,128)(2,1)S(1)}, u32[]{:S(2)}, u32[]{:S(2)}) collective-permute-start(bf16[2,240,128]{2,1,0:T(8,128)(2,1)} %get-tuple-element.40), channel_id=1, source_target_pairs={{0,7},{1,6},{2,5},{3,4},{4,3},{5,2},{6,1},{7,0},{8,15},{9,14},{10,... | collective-permute-start | bytes 368648 | tf_op jit(solution)/shard_map/ppermute | solution.py:448
  32.0 20.6 %collective-permute-start.10 = (bf16[2,240,128]{2,1,0:T(8,128)(2,1)}, bf16[2,240,128]{2,1,0:T(8,128)(2,1)S(1)}, u32[]{:S(2)}, u32[]{:S(2)}) collective-permute-start(bf16[2,240,128]{2,1,0:T(8,128)(2,1)} %get-tuple-element.41), channel_id=1, source_target_pairs={{0,12},{1,13},{2,14},{3,15},{4,8},{5,9},{6,10},{7,11},{8,4},{9,5},... | collective-permute-start | bytes 368648 | tf_op jit(solution)/shard_map/ppermute | solution.py:448
  32.0 22.2 %collective-permute-start.11 = (bf16[2,240,128]{2,1,0:T(8,128)(2,1)}, bf16[2,240,128]{2,1,0:T(8,128)(2,1)S(1)}, u32[]{:S(2)}, u32[]{:S(2)}) collective-permute-start(bf16[2,240,128]{2,1,0:T(8,128)(2,1)} %get-tuple-element.42), channel_id=1, source_target_pairs={{0,1},{1,0},{2,3},{3,2},{4,5},{5,4},{6,7},{7,6},{8,9},{9,8},{10,11... | collective-permute-start | bytes 368648 | tf_op jit(solution)/shard_map/ppermute | solution.py:448
  34.5 20.7 %collective-permute-start.12 = (bf16[2,240,128]{2,1,0:T(8,128)(2,1)}, bf16[2,240,128]{2,1,0:T(8,128)(2,1)S(1)}, u32[]{:S(2)}, u32[]{:S(2)}) collective-permute-start(bf16[2,240,128]{2,1,0:T(8,128)(2,1)} %get-tuple-element.43), channel_id=1, source_target_pairs={{0,13},{1,12},{2,15},{3,14},{4,9},{5,8},{6,11},{7,10},{8,5},{9,4},... | collective-permute-start | bytes 368648 | tf_op jit(solution)/shard_map/ppermute | solution.py:448
  39.0 16.2 %collective-permute-start.13 = (bf16[2,240,128]{2,1,0:T(8,128)(2,1)}, bf16[2,240,128]{2,1,0:T(8,128)(2,1)S(1)}, u32[]{:S(2)}, u32[]{:S(2)}) collective-permute-start(bf16[2,240,128]{2,1,0:T(8,128)(2,1)} %get-tuple-element.44), channel_id=1, source_target_pairs={{0,2},{1,3},{2,0},{3,1},{4,6},{5,7},{6,4},{7,5},{8,10},{9,11},{10,... | collective-permute-start | bytes 368648 | tf_op jit(solution)/shard_map/ppermute | solution.py:448
  40.7 18.1 %collective-permute-start.14 = (bf16[2,240,128]{2,1,0:T(8,128)(2,1)}, bf16[2,240,128]{2,1,0:T(8,128)(2,1)S(1)}, u32[]{:S(2)}, u32[]{:S(2)}) collective-permute-start(bf16[2,240,128]{2,1,0:T(8,128)(2,1)} %get-tuple-element.45), channel_id=1, source_target_pairs={{0,14},{1,15},{2,12},{3,13},{4,10},{5,11},{6,8},{7,9},{8,6},{9,7},... | collective-permute-start | bytes 368648 | tf_op jit(solution)/shard_map/ppermute | solution.py:448
  52.6 11.1 %collective-permute-start.15 = (bf16[2,240,128]{2,1,0:T(8,128)(2,1)}, bf16[2,240,128]{2,1,0:T(8,128)(2,1)S(1)}, u32[]{:S(2)}, u32[]{:S(2)}) collective-permute-start(bf16[2,240,128]{2,1,0:T(8,128)(2,1)} %get-tuple-element.46), channel_id=1, source_target_pairs={{0,3},{1,2},{2,1},{3,0},{4,7},{5,6},{6,5},{7,4},{8,11},{9,10},{10,... | collective-permute-start | bytes 368648 | tf_op jit(solution)/shard_map/ppermute | solution.py:448
  54.2 9.5 %collective-permute-start.16 = (bf16[2,240,128]{2,1,0:T(8,128)(2,1)}, bf16[2,240,128]{2,1,0:T(8,128)(2,1)S(1)}, u32[]{:S(2)}, u32[]{:S(2)}) collective-permute-start(bf16[2,240,128]{2,1,0:T(8,128)(2,1)} %get-tuple-element.47), channel_id=1, source_target_pairs={{0,15},{1,14},{2,13},{3,12},{4,11},{5,10},{6,9},{7,8},{8,7},{9,6},... | collective-permute-start | bytes 368648 | tf_op jit(solution)/shard_map/ppermute | solution.py:448

commit v5 on v4

--- a/solution.py
+++ b/solution.py
@@ -44,7 +44,7 @@
         self.rows = regions * ROWS
         self.main = round_up(FIELDS * self.span, 16)
         self.offsets = swap_order(regions)
-        self.sent = self.main + 16
+        self.sent = self.main + 8
 
 
 def stage(staged, tile):
@@ -69,19 +69,20 @@
 
 
 def add_side(sums, tile, column, fresh):
+    for parity, placed in enumerate(place_side(tile, column)):
+        for t, piece in enumerate(placed):
+            sums[parity, t + 1] = piece if fresh else sums[parity, t + 1] + piece
+
+
+def place_side(tile, column):
     pairs = jnp.concatenate([tile(t) for t in range(TILES)], 1)
     turned = pltpu.roll(pairs, PATCH, 1)
     lane = lax.broadcasted_iota(jnp.int32, pairs.shape, 1)
     left = (lane < PATCH) & (column == 0)
     right = (lane >= PATCH) & (column != 0)
-    placed = (
-        jnp.where(left, pairs, jnp.where(right, turned, 0.0)),
-        jnp.where(left, turned, jnp.where(right, pairs, 0.0)),
-    )
-    for parity in range(2):
-        for t in range(TILES):
-            piece = placed[parity][:, LANES * t : LANES * (t + 1)]
-            sums[parity, t + 1] = piece if fresh else sums[parity, t + 1] + piece
+    even = jnp.where(left, pairs, jnp.where(right, turned, 0.0))
+    odd = jnp.where(left, turned, jnp.where(right, pairs, 0.0))
+    return [[rows[:, LANES * t : LANES * (t + 1)] for t in range(TILES)] for rows in (even, odd)]
 
 
 def add_any(sums, tile, column, fresh):
@@ -188,30 +189,35 @@
     )(place, lists, tiles, table)
 
 
-def strength_kernel(z, smoothing, _, strength):
-    turned_strength = jnp.transpose(smoothing[...] - MID)
-    for dest in range(z.regions):
-        for g in range(z.span // 8):
-            top = z.width * dest + 8 * g
-            count, at = min(8, COLS - top), ROWS * (g % QUAD)
-            strength[dest, g // QUAD, 0:count, at : at + ROWS] = turned_strength[top : top + count]
-
-
-def strength_blocks(z, smoothing, before):
+def strength_kernel(z, place, gathered, strength):
+    start = place[0] * z.width
+    tile, shift = lax.div(start, LANES), lax.rem(start, LANES)
+    lane = lax.broadcasted_iota(jnp.int32, (z.rows, LANES), 1)
+    low, high = (
+        pltpu.roll(
+            gathered[:, pl.ds(pl.multiple_of(t * LANES, LANES), LANES)].astype(jnp.float32), LANES - shift, 1
+        )
+        for t in (tile, jnp.minimum(tile + 1, TILES - 1))
+    )
+    strength[...] = jnp.transpose(jnp.where(lane < LANES - shift, low, high))[0 : z.span] + MID
+
+
+def own_strength(z, place, gathered):
     return pl.pallas_call(
         functools.partial(strength_kernel, z),
-        out_shape=jax.ShapeDtypeStruct((z.regions, z.quads, 8, LANES), jnp.float32),
-        in_specs=[pl.BlockSpec(memory_space=pltpu.VMEM), pl.BlockSpec(memory_space=pl.ANY)],
+        out_shape=jax.ShapeDtypeStruct((z.span, z.rows), jnp.float32),
+        in_specs=[pl.BlockSpec(memory_space=pltpu.SMEM), pl.BlockSpec(memory_space=pltpu.VMEM)],
         out_specs=pl.BlockSpec(memory_space=pltpu.VMEM),
         compiler_params=pltpu.CompilerParams(vmem_limit_bytes=VMEM),
-        name="strength_blocks",
-    )(smoothing, before)
+        cost_estimate=pl.CostEstimate(flops=1_000_000, bytes_accessed=1_000_000, transcendentals=0),
+        name="own_strength",
+    )(place, gathered)
 
 
 def join_kernel(z, *refs):
     place, lists, refs = refs[0], refs[1 : 1 + z.makers], refs[1 + z.makers :]
     received, refs = refs[: z.makers - 1], refs[z.makers - 1 :]
-    half, (total, weights, strength), outs = refs[:FIELDS], refs[FIELDS : FIELDS + 3], refs[FIELDS + 3 : -6]
+    half, (total, weights), outs = refs[:FIELDS], refs[FIELDS : FIELDS + 2], refs[FIELDS + 2 : -6]
     staged, sums, lines, turned, blocks, sems = refs[-6:]
     me = place[0]
     first = lax.rem(me, z.makers) * z.block
@@ -234,27 +240,34 @@
                         stage(staged.at[index], received[maker - 1][first + j, slot])
                         entries.append((index, *(lists[maker][entry, slot, first + j] for entry in (1, 2))))
 
-                def begin(index, own):
+                def joined(own, index, tile_of):
+                    if add is add_side:
+                        ((_, column, _),) = entries
+                        placed = place_side(tile_of(entries[0]), column)
+                        return [
+                            [own[j, parity, t + 1] + piece for t, piece in enumerate(placed[parity])]
+                            for parity in range(2)
+                        ]
                     for parity in range(2):
                         for t in range(SLOTS):
                             sums[index, parity, t] = own[j, parity, t]
-
-                begin(FIELDS, total)
-                for _, column, kind in entries:
-                    add(sums.at[FIELDS], functools.partial(weight_tile, weights, kind), column, False)
-                inverse = [[1.0 / sums[FIELDS, parity, t + 1] for t in range(TILES)] for parity in range(2)]
+                    for entry in entries:
+                        add(sums.at[index], tile_of(entry), entry[1], False)
+                    return [[sums[index, parity, t + 1] for t in range(TILES)] for parity in range(2)]
+
+                def weight_of(entry):
+                    return functools.partial(weight_tile, weights, entry[2])
+
+                def field_of(field, entry):
+                    return lambda t: staged_tile(staged.at[entry[0]], field, t) * weight_tile(weights, entry[2], t)
+
+                inverse = [[1.0 / piece for piece in rows] for rows in joined(total, FIELDS, weight_of)]
                 for field in range(FIELDS):
-                    begin(field, half[field])
-                    for index, column, kind in entries:
-
-                        def tile(t):
-                            return staged_tile(staged.at[index], field, t) * weight_tile(weights, kind, t)
-
-                        add(sums.at[field], tile, column, False)
+                    pieces = joined(half[field], field, functools.partial(field_of, field))
                     for parity in range(2):
                         for t in range(TILES):
                             lines[field, t, pl.ds(ROWS * i + parity, PAIRS, stride=2), :] = (
-                                sums[field, parity, t + 1] * inverse[parity][t]
+                                pieces[parity][t] * inverse[parity][t]
                             )
 
             either_kind(z, lists[0][0, 1, first + j] >= 0, body)
@@ -280,7 +293,6 @@
                 target[low * z.span : (low + 2) * z.span, :] = jnp.concatenate(block, 0).astype(jnp.bfloat16)
             ends = (jnp.maximum(top - 1, 0), jnp.minimum(top + z.width, COLS - 1))
             edge = [turned[field, pl.ds(end, 1), :] for field in range(FIELDS) for end in ends]
-            edge.append(strength[dest, quad])
             target[z.main : z.sent, :] = jnp.concatenate(edge, 0).astype(jnp.bfloat16)
             if i:
                 send(i, quad).start()
@@ -327,7 +339,7 @@
 
 def score_kernel(z, place, *refs):
     blocks = dict(zip(z.offsets, refs))
-    analysis, crps, spread, strength, edges, padded = refs[z.regions :]
+    strength, analysis, crps, spread, edges, padded = refs[z.regions :]
     me = place[0]
     step = pl.program_id(0)
     rows = z.rows
@@ -338,21 +350,11 @@
 
     @pl.when(step == 0)
     def _():
-        slot = lax.broadcasted_iota(jnp.int32, (8, LANES), 1) // ROWS
-        for low in range(0, z.regions, QUAD):
-            offsets = range(low, low + QUAD)
-            slots = [lax.rem(me ^ offset, QUAD) for offset in offsets]
-            at = pl.multiple_of(lax.div(me ^ low, QUAD) * LANES, LANES)
+        for offset in range(z.regions):
             for quad in range(z.quads):
-                tails = [blocks[offset][quad, z.main : z.sent, :].astype(jnp.float32) for offset in offsets]
-                for offset, tail in zip(offsets, tails):
-                    edges[offset // z.makers, :, lanes_of(offset, quad)] = tail[0:8]
-                for g in range(quad * QUAD, min((quad + 1) * QUAD, z.span // 8)):
-                    joined = jnp.zeros((8, LANES), jnp.float32)
-                    for i, tail in zip(slots, tails):
-                        near = pltpu.roll(tail[8:16], lax.rem(i + QUAD - g % QUAD, QUAD) * ROWS, 1)
-                        joined = jnp.where(slot == i, near, joined)
-                    strength[8 * g : 8 * (g + 1), pl.ds(at, LANES)] = joined + MID
+                edges[offset // z.makers, :, lanes_of(offset, quad)] = blocks[offset][
+                    quad, z.main : z.sent, :
+                ].astype(jnp.float32)
 
     top = pl.multiple_of(step * STEP_FIELDS * z.span, 16)
     for offset in range(z.regions):
@@ -404,7 +406,7 @@
             spread[1, f, low:high, :] = ((average - target) ** 2).astype(jnp.bfloat16)
 
 
-def score(z, place, blocks, analysis):
+def score(z, place, blocks, strength, analysis):
     width, rows = z.width, z.rows
     return pl.pallas_call(
         functools.partial(score_kernel, z),
@@ -414,20 +416,19 @@
         ],
         grid=(FIELDS // STEP_FIELDS,),
         in_specs=[pl.BlockSpec(memory_space=pltpu.SMEM)]
-        + [pl.BlockSpec(memory_space=pltpu.VMEM)] * z.regions
+        + [pl.BlockSpec(memory_space=pltpu.VMEM)] * (z.regions + 1)
         + [pl.BlockSpec((STEP_FIELDS, width, rows), lambda i: (i, 0, 0))],
         out_specs=[
             pl.BlockSpec((STEP_FIELDS, width, rows), lambda i: (i, 0, 0)),
             pl.BlockSpec((2, STEP_FIELDS, width, rows), lambda i: (0, i, 0, 0)),
         ],
         scratch_shapes=[
-            pltpu.VMEM((z.span, rows), jnp.float32),
             pltpu.VMEM((SAMPLES, 8, rows), jnp.float32),
             pltpu.VMEM((SAMPLES, STEP_FIELDS, z.span + 16, rows), jnp.float32),
         ],
         compiler_params=pltpu.CompilerParams(vmem_limit_bytes=VMEM),
         name="score",
-    )(place, *blocks, analysis)
+    )(place, *blocks, strength, analysis)
 
 
 def shards(patch_tiles, slot_lists, blend_table, smoothing, analysis):
@@ -436,19 +437,20 @@
     turns = [
         [(i, i - i % z.makers + (i + k) % z.makers) for i in range(z.regions)] for k in range(1, z.makers)
     ]
+    gathered = lax.all_gather((smoothing - MID).astype(jnp.bfloat16), "region", tiled=True)
     tiles = patch_tiles.reshape(z.regions, CAP, FIELDS, PAIRS * TILES, LANES)
     tiles = jnp.swapaxes(tiles, 2, 3).reshape(z.regions, CAP, LINES, LANES)
     lists = jnp.transpose(slot_lists, (2, 1, 0))
     received = [lax.ppermute(tiles, "region", turn) for turn in turns]
     lists = [lists] + [lax.ppermute(lists, "region", turn) for turn in turns]
     shares = own_share(z, place, lists[0], tiles, blend_table)
-    shares = [*shares, strength_blocks(z, smoothing, shares[-1])]
     blocks = join(z, place, lists, received, shares)
     moved = [blocks[0]] + [
         lax.ppermute(block, "region", [(i, i ^ offset) for i in range(z.regions)])
         for block, offset in zip(blocks[1:], z.offsets[1:])
     ]
-    outs = score(z, place, moved, jnp.swapaxes(analysis, 1, 2))
+    strength = own_strength(z, place, gathered)
+    outs = score(z, place, moved, strength, jnp.swapaxes(analysis, 1, 2))
     return tuple(jnp.swapaxes(item, -1, -2) for item in outs)
 
 

time: 68.3 us -> 85.6 us (1.25)
  the two profiles are of different devices: /device:TPU:17 before, /device:TPU:1 now
where the time goes in v5:
time: 85.6 us; the launch traced here: 85.4 us
  starting transfers between devices  36.4 us (43%)
  blocking collectives  25.7 us (30%)
  Pallas kernels  15.8 us (18%)
  waiting for transfers between devices  4.84 us (6%)
  local copies, waits for them, and re-layouts  1.87 us (2%)
    ppermute x15, starting transfers between devices, shards(): lax.ppermute(block, 'region', [(i, i ^ offset) for i in range(z.regions)])  35.8 us
    all_gather x1, blocking collectives, shards(): lax.all_gather((smoothing - MID).astype(jnp.bfloat16), 'region', tiled=True)  25.7 us
    pallas_call x1, Pallas kernels, join(): pl.pallas_call(functools.partial(join_kernel, z), out_shape=[jax.ShapeDty...  6.65 us
    pallas_call x1, Pallas kernels, score(): pl.pallas_call(functools.partial(score_kernel, z), out_shape=[jax.ShapeDt...  5.53 us
    ppermute x15, waiting for transfers between devices, shards(): lax.ppermute(block, 'region', [(i, i ^ offset) for i in range(z.regions)])  3.89 us
    pallas_call x1, Pallas kernels, own_share(): pl.pallas_call(functools.partial(own_kernel, z), out_shape=[*[jax.ShapeDt...  3.42 us
    unnamed x8, local copies, waits for them, and re-layouts  1.87 us
  transfers between devices with their start and end apart: 17, of which 3 were waited for; matrix products, arithmetic and copies ran while one was open for 0% of the time, Pallas kernels for 4%

profile of v5, /device:TPU:1, one launch (start us, length us, event | category | flops | bytes accessed | tf_op | source)
XLA Modules:
  0.0 85.4 jit_solution(9037154955304285137)
XLA Ops:
  0.6 0.1 collective-permute-start.1
  0.8 0.5 collective-permute-start
  1.2 1.2 %copy-done = f32[14,14336]{1,0:T(8,128)S(1)} copy-done((f32[14,14336]{1,0:T(8,128)S(1)}, f32[14,14336]{1,0:T(8,128)}, u32[]{:S(2)}) %copy-start) | copy-done | bytes 802840
  2.4 0.7 copy-done.2
  3.1 3.4 %own_share.1 = (f32[8,2,9,16,128]{4,3,2,1,0:T(8,128)S(1)}, f32[8,2,9,16,128]{4,3,2,1,0:T(8,128)S(1)}, f32[8,2,9,16,128]{4,3,2,1,0:T(8,128)S(1)}, f32[8,2,9,16,12...) custom-call(s32[1]{0:T(128)} %bitcast.place.refs_0_, s32[3,2,16]{2,1,0:T(2,128)S(1)} %bitcast.12, ...), custom_call_target="tpu_custom_call" | custom-call | flops 5000000 | bytes 8000000 | tf_op jit(solution)/shard_map/own_share/pallas_call | solution.py:172
  6.5 0.9 %collective-permute-done.1.refs_3_ = bf16[16,2,448,128]{3,2,1,0:T(8,128)(2,1)} collective-permute-done((bf16[16,2,448,128]{3,2,1,0:T(8,128)(2,1)}, bf16[16,2,448,128]{3,2,1,0:T(8,128)(2,1)}, u32[]{:S(2)}, u32[]{:S(2)}) %collective-permute-start.1) | collective-permute-done | bytes 3670048 | tf_op jit(solution)/shard_map/ppermute | solution.py:444
  7.5 6.6 %join.1 = (bf16[2,232,128]{2,1,0:T(8,128)(2,1)S(1)}, bf16[2,232,128]{2,1,0:T(8,128)(2,1)}, bf16[2,232,128]{2,1,0:T(8,128)(2,1)}, bf16[2,232,128]{2,1,0:T(8,128)(...) custom-call(s32[1]{0:T(128)} %bitcast.place.refs_0_, ...), custom_call_target="tpu_custom_call" | custom-call | flops 5000000 | bytes 8000000 | tf_op jit(solution)/shard_map/join/pallas_call | solution.py:309
  14.1 4.5 %collective-permute-start.10 = (bf16[2,232,128]{2,1,0:T(8,128)(2,1)}, bf16[2,232,128]{2,1,0:T(8,128)(2,1)S(1)}, u32[]{:S(2)}, u32[]{:S(2)}) collective-permute-start(bf16[2,232,128]{2,1,0:T(8,128)(2,1)} %get-tuple-element.41), channel_id=1, source_target_pairs={{0,12},{1,13},{2,14},{3,15},{4,8},{5,9},{6,10},{7,11},{8,4},{9,5},... | collective-permute-start | bytes 356360 | tf_op jit(solution)/shard_map/ppermute | solution.py:449
  18.6 0.7 collective-permute-start.11
  19.3 1.2 %collective-permute-start.13 = (bf16[2,232,128]{2,1,0:T(8,128)(2,1)}, bf16[2,232,128]{2,1,0:T(8,128)(2,1)S(1)}, u32[]{:S(2)}, u32[]{:S(2)}) collective-permute-start(bf16[2,232,128]{2,1,0:T(8,128)(2,1)} %get-tuple-element.44), channel_id=1, source_target_pairs={{0,2},{1,3},{2,0},{3,1},{4,6},{5,7},{6,4},{7,5},{8,10},{9,11},{10,... | collective-permute-start | bytes 356360 | tf_op jit(solution)/shard_map/ppermute | solution.py:449
  20.6 3.1 %collective-permute-start.14 = (bf16[2,232,128]{2,1,0:T(8,128)(2,1)}, bf16[2,232,128]{2,1,0:T(8,128)(2,1)S(1)}, u32[]{:S(2)}, u32[]{:S(2)}) collective-permute-start(bf16[2,232,128]{2,1,0:T(8,128)(2,1)} %get-tuple-element.45), channel_id=1, source_target_pairs={{0,14},{1,15},{2,12},{3,13},{4,10},{5,11},{6,8},{7,9},{8,6},{9,7},... | collective-permute-start | bytes 356360 | tf_op jit(solution)/shard_map/ppermute | solution.py:449
  23.7 2.2 %collective-permute-start.15 = (bf16[2,232,128]{2,1,0:T(8,128)(2,1)}, bf16[2,232,128]{2,1,0:T(8,128)(2,1)S(1)}, u32[]{:S(2)}, u32[]{:S(2)}) collective-permute-start(bf16[2,232,128]{2,1,0:T(8,128)(2,1)} %get-tuple-element.46), channel_id=1, source_target_pairs={{0,3},{1,2},{2,1},{3,0},{4,7},{5,6},{6,5},{7,4},{8,11},{9,10},{10,... | collective-permute-start | bytes 356360 | tf_op jit(solution)/shard_map/ppermute | solution.py:449
  25.9 2.2 %collective-permute-start.16 = (bf16[2,232,128]{2,1,0:T(8,128)(2,1)}, bf16[2,232,128]{2,1,0:T(8,128)(2,1)S(1)}, u32[]{:S(2)}, u32[]{:S(2)}) collective-permute-start(bf16[2,232,128]{2,1,0:T(8,128)(2,1)} %get-tuple-element.47), channel_id=1, source_target_pairs={{0,15},{1,14},{2,13},{3,12},{4,11},{5,10},{6,9},{7,8},{8,7},{9,6},... | collective-permute-start | bytes 356360 | tf_op jit(solution)/shard_map/ppermute | solution.py:449
  28.1 8.3 %collective-permute-start.2 = (bf16[2,232,128]{2,1,0:T(8,128)(2,1)}, bf16[2,232,128]{2,1,0:T(8,128)(2,1)S(1)}, u32[]{:S(2)}, u32[]{:S(2)}) collective-permute-start(bf16[2,232,128]{2,1,0:T(8,128)(2,1)} %get-tuple-element.33), channel_id=1, source_target_pairs={{0,8},{1,9},{2,10},{3,11},{4,12},{5,13},{6,14},{7,15},{8,0},{9,1},... | collective-permute-start | bytes 356360 | tf_op jit(solution)/shard_map/ppermute | solution.py:449
  36.4 4.2 %collective-permute-start.4 = (bf16[2,232,128]{2,1,0:T(8,128)(2,1)}, bf16[2,232,128]{2,1,0:T(8,128)(2,1)S(1)}, u32[]{:S(2)}, u32[]{:S(2)}) collective-permute-start(bf16[2,232,128]{2,1,0:T(8,128)(2,1)} %get-tuple-element.35), channel_id=1, source_target_pairs={{0,9},{1,8},{2,11},{3,10},{4,13},{5,12},{6,15},{7,14},{8,1},{9,0},... | collective-permute-start | bytes 356360 | tf_op jit(solution)/shard_map/ppermute | solution.py:449
  40.6 0.1 collective-permute-start.5
  40.7 3.7 %collective-permute-start.6 = (bf16[2,232,128]{2,1,0:T(8,128)(2,1)}, bf16[2,232,128]{2,1,0:T(8,128)(2,1)S(1)}, u32[]{:S(2)}, u32[]{:S(2)}) collective-permute-start(bf16[2,232,128]{2,1,0:T(8,128)(2,1)} %get-tuple-element.37), channel_id=1, source_target_pairs={{0,10},{1,11},{2,8},{3,9},{4,14},{5,15},{6,12},{7,13},{8,2},{9,3},... | collective-permute-start | bytes 356360 | tf_op jit(solution)/shard_map/ppermute | solution.py:449
  44.4 2.8 %collective-permute-done.2.refs_1_ = bf16[2,232,128]{2,1,0:T(8,128)(2,1)S(1)} collective-permute-done((bf16[2,232,128]{2,1,0:T(8,128)(2,1)}, bf16[2,232,128]{2,1,0:T(8,128)(2,1)S(1)}, u32[]{:S(2)}, u32[]{:S(2)}) %collective-permute-start.2) | collective-permute-done | bytes 118816 | tf_op jit(solution)/shard_map/ppermute | solution.py:449
  47.2 4.1 %collective-permute-start.8 = (bf16[2,232,128]{2,1,0:T(8,128)(2,1)}, bf16[2,232,128]{2,1,0:T(8,128)(2,1)S(1)}, u32[]{:S(2)}, u32[]{:S(2)}) collective-permute-start(bf16[2,232,128]{2,1,0:T(8,128)(2,1)} %get-tuple-element.39), channel_id=1, source_target_pairs={{0,11},{1,10},{2,9},{3,8},{4,15},{5,14},{6,13},{7,12},{8,3},{9,2},... | collective-permute-start | bytes 356360 | tf_op jit(solution)/shard_map/ppermute | solution.py:449
  51.3 1.0 %collective-permute-done.4.refs_3_ = bf16[2,232,128]{2,1,0:T(8,128)(2,1)S(1)} collective-permute-done((bf16[2,232,128]{2,1,0:T(8,128)(2,1)}, bf16[2,232,128]{2,1,0:T(8,128)(2,1)S(1)}, u32[]{:S(2)}, u32[]{:S(2)}) %collective-permute-start.4) | collective-permute-done | bytes 118816 | tf_op jit(solution)/shard_map/ppermute | solution.py:449
  52.3 1.6 %collective-permute-start.9 = (bf16[2,232,128]{2,1,0:T(8,128)(2,1)}, bf16[2,232,128]{2,1,0:T(8,128)(2,1)S(1)}, u32[]{:S(2)}, u32[]{:S(2)}) collective-permute-start(bf16[2,232,128]{2,1,0:T(8,128)(2,1)} %get-tuple-element.40), channel_id=1, source_target_pairs={{0,7},{1,6},{2,5},{3,4},{4,3},{5,2},{6,1},{7,0},{8,15},{9,14},{10,... | collective-permute-start | bytes 356360 | tf_op jit(solution)/shard_map/ppermute | solution.py:449
  53.8 25.7 %all_gather.3.gathered = bf16[512,896]{1,0:T(8,128)(2,1)S(1)} all-gather(bf16[32,896]{1,0:T(8,128)(2,1)S(1)} %add_convert_fusion), channel_id=1, replica_groups=mesh['groups'=2,'region'=16] {'region'}, dimensions={0}, use_global_device_ids=true | all-gather | bytes 974848 | tf_op jit(solution)/shard_map/all_gather | solution.py:440
  79.6 0.2 own_strength.1.refs_16_
  79.8 5.5 %score.1 = (bf16[4,56,512]{2,1,0:T(8,128)(2,1)}, bf16[2,4,56,512]{3,2,1,0:T(8,128)(2,1)}) custom-call(s32[1]{0:T(128)} %bitcast.place.refs_0_, bf16[2,232,128]{2,1,0:T(8,128)(2,1)S(1)} %get-tuple-element.32.refs_0_, bf16[2,232,128]{2,1,0:T(8,128)(2,1)S(1)} %collective-permute-done.2.refs_1_, bf16[2,232,128]{2,1,0:T(8,128)(2,1)S(1)} %collective-permute-done.3.refs_2_, ...), custom_call_target="tpu_custom_call" | custom-call | tf_op jit(solution)/shard_map/score/pallas_call | solution.py:411
  (24 shorter events, 0.1 us)
Async XLA Ops:
  0.6 6.8 %collective-permute-start.1 = (bf16[16,2,448,128]{3,2,1,0:T(8,128)(2,1)}, bf16[16,2,448,128]{3,2,1,0:T(8,128)(2,1)}, u32[]{:S(2)}, u32[]{:S(2)}) collective-permute-start(bf16[16,2,448,128]{3,2,1,0:T(8,128)(2,1)} %bitcast.14), channel_id=1, source_target_pairs={{0,1},{1,0},{2,3},{3,2},{4,5},{5,4},{6,7},{7,6},{8,9},{9,8},{10,11... | collective-permute-start | bytes 11010056 | tf_op jit(solution)/shard_map/ppermute | solution.py:444
  0.8 5.7 %collective-permute-start = (s32[3,2,16]{2,1,0:T(2,128)}, s32[3,2,16]{2,1,0:T(2,128)S(1)}, u32[]{:S(2)}, u32[]{:S(2)}) collective-permute-start(s32[3,2,16]{2,1,0:T(2,128)} %bitcast.11), channel_id=1, source_target_pairs={{0,1},{1,0},{2,3},{3,2},{4,5},{5,4},{6,7},{7,6},{8,9},{9,8},{10,11... | collective-permute-start | bytes 1160 | tf_op jit(solution)/shard_map/ppermute | solution.py:445
  1.2 1.2 %copy-start = (f32[14,14336]{1,0:T(8,128)S(1)}, f32[14,14336]{1,0:T(8,128)}, u32[]{:S(2)}) copy-start(f32[14,14336]{1,0:T(8,128)} %table_hbm.1) | copy-start | bytes 2408452
  2.4 0.7 copy-start.2
  7.5 33.1 %copy-start.3 = (f32[32,896]{1,0:T(8,128)S(1)}, f32[32,896]{1,0:T(8,128)}, u32[]{:S(2)}) copy-start(f32[32,896]{1,0:T(8,128)} %param.8) | copy-start | bytes 344068
  14.1 65.7 %copy-start.1 = (bf16[4,512,56]{1,2,0:T(8,128)(2,1)S(1)}, bf16[4,512,56]{1,2,0:T(8,128)(2,1)}, u32[]{:S(2)}) copy-start(bf16[4,512,56]{1,2,0:T(8,128)(2,1)} %param.9) | copy-start | bytes 688132
  14.1 9.5 %collective-permute-start.10 = (bf16[2,232,128]{2,1,0:T(8,128)(2,1)}, bf16[2,232,128]{2,1,0:T(8,128)(2,1)S(1)}, u32[]{:S(2)}, u32[]{:S(2)}) collective-permute-start(bf16[2,232,128]{2,1,0:T(8,128)(2,1)} %get-tuple-element.41), channel_id=1, source_target_pairs={{0,12},{1,13},{2,14},{3,15},{4,8},{5,9},{6,10},{7,11},{8,4},{9,5},... | collective-permute-start | bytes 356360 | tf_op jit(solution)/shard_map/ppermute | solution.py:449
  18.6 7.2 %collective-permute-start.11 = (bf16[2,232,128]{2,1,0:T(8,128)(2,1)}, bf16[2,232,128]{2,1,0:T(8,128)(2,1)S(1)}, u32[]{:S(2)}, u32[]{:S(2)}) collective-permute-start(bf16[2,232,128]{2,1,0:T(8,128)(2,1)} %get-tuple-element.42), channel_id=1, source_target_pairs={{0,1},{1,0},{2,3},{3,2},{4,5},{5,4},{6,7},{7,6},{8,9},{9,8},{10,11... | collective-permute-start | bytes 356360 | tf_op jit(solution)/shard_map/ppermute | solution.py:449
  19.3 8.8 %collective-permute-start.12 = (bf16[2,232,128]{2,1,0:T(8,128)(2,1)}, bf16[2,232,128]{2,1,0:T(8,128)(2,1)S(1)}, u32[]{:S(2)}, u32[]{:S(2)}) collective-permute-start(bf16[2,232,128]{2,1,0:T(8,128)(2,1)} %get-tuple-element.43), channel_id=1, source_target_pairs={{0,13},{1,12},{2,15},{3,14},{4,9},{5,8},{6,11},{7,10},{8,5},{9,4},... | collective-permute-start | bytes 356360 | tf_op jit(solution)/shard_map/ppermute | solution.py:449
  19.3 17.0 %collective-permute-start.13 = (bf16[2,232,128]{2,1,0:T(8,128)(2,1)}, bf16[2,232,128]{2,1,0:T(8,128)(2,1)S(1)}, u32[]{:S(2)}, u32[]{:S(2)}) collective-permute-start(bf16[2,232,128]{2,1,0:T(8,128)(2,1)} %get-tuple-element.44), channel_id=1, source_target_pairs={{0,2},{1,3},{2,0},{3,1},{4,6},{5,7},{6,4},{7,5},{8,10},{9,11},{10,... | collective-permute-start | bytes 356360 | tf_op jit(solution)/shard_map/ppermute | solution.py:449
  20.6 15.8 %collective-permute-start.14 = (bf16[2,232,128]{2,1,0:T(8,128)(2,1)}, bf16[2,232,128]{2,1,0:T(8,128)(2,1)S(1)}, u32[]{:S(2)}, u32[]{:S(2)}) collective-permute-start(bf16[2,232,128]{2,1,0:T(8,128)(2,1)} %get-tuple-element.45), channel_id=1, source_target_pairs={{0,14},{1,15},{2,12},{3,13},{4,10},{5,11},{6,8},{7,9},{8,6},{9,7},... | collective-permute-start | bytes 356360 | tf_op jit(solution)/shard_map/ppermute | solution.py:449
  23.7 16.9 %collective-permute-start.15 = (bf16[2,232,128]{2,1,0:T(8,128)(2,1)}, bf16[2,232,128]{2,1,0:T(8,128)(2,1)S(1)}, u32[]{:S(2)}, u32[]{:S(2)}) collective-permute-start(bf16[2,232,128]{2,1,0:T(8,128)(2,1)} %get-tuple-element.46), channel_id=1, source_target_pairs={{0,3},{1,2},{2,1},{3,0},{4,7},{5,6},{6,5},{7,4},{8,11},{9,10},{10,... | collective-permute-start | bytes 356360 | tf_op jit(solution)/shard_map/ppermute | solution.py:449
  25.9 14.8 %collective-permute-start.16 = (bf16[2,232,128]{2,1,0:T(8,128)(2,1)}, bf16[2,232,128]{2,1,0:T(8,128)(2,1)S(1)}, u32[]{:S(2)}, u32[]{:S(2)}) collective-permute-start(bf16[2,232,128]{2,1,0:T(8,128)(2,1)} %get-tuple-element.47), channel_id=1, source_target_pairs={{0,15},{1,14},{2,13},{3,12},{4,11},{5,10},{6,9},{7,8},{8,7},{9,6},... | collective-permute-start | bytes 356360 | tf_op jit(solution)/shard_map/ppermute | solution.py:449
  28.1 19.1 %collective-permute-start.2 = (bf16[2,232,128]{2,1,0:T(8,128)(2,1)}, bf16[2,232,128]{2,1,0:T(8,128)(2,1)S(1)}, u32[]{:S(2)}, u32[]{:S(2)}) collective-permute-start(bf16[2,232,128]{2,1,0:T(8,128)(2,1)} %get-tuple-element.33), channel_id=1, source_target_pairs={{0,8},{1,9},{2,10},{3,11},{4,12},{5,13},{6,14},{7,15},{8,0},{9,1},... | collective-permute-start | bytes 356360 | tf_op jit(solution)/shard_map/ppermute | solution.py:449
  36.4 10.8 %collective-permute-start.3 = (bf16[2,232,128]{2,1,0:T(8,128)(2,1)}, bf16[2,232,128]{2,1,0:T(8,128)(2,1)S(1)}, u32[]{:S(2)}, u32[]{:S(2)}) collective-permute-start(bf16[2,232,128]{2,1,0:T(8,128)(2,1)} %get-tuple-element.34), channel_id=1, source_target_pairs={{0,4},{1,5},{2,6},{3,7},{4,0},{5,1},{6,2},{7,3},{8,12},{9,13},{10,... | collective-permute-start | bytes 356360 | tf_op jit(solution)/shard_map/ppermute | solution.py:449
  36.4 15.9 %collective-permute-start.4 = (bf16[2,232,128]{2,1,0:T(8,128)(2,1)}, bf16[2,232,128]{2,1,0:T(8,128)(2,1)S(1)}, u32[]{:S(2)}, u32[]{:S(2)}) collective-permute-start(bf16[2,232,128]{2,1,0:T(8,128)(2,1)} %get-tuple-element.35), channel_id=1, source_target_pairs={{0,9},{1,8},{2,11},{3,10},{4,13},{5,12},{6,15},{7,14},{8,1},{9,0},... | collective-permute-start | bytes 356360 | tf_op jit(solution)/shard_map/ppermute | solution.py:449
  40.6 39.2 %collective-permute-start.5 = (bf16[2,232,128]{2,1,0:T(8,128)(2,1)}, bf16[2,232,128]{2,1,0:T(8,128)(2,1)S(1)}, u32[]{:S(2)}, u32[]{:S(2)}) collective-permute-start(bf16[2,232,128]{2,1,0:T(8,128)(2,1)} %get-tuple-element.36), channel_id=1, source_target_pairs={{0,5},{1,4},{2,7},{3,6},{4,1},{5,0},{6,3},{7,2},{8,13},{9,12},{10,... | collective-permute-start | bytes 356360 | tf_op jit(solution)/shard_map/ppermute | solution.py:449
  40.7 39.1 %collective-permute-start.6 = (bf16[2,232,128]{2,1,0:T(8,128)(2,1)}, bf16[2,232,128]{2,1,0:T(8,128)(2,1)S(1)}, u32[]{:S(2)}, u32[]{:S(2)}) collective-permute-start(bf16[2,232,128]{2,1,0:T(8,128)(2,1)} %get-tuple-element.37), channel_id=1, source_target_pairs={{0,10},{1,11},{2,8},{3,9},{4,14},{5,15},{6,12},{7,13},{8,2},{9,3},... | collective-permute-start | bytes 356360 | tf_op jit(solution)/shard_map/ppermute | solution.py:449
  47.2 32.6 %collective-permute-start.7 = (bf16[2,232,128]{2,1,0:T(8,128)(2,1)}, bf16[2,232,128]{2,1,0:T(8,128)(2,1)S(1)}, u32[]{:S(2)}, u32[]{:S(2)}) collective-permute-start(bf16[2,232,128]{2,1,0:T(8,128)(2,1)} %get-tuple-element.38), channel_id=1, source_target_pairs={{0,6},{1,7},{2,4},{3,5},{4,2},{5,3},{6,0},{7,1},{8,14},{9,15},{10,... | collective-permute-start | bytes 356360 | tf_op jit(solution)/shard_map/ppermute | solution.py:449
  47.2 32.6 %collective-permute-start.8 = (bf16[2,232,128]{2,1,0:T(8,128)(2,1)}, bf16[2,232,128]{2,1,0:T(8,128)(2,1)S(1)}, u32[]{:S(2)}, u32[]{:S(2)}) collective-permute-start(bf16[2,232,128]{2,1,0:T(8,128)(2,1)} %get-tuple-element.39), channel_id=1, source_target_pairs={{0,11},{1,10},{2,9},{3,8},{4,15},{5,14},{6,13},{7,12},{8,3},{9,2},... | collective-permute-start | bytes 356360 | tf_op jit(solution)/shard_map/ppermute | solution.py:449
  52.3 27.5 %collective-permute-start.9 = (bf16[2,232,128]{2,1,0:T(8,128)(2,1)}, bf16[2,232,128]{2,1,0:T(8,128)(2,1)S(1)}, u32[]{:S(2)}, u32[]{:S(2)}) collective-permute-start(bf16[2,232,128]{2,1,0:T(8,128)(2,1)} %get-tuple-element.40), channel_id=1, source_target_pairs={{0,7},{1,6},{2,5},{3,4},{4,3},{5,2},{6,1},{7,0},{8,15},{9,14},{10,... | collective-permute-start | bytes 356360 | tf_op jit(solution)/shard_map/ppermute | solution.py:449

commit v6 on v4

--- a/solution.py
+++ b/solution.py
@@ -20,7 +20,7 @@
 QUAD = LANES // ROWS
 MID = 0.11
 VMEM = 40 * 1024 * 1024
-MOST_VMEM = 46 * 1024 * 1024
+MOST_VMEM = 48 * 1024 * 1024
 
 
 def round_up(value, step):
@@ -62,31 +62,18 @@
 SLOTS = TILES + 2
 
 
-def zero(sums):
-    for parity in range(2):
-        for t in range(SLOTS):
-            sums[parity, t] = jnp.zeros((PAIRS, LANES), jnp.float32)
-
-
-def add_side(sums, tile, column, fresh):
+def place_side(tile, column):
     pairs = jnp.concatenate([tile(t) for t in range(TILES)], 1)
     turned = pltpu.roll(pairs, PATCH, 1)
     lane = lax.broadcasted_iota(jnp.int32, pairs.shape, 1)
     left = (lane < PATCH) & (column == 0)
     right = (lane >= PATCH) & (column != 0)
-    placed = (
-        jnp.where(left, pairs, jnp.where(right, turned, 0.0)),
-        jnp.where(left, turned, jnp.where(right, pairs, 0.0)),
-    )
-    for parity in range(2):
-        for t in range(TILES):
-            piece = placed[parity][:, LANES * t : LANES * (t + 1)]
-            sums[parity, t + 1] = piece if fresh else sums[parity, t + 1] + piece
-
-
-def add_any(sums, tile, column, fresh):
-    if fresh:
-        zero(sums)
+    even = jnp.where(left, pairs, jnp.where(right, turned, 0.0))
+    odd = jnp.where(left, turned, jnp.where(right, pairs, 0.0))
+    return [[rows[:, LANES * t : LANES * (t + 1)] for t in range(TILES)] for rows in (even, odd)]
+
+
+def add_any(sums, tile, column):
     lane = lax.broadcasted_iota(jnp.int32, (PAIRS, LANES), 1)
     middle = PATCH // LANES
     split = PATCH % LANES
@@ -108,18 +95,31 @@
             sums[parity, at + v] = sums[parity, at + v] + jnp.where(lane < shift, low, high)
 
 
+def place_all(side, sums, items):
+    if side:
+        placed = [place_side(*item) for item in items]
+        return [[sum(item[parity][t] for item in placed) for t in range(TILES)] for parity in range(2)]
+    for parity in range(2):
+        for t in range(SLOTS):
+            sums[parity, t] = jnp.zeros((PAIRS, LANES), jnp.float32)
+    for item in items:
+        add_any(sums, *item)
+    return [[sums[parity, t + 1] for t in range(TILES)] for parity in range(2)]
+
+
 def either_kind(z, heavy, body):
     @pl.when(heavy)
     def _():
-        body(add_any, range(CAP))
+        body(False, range(CAP))
 
     @pl.when(jnp.logical_not(heavy))
     def _():
-        body(add_side if z.makers == 2 else add_any, range(1))
-
-
-def own_kernel(z, place, lists, tiles, table_hbm, *refs):
-    half, (total, weights, landed, staged, table, sems) = refs[:FIELDS], refs[FIELDS:]
+        body(z.makers == 2, range(1))
+
+
+def own_kernel(z, place, *refs):
+    lists, (tiles, table_hbm), refs = refs[: z.makers], refs[z.makers : z.makers + 2], refs[z.makers + 2 :]
+    half, (inverse, weights, landed, staged, sums, table, sems) = refs[:FIELDS], refs[FIELDS:]
     first = lax.rem(place[0], z.makers) * z.block
 
     def fetch(j):
@@ -143,21 +143,29 @@
     def region(j, carry):
         fetch(j).wait()
 
-        def body(add, slots):
+        def body(side, slots):
+            def weight_item(maker, slot):
+                column, kind = (lists[maker][entry, slot, first + j] for entry in (1, 2))
+                return functools.partial(weight_tile, weights, kind), column
+
+            def field_item(field, slot):
+                weight, column = weight_item(0, slot)
+                return lambda t: staged_tile(staged.at[slot], field, t) * weight(t), column
+
             for slot in slots:
                 stage(staged.at[slot], landed[j, slot])
-            entries = [(slot, *(lists[entry, slot, first + j] for entry in (1, 2))) for slot in slots]
-            for i, (_, column, kind) in enumerate(entries):
-                add(total.at[j], functools.partial(weight_tile, weights, kind), column, i == 0)
+            items = [weight_item(maker, slot) for maker in range(z.makers) for slot in slots]
+            inverses = [[1.0 / piece for piece in rows] for rows in place_all(side, sums.at[FIELDS], items)]
+            for parity in range(2):
+                for t in range(TILES):
+                    inverse[j, parity, t] = inverses[parity][t]
             for field in range(FIELDS):
-                for i, (slot, column, kind) in enumerate(entries):
-
-                    def tile(t):
-                        return staged_tile(staged.at[slot], field, t) * weight_tile(weights, kind, t)
-
-                    add(half[field].at[j], tile, column, i == 0)
-
-        either_kind(z, lists[0, 1, first + j] >= 0, body)
+                pieces = place_all(side, sums.at[field], [field_item(field, slot) for slot in slots])
+                for parity in range(2):
+                    for t in range(TILES):
+                        half[field][j, parity, t] = pieces[parity][t] * inverses[parity][t]
+
+        either_kind(z, lists[0][0, 1, first + j] >= 0, body)
         return carry
 
     lax.fori_loop(0, z.block, region, 0)
@@ -171,21 +179,22 @@
     return pl.pallas_call(
         functools.partial(own_kernel, z),
         out_shape=[
-            *[jax.ShapeDtypeStruct((z.block, 2, SLOTS, PAIRS, LANES), jnp.float32)] * (FIELDS + 1),
+            *[jax.ShapeDtypeStruct((z.block, 2, TILES, PAIRS, LANES), jnp.float32)] * (FIELDS + 1),
             jax.ShapeDtypeStruct((TILES, kinds * PAIRS, LANES), jnp.float32),
         ],
-        in_specs=[smem, smem, hbm, hbm],
+        in_specs=[smem] * (1 + z.makers) + [hbm, hbm],
         out_specs=[vmem] * (FIELDS + 2),
         scratch_shapes=[
             pltpu.VMEM((z.block, CAP, LINES, LANES), jnp.bfloat16),
             pltpu.VMEM((CAP, LINES, LANES), jnp.float32),
+            pltpu.VMEM((FIELDS + 1, 2, SLOTS, PAIRS, LANES), jnp.float32),
             pltpu.VMEM(table.shape, jnp.float32),
             pltpu.SemaphoreType.DMA((z.block + 1,)),
         ],
         compiler_params=pltpu.CompilerParams(vmem_limit_bytes=MOST_VMEM),
         cost_estimate=pl.CostEstimate(flops=5_000_000, bytes_accessed=8_000_000, transcendentals=0),
         name="own_share",
-    )(place, lists, tiles, table)
+    )(place, *lists, tiles, table)
 
 
 def strength_kernel(z, smoothing, _, strength):
@@ -211,7 +220,7 @@
 def join_kernel(z, *refs):
     place, lists, refs = refs[0], refs[1 : 1 + z.makers], refs[1 + z.makers :]
     received, refs = refs[: z.makers - 1], refs[z.makers - 1 :]
-    half, (total, weights, strength), outs = refs[:FIELDS], refs[FIELDS : FIELDS + 3], refs[FIELDS + 3 : -6]
+    half, (inverse, weights, strength), outs = refs[:FIELDS], refs[FIELDS : FIELDS + 3], refs[FIELDS + 3 : -6]
     staged, sums, lines, turned, blocks, sems = refs[-6:]
     me = place[0]
     first = lax.rem(me, z.makers) * z.block
@@ -226,35 +235,22 @@
         def region(i, carry):
             j = quad * QUAD + i
 
-            def body(add, slots):
-                entries = []
-                for maker in range(1, z.makers):
-                    for slot in slots:
-                        index = (maker - 1) * CAP + slot
-                        stage(staged.at[index], received[maker - 1][first + j, slot])
-                        entries.append((index, *(lists[maker][entry, slot, first + j] for entry in (1, 2))))
-
-                def begin(index, own):
-                    for parity in range(2):
-                        for t in range(SLOTS):
-                            sums[index, parity, t] = own[j, parity, t]
-
-                begin(FIELDS, total)
-                for _, column, kind in entries:
-                    add(sums.at[FIELDS], functools.partial(weight_tile, weights, kind), column, False)
-                inverse = [[1.0 / sums[FIELDS, parity, t + 1] for t in range(TILES)] for parity in range(2)]
+            def body(side, slots):
+                sources = [(maker, slot) for maker in range(1, z.makers) for slot in slots]
+
+                def field_item(field, maker, slot):
+                    column, kind = (lists[maker][entry, slot, first + j] for entry in (1, 2))
+                    own = staged.at[(maker - 1) * CAP + slot]
+                    return lambda t: staged_tile(own, field, t) * weight_tile(weights, kind, t), column
+
+                for maker, slot in sources:
+                    stage(staged.at[(maker - 1) * CAP + slot], received[maker - 1][first + j, slot])
                 for field in range(FIELDS):
-                    begin(field, half[field])
-                    for index, column, kind in entries:
-
-                        def tile(t):
-                            return staged_tile(staged.at[index], field, t) * weight_tile(weights, kind, t)
-
-                        add(sums.at[field], tile, column, False)
+                    pieces = place_all(side, sums.at[field], [field_item(field, *source) for source in sources])
                     for parity in range(2):
                         for t in range(TILES):
                             lines[field, t, pl.ds(ROWS * i + parity, PAIRS, stride=2), :] = (
-                                sums[field, parity, t + 1] * inverse[parity][t]
+                                half[field][j, parity, t] + pieces[parity][t] * inverse[j, parity, t]
                             )
 
             either_kind(z, lists[0][0, 1, first + j] >= 0, body)
@@ -302,7 +298,7 @@
         out_specs=[vmem] + [hbm] * (z.regions - 1),
         scratch_shapes=[
             pltpu.VMEM((CAP * (z.makers - 1), LINES, LANES), jnp.float32),
-            pltpu.VMEM((FIELDS + 1, 2, SLOTS, PAIRS, LANES), jnp.float32),
+            pltpu.VMEM((FIELDS, 2, SLOTS, PAIRS, LANES), jnp.float32),
             pltpu.VMEM((FIELDS, TILES, LANES, LANES), jnp.float32),
             pltpu.VMEM((FIELDS, COLS + 8, LANES), jnp.float32),
             pltpu.VMEM((z.regions, *shape), jnp.bfloat16),
@@ -332,9 +328,8 @@
     step = pl.program_id(0)
     rows = z.rows
 
-    def lanes_of(offset, quad):
-        at = (lax.rem(me ^ offset, z.makers) * z.quads + quad) * LANES
-        return pl.ds(pl.multiple_of(at, LANES), LANES)
+    def tile_of(offset, quad):
+        return lax.rem(me ^ offset, z.makers) * z.quads + quad
 
     @pl.when(step == 0)
     def _():
@@ -342,51 +337,52 @@
         for low in range(0, z.regions, QUAD):
             offsets = range(low, low + QUAD)
             slots = [lax.rem(me ^ offset, QUAD) for offset in offsets]
-            at = pl.multiple_of(lax.div(me ^ low, QUAD) * LANES, LANES)
+            at = lax.div(me ^ low, QUAD)
             for quad in range(z.quads):
                 tails = [blocks[offset][quad, z.main : z.sent, :].astype(jnp.float32) for offset in offsets]
                 for offset, tail in zip(offsets, tails):
-                    edges[offset // z.makers, :, lanes_of(offset, quad)] = tail[0:8]
+                    edges[offset // z.makers, tile_of(offset, quad)] = tail[0:8]
                 for g in range(quad * QUAD, min((quad + 1) * QUAD, z.span // 8)):
                     joined = jnp.zeros((8, LANES), jnp.float32)
                     for i, tail in zip(slots, tails):
                         near = pltpu.roll(tail[8:16], lax.rem(i + QUAD - g % QUAD, QUAD) * ROWS, 1)
                         joined = jnp.where(slot == i, near, joined)
-                    strength[8 * g : 8 * (g + 1), pl.ds(at, LANES)] = joined + MID
+                    strength[at, 8 * g : 8 * (g + 1), :] = joined + MID
 
     top = pl.multiple_of(step * STEP_FIELDS * z.span, 16)
     for offset in range(z.regions):
         for quad in range(z.quads):
             values = blocks[offset][quad, pl.ds(top, STEP_FIELDS * z.span), :].astype(jnp.float32)
             for f in range(STEP_FIELDS):
-                padded[offset // z.makers, f, 8 : 8 + z.span, lanes_of(offset, quad)] = values[
+                padded[offset // z.makers, f, tile_of(offset, quad), 8 : 8 + z.span, :] = values[
                     f * z.span : (f + 1) * z.span
                 ]
+    tiles = rows // LANES
     for sample in range(SAMPLES):
         for f in range(STEP_FIELDS):
             low = 2 * (step * STEP_FIELDS + f)
-            padded[sample, f, 7:8, :] = edges[sample, pl.ds(low, 1), :]
-            padded[sample, f, 8 + z.width : 9 + z.width, :] = edges[sample, pl.ds(low + 1, 1), :]
-    for f in range(STEP_FIELDS):
-        target_field = analysis[f].astype(jnp.float32)
-        for low in range(0, z.width, 16):
-            high = min(low + 16, z.width)
-            lane = lax.broadcasted_iota(jnp.int32, (high - low, LANES), 1)
-            strong = strength[low:high, :]
-            members = []
-            for sample in range(SAMPLES):
-                here = padded[sample, f, 8 + low : 8 + high, :]
-                sides = padded[sample, f, 7 + low : 7 + high, :] + padded[sample, f, 9 + low : 9 + high, :]
-                pieces = [here[:, at : at + LANES] for at in range(0, rows, LANES)]
-                later = [pltpu.roll(piece, 1, 1) for piece in pieces]
-                sooner = [pltpu.roll(piece, LANES - 1, 1) for piece in pieces]
-                above = [jnp.where(lane == 0, a, b) for a, b in zip([pieces[0]] + later[:-1], later)]
-                below = [jnp.where(lane == LANES - 1, a, b) for a, b in zip(sooner[1:] + [pieces[-1]], sooner)]
-                along = jnp.concatenate([a + b for a, b in zip(above, below)], 1)
-                smooth = here + strong * (along + sides - 4.0 * here)
-                members.append(smooth.astype(jnp.bfloat16))
+            for t in range(tiles):
+                padded[sample, f, t, 7:8, :] = edges[sample, t, pl.ds(low, 1), :]
+                padded[sample, f, t, 8 + z.width : 9 + z.width, :] = edges[sample, t, pl.ds(low + 1, 1), :]
+    for f, low in ((f, low) for f in range(STEP_FIELDS) for low in range(0, z.width, 16)):
+        high = min(low + 16, z.width)
+        lane = lax.broadcasted_iota(jnp.int32, (high - low, LANES), 1)
+        smoothed = [[] for _ in range(tiles)]
+        for sample in range(SAMPLES):
+            field = padded.at[sample, f]
+            pieces = [field[t, 8 + low : 8 + high, :] for t in range(tiles)]
+            later = [pltpu.roll(piece, 1, 1) for piece in pieces]
+            sooner = [pltpu.roll(piece, LANES - 1, 1) for piece in pieces]
+            for t, here in enumerate(pieces):
+                above = jnp.where(lane == 0, later[t - 1] if t else here, later[t])
+                below = jnp.where(lane == LANES - 1, sooner[t + 1] if t + 1 < tiles else here, sooner[t])
+                sides = field[t, 7 + low : 7 + high, :] + field[t, 9 + low : 9 + high, :]
+                smooth = here + strength[t, low:high, :] * (above + below + sides - 4.0 * here)
+                smoothed[t].append(smooth.astype(jnp.bfloat16))
+        for t, members in enumerate(smoothed):
+            lanes = slice(LANES * t, LANES * (t + 1))
             values = [member.astype(jnp.float32) for member in members]
-            target = target_field[low:high]
+            target = analysis[f, low:high, lanes].astype(jnp.float32)
             error = sum(jnp.abs(value - target) for value in values) * (1.0 / SAMPLES)
             average = sum(values) * (1.0 / SAMPLES)
             variance = sum((value - average) ** 2 for value in values) * (1.0 / (SAMPLES - 1.0))
@@ -399,9 +395,9 @@
                 (2 * k - SAMPLES + 1.0) * (ranked[k] - ranked[SAMPLES - 1 - k])
                 for k in range(SAMPLES // 2, SAMPLES)
             )
-            crps[f, low:high, :] = (error - pairs * (1.0 / (SAMPLES * SAMPLES))).astype(jnp.bfloat16)
-            spread[0, f, low:high, :] = variance.astype(jnp.bfloat16)
-            spread[1, f, low:high, :] = ((average - target) ** 2).astype(jnp.bfloat16)
+            crps[f, low:high, lanes] = (error - pairs * (1.0 / (SAMPLES * SAMPLES))).astype(jnp.bfloat16)
+            spread[0, f, low:high, lanes] = variance.astype(jnp.bfloat16)
+            spread[1, f, low:high, lanes] = ((average - target) ** 2).astype(jnp.bfloat16)
 
 
 def score(z, place, blocks, analysis):
@@ -421,9 +417,9 @@
             pl.BlockSpec((2, STEP_FIELDS, width, rows), lambda i: (0, i, 0, 0)),
         ],
         scratch_shapes=[
-            pltpu.VMEM((z.span, rows), jnp.float32),
-            pltpu.VMEM((SAMPLES, 8, rows), jnp.float32),
-            pltpu.VMEM((SAMPLES, STEP_FIELDS, z.span + 16, rows), jnp.float32),
+            pltpu.VMEM((rows // LANES, z.span, LANES), jnp.float32),
+            pltpu.VMEM((SAMPLES, rows // LANES, 8, LANES), jnp.float32),
+            pltpu.VMEM((SAMPLES, STEP_FIELDS, rows // LANES, z.span + 16, LANES), jnp.float32),
         ],
         compiler_params=pltpu.CompilerParams(vmem_limit_bytes=VMEM),
         name="score",
@@ -441,7 +437,7 @@
     lists = jnp.transpose(slot_lists, (2, 1, 0))
     received = [lax.ppermute(tiles, "region", turn) for turn in turns]
     lists = [lists] + [lax.ppermute(lists, "region", turn) for turn in turns]
-    shares = own_share(z, place, lists[0], tiles, blend_table)
+    shares = own_share(z, place, lists, tiles, blend_table)
     shares = [*shares, strength_blocks(z, smoothing, shares[-1])]
     blocks = join(z, place, lists, received, shares)
     moved = [blocks[0]] + [

time: 68.3 us -> 72.5 us (1.061)
  waiting for transfers between devices: 25.3 us -> 34.8 us
  starting transfers between devices: 25.4 us -> 20.8 us
  local copies, waits for them, and re-layouts: 1.87 us -> 0.7 us
    ppermute x1, waiting for transfers between devices: 0.23 us -> 5.83 us  [shards(): lists = [lists] + [lax.ppermute(lists, 'region', turn) for turn in turns]]
    ppermute x15, starting transfers between devices: 24.6 us -> 19.9 us  [shards(): lax.ppermute(block, 'region', [(i, i ^ offset) for i in range(z.regions)])]
    ppermute x15, waiting for transfers between devices: 24.6 us -> 29 us  [shards(): lax.ppermute(block, 'region', [(i, i ^ offset) for i in range(z.regions)])]
    unnamed x8, local copies, waits for them, and re-layouts: 1.87 us -> 0.7 us
    pallas_call x1, Pallas kernels: 3.42 us -> 4.35 us  [own_share(): pl.pallas_call(functools.partial(own_kernel, z), out_shape=[*[jax.ShapeDt...]
  transfers between devices with their start and end apart: 17 -> 17, of which waited for: 8 -> 10; matrix products, arithmetic and copies ran while one was open for 0% -> 0% of each run, Pallas kernels for 5% -> 6%
where the time goes in v6:
time: 72.5 us; the launch traced here: 73.7 us
  waiting for transfers between devices  34.8 us (48%)
  starting transfers between devices  20.8 us (29%)
  Pallas kernels  16.7 us (23%)
    ppermute x15, waiting for transfers between devices, shards(): lax.ppermute(block, 'region', [(i, i ^ offset) for i in range(z.regions)])  29 us
    ppermute x15, starting transfers between devices, shards(): lax.ppermute(block, 'region', [(i, i ^ offset) for i in range(z.regions)])  19.9 us
    pallas_call x1, Pallas kernels, join(): pl.pallas_call(functools.partial(join_kernel, z), out_shape=[jax.ShapeDty...  6.9 us
    ppermute x1, waiting for transfers between devices, shards(): lists = [lists] + [lax.ppermute(lists, 'region', turn) for turn in turns]  5.83 us
    pallas_call x1, Pallas kernels, score(): pl.pallas_call(functools.partial(score_kernel, z), out_shape=[jax.ShapeDt...  5.13 us
    pallas_call x1, Pallas kernels, own_share(): pl.pallas_call(functools.partial(own_kernel, z), out_shape=[*[jax.ShapeDt...  4.35 us
  transfers between devices with their start and end apart: 17, of which 10 were waited for; matrix products, arithmetic and copies ran while one was open for 0% of the time, Pallas kernels for 6%

profile of v6, /device:TPU:17, one launch (start us, length us, event | category | flops | bytes accessed | tf_op | source)
XLA Modules:
  0.0 73.7 jit_solution(7602935780162700989)
XLA Ops:
  0.6 0.7 %collective-permute-start.1 = (bf16[16,2,448,128]{3,2,1,0:T(8,128)(2,1)}, bf16[16,2,448,128]{3,2,1,0:T(8,128)(2,1)}, u32[]{:S(2)}, u32[]{:S(2)}) collective-permute-start(bf16[16,2,448,128]{3,2,1,0:T(8,128)(2,1)} %bitcast.14), channel_id=1, source_target_pairs={{0,1},{1,0},{2,3},{3,2},{4,5},{5,4},{6,7},{7,6},{8,9},{9,8},{10,11... | collective-permute-start | bytes 11010056 | tf_op jit(solution)/shard_map/ppermute | solution.py:438
  1.5 5.8 %collective-permute-done.refs_1_.refs_2_ = s32[3,2,16]{2,1,0:T(2,128)S(1)} collective-permute-done((s32[3,2,16]{2,1,0:T(2,128)}, s32[3,2,16]{2,1,0:T(2,128)S(1)}, u32[]{:S(2)}, u32[]{:S(2)}) %collective-permute-start) | collective-permute-done | bytes 416 | tf_op jit(solution)/shard_map/ppermute | solution.py:439
  7.3 0.7 copy-done.2
  8.0 4.3 %own_share.1 = (f32[8,2,7,16,128]{4,3,2,1,0:T(8,128)S(1)}, f32[8,2,7,16,128]{4,3,2,1,0:T(8,128)S(1)}, f32[8,2,7,16,128]{4,3,2,1,0:T(8,128)S(1)}, f32[8,2,7,16,12...) custom-call(s32[1]{0:T(128)} %bitcast.place.refs_0_, s32[3,2,16]{2,1,0:T(2,128)S(1)} %bitcast.12, ...), custom_call_target="tpu_custom_call" | custom-call | flops 5000000 | bytes 8000000 | tf_op jit(solution)/shard_map/own_share/pallas_call | solution.py:179
  12.7 6.9 %join.1 = (bf16[2,240,128]{2,1,0:T(8,128)(2,1)S(1)}, bf16[2,240,128]{2,1,0:T(8,128)(2,1)}, bf16[2,240,128]{2,1,0:T(8,128)(2,1)}, bf16[2,240,128]{2,1,0:T(8,128)(...) custom-call(s32[1]{0:T(128)} %bitcast.place.refs_0_, ...), custom_call_target="tpu_custom_call" | custom-call | flops 5000000 | bytes 8000000 | tf_op jit(solution)/shard_map/join/pallas_call | solution.py:293
  19.7 1.4 %collective-permute-start.3 = (bf16[2,240,128]{2,1,0:T(8,128)(2,1)}, bf16[2,240,128]{2,1,0:T(8,128)(2,1)S(1)}, u32[]{:S(2)}, u32[]{:S(2)}) collective-permute-start(bf16[2,240,128]{2,1,0:T(8,128)(2,1)} %get-tuple-element.34), channel_id=1, source_target_pairs={{0,4},{1,5},{2,6},{3,7},{4,0},{5,1},{6,2},{7,3},{8,12},{9,13},{10,... | collective-permute-start | bytes 368648 | tf_op jit(solution)/shard_map/ppermute | solution.py:444
  21.0 2.3 %collective-permute-start.4 = (bf16[2,240,128]{2,1,0:T(8,128)(2,1)}, bf16[2,240,128]{2,1,0:T(8,128)(2,1)S(1)}, u32[]{:S(2)}, u32[]{:S(2)}) collective-permute-start(bf16[2,240,128]{2,1,0:T(8,128)(2,1)} %get-tuple-element.35), channel_id=1, source_target_pairs={{0,9},{1,8},{2,11},{3,10},{4,13},{5,12},{6,15},{7,14},{8,1},{9,0},... | collective-permute-start | bytes 368648 | tf_op jit(solution)/shard_map/ppermute | solution.py:444
  23.8 1.0 %collective-permute-start.6 = (bf16[2,240,128]{2,1,0:T(8,128)(2,1)}, bf16[2,240,128]{2,1,0:T(8,128)(2,1)S(1)}, u32[]{:S(2)}, u32[]{:S(2)}) collective-permute-start(bf16[2,240,128]{2,1,0:T(8,128)(2,1)} %get-tuple-element.37), channel_id=1, source_target_pairs={{0,10},{1,11},{2,8},{3,9},{4,14},{5,15},{6,12},{7,13},{8,2},{9,3},... | collective-permute-start | bytes 368648 | tf_op jit(solution)/shard_map/ppermute | solution.py:444
  24.8 1.3 %collective-permute-done.2.refs_1_ = bf16[2,240,128]{2,1,0:T(8,128)(2,1)S(1)} collective-permute-done((bf16[2,240,128]{2,1,0:T(8,128)(2,1)}, bf16[2,240,128]{2,1,0:T(8,128)(2,1)S(1)}, u32[]{:S(2)}, u32[]{:S(2)}) %collective-permute-start.2) | collective-permute-done | bytes 122912 | tf_op jit(solution)/shard_map/ppermute | solution.py:444
  26.1 4.8 %collective-permute-start.7 = (bf16[2,240,128]{2,1,0:T(8,128)(2,1)}, bf16[2,240,128]{2,1,0:T(8,128)(2,1)S(1)}, u32[]{:S(2)}, u32[]{:S(2)}) collective-permute-start(bf16[2,240,128]{2,1,0:T(8,128)(2,1)} %get-tuple-element.38), channel_id=1, source_target_pairs={{0,6},{1,7},{2,4},{3,5},{4,2},{5,3},{6,0},{7,1},{8,14},{9,15},{10,... | collective-permute-start | bytes 368648 | tf_op jit(solution)/shard_map/ppermute | solution.py:444
  30.9 0.8 %collective-permute-start.8 = (bf16[2,240,128]{2,1,0:T(8,128)(2,1)}, bf16[2,240,128]{2,1,0:T(8,128)(2,1)S(1)}, u32[]{:S(2)}, u32[]{:S(2)}) collective-permute-start(bf16[2,240,128]{2,1,0:T(8,128)(2,1)} %get-tuple-element.39), channel_id=1, source_target_pairs={{0,11},{1,10},{2,9},{3,8},{4,15},{5,14},{6,13},{7,12},{8,3},{9,2},... | collective-permute-start | bytes 368648 | tf_op jit(solution)/shard_map/ppermute | solution.py:444
  31.7 4.8 %collective-permute-start.9 = (bf16[2,240,128]{2,1,0:T(8,128)(2,1)}, bf16[2,240,128]{2,1,0:T(8,128)(2,1)S(1)}, u32[]{:S(2)}, u32[]{:S(2)}) collective-permute-start(bf16[2,240,128]{2,1,0:T(8,128)(2,1)} %get-tuple-element.40), channel_id=1, source_target_pairs={{0,7},{1,6},{2,5},{3,4},{4,3},{5,2},{6,1},{7,0},{8,15},{9,14},{10,... | collective-permute-start | bytes 368648 | tf_op jit(solution)/shard_map/ppermute | solution.py:444
  36.6 1.9 %collective-permute-done.6.refs_5_ = bf16[2,240,128]{2,1,0:T(8,128)(2,1)S(1)} collective-permute-done((bf16[2,240,128]{2,1,0:T(8,128)(2,1)}, bf16[2,240,128]{2,1,0:T(8,128)(2,1)S(1)}, u32[]{:S(2)}, u32[]{:S(2)}) %collective-permute-start.6) | collective-permute-done | bytes 122912 | tf_op jit(solution)/shard_map/ppermute | solution.py:444
  38.4 0.8 %collective-permute-start.11 = (bf16[2,240,128]{2,1,0:T(8,128)(2,1)}, bf16[2,240,128]{2,1,0:T(8,128)(2,1)S(1)}, u32[]{:S(2)}, u32[]{:S(2)}) collective-permute-start(bf16[2,240,128]{2,1,0:T(8,128)(2,1)} %get-tuple-element.42), channel_id=1, source_target_pairs={{0,1},{1,0},{2,3},{3,2},{4,5},{5,4},{6,7},{7,6},{8,9},{9,8},{10,11... | collective-permute-start | bytes 368648 | tf_op jit(solution)/shard_map/ppermute | solution.py:444
  39.2 1.2 %collective-permute-done.7.refs_6_ = bf16[2,240,128]{2,1,0:T(8,128)(2,1)S(1)} collective-permute-done((bf16[2,240,128]{2,1,0:T(8,128)(2,1)}, bf16[2,240,128]{2,1,0:T(8,128)(2,1)S(1)}, u32[]{:S(2)}, u32[]{:S(2)}) %collective-permute-start.7) | collective-permute-done | bytes 122912 | tf_op jit(solution)/shard_map/ppermute | solution.py:444
  40.9 2.1 %collective-permute-done.8.refs_7_ = bf16[2,240,128]{2,1,0:T(8,128)(2,1)S(1)} collective-permute-done((bf16[2,240,128]{2,1,0:T(8,128)(2,1)}, bf16[2,240,128]{2,1,0:T(8,128)(2,1)S(1)}, u32[]{:S(2)}, u32[]{:S(2)}) %collective-permute-start.8) | collective-permute-done | bytes 122912 | tf_op jit(solution)/shard_map/ppermute | solution.py:444
  43.2 2.4 %collective-permute-done.9.refs_8_ = bf16[2,240,128]{2,1,0:T(8,128)(2,1)S(1)} collective-permute-done((bf16[2,240,128]{2,1,0:T(8,128)(2,1)}, bf16[2,240,128]{2,1,0:T(8,128)(2,1)S(1)}, u32[]{:S(2)}, u32[]{:S(2)}) %collective-permute-start.9) | collective-permute-done | bytes 122912 | tf_op jit(solution)/shard_map/ppermute | solution.py:444
  45.6 1.1 %collective-permute-start.14 = (bf16[2,240,128]{2,1,0:T(8,128)(2,1)}, bf16[2,240,128]{2,1,0:T(8,128)(2,1)S(1)}, u32[]{:S(2)}, u32[]{:S(2)}) collective-permute-start(bf16[2,240,128]{2,1,0:T(8,128)(2,1)} %get-tuple-element.45), channel_id=1, source_target_pairs={{0,14},{1,15},{2,12},{3,13},{4,10},{5,11},{6,8},{7,9},{8,6},{9,7},... | collective-permute-start | bytes 368648 | tf_op jit(solution)/shard_map/ppermute | solution.py:444
  46.8 11.0 %collective-permute-done.10.refs_9_ = bf16[2,240,128]{2,1,0:T(8,128)(2,1)S(1)} collective-permute-done((bf16[2,240,128]{2,1,0:T(8,128)(2,1)}, bf16[2,240,128]{2,1,0:T(8,128)(2,1)S(1)}, u32[]{:S(2)}, u32[]{:S(2)}) %collective-permute-start.10) | collective-permute-done | bytes 122912 | tf_op jit(solution)/shard_map/ppermute | solution.py:444
  57.7 1.6 %collective-permute-start.15 = (bf16[2,240,128]{2,1,0:T(8,128)(2,1)}, bf16[2,240,128]{2,1,0:T(8,128)(2,1)S(1)}, u32[]{:S(2)}, u32[]{:S(2)}) collective-permute-start(bf16[2,240,128]{2,1,0:T(8,128)(2,1)} %get-tuple-element.46), channel_id=1, source_target_pairs={{0,3},{1,2},{2,1},{3,0},{4,7},{5,6},{6,5},{7,4},{8,11},{9,10},{10,... | collective-permute-start | bytes 368648 | tf_op jit(solution)/shard_map/ppermute | solution.py:444
  59.3 1.0 %collective-permute-done.12.refs_11_ = bf16[2,240,128]{2,1,0:T(8,128)(2,1)S(1)} collective-permute-done((bf16[2,240,128]{2,1,0:T(8,128)(2,1)}, bf16[2,240,128]{2,1,0:T(8,128)(2,1)S(1)}, u32[]{:S(2)}, u32[]{:S(2)}) %collective-permute-start.12) | collective-permute-done | bytes 122912 | tf_op jit(solution)/shard_map/ppermute | solution.py:444
  60.4 3.7 %collective-permute-done.14.refs_13_ = bf16[2,240,128]{2,1,0:T(8,128)(2,1)S(1)} collective-permute-done((bf16[2,240,128]{2,1,0:T(8,128)(2,1)}, bf16[2,240,128]{2,1,0:T(8,128)(2,1)S(1)}, u32[]{:S(2)}, u32[]{:S(2)}) %collective-permute-start.14) | collective-permute-done | bytes 122912 | tf_op jit(solution)/shard_map/ppermute | solution.py:444
  64.1 4.5 %collective-permute-done.15.refs_14_ = bf16[2,240,128]{2,1,0:T(8,128)(2,1)S(1)} collective-permute-done((bf16[2,240,128]{2,1,0:T(8,128)(2,1)}, bf16[2,240,128]{2,1,0:T(8,128)(2,1)S(1)}, u32[]{:S(2)}, u32[]{:S(2)}) %collective-permute-start.15) | collective-permute-done | bytes 122912 | tf_op jit(solution)/shard_map/ppermute | solution.py:444
  68.5 5.1 %score.1 = (bf16[4,56,512]{2,1,0:T(8,128)(2,1)}, bf16[2,4,56,512]{3,2,1,0:T(8,128)(2,1)}) custom-call(s32[1]{0:T(128)} %bitcast.place.refs_0_, bf16[2,240,128]{2,1,0:T(8,128)(2,1)S(1)} %get-tuple-element.32.refs_0_, bf16[2,240,128]{2,1,0:T(8,128)(2,1)S(1)} %collective-permute-done.2.refs_1_, bf16[2,240,128]{2,1,0:T(8,128)(2,1)S(1)} %collective-permute-done.3.refs_2_, ...), custom_call_target="tpu_custom_call" | custom-call | tf_op jit(solution)/shard_map/score/pallas_call | solution.py:405
  (22 shorter events, 1.7 us)
Async XLA Ops:
  0.6 11.7 %copy-start.1 = (f32[32,896]{1,0:T(8,128)S(1)}, f32[32,896]{1,0:T(8,128)}, u32[]{:S(2)}) copy-start(f32[32,896]{1,0:T(8,128)} %smoothing.1) | copy-start | bytes 344068
  0.6 12.0 %collective-permute-start.1 = (bf16[16,2,448,128]{3,2,1,0:T(8,128)(2,1)}, bf16[16,2,448,128]{3,2,1,0:T(8,128)(2,1)}, u32[]{:S(2)}, u32[]{:S(2)}) collective-permute-start(bf16[16,2,448,128]{3,2,1,0:T(8,128)(2,1)} %bitcast.14), channel_id=1, source_target_pairs={{0,1},{1,0},{2,3},{3,2},{4,5},{5,4},{6,7},{7,6},{8,9},{9,8},{10,11... | collective-permute-start | bytes 11010056 | tf_op jit(solution)/shard_map/ppermute | solution.py:438
  1.4 5.9 %collective-permute-start = (s32[3,2,16]{2,1,0:T(2,128)}, s32[3,2,16]{2,1,0:T(2,128)S(1)}, u32[]{:S(2)}, u32[]{:S(2)}) collective-permute-start(s32[3,2,16]{2,1,0:T(2,128)} %bitcast.11), channel_id=1, source_target_pairs={{0,1},{1,0},{2,3},{3,2},{4,5},{5,4},{6,7},{7,6},{8,9},{9,8},{10,11... | collective-permute-start | bytes 1160 | tf_op jit(solution)/shard_map/ppermute | solution.py:439
  7.3 0.7 copy-start.2
  8.0 4.7 %copy-start.3 = (s32[16,2,3]{0,1,2:T(2,128)S(1)}, s32[16,2,3]{0,1,2:T(2,128)}, u32[]{:S(2)}) copy-start(s32[16,2,3]{0,1,2:T(2,128)} %param.6) | copy-start | bytes 1156
  12.7 55.9 %copy-start = (bf16[4,512,56]{1,2,0:T(8,128)(2,1)S(1)}, bf16[4,512,56]{1,2,0:T(8,128)(2,1)}, u32[]{:S(2)}) copy-start(bf16[4,512,56]{1,2,0:T(8,128)(2,1)} %param.9) | copy-start | bytes 688132
  19.6 6.5 %collective-permute-start.2 = (bf16[2,240,128]{2,1,0:T(8,128)(2,1)}, bf16[2,240,128]{2,1,0:T(8,128)(2,1)S(1)}, u32[]{:S(2)}, u32[]{:S(2)}) collective-permute-start(bf16[2,240,128]{2,1,0:T(8,128)(2,1)} %get-tuple-element.33), channel_id=1, source_target_pairs={{0,8},{1,9},{2,10},{3,11},{4,12},{5,13},{6,14},{7,15},{8,0},{9,1},... | collective-permute-start | bytes 368648 | tf_op jit(solution)/shard_map/ppermute | solution.py:444
  19.7 11.3 %collective-permute-start.3 = (bf16[2,240,128]{2,1,0:T(8,128)(2,1)}, bf16[2,240,128]{2,1,0:T(8,128)(2,1)S(1)}, u32[]{:S(2)}, u32[]{:S(2)}) collective-permute-start(bf16[2,240,128]{2,1,0:T(8,128)(2,1)} %get-tuple-element.34), channel_id=1, source_target_pairs={{0,4},{1,5},{2,6},{3,7},{4,0},{5,1},{6,2},{7,3},{8,12},{9,13},{10,... | collective-permute-start | bytes 368648 | tf_op jit(solution)/shard_map/ppermute | solution.py:444
  21.0 10.7 %collective-permute-start.4 = (bf16[2,240,128]{2,1,0:T(8,128)(2,1)}, bf16[2,240,128]{2,1,0:T(8,128)(2,1)S(1)}, u32[]{:S(2)}, u32[]{:S(2)}) collective-permute-start(bf16[2,240,128]{2,1,0:T(8,128)(2,1)} %get-tuple-element.35), channel_id=1, source_target_pairs={{0,9},{1,8},{2,11},{3,10},{4,13},{5,12},{6,15},{7,14},{8,1},{9,0},... | collective-permute-start | bytes 368648 | tf_op jit(solution)/shard_map/ppermute | solution.py:444
  23.3 13.2 %collective-permute-start.5 = (bf16[2,240,128]{2,1,0:T(8,128)(2,1)}, bf16[2,240,128]{2,1,0:T(8,128)(2,1)S(1)}, u32[]{:S(2)}, u32[]{:S(2)}) collective-permute-start(bf16[2,240,128]{2,1,0:T(8,128)(2,1)} %get-tuple-element.36), channel_id=1, source_target_pairs={{0,5},{1,4},{2,7},{3,6},{4,1},{5,0},{6,3},{7,2},{8,13},{9,12},{10,... | collective-permute-start | bytes 368648 | tf_op jit(solution)/shard_map/ppermute | solution.py:444
  23.8 14.7 %collective-permute-start.6 = (bf16[2,240,128]{2,1,0:T(8,128)(2,1)}, bf16[2,240,128]{2,1,0:T(8,128)(2,1)S(1)}, u32[]{:S(2)}, u32[]{:S(2)}) collective-permute-start(bf16[2,240,128]{2,1,0:T(8,128)(2,1)} %get-tuple-element.37), channel_id=1, source_target_pairs={{0,10},{1,11},{2,8},{3,9},{4,14},{5,15},{6,12},{7,13},{8,2},{9,3},... | collective-permute-start | bytes 368648 | tf_op jit(solution)/shard_map/ppermute | solution.py:444
  26.1 14.2 %collective-permute-start.7 = (bf16[2,240,128]{2,1,0:T(8,128)(2,1)}, bf16[2,240,128]{2,1,0:T(8,128)(2,1)S(1)}, u32[]{:S(2)}, u32[]{:S(2)}) collective-permute-start(bf16[2,240,128]{2,1,0:T(8,128)(2,1)} %get-tuple-element.38), channel_id=1, source_target_pairs={{0,6},{1,7},{2,4},{3,5},{4,2},{5,3},{6,0},{7,1},{8,14},{9,15},{10,... | collective-permute-start | bytes 368648 | tf_op jit(solution)/shard_map/ppermute | solution.py:444
  30.9 12.1 %collective-permute-start.8 = (bf16[2,240,128]{2,1,0:T(8,128)(2,1)}, bf16[2,240,128]{2,1,0:T(8,128)(2,1)S(1)}, u32[]{:S(2)}, u32[]{:S(2)}) collective-permute-start(bf16[2,240,128]{2,1,0:T(8,128)(2,1)} %get-tuple-element.39), channel_id=1, source_target_pairs={{0,11},{1,10},{2,9},{3,8},{4,15},{5,14},{6,13},{7,12},{8,3},{9,2},... | collective-permute-start | bytes 368648 | tf_op jit(solution)/shard_map/ppermute | solution.py:444
  31.7 13.9 %collective-permute-start.9 = (bf16[2,240,128]{2,1,0:T(8,128)(2,1)}, bf16[2,240,128]{2,1,0:T(8,128)(2,1)S(1)}, u32[]{:S(2)}, u32[]{:S(2)}) collective-permute-start(bf16[2,240,128]{2,1,0:T(8,128)(2,1)} %get-tuple-element.40), channel_id=1, source_target_pairs={{0,7},{1,6},{2,5},{3,4},{4,3},{5,2},{6,1},{7,0},{8,15},{9,14},{10,... | collective-permute-start | bytes 368648 | tf_op jit(solution)/shard_map/ppermute | solution.py:444
  36.6 21.2 %collective-permute-start.10 = (bf16[2,240,128]{2,1,0:T(8,128)(2,1)}, bf16[2,240,128]{2,1,0:T(8,128)(2,1)S(1)}, u32[]{:S(2)}, u32[]{:S(2)}) collective-permute-start(bf16[2,240,128]{2,1,0:T(8,128)(2,1)} %get-tuple-element.41), channel_id=1, source_target_pairs={{0,12},{1,13},{2,14},{3,15},{4,8},{5,9},{6,10},{7,11},{8,4},{9,5},... | collective-permute-start | bytes 368648 | tf_op jit(solution)/shard_map/ppermute | solution.py:444
  38.4 20.9 %collective-permute-start.11 = (bf16[2,240,128]{2,1,0:T(8,128)(2,1)}, bf16[2,240,128]{2,1,0:T(8,128)(2,1)S(1)}, u32[]{:S(2)}, u32[]{:S(2)}) collective-permute-start(bf16[2,240,128]{2,1,0:T(8,128)(2,1)} %get-tuple-element.42), channel_id=1, source_target_pairs={{0,1},{1,0},{2,3},{3,2},{4,5},{5,4},{6,7},{7,6},{8,9},{9,8},{10,11... | collective-permute-start | bytes 368648 | tf_op jit(solution)/shard_map/ppermute | solution.py:444
  40.3 20.0 %collective-permute-start.12 = (bf16[2,240,128]{2,1,0:T(8,128)(2,1)}, bf16[2,240,128]{2,1,0:T(8,128)(2,1)S(1)}, u32[]{:S(2)}, u32[]{:S(2)}) collective-permute-start(bf16[2,240,128]{2,1,0:T(8,128)(2,1)} %get-tuple-element.43), channel_id=1, source_target_pairs={{0,13},{1,12},{2,15},{3,14},{4,9},{5,8},{6,11},{7,10},{8,5},{9,4},... | collective-permute-start | bytes 368648 | tf_op jit(solution)/shard_map/ppermute | solution.py:444
  43.0 17.4 %collective-permute-start.13 = (bf16[2,240,128]{2,1,0:T(8,128)(2,1)}, bf16[2,240,128]{2,1,0:T(8,128)(2,1)S(1)}, u32[]{:S(2)}, u32[]{:S(2)}) collective-permute-start(bf16[2,240,128]{2,1,0:T(8,128)(2,1)} %get-tuple-element.44), channel_id=1, source_target_pairs={{0,2},{1,3},{2,0},{3,1},{4,6},{5,7},{6,4},{7,5},{8,10},{9,11},{10,... | collective-permute-start | bytes 368648 | tf_op jit(solution)/shard_map/ppermute | solution.py:444
  45.6 18.4 %collective-permute-start.14 = (bf16[2,240,128]{2,1,0:T(8,128)(2,1)}, bf16[2,240,128]{2,1,0:T(8,128)(2,1)S(1)}, u32[]{:S(2)}, u32[]{:S(2)}) collective-permute-start(bf16[2,240,128]{2,1,0:T(8,128)(2,1)} %get-tuple-element.45), channel_id=1, source_target_pairs={{0,14},{1,15},{2,12},{3,13},{4,10},{5,11},{6,8},{7,9},{8,6},{9,7},... | collective-permute-start | bytes 368648 | tf_op jit(solution)/shard_map/ppermute | solution.py:444
  57.7 10.8 %collective-permute-start.15 = (bf16[2,240,128]{2,1,0:T(8,128)(2,1)}, bf16[2,240,128]{2,1,0:T(8,128)(2,1)S(1)}, u32[]{:S(2)}, u32[]{:S(2)}) collective-permute-start(bf16[2,240,128]{2,1,0:T(8,128)(2,1)} %get-tuple-element.46), channel_id=1, source_target_pairs={{0,3},{1,2},{2,1},{3,0},{4,7},{5,6},{6,5},{7,4},{8,11},{9,10},{10,... | collective-permute-start | bytes 368648 | tf_op jit(solution)/shard_map/ppermute | solution.py:444
  59.3 9.2 %collective-permute-start.16 = (bf16[2,240,128]{2,1,0:T(8,128)(2,1)}, bf16[2,240,128]{2,1,0:T(8,128)(2,1)S(1)}, u32[]{:S(2)}, u32[]{:S(2)}) collective-permute-start(bf16[2,240,128]{2,1,0:T(8,128)(2,1)} %get-tuple-element.47), channel_id=1, source_target_pairs={{0,15},{1,14},{2,13},{3,12},{4,11},{5,10},{6,9},{7,8},{8,7},{9,6},... | collective-permute-start | bytes 368648 | tf_op jit(solution)/shard_map/ppermute | solution.py:444

commit v7 on v6

--- a/solution.py
+++ b/solution.py
@@ -28,8 +28,9 @@
 
 
 def swap_order(regions):
-    far, near = list(range(regions // 2, regions)), list(range(1, regions // 2))
-    near = near[regions // 4 - 1 :] + near[: regions // 4 - 1]
+    half, quarter = regions // 2, regions // 4
+    far = [offset for i in range(quarter) for offset in (half + quarter + i, half + i)]
+    near = list(range(quarter, half)) + list(range(1, quarter))
     return [0] + [item for pair in zip(far, near + [None]) for item in pair if item is not None]
 
 
@@ -117,9 +118,8 @@
         body(z.makers == 2, range(1))
 
 
-def own_kernel(z, place, *refs):
-    lists, (tiles, table_hbm), refs = refs[: z.makers], refs[z.makers : z.makers + 2], refs[z.makers + 2 :]
-    half, (inverse, weights, landed, staged, sums, table, sems) = refs[:FIELDS], refs[FIELDS:]
+def own_kernel(z, place, lists, tiles, table_hbm, *refs):
+    half, (total, weights, landed, staged, sums, table, sems) = refs[:FIELDS], refs[FIELDS:]
     first = lax.rem(place[0], z.makers) * z.block
 
     def fetch(j):
@@ -144,28 +144,25 @@
         fetch(j).wait()
 
         def body(side, slots):
-            def weight_item(maker, slot):
-                column, kind = (lists[maker][entry, slot, first + j] for entry in (1, 2))
+            def weight_item(slot):
+                column, kind = (lists[entry, slot, first + j] for entry in (1, 2))
                 return functools.partial(weight_tile, weights, kind), column
 
             def field_item(field, slot):
-                weight, column = weight_item(0, slot)
+                weight, column = weight_item(slot)
                 return lambda t: staged_tile(staged.at[slot], field, t) * weight(t), column
 
             for slot in slots:
                 stage(staged.at[slot], landed[j, slot])
-            items = [weight_item(maker, slot) for maker in range(z.makers) for slot in slots]
-            inverses = [[1.0 / piece for piece in rows] for rows in place_all(side, sums.at[FIELDS], items)]
-            for parity in range(2):
-                for t in range(TILES):
-                    inverse[j, parity, t] = inverses[parity][t]
-            for field in range(FIELDS):
-                pieces = place_all(side, sums.at[field], [field_item(field, slot) for slot in slots])
+            for index in range(FIELDS + 1):
+                items = [field_item(index, slot) if index < FIELDS else weight_item(slot) for slot in slots]
+                pieces = place_all(side, sums.at[index], items)
+                target = half[index] if index < FIELDS else total
                 for parity in range(2):
                     for t in range(TILES):
-                        half[field][j, parity, t] = pieces[parity][t] * inverses[parity][t]
-
-        either_kind(z, lists[0][0, 1, first + j] >= 0, body)
+                        target[j, parity, t] = pieces[parity][t]
+
+        either_kind(z, lists[0, 1, first + j] >= 0, body)
         return carry
 
     lax.fori_loop(0, z.block, region, 0)
@@ -182,7 +179,7 @@
             *[jax.ShapeDtypeStruct((z.block, 2, TILES, PAIRS, LANES), jnp.float32)] * (FIELDS + 1),
             jax.ShapeDtypeStruct((TILES, kinds * PAIRS, LANES), jnp.float32),
         ],
-        in_specs=[smem] * (1 + z.makers) + [hbm, hbm],
+        in_specs=[smem, smem, hbm, hbm],
         out_specs=[vmem] * (FIELDS + 2),
         scratch_shapes=[
             pltpu.VMEM((z.block, CAP, LINES, LANES), jnp.bfloat16),
@@ -194,7 +191,7 @@
         compiler_params=pltpu.CompilerParams(vmem_limit_bytes=MOST_VMEM),
         cost_estimate=pl.CostEstimate(flops=5_000_000, bytes_accessed=8_000_000, transcendentals=0),
         name="own_share",
-    )(place, *lists, tiles, table)
+    )(place, lists, tiles, table)
 
 
 def strength_kernel(z, smoothing, _, strength):
@@ -220,7 +217,7 @@
 def join_kernel(z, *refs):
     place, lists, refs = refs[0], refs[1 : 1 + z.makers], refs[1 + z.makers :]
     received, refs = refs[: z.makers - 1], refs[z.makers - 1 :]
-    half, (inverse, weights, strength), outs = refs[:FIELDS], refs[FIELDS : FIELDS + 3], refs[FIELDS + 3 : -6]
+    half, (total, weights, strength), outs = refs[:FIELDS], refs[FIELDS : FIELDS + 3], refs[FIELDS + 3 : -6]
     staged, sums, lines, turned, blocks, sems = refs[-6:]
     me = place[0]
     first = lax.rem(me, z.makers) * z.block
@@ -228,46 +225,54 @@
     identity = (row == column).astype(jnp.bfloat16)
 
     def send(i, quad):
-        return pltpu.make_async_copy(blocks.at[i, quad], outs[i].at[quad], sems.at[i, quad])
-
-    for quad in range(z.quads):
-
+        return pltpu.make_async_copy(blocks.at[z.offsets[i], quad], outs[i].at[quad], sems.at[i, quad])
+
+    def one_quad(quad, carry):
         def region(i, carry):
             j = quad * QUAD + i
 
             def body(side, slots):
                 sources = [(maker, slot) for maker in range(1, z.makers) for slot in slots]
 
+                def weight_item(maker, slot):
+                    column, kind = (lists[maker][entry, slot, first + j] for entry in (1, 2))
+                    return functools.partial(weight_tile, weights, kind), column
+
                 def field_item(field, maker, slot):
-                    column, kind = (lists[maker][entry, slot, first + j] for entry in (1, 2))
-                    own = staged.at[(maker - 1) * CAP + slot]
-                    return lambda t: staged_tile(own, field, t) * weight_tile(weights, kind, t), column
+                    weight, column = weight_item(maker, slot)
+                    return lambda t: staged_tile(staged.at[(maker - 1) * CAP + slot], field, t) * weight(t), column
 
                 for maker, slot in sources:
                     stage(staged.at[(maker - 1) * CAP + slot], received[maker - 1][first + j, slot])
+                others = place_all(side, sums.at[FIELDS], [weight_item(*source) for source in sources])
+                inverse = [[1.0 / (total[j, parity, t] + others[parity][t]) for t in range(TILES)] for parity in range(2)]
                 for field in range(FIELDS):
                     pieces = place_all(side, sums.at[field], [field_item(field, *source) for source in sources])
                     for parity in range(2):
                         for t in range(TILES):
                             lines[field, t, pl.ds(ROWS * i + parity, PAIRS, stride=2), :] = (
-                                half[field][j, parity, t] + pieces[parity][t] * inverse[j, parity, t]
-                            )
+                                half[field][j, parity, t] + pieces[parity][t]
+                            ) * inverse[parity][t]
 
             either_kind(z, lists[0][0, 1, first + j] >= 0, body)
             return carry
 
         lax.fori_loop(0, QUAD, region, 0)
-        for field in range(FIELDS):
-            for t in range(TILES):
-                turned[field, LANES * t : LANES * (t + 1), :] = lax.dot_general(
+
+        def transpose(t, carry):
+            for field in range(FIELDS):
+                turned[field, pl.ds(pl.multiple_of(LANES * t, LANES), LANES), :] = lax.dot_general(
                     identity,
                     lines[field, t].astype(jnp.bfloat16),
                     (((1,), (1,)), ((), ())),
                     preferred_element_type=jnp.float32,
                 )
-        for i, offset in enumerate(z.offsets):
-            target = blocks.at[i, quad] if i else outs[0].at[quad]
-            dest = me ^ offset
+            return carry
+
+        lax.fori_loop(0, TILES, transpose, 0)
+
+        def emit(dest, carry):
+            target = blocks.at[me ^ dest, quad]
             top = dest * z.width
             if z.width % 8 == 0:
                 top = pl.multiple_of(top, 8)
@@ -278,10 +283,16 @@
             edge = [turned[field, pl.ds(end, 1), :] for field in range(FIELDS) for end in ends]
             edge.append(strength[dest, quad])
             target[z.main : z.sent, :] = jnp.concatenate(edge, 0).astype(jnp.bfloat16)
-            if i:
-                send(i, quad).start()
+            return carry
+
+        lax.fori_loop(0, z.regions, emit, 0)
+        for i in range(z.regions):
+            send(i, quad).start()
+        return carry
+
+    lax.fori_loop(0, z.quads, one_quad, 0)
     for quad in range(z.quads):
-        for i in range(1, z.regions):
+        for i in range(z.regions):
             send(i, quad).wait()
 
 
@@ -298,7 +309,7 @@
         out_specs=[vmem] + [hbm] * (z.regions - 1),
         scratch_shapes=[
             pltpu.VMEM((CAP * (z.makers - 1), LINES, LANES), jnp.float32),
-            pltpu.VMEM((FIELDS, 2, SLOTS, PAIRS, LANES), jnp.float32),
+            pltpu.VMEM((FIELDS + 1, 2, SLOTS, PAIRS, LANES), jnp.float32),
             pltpu.VMEM((FIELDS, TILES, LANES, LANES), jnp.float32),
             pltpu.VMEM((FIELDS, COLS + 8, LANES), jnp.float32),
             pltpu.VMEM((z.regions, *shape), jnp.bfloat16),
@@ -364,25 +375,25 @@
             for t in range(tiles):
                 padded[sample, f, t, 7:8, :] = edges[sample, t, pl.ds(low, 1), :]
                 padded[sample, f, t, 8 + z.width : 9 + z.width, :] = edges[sample, t, pl.ds(low + 1, 1), :]
-    for f, low in ((f, low) for f in range(STEP_FIELDS) for low in range(0, z.width, 16)):
-        high = min(low + 16, z.width)
-        lane = lax.broadcasted_iota(jnp.int32, (high - low, LANES), 1)
+    def score_rows(f, low, count):
+        lane = lax.broadcasted_iota(jnp.int32, (count, LANES), 1)
+        here_rows = pl.ds(low, count)
         smoothed = [[] for _ in range(tiles)]
         for sample in range(SAMPLES):
             field = padded.at[sample, f]
-            pieces = [field[t, 8 + low : 8 + high, :] for t in range(tiles)]
+            pieces = [field[t, pl.ds(8 + low, count), :] for t in range(tiles)]
             later = [pltpu.roll(piece, 1, 1) for piece in pieces]
             sooner = [pltpu.roll(piece, LANES - 1, 1) for piece in pieces]
             for t, here in enumerate(pieces):
                 above = jnp.where(lane == 0, later[t - 1] if t else here, later[t])
                 below = jnp.where(lane == LANES - 1, sooner[t + 1] if t + 1 < tiles else here, sooner[t])
-                sides = field[t, 7 + low : 7 + high, :] + field[t, 9 + low : 9 + high, :]
-                smooth = here + strength[t, low:high, :] * (above + below + sides - 4.0 * here)
+                sides = field[t, pl.ds(7 + low, count), :] + field[t, pl.ds(9 + low, count), :]
+                smooth = here + strength[t, here_rows, :] * (above + below + sides - 4.0 * here)
                 smoothed[t].append(smooth.astype(jnp.bfloat16))
         for t, members in enumerate(smoothed):
             lanes = slice(LANES * t, LANES * (t + 1))
             values = [member.astype(jnp.float32) for member in members]
-            target = analysis[f, low:high, lanes].astype(jnp.float32)
+            target = analysis[f, here_rows, lanes].astype(jnp.float32)
             error = sum(jnp.abs(value - target) for value in values) * (1.0 / SAMPLES)
             average = sum(values) * (1.0 / SAMPLES)
             variance = sum((value - average) ** 2 for value in values) * (1.0 / (SAMPLES - 1.0))
@@ -395,9 +406,23 @@
                 (2 * k - SAMPLES + 1.0) * (ranked[k] - ranked[SAMPLES - 1 - k])
                 for k in range(SAMPLES // 2, SAMPLES)
             )
-            crps[f, low:high, lanes] = (error - pairs * (1.0 / (SAMPLES * SAMPLES))).astype(jnp.bfloat16)
-            spread[0, f, low:high, lanes] = variance.astype(jnp.bfloat16)
-            spread[1, f, low:high, lanes] = ((average - target) ** 2).astype(jnp.bfloat16)
+            crps[f, here_rows, lanes] = (error - pairs * (1.0 / (SAMPLES * SAMPLES))).astype(jnp.bfloat16)
+            spread[0, f, here_rows, lanes] = variance.astype(jnp.bfloat16)
+            spread[1, f, here_rows, lanes] = ((average - target) ** 2).astype(jnp.bfloat16)
+
+    def score_field(f, carry):
+        groups = z.width // 16
+
+        def group(g, carry):
+            score_rows(f, pl.multiple_of(16 * g, 16), 16)
+            return carry
+
+        lax.fori_loop(0, groups, group, 0)
+        if z.width % 16:
+            score_rows(f, 16 * groups, z.width % 16)
+        return carry
+
+    lax.fori_loop(0, STEP_FIELDS, score_field, 0)
 
 
 def score(z, place, blocks, analysis):
@@ -437,7 +462,7 @@
     lists = jnp.transpose(slot_lists, (2, 1, 0))
     received = [lax.ppermute(tiles, "region", turn) for turn in turns]
     lists = [lists] + [lax.ppermute(lists, "region", turn) for turn in turns]
-    shares = own_share(z, place, lists, tiles, blend_table)
+    shares = own_share(z, place, lists[0], tiles, blend_table)
     shares = [*shares, strength_blocks(z, smoothing, shares[-1])]
     blocks = join(z, place, lists, received, shares)
     moved = [blocks[0]] + [

time: 72.5 us -> 70.2 us (0.968)
  the two profiles are of different devices: /device:TPU:17 before, /device:TPU:1 now
where the time goes in v7:
time: 70.2 us; the launch traced here: 69.8 us
  starting transfers between devices  29.6 us (42%)
  waiting for transfers between devices  20.2 us (29%)
  Pallas kernels  18.5 us (26%)
    ppermute x15, starting transfers between devices, shards(): lax.ppermute(block, 'region', [(i, i ^ offset) for i in range(z.regions)])  29.1 us
    ppermute x15, waiting for transfers between devices, shards(): lax.ppermute(block, 'region', [(i, i ^ offset) for i in range(z.regions)])  18.9 us
    pallas_call x1, Pallas kernels, join(): pl.pallas_call(functools.partial(join_kernel, z), out_shape=[jax.ShapeDty...  8.62 us
    pallas_call x1, Pallas kernels, score(): pl.pallas_call(functools.partial(score_kernel, z), out_shape=[jax.ShapeDt...  5.7 us
    pallas_call x1, Pallas kernels, own_share(): pl.pallas_call(functools.partial(own_kernel, z), out_shape=[*[jax.ShapeDt...  3.92 us
  transfers between devices with their start and end apart: 17, of which 9 were waited for; matrix products, arithmetic and copies ran while one was open for 0% of the time, Pallas kernels for 6%

profile of v7, /device:TPU:1, one launch (start us, length us, event | category | flops | bytes accessed | tf_op | source)
XLA Modules:
  0.0 69.8 jit_solution(9650720806518046380)
XLA Ops:
  0.8 0.5 collective-permute-start
  1.2 0.7 copy-done.2
  1.9 3.9 %own_share.1 = (f32[8,2,7,16,128]{4,3,2,1,0:T(8,128)S(1)}, f32[8,2,7,16,128]{4,3,2,1,0:T(8,128)S(1)}, f32[8,2,7,16,128]{4,3,2,1,0:T(8,128)S(1)}, f32[8,2,7,16,12...) custom-call(s32[1]{0:T(128)} %bitcast.place.refs_0_, s32[3,2,16]{2,1,0:T(2,128)S(1)} %bitcast.12, ...), custom_call_target="tpu_custom_call" | custom-call | flops 5000000 | bytes 8000000 | tf_op jit(solution)/shard_map/own_share/pallas_call | solution.py:176
  6.3 1.2 %collective-permute-done.1.refs_3_ = bf16[16,2,448,128]{3,2,1,0:T(8,128)(2,1)} collective-permute-done((bf16[16,2,448,128]{3,2,1,0:T(8,128)(2,1)}, bf16[16,2,448,128]{3,2,1,0:T(8,128)(2,1)}, u32[]{:S(2)}, u32[]{:S(2)}) %collective-permute-start.1) | collective-permute-done | bytes 3670048 | tf_op jit(solution)/shard_map/ppermute | solution.py:463
  7.5 8.6 %join.1 = (bf16[2,240,128]{2,1,0:T(8,128)(2,1)S(1)}, bf16[2,240,128]{2,1,0:T(8,128)(2,1)}, bf16[2,240,128]{2,1,0:T(8,128)(2,1)}, bf16[2,240,128]{2,1,0:T(8,128)(...) custom-call(s32[1]{0:T(128)} %bitcast.place.refs_0_, ...), custom_call_target="tpu_custom_call" | custom-call | flops 5000000 | bytes 8000000 | tf_op jit(solution)/shard_map/join/pallas_call | solution.py:304
  16.1 4.5 %collective-permute-start.2 = (bf16[2,240,128]{2,1,0:T(8,128)(2,1)}, bf16[2,240,128]{2,1,0:T(8,128)(2,1)S(1)}, u32[]{:S(2)}, u32[]{:S(2)}) collective-permute-start(bf16[2,240,128]{2,1,0:T(8,128)(2,1)} %get-tuple-element.33), channel_id=1, source_target_pairs={{0,12},{1,13},{2,14},{3,15},{4,8},{5,9},{6,10},{7,11},{8,4},{9,5},... | collective-permute-start | bytes 368648 | tf_op jit(solution)/shard_map/ppermute | solution.py:469
  20.6 0.4 collective-permute-start.4
  21.0 2.2 %collective-permute-start.5 = (bf16[2,240,128]{2,1,0:T(8,128)(2,1)}, bf16[2,240,128]{2,1,0:T(8,128)(2,1)S(1)}, u32[]{:S(2)}, u32[]{:S(2)}) collective-permute-start(bf16[2,240,128]{2,1,0:T(8,128)(2,1)} %get-tuple-element.36), channel_id=1, source_target_pairs={{0,5},{1,4},{2,7},{3,6},{4,1},{5,0},{6,3},{7,2},{8,13},{9,12},{10,... | collective-permute-start | bytes 368648 | tf_op jit(solution)/shard_map/ppermute | solution.py:469
  23.2 2.4 %collective-permute-start.6 = (bf16[2,240,128]{2,1,0:T(8,128)(2,1)}, bf16[2,240,128]{2,1,0:T(8,128)(2,1)S(1)}, u32[]{:S(2)}, u32[]{:S(2)}) collective-permute-start(bf16[2,240,128]{2,1,0:T(8,128)(2,1)} %get-tuple-element.37), channel_id=1, source_target_pairs={{0,13},{1,12},{2,15},{3,14},{4,9},{5,8},{6,11},{7,10},{8,5},{9,4},... | collective-permute-start | bytes 368648 | tf_op jit(solution)/shard_map/ppermute | solution.py:469
  25.5 0.9 %collective-permute-start.7 = (bf16[2,240,128]{2,1,0:T(8,128)(2,1)}, bf16[2,240,128]{2,1,0:T(8,128)(2,1)S(1)}, u32[]{:S(2)}, u32[]{:S(2)}) collective-permute-start(bf16[2,240,128]{2,1,0:T(8,128)(2,1)} %get-tuple-element.38), channel_id=1, source_target_pairs={{0,6},{1,7},{2,4},{3,5},{4,2},{5,3},{6,0},{7,1},{8,14},{9,15},{10,... | collective-permute-start | bytes 368648 | tf_op jit(solution)/shard_map/ppermute | solution.py:469
  26.5 1.3 %collective-permute-done.3.refs_2_ = bf16[2,240,128]{2,1,0:T(8,128)(2,1)S(1)} collective-permute-done((bf16[2,240,128]{2,1,0:T(8,128)(2,1)}, bf16[2,240,128]{2,1,0:T(8,128)(2,1)S(1)}, u32[]{:S(2)}, u32[]{:S(2)}) %collective-permute-start.3) | collective-permute-done | bytes 122912 | tf_op jit(solution)/shard_map/ppermute | solution.py:469
  27.8 3.1 %collective-permute-start.8 = (bf16[2,240,128]{2,1,0:T(8,128)(2,1)}, bf16[2,240,128]{2,1,0:T(8,128)(2,1)S(1)}, u32[]{:S(2)}, u32[]{:S(2)}) collective-permute-start(bf16[2,240,128]{2,1,0:T(8,128)(2,1)} %get-tuple-element.39), channel_id=1, source_target_pairs={{0,9},{1,8},{2,11},{3,10},{4,13},{5,12},{6,15},{7,14},{8,1},{9,0},... | collective-permute-start | bytes 368648 | tf_op jit(solution)/shard_map/ppermute | solution.py:469
  30.9 1.8 %collective-permute-start.9 = (bf16[2,240,128]{2,1,0:T(8,128)(2,1)}, bf16[2,240,128]{2,1,0:T(8,128)(2,1)S(1)}, u32[]{:S(2)}, u32[]{:S(2)}) collective-permute-start(bf16[2,240,128]{2,1,0:T(8,128)(2,1)} %get-tuple-element.40), channel_id=1, source_target_pairs={{0,7},{1,6},{2,5},{3,4},{4,3},{5,2},{6,1},{7,0},{8,15},{9,14},{10,... | collective-permute-start | bytes 368648 | tf_op jit(solution)/shard_map/ppermute | solution.py:469
  32.8 2.4 %collective-permute-done.5.refs_4_ = bf16[2,240,128]{2,1,0:T(8,128)(2,1)S(1)} collective-permute-done((bf16[2,240,128]{2,1,0:T(8,128)(2,1)}, bf16[2,240,128]{2,1,0:T(8,128)(2,1)S(1)}, u32[]{:S(2)}, u32[]{:S(2)}) %collective-permute-start.5) | collective-permute-done | bytes 122912 | tf_op jit(solution)/shard_map/ppermute | solution.py:469
  35.2 0.7 collective-permute-start.10
  36.2 2.9 %collective-permute-done.7.refs_6_ = bf16[2,240,128]{2,1,0:T(8,128)(2,1)S(1)} collective-permute-done((bf16[2,240,128]{2,1,0:T(8,128)(2,1)}, bf16[2,240,128]{2,1,0:T(8,128)(2,1)S(1)}, u32[]{:S(2)}, u32[]{:S(2)}) %collective-permute-start.7) | collective-permute-done | bytes 122912 | tf_op jit(solution)/shard_map/ppermute | solution.py:469
  39.1 0.8 %collective-permute-start.12 = (bf16[2,240,128]{2,1,0:T(8,128)(2,1)}, bf16[2,240,128]{2,1,0:T(8,128)(2,1)S(1)}, u32[]{:S(2)}, u32[]{:S(2)}) collective-permute-start(bf16[2,240,128]{2,1,0:T(8,128)(2,1)} %get-tuple-element.43), channel_id=1, source_target_pairs={{0,10},{1,11},{2,8},{3,9},{4,14},{5,15},{6,12},{7,13},{8,2},{9,3},... | collective-permute-start | bytes 368648 | tf_op jit(solution)/shard_map/ppermute | solution.py:469
  39.9 3.8 %collective-permute-done.8.refs_7_ = bf16[2,240,128]{2,1,0:T(8,128)(2,1)S(1)} collective-permute-done((bf16[2,240,128]{2,1,0:T(8,128)(2,1)}, bf16[2,240,128]{2,1,0:T(8,128)(2,1)S(1)}, u32[]{:S(2)}, u32[]{:S(2)}) %collective-permute-start.8) | collective-permute-done | bytes 122912 | tf_op jit(solution)/shard_map/ppermute | solution.py:469
  43.7 1.8 %collective-permute-start.13 = (bf16[2,240,128]{2,1,0:T(8,128)(2,1)}, bf16[2,240,128]{2,1,0:T(8,128)(2,1)S(1)}, u32[]{:S(2)}, u32[]{:S(2)}) collective-permute-start(bf16[2,240,128]{2,1,0:T(8,128)(2,1)} %get-tuple-element.44), channel_id=1, source_target_pairs={{0,2},{1,3},{2,0},{3,1},{4,6},{5,7},{6,4},{7,5},{8,10},{9,11},{10,... | collective-permute-start | bytes 368648 | tf_op jit(solution)/shard_map/ppermute | solution.py:469
  45.8 2.5 %collective-permute-start.15 = (bf16[2,240,128]{2,1,0:T(8,128)(2,1)}, bf16[2,240,128]{2,1,0:T(8,128)(2,1)S(1)}, u32[]{:S(2)}, u32[]{:S(2)}) collective-permute-start(bf16[2,240,128]{2,1,0:T(8,128)(2,1)} %get-tuple-element.46), channel_id=1, source_target_pairs={{0,3},{1,2},{2,1},{3,0},{4,7},{5,6},{6,5},{7,4},{8,11},{9,10},{10,... | collective-permute-start | bytes 368648 | tf_op jit(solution)/shard_map/ppermute | solution.py:469
  48.3 7.6 %collective-permute-start.16 = (bf16[2,240,128]{2,1,0:T(8,128)(2,1)}, bf16[2,240,128]{2,1,0:T(8,128)(2,1)S(1)}, u32[]{:S(2)}, u32[]{:S(2)}) collective-permute-start(bf16[2,240,128]{2,1,0:T(8,128)(2,1)} %get-tuple-element.47), channel_id=1, source_target_pairs={{0,11},{1,10},{2,9},{3,8},{4,15},{5,14},{6,13},{7,12},{8,3},{9,2},... | collective-permute-start | bytes 368648 | tf_op jit(solution)/shard_map/ppermute | solution.py:469
  55.9 1.1 %collective-permute-done.15.refs_14_ = bf16[2,240,128]{2,1,0:T(8,128)(2,1)S(1)} collective-permute-done((bf16[2,240,128]{2,1,0:T(8,128)(2,1)}, bf16[2,240,128]{2,1,0:T(8,128)(2,1)S(1)}, u32[]{:S(2)}, u32[]{:S(2)}) %collective-permute-start.15) | collective-permute-done | bytes 122912 | tf_op jit(solution)/shard_map/ppermute | solution.py:469
  57.0 7.1 %collective-permute-done.16.refs_15_ = bf16[2,240,128]{2,1,0:T(8,128)(2,1)S(1)} collective-permute-done((bf16[2,240,128]{2,1,0:T(8,128)(2,1)}, bf16[2,240,128]{2,1,0:T(8,128)(2,1)S(1)}, u32[]{:S(2)}, u32[]{:S(2)}) %collective-permute-start.16) | collective-permute-done | bytes 122912 | tf_op jit(solution)/shard_map/ppermute | solution.py:469
  64.1 5.7 %score.1 = (bf16[4,56,512]{2,1,0:T(8,128)(2,1)}, bf16[2,4,56,512]{3,2,1,0:T(8,128)(2,1)}) custom-call(s32[1]{0:T(128)} %bitcast.place.refs_0_, bf16[2,240,128]{2,1,0:T(8,128)(2,1)S(1)} %get-tuple-element.32.refs_0_, bf16[2,240,128]{2,1,0:T(8,128)(2,1)S(1)} %collective-permute-done.2.refs_1_, bf16[2,240,128]{2,1,0:T(8,128)(2,1)S(1)} %collective-permute-done.3.refs_2_, ...), custom_call_target="tpu_custom_call" | custom-call | tf_op jit(solution)/shard_map/score/pallas_call | solution.py:430
  (22 shorter events, 1.2 us)
Async XLA Ops:
  0.6 5.2 %copy-start.1 = (f32[32,896]{1,0:T(8,128)S(1)}, f32[32,896]{1,0:T(8,128)}, u32[]{:S(2)}) copy-start(f32[32,896]{1,0:T(8,128)} %smoothing.1) | copy-start | bytes 344068
  0.6 6.8 %collective-permute-start.1 = (bf16[16,2,448,128]{3,2,1,0:T(8,128)(2,1)}, bf16[16,2,448,128]{3,2,1,0:T(8,128)(2,1)}, u32[]{:S(2)}, u32[]{:S(2)}) collective-permute-start(bf16[16,2,448,128]{3,2,1,0:T(8,128)(2,1)} %bitcast.14), channel_id=1, source_target_pairs={{0,1},{1,0},{2,3},{3,2},{4,5},{5,4},{6,7},{7,6},{8,9},{9,8},{10,11... | collective-permute-start | bytes 11010056 | tf_op jit(solution)/shard_map/ppermute | solution.py:463
  0.8 5.5 %collective-permute-start = (s32[3,2,16]{2,1,0:T(2,128)}, s32[3,2,16]{2,1,0:T(2,128)S(1)}, u32[]{:S(2)}, u32[]{:S(2)}) collective-permute-start(s32[3,2,16]{2,1,0:T(2,128)} %bitcast.11), channel_id=1, source_target_pairs={{0,1},{1,0},{2,3},{3,2},{4,5},{5,4},{6,7},{7,6},{8,9},{9,8},{10,11... | collective-permute-start | bytes 1160 | tf_op jit(solution)/shard_map/ppermute | solution.py:464
  1.2 0.7 copy-start.2
  1.9 5.6 %copy-start.3 = (s32[16,2,3]{0,1,2:T(2,128)S(1)}, s32[16,2,3]{0,1,2:T(2,128)}, u32[]{:S(2)}) copy-start(s32[16,2,3]{0,1,2:T(2,128)} %param.6) | copy-start | bytes 1156
  7.5 56.6 %copy-start = (bf16[4,512,56]{1,2,0:T(8,128)(2,1)S(1)}, bf16[4,512,56]{1,2,0:T(8,128)(2,1)}, u32[]{:S(2)}) copy-start(bf16[4,512,56]{1,2,0:T(8,128)(2,1)} %param.9) | copy-start | bytes 688132
  16.1 9.4 %collective-permute-start.2 = (bf16[2,240,128]{2,1,0:T(8,128)(2,1)}, bf16[2,240,128]{2,1,0:T(8,128)(2,1)S(1)}, u32[]{:S(2)}, u32[]{:S(2)}) collective-permute-start(bf16[2,240,128]{2,1,0:T(8,128)(2,1)} %get-tuple-element.33), channel_id=1, source_target_pairs={{0,12},{1,13},{2,14},{3,15},{4,8},{5,9},{6,10},{7,11},{8,4},{9,5},... | collective-permute-start | bytes 368648 | tf_op jit(solution)/shard_map/ppermute | solution.py:469
  20.6 7.2 %collective-permute-start.3 = (bf16[2,240,128]{2,1,0:T(8,128)(2,1)}, bf16[2,240,128]{2,1,0:T(8,128)(2,1)S(1)}, u32[]{:S(2)}, u32[]{:S(2)}) collective-permute-start(bf16[2,240,128]{2,1,0:T(8,128)(2,1)} %get-tuple-element.34), channel_id=1, source_target_pairs={{0,4},{1,5},{2,6},{3,7},{4,0},{5,1},{6,2},{7,3},{8,12},{9,13},{10,... | collective-permute-start | bytes 368648 | tf_op jit(solution)/shard_map/ppermute | solution.py:469
  20.6 10.3 %collective-permute-start.4 = (bf16[2,240,128]{2,1,0:T(8,128)(2,1)}, bf16[2,240,128]{2,1,0:T(8,128)(2,1)S(1)}, u32[]{:S(2)}, u32[]{:S(2)}) collective-permute-start(bf16[2,240,128]{2,1,0:T(8,128)(2,1)} %get-tuple-element.35), channel_id=1, source_target_pairs={{0,8},{1,9},{2,10},{3,11},{4,12},{5,13},{6,14},{7,15},{8,0},{9,1},... | collective-permute-start | bytes 368648 | tf_op jit(solution)/shard_map/ppermute | solution.py:469
  21.0 14.2 %collective-permute-start.5 = (bf16[2,240,128]{2,1,0:T(8,128)(2,1)}, bf16[2,240,128]{2,1,0:T(8,128)(2,1)S(1)}, u32[]{:S(2)}, u32[]{:S(2)}) collective-permute-start(bf16[2,240,128]{2,1,0:T(8,128)(2,1)} %get-tuple-element.36), channel_id=1, source_target_pairs={{0,5},{1,4},{2,7},{3,6},{4,1},{5,0},{6,3},{7,2},{8,13},{9,12},{10,... | collective-permute-start | bytes 368648 | tf_op jit(solution)/shard_map/ppermute | solution.py:469
  23.2 12.7 %collective-permute-start.6 = (bf16[2,240,128]{2,1,0:T(8,128)(2,1)}, bf16[2,240,128]{2,1,0:T(8,128)(2,1)S(1)}, u32[]{:S(2)}, u32[]{:S(2)}) collective-permute-start(bf16[2,240,128]{2,1,0:T(8,128)(2,1)} %get-tuple-element.37), channel_id=1, source_target_pairs={{0,13},{1,12},{2,15},{3,14},{4,9},{5,8},{6,11},{7,10},{8,5},{9,4},... | collective-permute-start | bytes 368648 | tf_op jit(solution)/shard_map/ppermute | solution.py:469
  25.5 13.5 %collective-permute-start.7 = (bf16[2,240,128]{2,1,0:T(8,128)(2,1)}, bf16[2,240,128]{2,1,0:T(8,128)(2,1)S(1)}, u32[]{:S(2)}, u32[]{:S(2)}) collective-permute-start(bf16[2,240,128]{2,1,0:T(8,128)(2,1)} %get-tuple-element.38), channel_id=1, source_target_pairs={{0,6},{1,7},{2,4},{3,5},{4,2},{5,3},{6,0},{7,1},{8,14},{9,15},{10,... | collective-permute-start | bytes 368648 | tf_op jit(solution)/shard_map/ppermute | solution.py:469
  27.8 15.9 %collective-permute-start.8 = (bf16[2,240,128]{2,1,0:T(8,128)(2,1)}, bf16[2,240,128]{2,1,0:T(8,128)(2,1)S(1)}, u32[]{:S(2)}, u32[]{:S(2)}) collective-permute-start(bf16[2,240,128]{2,1,0:T(8,128)(2,1)} %get-tuple-element.39), channel_id=1, source_target_pairs={{0,9},{1,8},{2,11},{3,10},{4,13},{5,12},{6,15},{7,14},{8,1},{9,0},... | collective-permute-start | bytes 368648 | tf_op jit(solution)/shard_map/ppermute | solution.py:469
  30.9 14.6 %collective-permute-start.9 = (bf16[2,240,128]{2,1,0:T(8,128)(2,1)}, bf16[2,240,128]{2,1,0:T(8,128)(2,1)S(1)}, u32[]{:S(2)}, u32[]{:S(2)}) collective-permute-start(bf16[2,240,128]{2,1,0:T(8,128)(2,1)} %get-tuple-element.40), channel_id=1, source_target_pairs={{0,7},{1,6},{2,5},{3,4},{4,3},{5,2},{6,1},{7,0},{8,15},{9,14},{10,... | collective-permute-start | bytes 368648 | tf_op jit(solution)/shard_map/ppermute | solution.py:469
  35.2 10.6 %collective-permute-start.10 = (bf16[2,240,128]{2,1,0:T(8,128)(2,1)}, bf16[2,240,128]{2,1,0:T(8,128)(2,1)S(1)}, u32[]{:S(2)}, u32[]{:S(2)}) collective-permute-start(bf16[2,240,128]{2,1,0:T(8,128)(2,1)} %get-tuple-element.41), channel_id=1, source_target_pairs={{0,14},{1,15},{2,12},{3,13},{4,10},{5,11},{6,8},{7,9},{8,6},{9,7},... | collective-permute-start | bytes 368648 | tf_op jit(solution)/shard_map/ppermute | solution.py:469
  35.9 12.4 %collective-permute-start.11 = (bf16[2,240,128]{2,1,0:T(8,128)(2,1)}, bf16[2,240,128]{2,1,0:T(8,128)(2,1)S(1)}, u32[]{:S(2)}, u32[]{:S(2)}) collective-permute-start(bf16[2,240,128]{2,1,0:T(8,128)(2,1)} %get-tuple-element.42), channel_id=1, source_target_pairs={{0,1},{1,0},{2,3},{3,2},{4,5},{5,4},{6,7},{7,6},{8,9},{9,8},{10,11... | collective-permute-start | bytes 368648 | tf_op jit(solution)/shard_map/ppermute | solution.py:469
  39.1 16.8 %collective-permute-start.12 = (bf16[2,240,128]{2,1,0:T(8,128)(2,1)}, bf16[2,240,128]{2,1,0:T(8,128)(2,1)S(1)}, u32[]{:S(2)}, u32[]{:S(2)}) collective-permute-start(bf16[2,240,128]{2,1,0:T(8,128)(2,1)} %get-tuple-element.43), channel_id=1, source_target_pairs={{0,10},{1,11},{2,8},{3,9},{4,14},{5,15},{6,12},{7,13},{8,2},{9,3},... | collective-permute-start | bytes 368648 | tf_op jit(solution)/shard_map/ppermute | solution.py:469
  43.7 12.2 %collective-permute-start.13 = (bf16[2,240,128]{2,1,0:T(8,128)(2,1)}, bf16[2,240,128]{2,1,0:T(8,128)(2,1)S(1)}, u32[]{:S(2)}, u32[]{:S(2)}) collective-permute-start(bf16[2,240,128]{2,1,0:T(8,128)(2,1)} %get-tuple-element.44), channel_id=1, source_target_pairs={{0,2},{1,3},{2,0},{3,1},{4,6},{5,7},{6,4},{7,5},{8,10},{9,11},{10,... | collective-permute-start | bytes 368648 | tf_op jit(solution)/shard_map/ppermute | solution.py:469
  45.5 10.4 %collective-permute-start.14 = (bf16[2,240,128]{2,1,0:T(8,128)(2,1)}, bf16[2,240,128]{2,1,0:T(8,128)(2,1)S(1)}, u32[]{:S(2)}, u32[]{:S(2)}) collective-permute-start(bf16[2,240,128]{2,1,0:T(8,128)(2,1)} %get-tuple-element.45), channel_id=1, source_target_pairs={{0,15},{1,14},{2,13},{3,12},{4,11},{5,10},{6,9},{7,8},{8,7},{9,6},... | collective-permute-start | bytes 368648 | tf_op jit(solution)/shard_map/ppermute | solution.py:469
  45.8 11.2 %collective-permute-start.15 = (bf16[2,240,128]{2,1,0:T(8,128)(2,1)}, bf16[2,240,128]{2,1,0:T(8,128)(2,1)S(1)}, u32[]{:S(2)}, u32[]{:S(2)}) collective-permute-start(bf16[2,240,128]{2,1,0:T(8,128)(2,1)} %get-tuple-element.46), channel_id=1, source_target_pairs={{0,3},{1,2},{2,1},{3,0},{4,7},{5,6},{6,5},{7,4},{8,11},{9,10},{10,... | collective-permute-start | bytes 368648 | tf_op jit(solution)/shard_map/ppermute | solution.py:469
  48.3 15.7 %collective-permute-start.16 = (bf16[2,240,128]{2,1,0:T(8,128)(2,1)}, bf16[2,240,128]{2,1,0:T(8,128)(2,1)S(1)}, u32[]{:S(2)}, u32[]{:S(2)}) collective-permute-start(bf16[2,240,128]{2,1,0:T(8,128)(2,1)} %get-tuple-element.47), channel_id=1, source_target_pairs={{0,11},{1,10},{2,9},{3,8},{4,15},{5,14},{6,13},{7,12},{8,3},{9,2},... | collective-permute-start | bytes 368648 | tf_op jit(solution)/shard_map/ppermute | solution.py:469

commit v8 on v7

--- a/solution.py
+++ b/solution.py
@@ -217,17 +217,15 @@
 def join_kernel(z, *refs):
     place, lists, refs = refs[0], refs[1 : 1 + z.makers], refs[1 + z.makers :]
     received, refs = refs[: z.makers - 1], refs[z.makers - 1 :]
-    half, (total, weights, strength), outs = refs[:FIELDS], refs[FIELDS : FIELDS + 3], refs[FIELDS + 3 : -6]
-    staged, sums, lines, turned, blocks, sems = refs[-6:]
+    half, (total, weights, strength), outs = refs[:FIELDS], refs[FIELDS : FIELDS + 3], refs[FIELDS + 3 : -4]
+    staged, sums, lines, turned = refs[-4:]
     me = place[0]
     first = lax.rem(me, z.makers) * z.block
     row, column = (lax.broadcasted_iota(jnp.int32, (LANES, LANES), axis) for axis in (0, 1))
     identity = (row == column).astype(jnp.bfloat16)
 
-    def send(i, quad):
-        return pltpu.make_async_copy(blocks.at[z.offsets[i], quad], outs[i].at[quad], sems.at[i, quad])
-
-    def one_quad(quad, carry):
+    for quad in range(z.quads):
+
         def region(i, carry):
             j = quad * QUAD + i
 
@@ -259,61 +257,42 @@
 
         lax.fori_loop(0, QUAD, region, 0)
 
-        def transpose(t, carry):
-            for field in range(FIELDS):
-                turned[field, pl.ds(pl.multiple_of(LANES * t, LANES), LANES), :] = lax.dot_general(
+        for field in range(FIELDS):
+            for t in range(TILES):
+                turned[field, LANES * t : LANES * (t + 1), :] = lax.dot_general(
                     identity,
                     lines[field, t].astype(jnp.bfloat16),
                     (((1,), (1,)), ((), ())),
                     preferred_element_type=jnp.float32,
                 )
-            return carry
-
-        lax.fori_loop(0, TILES, transpose, 0)
-
-        def emit(dest, carry):
-            target = blocks.at[me ^ dest, quad]
+        for out, offset in zip(outs, z.offsets):
+            dest = me ^ offset
             top = dest * z.width
             if z.width % 8 == 0:
                 top = pl.multiple_of(top, 8)
             for low in range(0, FIELDS, 2):
                 block = [turned[field, pl.ds(top, z.span), :] for field in (low, low + 1)]
-                target[low * z.span : (low + 2) * z.span, :] = jnp.concatenate(block, 0).astype(jnp.bfloat16)
+                out[quad, low * z.span : (low + 2) * z.span, :] = jnp.concatenate(block, 0).astype(jnp.bfloat16)
             ends = (jnp.maximum(top - 1, 0), jnp.minimum(top + z.width, COLS - 1))
             edge = [turned[field, pl.ds(end, 1), :] for field in range(FIELDS) for end in ends]
             edge.append(strength[dest, quad])
-            target[z.main : z.sent, :] = jnp.concatenate(edge, 0).astype(jnp.bfloat16)
-            return carry
-
-        lax.fori_loop(0, z.regions, emit, 0)
-        for i in range(z.regions):
-            send(i, quad).start()
-        return carry
-
-    lax.fori_loop(0, z.quads, one_quad, 0)
-    for quad in range(z.quads):
-        for i in range(z.regions):
-            send(i, quad).wait()
+            out[quad, z.main : z.sent, :] = jnp.concatenate(edge, 0).astype(jnp.bfloat16)
 
 
 def join(z, place, lists, received, shares):
     smem = pl.BlockSpec(memory_space=pltpu.SMEM)
     vmem = pl.BlockSpec(memory_space=pltpu.VMEM)
-    hbm = pl.BlockSpec(memory_space=pltpu.HBM)
     shape = (z.quads, z.sent, LANES)
     return pl.pallas_call(
         functools.partial(join_kernel, z),
-        out_shape=[jax.ShapeDtypeStruct(shape, jnp.bfloat16)]
-        + [pltpu.HBM(shape, jnp.bfloat16)] * (z.regions - 1),
+        out_shape=[jax.ShapeDtypeStruct(shape, jnp.bfloat16)] * z.regions,
         in_specs=[smem] * (1 + z.makers) + [vmem] * (z.makers - 1 + len(shares)),
-        out_specs=[vmem] + [hbm] * (z.regions - 1),
+        out_specs=[vmem] * z.regions,
         scratch_shapes=[
             pltpu.VMEM((CAP * (z.makers - 1), LINES, LANES), jnp.float32),
             pltpu.VMEM((FIELDS + 1, 2, SLOTS, PAIRS, LANES), jnp.float32),
             pltpu.VMEM((FIELDS, TILES, LANES, LANES), jnp.float32),
             pltpu.VMEM((FIELDS, COLS + 8, LANES), jnp.float32),
-            pltpu.VMEM((z.regions, *shape), jnp.bfloat16),
-            pltpu.SemaphoreType.DMA((z.regions, z.quads)),
         ],
         compiler_params=pltpu.CompilerParams(vmem_limit_bytes=VMEM),
         cost_estimate=pl.CostEstimate(flops=5_000_000, bytes_accessed=8_000_000, transcendentals=0),
@@ -375,25 +354,25 @@
             for t in range(tiles):
                 padded[sample, f, t, 7:8, :] = edges[sample, t, pl.ds(low, 1), :]
                 padded[sample, f, t, 8 + z.width : 9 + z.width, :] = edges[sample, t, pl.ds(low + 1, 1), :]
-    def score_rows(f, low, count):
-        lane = lax.broadcasted_iota(jnp.int32, (count, LANES), 1)
-        here_rows = pl.ds(low, count)
+    for f, low in ((f, low) for f in range(STEP_FIELDS) for low in range(0, z.width, 16)):
+        high = min(low + 16, z.width)
+        lane = lax.broadcasted_iota(jnp.int32, (high - low, LANES), 1)
         smoothed = [[] for _ in range(tiles)]
         for sample in range(SAMPLES):
             field = padded.at[sample, f]
-            pieces = [field[t, pl.ds(8 + low, count), :] for t in range(tiles)]
+            pieces = [field[t, 8 + low : 8 + high, :] for t in range(tiles)]
             later = [pltpu.roll(piece, 1, 1) for piece in pieces]
             sooner = [pltpu.roll(piece, LANES - 1, 1) for piece in pieces]
             for t, here in enumerate(pieces):
                 above = jnp.where(lane == 0, later[t - 1] if t else here, later[t])
                 below = jnp.where(lane == LANES - 1, sooner[t + 1] if t + 1 < tiles else here, sooner[t])
-                sides = field[t, pl.ds(7 + low, count), :] + field[t, pl.ds(9 + low, count), :]
-                smooth = here + strength[t, here_rows, :] * (above + below + sides - 4.0 * here)
+                sides = field[t, 7 + low : 7 + high, :] + field[t, 9 + low : 9 + high, :]
+                smooth = here + strength[t, low:high, :] * (above + below + sides - 4.0 * here)
                 smoothed[t].append(smooth.astype(jnp.bfloat16))
         for t, members in enumerate(smoothed):
             lanes = slice(LANES * t, LANES * (t + 1))
             values = [member.astype(jnp.float32) for member in members]
-            target = analysis[f, here_rows, lanes].astype(jnp.float32)
+            target = analysis[f, low:high, lanes].astype(jnp.float32)
             error = sum(jnp.abs(value - target) for value in values) * (1.0 / SAMPLES)
             average = sum(values) * (1.0 / SAMPLES)
             variance = sum((value - average) ** 2 for value in values) * (1.0 / (SAMPLES - 1.0))
@@ -406,23 +385,9 @@
                 (2 * k - SAMPLES + 1.0) * (ranked[k] - ranked[SAMPLES - 1 - k])
                 for k in range(SAMPLES // 2, SAMPLES)
             )
-            crps[f, here_rows, lanes] = (error - pairs * (1.0 / (SAMPLES * SAMPLES))).astype(jnp.bfloat16)
-            spread[0, f, here_rows, lanes] = variance.astype(jnp.bfloat16)
-            spread[1, f, here_rows, lanes] = ((average - target) ** 2).astype(jnp.bfloat16)
-
-    def score_field(f, carry):
-        groups = z.width // 16
-
-        def group(g, carry):
-            score_rows(f, pl.multiple_of(16 * g, 16), 16)
-            return carry
-
-        lax.fori_loop(0, groups, group, 0)
-        if z.width % 16:
-            score_rows(f, 16 * groups, z.width % 16)
-        return carry
-
-    lax.fori_loop(0, STEP_FIELDS, score_field, 0)
+            crps[f, low:high, lanes] = (error - pairs * (1.0 / (SAMPLES * SAMPLES))).astype(jnp.bfloat16)
+            spread[0, f, low:high, lanes] = variance.astype(jnp.bfloat16)
+            spread[1, f, low:high, lanes] = ((average - target) ** 2).astype(jnp.bfloat16)
 
 
 def score(z, place, blocks, analysis):

time: 70.2 us -> 66.1 us (0.942)
  Pallas kernels: 18.5 us -> 15.1 us
  starting transfers between devices: 29.6 us -> 28.3 us
  waiting for transfers between devices: 20.2 us -> 21.2 us
    pallas_call x1, Pallas kernels: 8.62 us -> 5.67 us  [join(): pl.pallas_call(functools.partial(join_kernel, z), out_shape=[jax.ShapeDty...]
    ppermute x15, starting transfers between devices: 29.1 us -> 27.7 us  [shards(): lax.ppermute(block, 'region', [(i, i ^ offset) for i in range(z.regions)])]
    ppermute x15, waiting for transfers between devices: 18.9 us -> 20 us  [shards(): lax.ppermute(block, 'region', [(i, i ^ offset) for i in range(z.regions)])]
  transfers between devices with their start and end apart: 17 -> 17, of which waited for: 9 -> 9; matrix products, arithmetic and copies ran while one was open for 0% -> 0% of each run, Pallas kernels for 6% -> 7%
where the time goes in v8:
time: 66.1 us; the launch traced here: 66 us
  starting transfers between devices  28.3 us (43%)
  waiting for transfers between devices  21.2 us (32%)
  Pallas kernels  15.1 us (23%)
  local copies, waits for them, and re-layouts  0.7 us (1%)
  between operations  0.69 us (1%)
    ppermute x15, starting transfers between devices, shards(): lax.ppermute(block, 'region', [(i, i ^ offset) for i in range(z.regions)])  27.7 us
    ppermute x15, waiting for transfers between devices, shards(): lax.ppermute(block, 'region', [(i, i ^ offset) for i in range(z.regions)])  20 us
    pallas_call x1, Pallas kernels, join(): pl.pallas_call(functools.partial(join_kernel, z), out_shape=[jax.ShapeDty...  5.67 us
    pallas_call x1, Pallas kernels, score(): pl.pallas_call(functools.partial(score_kernel, z), out_shape=[jax.ShapeDt...  5.09 us
    pallas_call x1, Pallas kernels, own_share(): pl.pallas_call(functools.partial(own_kernel, z), out_shape=[*[jax.ShapeDt...  4.06 us
  transfers between devices with their start and end apart: 17, of which 9 were waited for; matrix products, arithmetic and copies ran while one was open for 0% of the time, Pallas kernels for 7%

profile of v8, /device:TPU:1, one launch (start us, length us, event | category | flops | bytes accessed | tf_op | source)
XLA Modules:
  0.0 66.0 jit_solution(98509690789824468)
XLA Ops:
  1.2 0.7 %copy-done.2 = s32[16,2,3]{0,1,2:T(2,128)S(1)} copy-done((s32[16,2,3]{0,1,2:T(2,128)S(1)}, s32[16,2,3]{0,1,2:T(2,128)}, u32[]{:S(2)}) %copy-start.2) | copy-done | bytes 408
  1.9 4.1 %own_share.1 = (f32[8,2,7,16,128]{4,3,2,1,0:T(8,128)S(1)}, f32[8,2,7,16,128]{4,3,2,1,0:T(8,128)S(1)}, f32[8,2,7,16,128]{4,3,2,1,0:T(8,128)S(1)}, f32[8,2,7,16,12...) custom-call(s32[1]{0:T(128)} %bitcast.place.refs_0_, s32[3,2,16]{2,1,0:T(2,128)S(1)} %bitcast.12, ...), custom_call_target="tpu_custom_call" | custom-call | flops 5000000 | bytes 8000000 | tf_op jit(solution)/shard_map/own_share/pallas_call | solution.py:176
  6.3 1.2 %collective-permute-done.1.refs_3_ = bf16[16,2,448,128]{3,2,1,0:T(8,128)(2,1)} collective-permute-done((bf16[16,2,448,128]{3,2,1,0:T(8,128)(2,1)}, bf16[16,2,448,128]{3,2,1,0:T(8,128)(2,1)}, u32[]{:S(2)}, u32[]{:S(2)}) %collective-permute-start.1) | collective-permute-done | bytes 3670048 | tf_op jit(solution)/shard_map/ppermute | solution.py:428
  7.5 5.7 %join.1 = (bf16[2,240,128]{2,1,0:T(8,128)(2,1)S(1)}, bf16[2,240,128]{2,1,0:T(8,128)(2,1)S(1)}, bf16[2,240,128]{2,1,0:T(8,128)(2,1)S(1)}, bf16[2,240,128]{2,1,0:T...) custom-call(s32[1]{0:T(128)} %bitcast.place.refs_0_, ...), custom_call_target="tpu_custom_call" | custom-call | flops 5000000 | bytes 8000000 | tf_op jit(solution)/shard_map/join/pallas_call | solution.py:286
  13.1 4.5 %collective-permute-start.2 = (bf16[2,240,128]{2,1,0:T(8,128)(2,1)S(1)}, bf16[2,240,128]{2,1,0:T(8,128)(2,1)S(1)}, u32[]{:S(2)}, u32[]{:S(2)}) collective-permute-start(bf16[2,240,128]{2,1,0:T(8,128)(2,1)S(1)} %get-tuple-element.33), channel_id=1, source_target_pairs={{0,12},{1,13},{2,14},{3,15},{4,8},{5,9},{6,10},{7,11},{8,4},{9,5},... | collective-permute-start | bytes 368648 | tf_op jit(solution)/shard_map/ppermute | solution.py:434
  18.0 1.9 %collective-permute-start.5 = (bf16[2,240,128]{2,1,0:T(8,128)(2,1)S(1)}, bf16[2,240,128]{2,1,0:T(8,128)(2,1)S(1)}, u32[]{:S(2)}, u32[]{:S(2)}) collective-permute-start(bf16[2,240,128]{2,1,0:T(8,128)(2,1)S(1)} %get-tuple-element.36), channel_id=1, source_target_pairs={{0,5},{1,4},{2,7},{3,6},{4,1},{5,0},{6,3},{7,2},{8,13},{9,12},{10,... | collective-permute-start | bytes 368648 | tf_op jit(solution)/shard_map/ppermute | solution.py:434
  19.9 2.4 %collective-permute-start.6 = (bf16[2,240,128]{2,1,0:T(8,128)(2,1)S(1)}, bf16[2,240,128]{2,1,0:T(8,128)(2,1)S(1)}, u32[]{:S(2)}, u32[]{:S(2)}) collective-permute-start(bf16[2,240,128]{2,1,0:T(8,128)(2,1)S(1)} %get-tuple-element.37), channel_id=1, source_target_pairs={{0,13},{1,12},{2,15},{3,14},{4,9},{5,8},{6,11},{7,10},{8,5},{9,4},... | collective-permute-start | bytes 368648 | tf_op jit(solution)/shard_map/ppermute | solution.py:434
  22.3 1.4 %collective-permute-start.7 = (bf16[2,240,128]{2,1,0:T(8,128)(2,1)S(1)}, bf16[2,240,128]{2,1,0:T(8,128)(2,1)S(1)}, u32[]{:S(2)}, u32[]{:S(2)}) collective-permute-start(bf16[2,240,128]{2,1,0:T(8,128)(2,1)S(1)} %get-tuple-element.38), channel_id=1, source_target_pairs={{0,6},{1,7},{2,4},{3,5},{4,2},{5,3},{6,0},{7,1},{8,14},{9,15},{10,... | collective-permute-start | bytes 368648 | tf_op jit(solution)/shard_map/ppermute | solution.py:434
  23.7 1.4 %collective-permute-done.3.refs_2_ = bf16[2,240,128]{2,1,0:T(8,128)(2,1)S(1)} collective-permute-done((bf16[2,240,128]{2,1,0:T(8,128)(2,1)S(1)}, bf16[2,240,128]{2,1,0:T(8,128)(2,1)S(1)}, u32[]{:S(2)}, u32[]{:S(2)}) %collective-permute-start.3) | collective-permute-done | bytes 122912 | tf_op jit(solution)/shard_map/ppermute | solution.py:434
  25.1 2.3 %collective-permute-start.8 = (bf16[2,240,128]{2,1,0:T(8,128)(2,1)S(1)}, bf16[2,240,128]{2,1,0:T(8,128)(2,1)S(1)}, u32[]{:S(2)}, u32[]{:S(2)}) collective-permute-start(bf16[2,240,128]{2,1,0:T(8,128)(2,1)S(1)} %get-tuple-element.39), channel_id=1, source_target_pairs={{0,9},{1,8},{2,11},{3,10},{4,13},{5,12},{6,15},{7,14},{8,1},{9,0},... | collective-permute-start | bytes 368648 | tf_op jit(solution)/shard_map/ppermute | solution.py:434
  27.8 1.8 %collective-permute-start.9 = (bf16[2,240,128]{2,1,0:T(8,128)(2,1)S(1)}, bf16[2,240,128]{2,1,0:T(8,128)(2,1)S(1)}, u32[]{:S(2)}, u32[]{:S(2)}) collective-permute-start(bf16[2,240,128]{2,1,0:T(8,128)(2,1)S(1)} %get-tuple-element.40), channel_id=1, source_target_pairs={{0,7},{1,6},{2,5},{3,4},{4,3},{5,2},{6,1},{7,0},{8,15},{9,14},{10,... | collective-permute-start | bytes 368648 | tf_op jit(solution)/shard_map/ppermute | solution.py:434
  29.6 2.1 %collective-permute-done.5.refs_4_ = bf16[2,240,128]{2,1,0:T(8,128)(2,1)S(1)} collective-permute-done((bf16[2,240,128]{2,1,0:T(8,128)(2,1)S(1)}, bf16[2,240,128]{2,1,0:T(8,128)(2,1)S(1)}, u32[]{:S(2)}, u32[]{:S(2)}) %collective-permute-start.5) | collective-permute-done | bytes 122912 | tf_op jit(solution)/shard_map/ppermute | solution.py:434
  31.7 0.7 %collective-permute-start.10 = (bf16[2,240,128]{2,1,0:T(8,128)(2,1)S(1)}, bf16[2,240,128]{2,1,0:T(8,128)(2,1)S(1)}, u32[]{:S(2)}, u32[]{:S(2)}) collective-permute-start(bf16[2,240,128]{2,1,0:T(8,128)(2,1)S(1)} %get-tuple-element.41), channel_id=1, source_target_pairs={{0,14},{1,15},{2,12},{3,13},{4,10},{5,11},{6,8},{7,9},{8,6},{9,7},... | collective-permute-start | bytes 368648 | tf_op jit(solution)/shard_map/ppermute | solution.py:434
  32.4 0.6 collective-permute-start.11
  33.0 3.4 %collective-permute-done.7.refs_6_ = bf16[2,240,128]{2,1,0:T(8,128)(2,1)S(1)} collective-permute-done((bf16[2,240,128]{2,1,0:T(8,128)(2,1)S(1)}, bf16[2,240,128]{2,1,0:T(8,128)(2,1)S(1)}, u32[]{:S(2)}, u32[]{:S(2)}) %collective-permute-start.7) | collective-permute-done | bytes 122912 | tf_op jit(solution)/shard_map/ppermute | solution.py:434
  36.5 3.7 %collective-permute-done.8.refs_7_ = bf16[2,240,128]{2,1,0:T(8,128)(2,1)S(1)} collective-permute-done((bf16[2,240,128]{2,1,0:T(8,128)(2,1)S(1)}, bf16[2,240,128]{2,1,0:T(8,128)(2,1)S(1)}, u32[]{:S(2)}, u32[]{:S(2)}) %collective-permute-start.8) | collective-permute-done | bytes 122912 | tf_op jit(solution)/shard_map/ppermute | solution.py:434
  40.2 1.2 %collective-permute-start.13 = (bf16[2,240,128]{2,1,0:T(8,128)(2,1)S(1)}, bf16[2,240,128]{2,1,0:T(8,128)(2,1)S(1)}, u32[]{:S(2)}, u32[]{:S(2)}) collective-permute-start(bf16[2,240,128]{2,1,0:T(8,128)(2,1)S(1)} %get-tuple-element.44), channel_id=1, source_target_pairs={{0,2},{1,3},{2,0},{3,1},{4,6},{5,7},{6,4},{7,5},{8,10},{9,11},{10,... | collective-permute-start | bytes 368648 | tf_op jit(solution)/shard_map/ppermute | solution.py:434
  41.4 0.7 %collective-permute-start.14 = (bf16[2,240,128]{2,1,0:T(8,128)(2,1)S(1)}, bf16[2,240,128]{2,1,0:T(8,128)(2,1)S(1)}, u32[]{:S(2)}, u32[]{:S(2)}) collective-permute-start(bf16[2,240,128]{2,1,0:T(8,128)(2,1)S(1)} %get-tuple-element.45), channel_id=1, source_target_pairs={{0,15},{1,14},{2,13},{3,12},{4,11},{5,10},{6,9},{7,8},{8,7},{9,6},... | collective-permute-start | bytes 368648 | tf_op jit(solution)/shard_map/ppermute | solution.py:434
  42.1 0.9 %collective-permute-done.10.refs_9_ = bf16[2,240,128]{2,1,0:T(8,128)(2,1)S(1)} collective-permute-done((bf16[2,240,128]{2,1,0:T(8,128)(2,1)S(1)}, bf16[2,240,128]{2,1,0:T(8,128)(2,1)S(1)}, u32[]{:S(2)}, u32[]{:S(2)}) %collective-permute-start.10) | collective-permute-done | bytes 122912 | tf_op jit(solution)/shard_map/ppermute | solution.py:434
  43.0 1.8 %collective-permute-start.15 = (bf16[2,240,128]{2,1,0:T(8,128)(2,1)S(1)}, bf16[2,240,128]{2,1,0:T(8,128)(2,1)S(1)}, u32[]{:S(2)}, u32[]{:S(2)}) collective-permute-start(bf16[2,240,128]{2,1,0:T(8,128)(2,1)S(1)} %get-tuple-element.46), channel_id=1, source_target_pairs={{0,3},{1,2},{2,1},{3,0},{4,7},{5,6},{6,5},{7,4},{8,11},{9,10},{10,... | collective-permute-start | bytes 368648 | tf_op jit(solution)/shard_map/ppermute | solution.py:434
  44.8 7.9 %collective-permute-start.16 = (bf16[2,240,128]{2,1,0:T(8,128)(2,1)S(1)}, bf16[2,240,128]{2,1,0:T(8,128)(2,1)S(1)}, u32[]{:S(2)}, u32[]{:S(2)}) collective-permute-start(bf16[2,240,128]{2,1,0:T(8,128)(2,1)S(1)} %get-tuple-element.47), channel_id=1, source_target_pairs={{0,11},{1,10},{2,9},{3,8},{4,15},{5,14},{6,13},{7,12},{8,3},{9,2},... | collective-permute-start | bytes 368648 | tf_op jit(solution)/shard_map/ppermute | solution.py:434
  52.8 1.3 %collective-permute-done.15.refs_14_ = bf16[2,240,128]{2,1,0:T(8,128)(2,1)S(1)} collective-permute-done((bf16[2,240,128]{2,1,0:T(8,128)(2,1)S(1)}, bf16[2,240,128]{2,1,0:T(8,128)(2,1)S(1)}, u32[]{:S(2)}, u32[]{:S(2)}) %collective-permute-start.15) | collective-permute-done | bytes 122912 | tf_op jit(solution)/shard_map/ppermute | solution.py:434
  54.1 6.8 %collective-permute-done.16.refs_15_ = bf16[2,240,128]{2,1,0:T(8,128)(2,1)S(1)} collective-permute-done((bf16[2,240,128]{2,1,0:T(8,128)(2,1)S(1)}, bf16[2,240,128]{2,1,0:T(8,128)(2,1)S(1)}, u32[]{:S(2)}, u32[]{:S(2)}) %collective-permute-start.16) | collective-permute-done | bytes 122912 | tf_op jit(solution)/shard_map/ppermute | solution.py:434
  60.9 5.1 %score.1 = (bf16[4,56,512]{2,1,0:T(8,128)(2,1)}, bf16[2,4,56,512]{3,2,1,0:T(8,128)(2,1)}) custom-call(s32[1]{0:T(128)} %bitcast.place.refs_0_, bf16[2,240,128]{2,1,0:T(8,128)(2,1)S(1)} %get-tuple-element.32.refs_0_, bf16[2,240,128]{2,1,0:T(8,128)(2,1)S(1)} %collective-permute-done.2.refs_1_, bf16[2,240,128]{2,1,0:T(8,128)(2,1)S(1)} %collective-permute-done.3.refs_2_, ...), custom_call_target="tpu_custom_call" | custom-call | tf_op jit(solution)/shard_map/score/pallas_call | solution.py:395
  (22 shorter events, 1.7 us)
Async XLA Ops:
  0.6 5.3 %copy-start.1 = (f32[32,896]{1,0:T(8,128)S(1)}, f32[32,896]{1,0:T(8,128)}, u32[]{:S(2)}) copy-start(f32[32,896]{1,0:T(8,128)} %smoothing.1) | copy-start | bytes 344068
  0.6 6.8 %collective-permute-start.1 = (bf16[16,2,448,128]{3,2,1,0:T(8,128)(2,1)}, bf16[16,2,448,128]{3,2,1,0:T(8,128)(2,1)}, u32[]{:S(2)}, u32[]{:S(2)}) collective-permute-start(bf16[16,2,448,128]{3,2,1,0:T(8,128)(2,1)} %bitcast.14), channel_id=1, source_target_pairs={{0,1},{1,0},{2,3},{3,2},{4,5},{5,4},{6,7},{7,6},{8,9},{9,8},{10,11... | collective-permute-start | bytes 11010056 | tf_op jit(solution)/shard_map/ppermute | solution.py:428
  0.8 5.5 %collective-permute-start = (s32[3,2,16]{2,1,0:T(2,128)}, s32[3,2,16]{2,1,0:T(2,128)S(1)}, u32[]{:S(2)}, u32[]{:S(2)}) collective-permute-start(s32[3,2,16]{2,1,0:T(2,128)} %bitcast.11), channel_id=1, source_target_pairs={{0,1},{1,0},{2,3},{3,2},{4,5},{5,4},{6,7},{7,6},{8,9},{9,8},{10,11... | collective-permute-start | bytes 1160 | tf_op jit(solution)/shard_map/ppermute | solution.py:429
  1.2 0.7 %copy-start.2 = (s32[16,2,3]{0,1,2:T(2,128)S(1)}, s32[16,2,3]{0,1,2:T(2,128)}, u32[]{:S(2)}) copy-start(s32[16,2,3]{0,1,2:T(2,128)} %param.6) | copy-start | bytes 1156
  1.9 5.6 %copy-start.3 = (s32[16,2,3]{0,1,2:T(2,128)S(1)}, s32[16,2,3]{0,1,2:T(2,128)}, u32[]{:S(2)}) copy-start(s32[16,2,3]{0,1,2:T(2,128)} %param.6) | copy-start | bytes 1156
  7.5 53.4 %copy-start = (bf16[4,512,56]{1,2,0:T(8,128)(2,1)S(1)}, bf16[4,512,56]{1,2,0:T(8,128)(2,1)}, u32[]{:S(2)}) copy-start(bf16[4,512,56]{1,2,0:T(8,128)(2,1)} %param.9) | copy-start | bytes 688132
  13.1 9.2 %collective-permute-start.2 = (bf16[2,240,128]{2,1,0:T(8,128)(2,1)S(1)}, bf16[2,240,128]{2,1,0:T(8,128)(2,1)S(1)}, u32[]{:S(2)}, u32[]{:S(2)}) collective-permute-start(bf16[2,240,128]{2,1,0:T(8,128)(2,1)S(1)} %get-tuple-element.33), channel_id=1, source_target_pairs={{0,12},{1,13},{2,14},{3,15},{4,8},{5,9},{6,10},{7,11},{8,4},{9,5},... | collective-permute-start | bytes 368648 | tf_op jit(solution)/shard_map/ppermute | solution.py:434
  17.7 7.5 %collective-permute-start.3 = (bf16[2,240,128]{2,1,0:T(8,128)(2,1)S(1)}, bf16[2,240,128]{2,1,0:T(8,128)(2,1)S(1)}, u32[]{:S(2)}, u32[]{:S(2)}) collective-permute-start(bf16[2,240,128]{2,1,0:T(8,128)(2,1)S(1)} %get-tuple-element.34), channel_id=1, source_target_pairs={{0,4},{1,5},{2,6},{3,7},{4,0},{5,1},{6,2},{7,3},{8,12},{9,13},{10,... | collective-permute-start | bytes 368648 | tf_op jit(solution)/shard_map/ppermute | solution.py:434
  17.7 10.1 %collective-permute-start.4 = (bf16[2,240,128]{2,1,0:T(8,128)(2,1)S(1)}, bf16[2,240,128]{2,1,0:T(8,128)(2,1)S(1)}, u32[]{:S(2)}, u32[]{:S(2)}) collective-permute-start(bf16[2,240,128]{2,1,0:T(8,128)(2,1)S(1)} %get-tuple-element.35), channel_id=1, source_target_pairs={{0,8},{1,9},{2,10},{3,11},{4,12},{5,13},{6,14},{7,15},{8,0},{9,1},... | collective-permute-start | bytes 368648 | tf_op jit(solution)/shard_map/ppermute | solution.py:434
  18.0 13.7 %collective-permute-start.5 = (bf16[2,240,128]{2,1,0:T(8,128)(2,1)S(1)}, bf16[2,240,128]{2,1,0:T(8,128)(2,1)S(1)}, u32[]{:S(2)}, u32[]{:S(2)}) collective-permute-start(bf16[2,240,128]{2,1,0:T(8,128)(2,1)S(1)} %get-tuple-element.36), channel_id=1, source_target_pairs={{0,5},{1,4},{2,7},{3,6},{4,1},{5,0},{6,3},{7,2},{8,13},{9,12},{10,... | collective-permute-start | bytes 368648 | tf_op jit(solution)/shard_map/ppermute | solution.py:434
  19.9 12.5 %collective-permute-start.6 = (bf16[2,240,128]{2,1,0:T(8,128)(2,1)S(1)}, bf16[2,240,128]{2,1,0:T(8,128)(2,1)S(1)}, u32[]{:S(2)}, u32[]{:S(2)}) collective-permute-start(bf16[2,240,128]{2,1,0:T(8,128)(2,1)S(1)} %get-tuple-element.37), channel_id=1, source_target_pairs={{0,13},{1,12},{2,15},{3,14},{4,9},{5,8},{6,11},{7,10},{8,5},{9,4},... | collective-permute-start | bytes 368648 | tf_op jit(solution)/shard_map/ppermute | solution.py:434
  22.3 14.1 %collective-permute-start.7 = (bf16[2,240,128]{2,1,0:T(8,128)(2,1)S(1)}, bf16[2,240,128]{2,1,0:T(8,128)(2,1)S(1)}, u32[]{:S(2)}, u32[]{:S(2)}) collective-permute-start(bf16[2,240,128]{2,1,0:T(8,128)(2,1)S(1)} %get-tuple-element.38), channel_id=1, source_target_pairs={{0,6},{1,7},{2,4},{3,5},{4,2},{5,3},{6,0},{7,1},{8,14},{9,15},{10,... | collective-permute-start | bytes 368648 | tf_op jit(solution)/shard_map/ppermute | solution.py:434
  25.1 15.1 %collective-permute-start.8 = (bf16[2,240,128]{2,1,0:T(8,128)(2,1)S(1)}, bf16[2,240,128]{2,1,0:T(8,128)(2,1)S(1)}, u32[]{:S(2)}, u32[]{:S(2)}) collective-permute-start(bf16[2,240,128]{2,1,0:T(8,128)(2,1)S(1)} %get-tuple-element.39), channel_id=1, source_target_pairs={{0,9},{1,8},{2,11},{3,10},{4,13},{5,12},{6,15},{7,14},{8,1},{9,0},... | collective-permute-start | bytes 368648 | tf_op jit(solution)/shard_map/ppermute | solution.py:434
  27.8 13.6 %collective-permute-start.9 = (bf16[2,240,128]{2,1,0:T(8,128)(2,1)S(1)}, bf16[2,240,128]{2,1,0:T(8,128)(2,1)S(1)}, u32[]{:S(2)}, u32[]{:S(2)}) collective-permute-start(bf16[2,240,128]{2,1,0:T(8,128)(2,1)S(1)} %get-tuple-element.40), channel_id=1, source_target_pairs={{0,7},{1,6},{2,5},{3,4},{4,3},{5,2},{6,1},{7,0},{8,15},{9,14},{10,... | collective-permute-start | bytes 368648 | tf_op jit(solution)/shard_map/ppermute | solution.py:434
  31.7 11.3 %collective-permute-start.10 = (bf16[2,240,128]{2,1,0:T(8,128)(2,1)S(1)}, bf16[2,240,128]{2,1,0:T(8,128)(2,1)S(1)}, u32[]{:S(2)}, u32[]{:S(2)}) collective-permute-start(bf16[2,240,128]{2,1,0:T(8,128)(2,1)S(1)} %get-tuple-element.41), channel_id=1, source_target_pairs={{0,14},{1,15},{2,12},{3,13},{4,10},{5,11},{6,8},{7,9},{8,6},{9,7},... | collective-permute-start | bytes 368648 | tf_op jit(solution)/shard_map/ppermute | solution.py:434
  32.4 12.4 %collective-permute-start.11 = (bf16[2,240,128]{2,1,0:T(8,128)(2,1)S(1)}, bf16[2,240,128]{2,1,0:T(8,128)(2,1)S(1)}, u32[]{:S(2)}, u32[]{:S(2)}) collective-permute-start(bf16[2,240,128]{2,1,0:T(8,128)(2,1)S(1)} %get-tuple-element.42), channel_id=1, source_target_pairs={{0,1},{1,0},{2,3},{3,2},{4,5},{5,4},{6,7},{7,6},{8,9},{9,8},{10,11... | collective-permute-start | bytes 368648 | tf_op jit(solution)/shard_map/ppermute | solution.py:434
  36.4 16.3 %collective-permute-start.12 = (bf16[2,240,128]{2,1,0:T(8,128)(2,1)S(1)}, bf16[2,240,128]{2,1,0:T(8,128)(2,1)S(1)}, u32[]{:S(2)}, u32[]{:S(2)}) collective-permute-start(bf16[2,240,128]{2,1,0:T(8,128)(2,1)S(1)} %get-tuple-element.43), channel_id=1, source_target_pairs={{0,10},{1,11},{2,8},{3,9},{4,14},{5,15},{6,12},{7,13},{8,2},{9,3},... | collective-permute-start | bytes 368648 | tf_op jit(solution)/shard_map/ppermute | solution.py:434
  40.2 12.6 %collective-permute-start.13 = (bf16[2,240,128]{2,1,0:T(8,128)(2,1)S(1)}, bf16[2,240,128]{2,1,0:T(8,128)(2,1)S(1)}, u32[]{:S(2)}, u32[]{:S(2)}) collective-permute-start(bf16[2,240,128]{2,1,0:T(8,128)(2,1)S(1)} %get-tuple-element.44), channel_id=1, source_target_pairs={{0,2},{1,3},{2,0},{3,1},{4,6},{5,7},{6,4},{7,5},{8,10},{9,11},{10,... | collective-permute-start | bytes 368648 | tf_op jit(solution)/shard_map/ppermute | solution.py:434
  41.4 11.4 %collective-permute-start.14 = (bf16[2,240,128]{2,1,0:T(8,128)(2,1)S(1)}, bf16[2,240,128]{2,1,0:T(8,128)(2,1)S(1)}, u32[]{:S(2)}, u32[]{:S(2)}) collective-permute-start(bf16[2,240,128]{2,1,0:T(8,128)(2,1)S(1)} %get-tuple-element.45), channel_id=1, source_target_pairs={{0,15},{1,14},{2,13},{3,12},{4,11},{5,10},{6,9},{7,8},{8,7},{9,6},... | collective-permute-start | bytes 368648 | tf_op jit(solution)/shard_map/ppermute | solution.py:434
  43.0 11.1 %collective-permute-start.15 = (bf16[2,240,128]{2,1,0:T(8,128)(2,1)S(1)}, bf16[2,240,128]{2,1,0:T(8,128)(2,1)S(1)}, u32[]{:S(2)}, u32[]{:S(2)}) collective-permute-start(bf16[2,240,128]{2,1,0:T(8,128)(2,1)S(1)} %get-tuple-element.46), channel_id=1, source_target_pairs={{0,3},{1,2},{2,1},{3,0},{4,7},{5,6},{6,5},{7,4},{8,11},{9,10},{10,... | collective-permute-start | bytes 368648 | tf_op jit(solution)/shard_map/ppermute | solution.py:434
  44.8 16.1 %collective-permute-start.16 = (bf16[2,240,128]{2,1,0:T(8,128)(2,1)S(1)}, bf16[2,240,128]{2,1,0:T(8,128)(2,1)S(1)}, u32[]{:S(2)}, u32[]{:S(2)}) collective-permute-start(bf16[2,240,128]{2,1,0:T(8,128)(2,1)S(1)} %get-tuple-element.47), channel_id=1, source_target_pairs={{0,11},{1,10},{2,9},{3,8},{4,15},{5,14},{6,13},{7,12},{8,3},{9,2},... | collective-permute-start | bytes 368648 | tf_op jit(solution)/shard_map/ppermute | solution.py:434

commit v9 on v8

--- a/solution.py
+++ b/solution.py
@@ -108,14 +108,22 @@
     return [[sums[parity, t + 1] for t in range(TILES)] for parity in range(2)]
 
 
-def either_kind(z, heavy, body):
-    @pl.when(heavy)
-    def _():
-        body(False, range(CAP))
-
-    @pl.when(jnp.logical_not(heavy))
-    def _():
-        body(z.makers == 2, range(1))
+def each_region(z, heavy, body):
+    for i in range(QUAD):
+        if z.makers == 2:
+            body(i, True, range(1))
+        else:
+            pl.when(jnp.logical_not(heavy(i)))(functools.partial(body, i, False, range(1)))
+
+    def again(i, carry):
+        pl.when(heavy(i))(functools.partial(body, i, False, range(CAP)))
+        return carry
+
+    lax.fori_loop(0, QUAD, again, 0)
+
+
+def staged_index(i, side, maker, slot, others):
+    return i * others + maker if side else QUAD * others + maker * CAP + slot
 
 
 def own_kernel(z, place, lists, tiles, table_hbm, *refs):
@@ -140,20 +148,24 @@
                     low : low + count, at : at + LANES
                 ]
 
-    def region(j, carry):
-        fetch(j).wait()
-
-        def body(side, slots):
+    def group(quad, carry):
+        for i in range(QUAD):
+            fetch(quad * QUAD + i).wait()
+
+        def body(i, side, slots):
+            j = quad * QUAD + i
+
             def weight_item(slot):
                 column, kind = (lists[entry, slot, first + j] for entry in (1, 2))
                 return functools.partial(weight_tile, weights, kind), column
 
             def field_item(field, slot):
                 weight, column = weight_item(slot)
-                return lambda t: staged_tile(staged.at[slot], field, t) * weight(t), column
+                own = staged.at[staged_index(i, side, 0, slot, 1)]
+                return lambda t: staged_tile(own, field, t) * weight(t), column
 
             for slot in slots:
-                stage(staged.at[slot], landed[j, slot])
+                stage(staged.at[staged_index(i, side, 0, slot, 1)], landed[j, slot])
             for index in range(FIELDS + 1):
                 items = [field_item(index, slot) if index < FIELDS else weight_item(slot) for slot in slots]
                 pieces = place_all(side, sums.at[index], items)
@@ -162,10 +174,10 @@
                     for t in range(TILES):
                         target[j, parity, t] = pieces[parity][t]
 
-        either_kind(z, lists[0, 1, first + j] >= 0, body)
+        each_region(z, lambda i: lists[0, 1, first + quad * QUAD + i] >= 0, body)
         return carry
 
-    lax.fori_loop(0, z.block, region, 0)
+    lax.fori_loop(0, z.quads, group, 0)
 
 
 def own_share(z, place, lists, tiles, table):
@@ -183,7 +195,7 @@
         out_specs=[vmem] * (FIELDS + 2),
         scratch_shapes=[
             pltpu.VMEM((z.block, CAP, LINES, LANES), jnp.bfloat16),
-            pltpu.VMEM((CAP, LINES, LANES), jnp.float32),
+            pltpu.VMEM((QUAD + CAP, LINES, LANES), jnp.float32),
             pltpu.VMEM((FIELDS + 1, 2, SLOTS, PAIRS, LANES), jnp.float32),
             pltpu.VMEM(table.shape, jnp.float32),
             pltpu.SemaphoreType.DMA((z.block + 1,)),
@@ -226,37 +238,34 @@
 
     for quad in range(z.quads):
 
-        def region(i, carry):
+        def body(i, side, slots):
             j = quad * QUAD + i
-
-            def body(side, slots):
-                sources = [(maker, slot) for maker in range(1, z.makers) for slot in slots]
-
-                def weight_item(maker, slot):
-                    column, kind = (lists[maker][entry, slot, first + j] for entry in (1, 2))
-                    return functools.partial(weight_tile, weights, kind), column
-
-                def field_item(field, maker, slot):
-                    weight, column = weight_item(maker, slot)
-                    return lambda t: staged_tile(staged.at[(maker - 1) * CAP + slot], field, t) * weight(t), column
-
-                for maker, slot in sources:
-                    stage(staged.at[(maker - 1) * CAP + slot], received[maker - 1][first + j, slot])
-                others = place_all(side, sums.at[FIELDS], [weight_item(*source) for source in sources])
-                inverse = [[1.0 / (total[j, parity, t] + others[parity][t]) for t in range(TILES)] for parity in range(2)]
-                for field in range(FIELDS):
-                    pieces = place_all(side, sums.at[field], [field_item(field, *source) for source in sources])
-                    for parity in range(2):
-                        for t in range(TILES):
-                            lines[field, t, pl.ds(ROWS * i + parity, PAIRS, stride=2), :] = (
-                                half[field][j, parity, t] + pieces[parity][t]
-                            ) * inverse[parity][t]
-
-            either_kind(z, lists[0][0, 1, first + j] >= 0, body)
-            return carry
-
-        lax.fori_loop(0, QUAD, region, 0)
-
+            sources = [(maker, slot) for maker in range(1, z.makers) for slot in slots]
+
+            def staged_of(maker, slot):
+                return staged.at[staged_index(i, side, maker - 1, slot, z.makers - 1)]
+
+            def weight_item(maker, slot):
+                column, kind = (lists[maker][entry, slot, first + j] for entry in (1, 2))
+                return functools.partial(weight_tile, weights, kind), column
+
+            def field_item(field, maker, slot):
+                weight, column = weight_item(maker, slot)
+                return lambda t: staged_tile(staged_of(maker, slot), field, t) * weight(t), column
+
+            for maker, slot in sources:
+                stage(staged_of(maker, slot), received[maker - 1][first + j, slot])
+            others = place_all(side, sums.at[FIELDS], [weight_item(*source) for source in sources])
+            inverse = [[1.0 / (total[j, parity, t] + others[parity][t]) for t in range(TILES)] for parity in range(2)]
+            for field in range(FIELDS):
+                pieces = place_all(side, sums.at[field], [field_item(field, *source) for source in sources])
+                for parity in range(2):
+                    for t in range(TILES):
+                        lines[field, t, pl.ds(ROWS * i + parity, PAIRS, stride=2), :] = (
+                            half[field][j, parity, t] + pieces[parity][t]
+                        ) * inverse[parity][t]
+
+        each_region(z, lambda i: lists[0][0, 1, first + quad * QUAD + i] >= 0, body)
         for field in range(FIELDS):
             for t in range(TILES):
                 turned[field, LANES * t : LANES * (t + 1), :] = lax.dot_general(
@@ -289,7 +298,7 @@
         in_specs=[smem] * (1 + z.makers) + [vmem] * (z.makers - 1 + len(shares)),
         out_specs=[vmem] * z.regions,
         scratch_shapes=[
-            pltpu.VMEM((CAP * (z.makers - 1), LINES, LANES), jnp.float32),
+            pltpu.VMEM(((QUAD + CAP) * (z.makers - 1), LINES, LANES), jnp.float32),
             pltpu.VMEM((FIELDS + 1, 2, SLOTS, PAIRS, LANES), jnp.float32),
             pltpu.VMEM((FIELDS, TILES, LANES, LANES), jnp.float32),
             pltpu.VMEM((FIELDS, COLS + 8, LANES), jnp.float32),

time: 66.1 us -> 66.2 us (level)
  starting transfers between devices: 28.3 us -> 27.5 us
  waiting for transfers between devices: 21.2 us -> 22 us
    ppermute x15, waiting for transfers between devices: 20 us -> 20.9 us  [shards(): lax.ppermute(block, 'region', [(i, i ^ offset) for i in range(z.regions)])]
    ppermute x15, starting transfers between devices: 27.7 us -> 26.9 us  [shards(): lax.ppermute(block, 'region', [(i, i ^ offset) for i in range(z.regions)])]
  transfers between devices with their start and end apart: 17 -> 17, of which waited for: 9 -> 11; matrix products, arithmetic and copies ran while one was open for 0% -> 0% of each run, Pallas kernels for 7% -> 7%
where the time goes in v9:
time: 66.2 us; the launch traced here: 66.1 us
  starting transfers between devices  27.5 us (42%)
  waiting for transfers between devices  22 us (33%)
  Pallas kernels  15.3 us (23%)
  local copies, waits for them, and re-layouts  0.7 us (1%)
  between operations  0.7 us (1%)
    ppermute x15, starting transfers between devices, shards(): lax.ppermute(block, 'region', [(i, i ^ offset) for i in range(z.regions)])  26.9 us
    ppermute x15, waiting for transfers between devices, shards(): lax.ppermute(block, 'region', [(i, i ^ offset) for i in range(z.regions)])  20.9 us
    pallas_call x1, Pallas kernels, join(): pl.pallas_call(functools.partial(join_kernel, z), out_shape=[jax.ShapeDty...  5.67 us
    pallas_call x1, Pallas kernels, score(): pl.pallas_call(functools.partial(score_kernel, z), out_shape=[jax.ShapeDt...  5.09 us
    pallas_call x1, Pallas kernels, own_share(): pl.pallas_call(functools.partial(own_kernel, z), out_shape=[*[jax.ShapeDt...  4.22 us
  transfers between devices with their start and end apart: 17, of which 11 were waited for; matrix products, arithmetic and copies ran while one was open for 0% of the time, Pallas kernels for 7%

profile of v9, /device:TPU:1, one launch (start us, length us, event | category | flops | bytes accessed | tf_op | source)
XLA Modules:
  0.0 66.1 jit_solution(15882178970918469587)
XLA Ops:
  1.2 0.7 %copy-done.2 = s32[16,2,3]{0,1,2:T(2,128)S(1)} copy-done((s32[16,2,3]{0,1,2:T(2,128)S(1)}, s32[16,2,3]{0,1,2:T(2,128)}, u32[]{:S(2)}) %copy-start.2) | copy-done | bytes 408
  1.9 4.2 %own_share.1 = (f32[8,2,7,16,128]{4,3,2,1,0:T(8,128)S(1)}, f32[8,2,7,16,128]{4,3,2,1,0:T(8,128)S(1)}, f32[8,2,7,16,128]{4,3,2,1,0:T(8,128)S(1)}, f32[8,2,7,16,12...) custom-call(s32[1]{0:T(128)} %bitcast.place.refs_0_, s32[3,2,16]{2,1,0:T(2,128)S(1)} %bitcast.12, ...), custom_call_target="tpu_custom_call" | custom-call | flops 5000000 | bytes 8000000 | tf_op jit(solution)/shard_map/own_share/pallas_call | solution.py:188
  6.4 1.0 %collective-permute-done.1.refs_3_ = bf16[16,2,448,128]{3,2,1,0:T(8,128)(2,1)} collective-permute-done((bf16[16,2,448,128]{3,2,1,0:T(8,128)(2,1)}, bf16[16,2,448,128]{3,2,1,0:T(8,128)(2,1)}, u32[]{:S(2)}, u32[]{:S(2)}) %collective-permute-start.1) | collective-permute-done | bytes 3670048 | tf_op jit(solution)/shard_map/ppermute | solution.py:437
  7.5 5.7 %join.1 = (bf16[2,240,128]{2,1,0:T(8,128)(2,1)S(1)}, bf16[2,240,128]{2,1,0:T(8,128)(2,1)S(1)}, bf16[2,240,128]{2,1,0:T(8,128)(2,1)S(1)}, bf16[2,240,128]{2,1,0:T...) custom-call(s32[1]{0:T(128)} %bitcast.place.refs_0_, ...), custom_call_target="tpu_custom_call" | custom-call | flops 5000000 | bytes 8000000 | tf_op jit(solution)/shard_map/join/pallas_call | solution.py:295
  13.1 4.5 %collective-permute-start.2 = (bf16[2,240,128]{2,1,0:T(8,128)(2,1)S(1)}, bf16[2,240,128]{2,1,0:T(8,128)(2,1)S(1)}, u32[]{:S(2)}, u32[]{:S(2)}) collective-permute-start(bf16[2,240,128]{2,1,0:T(8,128)(2,1)S(1)} %get-tuple-element.33), channel_id=1, source_target_pairs={{0,12},{1,13},{2,14},{3,15},{4,8},{5,9},{6,10},{7,11},{8,4},{9,5},... | collective-permute-start | bytes 368648 | tf_op jit(solution)/shard_map/ppermute | solution.py:443
  18.0 1.3 %collective-permute-start.5 = (bf16[2,240,128]{2,1,0:T(8,128)(2,1)S(1)}, bf16[2,240,128]{2,1,0:T(8,128)(2,1)S(1)}, u32[]{:S(2)}, u32[]{:S(2)}) collective-permute-start(bf16[2,240,128]{2,1,0:T(8,128)(2,1)S(1)} %get-tuple-element.36), channel_id=1, source_target_pairs={{0,5},{1,4},{2,7},{3,6},{4,1},{5,0},{6,3},{7,2},{8,13},{9,12},{10,... | collective-permute-start | bytes 368648 | tf_op jit(solution)/shard_map/ppermute | solution.py:443
  19.4 2.4 %collective-permute-start.6 = (bf16[2,240,128]{2,1,0:T(8,128)(2,1)S(1)}, bf16[2,240,128]{2,1,0:T(8,128)(2,1)S(1)}, u32[]{:S(2)}, u32[]{:S(2)}) collective-permute-start(bf16[2,240,128]{2,1,0:T(8,128)(2,1)S(1)} %get-tuple-element.37), channel_id=1, source_target_pairs={{0,13},{1,12},{2,15},{3,14},{4,9},{5,8},{6,11},{7,10},{8,5},{9,4},... | collective-permute-start | bytes 368648 | tf_op jit(solution)/shard_map/ppermute | solution.py:443
  21.7 2.6 %collective-permute-start.7 = (bf16[2,240,128]{2,1,0:T(8,128)(2,1)S(1)}, bf16[2,240,128]{2,1,0:T(8,128)(2,1)S(1)}, u32[]{:S(2)}, u32[]{:S(2)}) collective-permute-start(bf16[2,240,128]{2,1,0:T(8,128)(2,1)S(1)} %get-tuple-element.38), channel_id=1, source_target_pairs={{0,6},{1,7},{2,4},{3,5},{4,2},{5,3},{6,0},{7,1},{8,14},{9,15},{10,... | collective-permute-start | bytes 368648 | tf_op jit(solution)/shard_map/ppermute | solution.py:443
  24.3 0.8 %collective-permute-done.3.refs_2_ = bf16[2,240,128]{2,1,0:T(8,128)(2,1)S(1)} collective-permute-done((bf16[2,240,128]{2,1,0:T(8,128)(2,1)S(1)}, bf16[2,240,128]{2,1,0:T(8,128)(2,1)S(1)}, u32[]{:S(2)}, u32[]{:S(2)}) %collective-permute-start.3) | collective-permute-done | bytes 122912 | tf_op jit(solution)/shard_map/ppermute | solution.py:443
  25.1 1.7 %collective-permute-start.8 = (bf16[2,240,128]{2,1,0:T(8,128)(2,1)S(1)}, bf16[2,240,128]{2,1,0:T(8,128)(2,1)S(1)}, u32[]{:S(2)}, u32[]{:S(2)}) collective-permute-start(bf16[2,240,128]{2,1,0:T(8,128)(2,1)S(1)} %get-tuple-element.39), channel_id=1, source_target_pairs={{0,9},{1,8},{2,11},{3,10},{4,13},{5,12},{6,15},{7,14},{8,1},{9,0},... | collective-permute-start | bytes 368648 | tf_op jit(solution)/shard_map/ppermute | solution.py:443
  26.9 1.5 %collective-permute-done.4.refs_3_ = bf16[2,240,128]{2,1,0:T(8,128)(2,1)S(1)} collective-permute-done((bf16[2,240,128]{2,1,0:T(8,128)(2,1)S(1)}, bf16[2,240,128]{2,1,0:T(8,128)(2,1)S(1)}, u32[]{:S(2)}, u32[]{:S(2)}) %collective-permute-start.4) | collective-permute-done | bytes 122912 | tf_op jit(solution)/shard_map/ppermute | solution.py:443
  28.4 0.9 %collective-permute-start.9 = (bf16[2,240,128]{2,1,0:T(8,128)(2,1)S(1)}, bf16[2,240,128]{2,1,0:T(8,128)(2,1)S(1)}, u32[]{:S(2)}, u32[]{:S(2)}) collective-permute-start(bf16[2,240,128]{2,1,0:T(8,128)(2,1)S(1)} %get-tuple-element.40), channel_id=1, source_target_pairs={{0,7},{1,6},{2,5},{3,4},{4,3},{5,2},{6,1},{7,0},{8,15},{9,14},{10,... | collective-permute-start | bytes 368648 | tf_op jit(solution)/shard_map/ppermute | solution.py:443
  29.6 2.6 %collective-permute-start.10 = (bf16[2,240,128]{2,1,0:T(8,128)(2,1)S(1)}, bf16[2,240,128]{2,1,0:T(8,128)(2,1)S(1)}, u32[]{:S(2)}, u32[]{:S(2)}) collective-permute-start(bf16[2,240,128]{2,1,0:T(8,128)(2,1)S(1)} %get-tuple-element.41), channel_id=1, source_target_pairs={{0,14},{1,15},{2,12},{3,13},{4,10},{5,11},{6,8},{7,9},{8,6},{9,7},... | collective-permute-start | bytes 368648 | tf_op jit(solution)/shard_map/ppermute | solution.py:443
  32.7 4.1 %collective-permute-done.7.refs_6_ = bf16[2,240,128]{2,1,0:T(8,128)(2,1)S(1)} collective-permute-done((bf16[2,240,128]{2,1,0:T(8,128)(2,1)S(1)}, bf16[2,240,128]{2,1,0:T(8,128)(2,1)S(1)}, u32[]{:S(2)}, u32[]{:S(2)}) %collective-permute-start.7) | collective-permute-done | bytes 122912 | tf_op jit(solution)/shard_map/ppermute | solution.py:443
  36.7 2.7 %collective-permute-done.8.refs_7_ = bf16[2,240,128]{2,1,0:T(8,128)(2,1)S(1)} collective-permute-done((bf16[2,240,128]{2,1,0:T(8,128)(2,1)S(1)}, bf16[2,240,128]{2,1,0:T(8,128)(2,1)S(1)}, u32[]{:S(2)}, u32[]{:S(2)}) %collective-permute-start.8) | collective-permute-done | bytes 122912 | tf_op jit(solution)/shard_map/ppermute | solution.py:443
  39.5 1.2 %collective-permute-start.13 = (bf16[2,240,128]{2,1,0:T(8,128)(2,1)S(1)}, bf16[2,240,128]{2,1,0:T(8,128)(2,1)S(1)}, u32[]{:S(2)}, u32[]{:S(2)}) collective-permute-start(bf16[2,240,128]{2,1,0:T(8,128)(2,1)S(1)} %get-tuple-element.44), channel_id=1, source_target_pairs={{0,2},{1,3},{2,0},{3,1},{4,6},{5,7},{6,4},{7,5},{8,10},{9,11},{10,... | collective-permute-start | bytes 368648 | tf_op jit(solution)/shard_map/ppermute | solution.py:443
  41.0 1.9 %collective-permute-start.14 = (bf16[2,240,128]{2,1,0:T(8,128)(2,1)S(1)}, bf16[2,240,128]{2,1,0:T(8,128)(2,1)S(1)}, u32[]{:S(2)}, u32[]{:S(2)}) collective-permute-start(bf16[2,240,128]{2,1,0:T(8,128)(2,1)S(1)} %get-tuple-element.45), channel_id=1, source_target_pairs={{0,15},{1,14},{2,13},{3,12},{4,11},{5,10},{6,9},{7,8},{8,7},{9,6},... | collective-permute-start | bytes 368648 | tf_op jit(solution)/shard_map/ppermute | solution.py:443
  42.9 0.7 collective-permute-done.10.refs_9_
  43.6 1.2 %collective-permute-start.15 = (bf16[2,240,128]{2,1,0:T(8,128)(2,1)S(1)}, bf16[2,240,128]{2,1,0:T(8,128)(2,1)S(1)}, u32[]{:S(2)}, u32[]{:S(2)}) collective-permute-start(bf16[2,240,128]{2,1,0:T(8,128)(2,1)S(1)} %get-tuple-element.46), channel_id=1, source_target_pairs={{0,3},{1,2},{2,1},{3,0},{4,7},{5,6},{6,5},{7,4},{8,11},{9,10},{10,... | collective-permute-start | bytes 368648 | tf_op jit(solution)/shard_map/ppermute | solution.py:443
  44.7 5.7 %collective-permute-start.16 = (bf16[2,240,128]{2,1,0:T(8,128)(2,1)S(1)}, bf16[2,240,128]{2,1,0:T(8,128)(2,1)S(1)}, u32[]{:S(2)}, u32[]{:S(2)}) collective-permute-start(bf16[2,240,128]{2,1,0:T(8,128)(2,1)S(1)} %get-tuple-element.47), channel_id=1, source_target_pairs={{0,11},{1,10},{2,9},{3,8},{4,15},{5,14},{6,13},{7,12},{8,3},{9,2},... | collective-permute-start | bytes 368648 | tf_op jit(solution)/shard_map/ppermute | solution.py:443
  50.5 2.6 %collective-permute-done.12.refs_11_ = bf16[2,240,128]{2,1,0:T(8,128)(2,1)S(1)} collective-permute-done((bf16[2,240,128]{2,1,0:T(8,128)(2,1)S(1)}, bf16[2,240,128]{2,1,0:T(8,128)(2,1)S(1)}, u32[]{:S(2)}, u32[]{:S(2)}) %collective-permute-start.12) | collective-permute-done | bytes 122912 | tf_op jit(solution)/shard_map/ppermute | solution.py:443
  53.1 1.5 %collective-permute-done.15.refs_14_ = bf16[2,240,128]{2,1,0:T(8,128)(2,1)S(1)} collective-permute-done((bf16[2,240,128]{2,1,0:T(8,128)(2,1)S(1)}, bf16[2,240,128]{2,1,0:T(8,128)(2,1)S(1)}, u32[]{:S(2)}, u32[]{:S(2)}) %collective-permute-start.15) | collective-permute-done | bytes 122912 | tf_op jit(solution)/shard_map/ppermute | solution.py:443
  54.6 6.4 %collective-permute-done.16.refs_15_ = bf16[2,240,128]{2,1,0:T(8,128)(2,1)S(1)} collective-permute-done((bf16[2,240,128]{2,1,0:T(8,128)(2,1)S(1)}, bf16[2,240,128]{2,1,0:T(8,128)(2,1)S(1)}, u32[]{:S(2)}, u32[]{:S(2)}) %collective-permute-start.16) | collective-permute-done | bytes 122912 | tf_op jit(solution)/shard_map/ppermute | solution.py:443
  61.0 5.1 %score.1 = (bf16[4,56,512]{2,1,0:T(8,128)(2,1)}, bf16[2,4,56,512]{3,2,1,0:T(8,128)(2,1)}) custom-call(s32[1]{0:T(128)} %bitcast.place.refs_0_, bf16[2,240,128]{2,1,0:T(8,128)(2,1)S(1)} %get-tuple-element.32.refs_0_, bf16[2,240,128]{2,1,0:T(8,128)(2,1)S(1)} %collective-permute-done.2.refs_1_, bf16[2,240,128]{2,1,0:T(8,128)(2,1)S(1)} %collective-permute-done.3.refs_2_, ...), custom_call_target="tpu_custom_call" | custom-call | tf_op jit(solution)/shard_map/score/pallas_call | solution.py:404
  (22 shorter events, 2.3 us)
Async XLA Ops:
  0.6 5.5 %copy-start.1 = (f32[32,896]{1,0:T(8,128)S(1)}, f32[32,896]{1,0:T(8,128)}, u32[]{:S(2)}) copy-start(f32[32,896]{1,0:T(8,128)} %smoothing.1) | copy-start | bytes 344068
  0.6 6.8 %collective-permute-start.1 = (bf16[16,2,448,128]{3,2,1,0:T(8,128)(2,1)}, bf16[16,2,448,128]{3,2,1,0:T(8,128)(2,1)}, u32[]{:S(2)}, u32[]{:S(2)}) collective-permute-start(bf16[16,2,448,128]{3,2,1,0:T(8,128)(2,1)} %bitcast.14), channel_id=1, source_target_pairs={{0,1},{1,0},{2,3},{3,2},{4,5},{5,4},{6,7},{7,6},{8,9},{9,8},{10,11... | collective-permute-start | bytes 11010056 | tf_op jit(solution)/shard_map/ppermute | solution.py:437
  0.8 5.7 %collective-permute-start = (s32[3,2,16]{2,1,0:T(2,128)}, s32[3,2,16]{2,1,0:T(2,128)S(1)}, u32[]{:S(2)}, u32[]{:S(2)}) collective-permute-start(s32[3,2,16]{2,1,0:T(2,128)} %bitcast.11), channel_id=1, source_target_pairs={{0,1},{1,0},{2,3},{3,2},{4,5},{5,4},{6,7},{7,6},{8,9},{9,8},{10,11... | collective-permute-start | bytes 1160 | tf_op jit(solution)/shard_map/ppermute | solution.py:438
  1.2 0.7 %copy-start.2 = (s32[16,2,3]{0,1,2:T(2,128)S(1)}, s32[16,2,3]{0,1,2:T(2,128)}, u32[]{:S(2)}) copy-start(s32[16,2,3]{0,1,2:T(2,128)} %param.6) | copy-start | bytes 1156
  1.9 5.6 %copy-start.3 = (s32[16,2,3]{0,1,2:T(2,128)S(1)}, s32[16,2,3]{0,1,2:T(2,128)}, u32[]{:S(2)}) copy-start(s32[16,2,3]{0,1,2:T(2,128)} %param.6) | copy-start | bytes 1156
  7.5 53.6 %copy-start = (bf16[4,512,56]{1,2,0:T(8,128)(2,1)S(1)}, bf16[4,512,56]{1,2,0:T(8,128)(2,1)}, u32[]{:S(2)}) copy-start(bf16[4,512,56]{1,2,0:T(8,128)(2,1)} %param.9) | copy-start | bytes 688132
  13.1 8.6 %collective-permute-start.2 = (bf16[2,240,128]{2,1,0:T(8,128)(2,1)S(1)}, bf16[2,240,128]{2,1,0:T(8,128)(2,1)S(1)}, u32[]{:S(2)}, u32[]{:S(2)}) collective-permute-start(bf16[2,240,128]{2,1,0:T(8,128)(2,1)S(1)} %get-tuple-element.33), channel_id=1, source_target_pairs={{0,12},{1,13},{2,14},{3,15},{4,8},{5,9},{6,10},{7,11},{8,4},{9,5},... | collective-permute-start | bytes 368648 | tf_op jit(solution)/shard_map/ppermute | solution.py:443
  17.7 7.5 %collective-permute-start.3 = (bf16[2,240,128]{2,1,0:T(8,128)(2,1)S(1)}, bf16[2,240,128]{2,1,0:T(8,128)(2,1)S(1)}, u32[]{:S(2)}, u32[]{:S(2)}) collective-permute-start(bf16[2,240,128]{2,1,0:T(8,128)(2,1)S(1)} %get-tuple-element.34), channel_id=1, source_target_pairs={{0,4},{1,5},{2,6},{3,7},{4,0},{5,1},{6,2},{7,3},{8,12},{9,13},{10,... | collective-permute-start | bytes 368648 | tf_op jit(solution)/shard_map/ppermute | solution.py:443
  17.7 10.7 %collective-permute-start.4 = (bf16[2,240,128]{2,1,0:T(8,128)(2,1)S(1)}, bf16[2,240,128]{2,1,0:T(8,128)(2,1)S(1)}, u32[]{:S(2)}, u32[]{:S(2)}) collective-permute-start(bf16[2,240,128]{2,1,0:T(8,128)(2,1)S(1)} %get-tuple-element.35), channel_id=1, source_target_pairs={{0,8},{1,9},{2,10},{3,11},{4,12},{5,13},{6,14},{7,15},{8,0},{9,1},... | collective-permute-start | bytes 368648 | tf_op jit(solution)/shard_map/ppermute | solution.py:443
  18.0 11.6 %collective-permute-start.5 = (bf16[2,240,128]{2,1,0:T(8,128)(2,1)S(1)}, bf16[2,240,128]{2,1,0:T(8,128)(2,1)S(1)}, u32[]{:S(2)}, u32[]{:S(2)}) collective-permute-start(bf16[2,240,128]{2,1,0:T(8,128)(2,1)S(1)} %get-tuple-element.36), channel_id=1, source_target_pairs={{0,5},{1,4},{2,7},{3,6},{4,1},{5,0},{6,3},{7,2},{8,13},{9,12},{10,... | collective-permute-start | bytes 368648 | tf_op jit(solution)/shard_map/ppermute | solution.py:443
  19.4 12.9 %collective-permute-start.6 = (bf16[2,240,128]{2,1,0:T(8,128)(2,1)S(1)}, bf16[2,240,128]{2,1,0:T(8,128)(2,1)S(1)}, u32[]{:S(2)}, u32[]{:S(2)}) collective-permute-start(bf16[2,240,128]{2,1,0:T(8,128)(2,1)S(1)} %get-tuple-element.37), channel_id=1, source_target_pairs={{0,13},{1,12},{2,15},{3,14},{4,9},{5,8},{6,11},{7,10},{8,5},{9,4},... | collective-permute-start | bytes 368648 | tf_op jit(solution)/shard_map/ppermute | solution.py:443
  21.7 15.0 %collective-permute-start.7 = (bf16[2,240,128]{2,1,0:T(8,128)(2,1)S(1)}, bf16[2,240,128]{2,1,0:T(8,128)(2,1)S(1)}, u32[]{:S(2)}, u32[]{:S(2)}) collective-permute-start(bf16[2,240,128]{2,1,0:T(8,128)(2,1)S(1)} %get-tuple-element.38), channel_id=1, source_target_pairs={{0,6},{1,7},{2,4},{3,5},{4,2},{5,3},{6,0},{7,1},{8,14},{9,15},{10,... | collective-permute-start | bytes 368648 | tf_op jit(solution)/shard_map/ppermute | solution.py:443
  25.1 14.3 %collective-permute-start.8 = (bf16[2,240,128]{2,1,0:T(8,128)(2,1)S(1)}, bf16[2,240,128]{2,1,0:T(8,128)(2,1)S(1)}, u32[]{:S(2)}, u32[]{:S(2)}) collective-permute-start(bf16[2,240,128]{2,1,0:T(8,128)(2,1)S(1)} %get-tuple-element.39), channel_id=1, source_target_pairs={{0,9},{1,8},{2,11},{3,10},{4,13},{5,12},{6,15},{7,14},{8,1},{9,0},... | collective-permute-start | bytes 368648 | tf_op jit(solution)/shard_map/ppermute | solution.py:443
  28.4 12.6 %collective-permute-start.9 = (bf16[2,240,128]{2,1,0:T(8,128)(2,1)S(1)}, bf16[2,240,128]{2,1,0:T(8,128)(2,1)S(1)}, u32[]{:S(2)}, u32[]{:S(2)}) collective-permute-start(bf16[2,240,128]{2,1,0:T(8,128)(2,1)S(1)} %get-tuple-element.40), channel_id=1, source_target_pairs={{0,7},{1,6},{2,5},{3,4},{4,3},{5,2},{6,1},{7,0},{8,15},{9,14},{10,... | collective-permute-start | bytes 368648 | tf_op jit(solution)/shard_map/ppermute | solution.py:443
  29.6 14.0 %collective-permute-start.10 = (bf16[2,240,128]{2,1,0:T(8,128)(2,1)S(1)}, bf16[2,240,128]{2,1,0:T(8,128)(2,1)S(1)}, u32[]{:S(2)}, u32[]{:S(2)}) collective-permute-start(bf16[2,240,128]{2,1,0:T(8,128)(2,1)S(1)} %get-tuple-element.41), channel_id=1, source_target_pairs={{0,14},{1,15},{2,12},{3,13},{4,10},{5,11},{6,8},{7,9},{8,6},{9,7},... | collective-permute-start | bytes 368648 | tf_op jit(solution)/shard_map/ppermute | solution.py:443
  32.2 12.5 %collective-permute-start.11 = (bf16[2,240,128]{2,1,0:T(8,128)(2,1)S(1)}, bf16[2,240,128]{2,1,0:T(8,128)(2,1)S(1)}, u32[]{:S(2)}, u32[]{:S(2)}) collective-permute-start(bf16[2,240,128]{2,1,0:T(8,128)(2,1)S(1)} %get-tuple-element.42), channel_id=1, source_target_pairs={{0,1},{1,0},{2,3},{3,2},{4,5},{5,4},{6,7},{7,6},{8,9},{9,8},{10,11... | collective-permute-start | bytes 368648 | tf_op jit(solution)/shard_map/ppermute | solution.py:443
  36.7 16.3 %collective-permute-start.12 = (bf16[2,240,128]{2,1,0:T(8,128)(2,1)S(1)}, bf16[2,240,128]{2,1,0:T(8,128)(2,1)S(1)}, u32[]{:S(2)}, u32[]{:S(2)}) collective-permute-start(bf16[2,240,128]{2,1,0:T(8,128)(2,1)S(1)} %get-tuple-element.43), channel_id=1, source_target_pairs={{0,10},{1,11},{2,8},{3,9},{4,14},{5,15},{6,12},{7,13},{8,2},{9,3},... | collective-permute-start | bytes 368648 | tf_op jit(solution)/shard_map/ppermute | solution.py:443
  39.5 13.6 %collective-permute-start.13 = (bf16[2,240,128]{2,1,0:T(8,128)(2,1)S(1)}, bf16[2,240,128]{2,1,0:T(8,128)(2,1)S(1)}, u32[]{:S(2)}, u32[]{:S(2)}) collective-permute-start(bf16[2,240,128]{2,1,0:T(8,128)(2,1)S(1)} %get-tuple-element.44), channel_id=1, source_target_pairs={{0,2},{1,3},{2,0},{3,1},{4,6},{5,7},{6,4},{7,5},{8,10},{9,11},{10,... | collective-permute-start | bytes 368648 | tf_op jit(solution)/shard_map/ppermute | solution.py:443
  41.0 12.0 %collective-permute-start.14 = (bf16[2,240,128]{2,1,0:T(8,128)(2,1)S(1)}, bf16[2,240,128]{2,1,0:T(8,128)(2,1)S(1)}, u32[]{:S(2)}, u32[]{:S(2)}) collective-permute-start(bf16[2,240,128]{2,1,0:T(8,128)(2,1)S(1)} %get-tuple-element.45), channel_id=1, source_target_pairs={{0,15},{1,14},{2,13},{3,12},{4,11},{5,10},{6,9},{7,8},{8,7},{9,6},... | collective-permute-start | bytes 368648 | tf_op jit(solution)/shard_map/ppermute | solution.py:443
  43.6 11.0 %collective-permute-start.15 = (bf16[2,240,128]{2,1,0:T(8,128)(2,1)S(1)}, bf16[2,240,128]{2,1,0:T(8,128)(2,1)S(1)}, u32[]{:S(2)}, u32[]{:S(2)}) collective-permute-start(bf16[2,240,128]{2,1,0:T(8,128)(2,1)S(1)} %get-tuple-element.46), channel_id=1, source_target_pairs={{0,3},{1,2},{2,1},{3,0},{4,7},{5,6},{6,5},{7,4},{8,11},{9,10},{10,... | collective-permute-start | bytes 368648 | tf_op jit(solution)/shard_map/ppermute | solution.py:443
  44.7 16.3 %collective-permute-start.16 = (bf16[2,240,128]{2,1,0:T(8,128)(2,1)S(1)}, bf16[2,240,128]{2,1,0:T(8,128)(2,1)S(1)}, u32[]{:S(2)}, u32[]{:S(2)}) collective-permute-start(bf16[2,240,128]{2,1,0:T(8,128)(2,1)S(1)} %get-tuple-element.47), channel_id=1, source_target_pairs={{0,11},{1,10},{2,9},{3,8},{4,15},{5,14},{6,13},{7,12},{8,3},{9,2},... | collective-permute-start | bytes 368648 | tf_op jit(solution)/shard_map/ppermute | solution.py:443

commit v10 on v9

--- a/solution.py
+++ b/solution.py
@@ -229,8 +229,8 @@
 def join_kernel(z, *refs):
     place, lists, refs = refs[0], refs[1 : 1 + z.makers], refs[1 + z.makers :]
     received, refs = refs[: z.makers - 1], refs[z.makers - 1 :]
-    half, (total, weights, strength), outs = refs[:FIELDS], refs[FIELDS : FIELDS + 3], refs[FIELDS + 3 : -4]
-    staged, sums, lines, turned = refs[-4:]
+    half, (total, weights, strength), outs = refs[:FIELDS], refs[FIELDS : FIELDS + 3], refs[FIELDS + 3 : -5]
+    staged, sums, lines, turned, edges = refs[-5:]
     me = place[0]
     first = lax.rem(me, z.makers) * z.block
     row, column = (lax.broadcasted_iota(jnp.int32, (LANES, LANES), axis) for axis in (0, 1))
@@ -266,26 +266,32 @@
                         ) * inverse[parity][t]
 
         each_region(z, lambda i: lists[0][0, 1, first + quad * QUAD + i] >= 0, body)
-        for field in range(FIELDS):
-            for t in range(TILES):
-                turned[field, LANES * t : LANES * (t + 1), :] = lax.dot_general(
-                    identity,
-                    lines[field, t].astype(jnp.bfloat16),
-                    (((1,), (1,)), ((), ())),
-                    preferred_element_type=jnp.float32,
-                )
-        for out, offset in zip(outs, z.offsets):
+        for t in range(TILES):
+            for field in range(FIELDS):
+                here = slice(LANES * t, LANES * (t + 1))
+                if field % 2:
+                    turned[field, here, :] = jnp.transpose(lines[field, t])
+                else:
+                    turned[field, here, :] = lax.dot_general(
+                        identity,
+                        lines[field, t].astype(jnp.bfloat16),
+                        (((1,), (1,)), ((), ())),
+                        preferred_element_type=jnp.float32,
+                    )
+        for i, (out, offset) in enumerate(zip(outs, z.offsets)):
             dest = me ^ offset
             top = dest * z.width
             if z.width % 8 == 0:
                 top = pl.multiple_of(top, 8)
+            ends = (jnp.maximum(top - 1, 0), jnp.minimum(top + z.width, COLS - 1))
+            for field in range(FIELDS):
+                for side, end in enumerate(ends):
+                    edges[i, 2 * field + side : 2 * field + side + 1, :] = turned[field, pl.ds(end, 1), :]
             for low in range(0, FIELDS, 2):
                 block = [turned[field, pl.ds(top, z.span), :] for field in (low, low + 1)]
                 out[quad, low * z.span : (low + 2) * z.span, :] = jnp.concatenate(block, 0).astype(jnp.bfloat16)
-            ends = (jnp.maximum(top - 1, 0), jnp.minimum(top + z.width, COLS - 1))
-            edge = [turned[field, pl.ds(end, 1), :] for field in range(FIELDS) for end in ends]
-            edge.append(strength[dest, quad])
-            out[quad, z.main : z.sent, :] = jnp.concatenate(edge, 0).astype(jnp.bfloat16)
+            tail = jnp.concatenate([edges[i], strength[dest, quad]], 0)
+            out[quad, z.main : z.sent, :] = tail.astype(jnp.bfloat16)
 
 
 def join(z, place, lists, received, shares):
@@ -302,6 +308,7 @@
             pltpu.VMEM((FIELDS + 1, 2, SLOTS, PAIRS, LANES), jnp.float32),
             pltpu.VMEM((FIELDS, TILES, LANES, LANES), jnp.float32),
             pltpu.VMEM((FIELDS, COLS + 8, LANES), jnp.float32),
+            pltpu.VMEM((z.regions, 8, LANES), jnp.float32),
         ],
         compiler_params=pltpu.CompilerParams(vmem_limit_bytes=VMEM),
         cost_estimate=pl.CostEstimate(flops=5_000_000, bytes_accessed=8_000_000, transcendentals=0),

time: 66.2 us -> 65.3 us (0.986)
  Pallas kernels: 15.3 us -> 14.3 us
  starting transfers between devices: 27.5 us -> 28.4 us
  waiting for transfers between devices: 22 us -> 21.3 us
    ppermute x15, waiting for transfers between devices: 20.9 us -> 19.9 us  [shards(): lax.ppermute(block, 'region', [(i, i ^ offset) for i in range(z.regions)])]
    ppermute x15, starting transfers between devices: 26.9 us -> 27.8 us  [shards(): lax.ppermute(block, 'region', [(i, i ^ offset) for i in range(z.regions)])]
    pallas_call x1, Pallas kernels: 5.67 us -> 5 us  [join(): pl.pallas_call(functools.partial(join_kernel, z), out_shape=[jax.ShapeDty...]
  transfers between devices with their start and end apart: 17 -> 17, of which waited for: 11 -> 10; matrix products, arithmetic and copies ran while one was open for 0% -> 0% of each run, Pallas kernels for 7% -> 6%
where the time goes in v10:
time: 65.3 us
  starting transfers between devices  28.4 us (43%)
  waiting for transfers between devices  21.3 us (33%)
  Pallas kernels  14.3 us (22%)
  local copies, waits for them, and re-layouts  0.7 us (1%)
  between operations  0.69 us (1%)
    ppermute x15, starting transfers between devices, shards(): lax.ppermute(block, 'region', [(i, i ^ offset) for i in range(z.regions)])  27.8 us
    ppermute x15, waiting for transfers between devices, shards(): lax.ppermute(block, 'region', [(i, i ^ offset) for i in range(z.regions)])  19.9 us
    pallas_call x1, Pallas kernels, score(): pl.pallas_call(functools.partial(score_kernel, z), out_shape=[jax.ShapeDt...  5.09 us
    pallas_call x1, Pallas kernels, join(): pl.pallas_call(functools.partial(join_kernel, z), out_shape=[jax.ShapeDty...  5 us
    pallas_call x1, Pallas kernels, own_share(): pl.pallas_call(functools.partial(own_kernel, z), out_shape=[*[jax.ShapeDt...  3.92 us
  transfers between devices with their start and end apart: 17, of which 10 were waited for; matrix products, arithmetic and copies ran while one was open for 0% of the time, Pallas kernels for 6%

profile of v10, /device:TPU:1, one launch (start us, length us, event | category | flops | bytes accessed | tf_op | source)
XLA Modules:
  0.0 65.3 jit_solution(13737405344948827747)
XLA Ops:
  1.2 0.7 %copy-done.2 = s32[16,2,3]{0,1,2:T(2,128)S(1)} copy-done((s32[16,2,3]{0,1,2:T(2,128)S(1)}, s32[16,2,3]{0,1,2:T(2,128)}, u32[]{:S(2)}) %copy-start.2) | copy-done | bytes 408
  1.9 3.9 %own_share.1 = (f32[8,2,7,16,128]{4,3,2,1,0:T(8,128)S(1)}, f32[8,2,7,16,128]{4,3,2,1,0:T(8,128)S(1)}, f32[8,2,7,16,128]{4,3,2,1,0:T(8,128)S(1)}, f32[8,2,7,16,12...) custom-call(s32[1]{0:T(128)} %bitcast.place.refs_0_, s32[3,2,16]{2,1,0:T(2,128)S(1)} %bitcast.12, ...), custom_call_target="tpu_custom_call" | custom-call | flops 5000000 | bytes 8000000 | tf_op jit(solution)/shard_map/own_share/pallas_call | solution.py:188
  6.3 1.2 %collective-permute-done.1.refs_3_ = bf16[16,2,448,128]{3,2,1,0:T(8,128)(2,1)} collective-permute-done((bf16[16,2,448,128]{3,2,1,0:T(8,128)(2,1)}, bf16[16,2,448,128]{3,2,1,0:T(8,128)(2,1)}, u32[]{:S(2)}, u32[]{:S(2)}) %collective-permute-start.1) | collective-permute-done | bytes 3670048 | tf_op jit(solution)/shard_map/ppermute | solution.py:444
  7.5 5.0 %join.1 = (bf16[2,240,128]{2,1,0:T(8,128)(2,1)S(1)}, bf16[2,240,128]{2,1,0:T(8,128)(2,1)S(1)}, bf16[2,240,128]{2,1,0:T(8,128)(2,1)S(1)}, bf16[2,240,128]{2,1,0:T...) custom-call(s32[1]{0:T(128)} %bitcast.place.refs_0_, ...), custom_call_target="tpu_custom_call" | custom-call | flops 5000000 | bytes 8000000 | tf_op jit(solution)/shard_map/join/pallas_call | solution.py:301
  12.5 4.5 %collective-permute-start.2 = (bf16[2,240,128]{2,1,0:T(8,128)(2,1)S(1)}, bf16[2,240,128]{2,1,0:T(8,128)(2,1)S(1)}, u32[]{:S(2)}, u32[]{:S(2)}) collective-permute-start(bf16[2,240,128]{2,1,0:T(8,128)(2,1)S(1)} %get-tuple-element.33), channel_id=1, source_target_pairs={{0,12},{1,13},{2,14},{3,15},{4,8},{5,9},{6,10},{7,11},{8,4},{9,5},... | collective-permute-start | bytes 368648 | tf_op jit(solution)/shard_map/ppermute | solution.py:450
  17.4 1.9 %collective-permute-start.5 = (bf16[2,240,128]{2,1,0:T(8,128)(2,1)S(1)}, bf16[2,240,128]{2,1,0:T(8,128)(2,1)S(1)}, u32[]{:S(2)}, u32[]{:S(2)}) collective-permute-start(bf16[2,240,128]{2,1,0:T(8,128)(2,1)S(1)} %get-tuple-element.36), channel_id=1, source_target_pairs={{0,5},{1,4},{2,7},{3,6},{4,1},{5,0},{6,3},{7,2},{8,13},{9,12},{10,... | collective-permute-start | bytes 368648 | tf_op jit(solution)/shard_map/ppermute | solution.py:450
  19.3 2.4 %collective-permute-start.6 = (bf16[2,240,128]{2,1,0:T(8,128)(2,1)S(1)}, bf16[2,240,128]{2,1,0:T(8,128)(2,1)S(1)}, u32[]{:S(2)}, u32[]{:S(2)}) collective-permute-start(bf16[2,240,128]{2,1,0:T(8,128)(2,1)S(1)} %get-tuple-element.37), channel_id=1, source_target_pairs={{0,13},{1,12},{2,15},{3,14},{4,9},{5,8},{6,11},{7,10},{8,5},{9,4},... | collective-permute-start | bytes 368648 | tf_op jit(solution)/shard_map/ppermute | solution.py:450
  21.7 1.4 %collective-permute-start.7 = (bf16[2,240,128]{2,1,0:T(8,128)(2,1)S(1)}, bf16[2,240,128]{2,1,0:T(8,128)(2,1)S(1)}, u32[]{:S(2)}, u32[]{:S(2)}) collective-permute-start(bf16[2,240,128]{2,1,0:T(8,128)(2,1)S(1)} %get-tuple-element.38), channel_id=1, source_target_pairs={{0,6},{1,7},{2,4},{3,5},{4,2},{5,3},{6,0},{7,1},{8,14},{9,15},{10,... | collective-permute-start | bytes 368648 | tf_op jit(solution)/shard_map/ppermute | solution.py:450
  23.1 1.4 %collective-permute-done.3.refs_2_ = bf16[2,240,128]{2,1,0:T(8,128)(2,1)S(1)} collective-permute-done((bf16[2,240,128]{2,1,0:T(8,128)(2,1)S(1)}, bf16[2,240,128]{2,1,0:T(8,128)(2,1)S(1)}, u32[]{:S(2)}, u32[]{:S(2)}) %collective-permute-start.3) | collective-permute-done | bytes 122912 | tf_op jit(solution)/shard_map/ppermute | solution.py:450
  24.5 2.4 %collective-permute-start.8 = (bf16[2,240,128]{2,1,0:T(8,128)(2,1)S(1)}, bf16[2,240,128]{2,1,0:T(8,128)(2,1)S(1)}, u32[]{:S(2)}, u32[]{:S(2)}) collective-permute-start(bf16[2,240,128]{2,1,0:T(8,128)(2,1)S(1)} %get-tuple-element.39), channel_id=1, source_target_pairs={{0,9},{1,8},{2,11},{3,10},{4,13},{5,12},{6,15},{7,14},{8,1},{9,0},... | collective-permute-start | bytes 368648 | tf_op jit(solution)/shard_map/ppermute | solution.py:450
  27.1 1.9 %collective-permute-start.9 = (bf16[2,240,128]{2,1,0:T(8,128)(2,1)S(1)}, bf16[2,240,128]{2,1,0:T(8,128)(2,1)S(1)}, u32[]{:S(2)}, u32[]{:S(2)}) collective-permute-start(bf16[2,240,128]{2,1,0:T(8,128)(2,1)S(1)} %get-tuple-element.40), channel_id=1, source_target_pairs={{0,7},{1,6},{2,5},{3,4},{4,3},{5,2},{6,1},{7,0},{8,15},{9,14},{10,... | collective-permute-start | bytes 368648 | tf_op jit(solution)/shard_map/ppermute | solution.py:450
  29.0 2.1 %collective-permute-done.5.refs_4_ = bf16[2,240,128]{2,1,0:T(8,128)(2,1)S(1)} collective-permute-done((bf16[2,240,128]{2,1,0:T(8,128)(2,1)S(1)}, bf16[2,240,128]{2,1,0:T(8,128)(2,1)S(1)}, u32[]{:S(2)}, u32[]{:S(2)}) %collective-permute-start.5) | collective-permute-done | bytes 122912 | tf_op jit(solution)/shard_map/ppermute | solution.py:450
  31.0 0.7 %collective-permute-start.10 = (bf16[2,240,128]{2,1,0:T(8,128)(2,1)S(1)}, bf16[2,240,128]{2,1,0:T(8,128)(2,1)S(1)}, u32[]{:S(2)}, u32[]{:S(2)}) collective-permute-start(bf16[2,240,128]{2,1,0:T(8,128)(2,1)S(1)} %get-tuple-element.41), channel_id=1, source_target_pairs={{0,14},{1,15},{2,12},{3,13},{4,10},{5,11},{6,8},{7,9},{8,6},{9,7},... | collective-permute-start | bytes 368648 | tf_op jit(solution)/shard_map/ppermute | solution.py:450
  31.8 0.6 collective-permute-start.11
  32.3 3.4 %collective-permute-done.7.refs_6_ = bf16[2,240,128]{2,1,0:T(8,128)(2,1)S(1)} collective-permute-done((bf16[2,240,128]{2,1,0:T(8,128)(2,1)S(1)}, bf16[2,240,128]{2,1,0:T(8,128)(2,1)S(1)}, u32[]{:S(2)}, u32[]{:S(2)}) %collective-permute-start.7) | collective-permute-done | bytes 122912 | tf_op jit(solution)/shard_map/ppermute | solution.py:450
  35.9 3.7 %collective-permute-done.8.refs_7_ = bf16[2,240,128]{2,1,0:T(8,128)(2,1)S(1)} collective-permute-done((bf16[2,240,128]{2,1,0:T(8,128)(2,1)S(1)}, bf16[2,240,128]{2,1,0:T(8,128)(2,1)S(1)}, u32[]{:S(2)}, u32[]{:S(2)}) %collective-permute-start.8) | collective-permute-done | bytes 122912 | tf_op jit(solution)/shard_map/ppermute | solution.py:450
  39.6 1.2 %collective-permute-start.13 = (bf16[2,240,128]{2,1,0:T(8,128)(2,1)S(1)}, bf16[2,240,128]{2,1,0:T(8,128)(2,1)S(1)}, u32[]{:S(2)}, u32[]{:S(2)}) collective-permute-start(bf16[2,240,128]{2,1,0:T(8,128)(2,1)S(1)} %get-tuple-element.44), channel_id=1, source_target_pairs={{0,2},{1,3},{2,0},{3,1},{4,6},{5,7},{6,4},{7,5},{8,10},{9,11},{10,... | collective-permute-start | bytes 368648 | tf_op jit(solution)/shard_map/ppermute | solution.py:450
  40.8 0.7 %collective-permute-start.14 = (bf16[2,240,128]{2,1,0:T(8,128)(2,1)S(1)}, bf16[2,240,128]{2,1,0:T(8,128)(2,1)S(1)}, u32[]{:S(2)}, u32[]{:S(2)}) collective-permute-start(bf16[2,240,128]{2,1,0:T(8,128)(2,1)S(1)} %get-tuple-element.45), channel_id=1, source_target_pairs={{0,15},{1,14},{2,13},{3,12},{4,11},{5,10},{6,9},{7,8},{8,7},{9,6},... | collective-permute-start | bytes 368648 | tf_op jit(solution)/shard_map/ppermute | solution.py:450
  41.5 0.9 %collective-permute-done.10.refs_9_ = bf16[2,240,128]{2,1,0:T(8,128)(2,1)S(1)} collective-permute-done((bf16[2,240,128]{2,1,0:T(8,128)(2,1)S(1)}, bf16[2,240,128]{2,1,0:T(8,128)(2,1)S(1)}, u32[]{:S(2)}, u32[]{:S(2)}) %collective-permute-start.10) | collective-permute-done | bytes 122912 | tf_op jit(solution)/shard_map/ppermute | solution.py:450
  42.4 1.8 %collective-permute-start.15 = (bf16[2,240,128]{2,1,0:T(8,128)(2,1)S(1)}, bf16[2,240,128]{2,1,0:T(8,128)(2,1)S(1)}, u32[]{:S(2)}, u32[]{:S(2)}) collective-permute-start(bf16[2,240,128]{2,1,0:T(8,128)(2,1)S(1)} %get-tuple-element.46), channel_id=1, source_target_pairs={{0,3},{1,2},{2,1},{3,0},{4,7},{5,6},{6,5},{7,4},{8,11},{9,10},{10,... | collective-permute-start | bytes 368648 | tf_op jit(solution)/shard_map/ppermute | solution.py:450
  44.2 7.9 %collective-permute-start.16 = (bf16[2,240,128]{2,1,0:T(8,128)(2,1)S(1)}, bf16[2,240,128]{2,1,0:T(8,128)(2,1)S(1)}, u32[]{:S(2)}, u32[]{:S(2)}) collective-permute-start(bf16[2,240,128]{2,1,0:T(8,128)(2,1)S(1)} %get-tuple-element.47), channel_id=1, source_target_pairs={{0,11},{1,10},{2,9},{3,8},{4,15},{5,14},{6,13},{7,12},{8,3},{9,2},... | collective-permute-start | bytes 368648 | tf_op jit(solution)/shard_map/ppermute | solution.py:450
  52.1 1.3 %collective-permute-done.15.refs_14_ = bf16[2,240,128]{2,1,0:T(8,128)(2,1)S(1)} collective-permute-done((bf16[2,240,128]{2,1,0:T(8,128)(2,1)S(1)}, bf16[2,240,128]{2,1,0:T(8,128)(2,1)S(1)}, u32[]{:S(2)}, u32[]{:S(2)}) %collective-permute-start.15) | collective-permute-done | bytes 122912 | tf_op jit(solution)/shard_map/ppermute | solution.py:450
  53.5 6.8 %collective-permute-done.16.refs_15_ = bf16[2,240,128]{2,1,0:T(8,128)(2,1)S(1)} collective-permute-done((bf16[2,240,128]{2,1,0:T(8,128)(2,1)S(1)}, bf16[2,240,128]{2,1,0:T(8,128)(2,1)S(1)}, u32[]{:S(2)}, u32[]{:S(2)}) %collective-permute-start.16) | collective-permute-done | bytes 122912 | tf_op jit(solution)/shard_map/ppermute | solution.py:450
  60.2 5.1 %score.1 = (bf16[4,56,512]{2,1,0:T(8,128)(2,1)}, bf16[2,4,56,512]{3,2,1,0:T(8,128)(2,1)}) custom-call(s32[1]{0:T(128)} %bitcast.place.refs_0_, bf16[2,240,128]{2,1,0:T(8,128)(2,1)S(1)} %get-tuple-element.32.refs_0_, bf16[2,240,128]{2,1,0:T(8,128)(2,1)S(1)} %collective-permute-done.2.refs_1_, bf16[2,240,128]{2,1,0:T(8,128)(2,1)S(1)} %collective-permute-done.3.refs_2_, ...), custom_call_target="tpu_custom_call" | custom-call | tf_op jit(solution)/shard_map/score/pallas_call | solution.py:411
  (22 shorter events, 1.8 us)
Async XLA Ops:
  0.6 5.2 %copy-start.1 = (f32[32,896]{1,0:T(8,128)S(1)}, f32[32,896]{1,0:T(8,128)}, u32[]{:S(2)}) copy-start(f32[32,896]{1,0:T(8,128)} %smoothing.1) | copy-start | bytes 344068
  0.6 6.8 %collective-permute-start.1 = (bf16[16,2,448,128]{3,2,1,0:T(8,128)(2,1)}, bf16[16,2,448,128]{3,2,1,0:T(8,128)(2,1)}, u32[]{:S(2)}, u32[]{:S(2)}) collective-permute-start(bf16[16,2,448,128]{3,2,1,0:T(8,128)(2,1)} %bitcast.14), channel_id=1, source_target_pairs={{0,1},{1,0},{2,3},{3,2},{4,5},{5,4},{6,7},{7,6},{8,9},{9,8},{10,11... | collective-permute-start | bytes 11010056 | tf_op jit(solution)/shard_map/ppermute | solution.py:444
  0.8 5.5 %collective-permute-start = (s32[3,2,16]{2,1,0:T(2,128)}, s32[3,2,16]{2,1,0:T(2,128)S(1)}, u32[]{:S(2)}, u32[]{:S(2)}) collective-permute-start(s32[3,2,16]{2,1,0:T(2,128)} %bitcast.11), channel_id=1, source_target_pairs={{0,1},{1,0},{2,3},{3,2},{4,5},{5,4},{6,7},{7,6},{8,9},{9,8},{10,11... | collective-permute-start | bytes 1160 | tf_op jit(solution)/shard_map/ppermute | solution.py:445
  1.2 0.7 %copy-start.2 = (s32[16,2,3]{0,1,2:T(2,128)S(1)}, s32[16,2,3]{0,1,2:T(2,128)}, u32[]{:S(2)}) copy-start(s32[16,2,3]{0,1,2:T(2,128)} %param.6) | copy-start | bytes 1156
  1.9 5.6 %copy-start.3 = (s32[16,2,3]{0,1,2:T(2,128)S(1)}, s32[16,2,3]{0,1,2:T(2,128)}, u32[]{:S(2)}) copy-start(s32[16,2,3]{0,1,2:T(2,128)} %param.6) | copy-start | bytes 1156
  7.5 52.8 %copy-start = (bf16[4,512,56]{1,2,0:T(8,128)(2,1)S(1)}, bf16[4,512,56]{1,2,0:T(8,128)(2,1)}, u32[]{:S(2)}) copy-start(bf16[4,512,56]{1,2,0:T(8,128)(2,1)} %param.9) | copy-start | bytes 688132
  12.5 9.2 %collective-permute-start.2 = (bf16[2,240,128]{2,1,0:T(8,128)(2,1)S(1)}, bf16[2,240,128]{2,1,0:T(8,128)(2,1)S(1)}, u32[]{:S(2)}, u32[]{:S(2)}) collective-permute-start(bf16[2,240,128]{2,1,0:T(8,128)(2,1)S(1)} %get-tuple-element.33), channel_id=1, source_target_pairs={{0,12},{1,13},{2,14},{3,15},{4,8},{5,9},{6,10},{7,11},{8,4},{9,5},... | collective-permute-start | bytes 368648 | tf_op jit(solution)/shard_map/ppermute | solution.py:450
  17.0 7.5 %collective-permute-start.3 = (bf16[2,240,128]{2,1,0:T(8,128)(2,1)S(1)}, bf16[2,240,128]{2,1,0:T(8,128)(2,1)S(1)}, u32[]{:S(2)}, u32[]{:S(2)}) collective-permute-start(bf16[2,240,128]{2,1,0:T(8,128)(2,1)S(1)} %get-tuple-element.34), channel_id=1, source_target_pairs={{0,4},{1,5},{2,6},{3,7},{4,0},{5,1},{6,2},{7,3},{8,12},{9,13},{10,... | collective-permute-start | bytes 368648 | tf_op jit(solution)/shard_map/ppermute | solution.py:450
  17.0 10.1 %collective-permute-start.4 = (bf16[2,240,128]{2,1,0:T(8,128)(2,1)S(1)}, bf16[2,240,128]{2,1,0:T(8,128)(2,1)S(1)}, u32[]{:S(2)}, u32[]{:S(2)}) collective-permute-start(bf16[2,240,128]{2,1,0:T(8,128)(2,1)S(1)} %get-tuple-element.35), channel_id=1, source_target_pairs={{0,8},{1,9},{2,10},{3,11},{4,12},{5,13},{6,14},{7,15},{8,0},{9,1},... | collective-permute-start | bytes 368648 | tf_op jit(solution)/shard_map/ppermute | solution.py:450
  17.4 13.7 %collective-permute-start.5 = (bf16[2,240,128]{2,1,0:T(8,128)(2,1)S(1)}, bf16[2,240,128]{2,1,0:T(8,128)(2,1)S(1)}, u32[]{:S(2)}, u32[]{:S(2)}) collective-permute-start(bf16[2,240,128]{2,1,0:T(8,128)(2,1)S(1)} %get-tuple-element.36), channel_id=1, source_target_pairs={{0,5},{1,4},{2,7},{3,6},{4,1},{5,0},{6,3},{7,2},{8,13},{9,12},{10,... | collective-permute-start | bytes 368648 | tf_op jit(solution)/shard_map/ppermute | solution.py:450
  19.3 12.5 %collective-permute-start.6 = (bf16[2,240,128]{2,1,0:T(8,128)(2,1)S(1)}, bf16[2,240,128]{2,1,0:T(8,128)(2,1)S(1)}, u32[]{:S(2)}, u32[]{:S(2)}) collective-permute-start(bf16[2,240,128]{2,1,0:T(8,128)(2,1)S(1)} %get-tuple-element.37), channel_id=1, source_target_pairs={{0,13},{1,12},{2,15},{3,14},{4,9},{5,8},{6,11},{7,10},{8,5},{9,4},... | collective-permute-start | bytes 368648 | tf_op jit(solution)/shard_map/ppermute | solution.py:450
  21.7 14.1 %collective-permute-start.7 = (bf16[2,240,128]{2,1,0:T(8,128)(2,1)S(1)}, bf16[2,240,128]{2,1,0:T(8,128)(2,1)S(1)}, u32[]{:S(2)}, u32[]{:S(2)}) collective-permute-start(bf16[2,240,128]{2,1,0:T(8,128)(2,1)S(1)} %get-tuple-element.38), channel_id=1, source_target_pairs={{0,6},{1,7},{2,4},{3,5},{4,2},{5,3},{6,0},{7,1},{8,14},{9,15},{10,... | collective-permute-start | bytes 368648 | tf_op jit(solution)/shard_map/ppermute | solution.py:450
  24.5 15.1 %collective-permute-start.8 = (bf16[2,240,128]{2,1,0:T(8,128)(2,1)S(1)}, bf16[2,240,128]{2,1,0:T(8,128)(2,1)S(1)}, u32[]{:S(2)}, u32[]{:S(2)}) collective-permute-start(bf16[2,240,128]{2,1,0:T(8,128)(2,1)S(1)} %get-tuple-element.39), channel_id=1, source_target_pairs={{0,9},{1,8},{2,11},{3,10},{4,13},{5,12},{6,15},{7,14},{8,1},{9,0},... | collective-permute-start | bytes 368648 | tf_op jit(solution)/shard_map/ppermute | solution.py:450
  27.1 13.6 %collective-permute-start.9 = (bf16[2,240,128]{2,1,0:T(8,128)(2,1)S(1)}, bf16[2,240,128]{2,1,0:T(8,128)(2,1)S(1)}, u32[]{:S(2)}, u32[]{:S(2)}) collective-permute-start(bf16[2,240,128]{2,1,0:T(8,128)(2,1)S(1)} %get-tuple-element.40), channel_id=1, source_target_pairs={{0,7},{1,6},{2,5},{3,4},{4,3},{5,2},{6,1},{7,0},{8,15},{9,14},{10,... | collective-permute-start | bytes 368648 | tf_op jit(solution)/shard_map/ppermute | solution.py:450
  31.0 11.3 %collective-permute-start.10 = (bf16[2,240,128]{2,1,0:T(8,128)(2,1)S(1)}, bf16[2,240,128]{2,1,0:T(8,128)(2,1)S(1)}, u32[]{:S(2)}, u32[]{:S(2)}) collective-permute-start(bf16[2,240,128]{2,1,0:T(8,128)(2,1)S(1)} %get-tuple-element.41), channel_id=1, source_target_pairs={{0,14},{1,15},{2,12},{3,13},{4,10},{5,11},{6,8},{7,9},{8,6},{9,7},... | collective-permute-start | bytes 368648 | tf_op jit(solution)/shard_map/ppermute | solution.py:450
  31.8 12.4 %collective-permute-start.11 = (bf16[2,240,128]{2,1,0:T(8,128)(2,1)S(1)}, bf16[2,240,128]{2,1,0:T(8,128)(2,1)S(1)}, u32[]{:S(2)}, u32[]{:S(2)}) collective-permute-start(bf16[2,240,128]{2,1,0:T(8,128)(2,1)S(1)} %get-tuple-element.42), channel_id=1, source_target_pairs={{0,1},{1,0},{2,3},{3,2},{4,5},{5,4},{6,7},{7,6},{8,9},{9,8},{10,11... | collective-permute-start | bytes 368648 | tf_op jit(solution)/shard_map/ppermute | solution.py:450
  35.8 16.3 %collective-permute-start.12 = (bf16[2,240,128]{2,1,0:T(8,128)(2,1)S(1)}, bf16[2,240,128]{2,1,0:T(8,128)(2,1)S(1)}, u32[]{:S(2)}, u32[]{:S(2)}) collective-permute-start(bf16[2,240,128]{2,1,0:T(8,128)(2,1)S(1)} %get-tuple-element.43), channel_id=1, source_target_pairs={{0,10},{1,11},{2,8},{3,9},{4,14},{5,15},{6,12},{7,13},{8,2},{9,3},... | collective-permute-start | bytes 368648 | tf_op jit(solution)/shard_map/ppermute | solution.py:450
  39.6 12.5 %collective-permute-start.13 = (bf16[2,240,128]{2,1,0:T(8,128)(2,1)S(1)}, bf16[2,240,128]{2,1,0:T(8,128)(2,1)S(1)}, u32[]{:S(2)}, u32[]{:S(2)}) collective-permute-start(bf16[2,240,128]{2,1,0:T(8,128)(2,1)S(1)} %get-tuple-element.44), channel_id=1, source_target_pairs={{0,2},{1,3},{2,0},{3,1},{4,6},{5,7},{6,4},{7,5},{8,10},{9,11},{10,... | collective-permute-start | bytes 368648 | tf_op jit(solution)/shard_map/ppermute | solution.py:450
  40.8 11.4 %collective-permute-start.14 = (bf16[2,240,128]{2,1,0:T(8,128)(2,1)S(1)}, bf16[2,240,128]{2,1,0:T(8,128)(2,1)S(1)}, u32[]{:S(2)}, u32[]{:S(2)}) collective-permute-start(bf16[2,240,128]{2,1,0:T(8,128)(2,1)S(1)} %get-tuple-element.45), channel_id=1, source_target_pairs={{0,15},{1,14},{2,13},{3,12},{4,11},{5,10},{6,9},{7,8},{8,7},{9,6},... | collective-permute-start | bytes 368648 | tf_op jit(solution)/shard_map/ppermute | solution.py:450
  42.4 11.1 %collective-permute-start.15 = (bf16[2,240,128]{2,1,0:T(8,128)(2,1)S(1)}, bf16[2,240,128]{2,1,0:T(8,128)(2,1)S(1)}, u32[]{:S(2)}, u32[]{:S(2)}) collective-permute-start(bf16[2,240,128]{2,1,0:T(8,128)(2,1)S(1)} %get-tuple-element.46), channel_id=1, source_target_pairs={{0,3},{1,2},{2,1},{3,0},{4,7},{5,6},{6,5},{7,4},{8,11},{9,10},{10,... | collective-permute-start | bytes 368648 | tf_op jit(solution)/shard_map/ppermute | solution.py:450
  44.2 16.1 %collective-permute-start.16 = (bf16[2,240,128]{2,1,0:T(8,128)(2,1)S(1)}, bf16[2,240,128]{2,1,0:T(8,128)(2,1)S(1)}, u32[]{:S(2)}, u32[]{:S(2)}) collective-permute-start(bf16[2,240,128]{2,1,0:T(8,128)(2,1)S(1)} %get-tuple-element.47), channel_id=1, source_target_pairs={{0,11},{1,10},{2,9},{3,8},{4,15},{5,14},{6,13},{7,12},{8,3},{9,2},... | collective-permute-start | bytes 368648 | tf_op jit(solution)/shard_map/ppermute | solution.py:450

commit v11 on v10

--- a/solution.py
+++ b/solution.py
@@ -45,6 +45,9 @@
         self.rows = regions * ROWS
         self.main = round_up(FIELDS * self.span, 16)
         self.offsets = swap_order(regions)
+        arrived = self.offsets[: regions - 5]
+        groups = [range(sample * self.makers, (sample + 1) * self.makers) for sample in range(SAMPLES)]
+        self.early = [sample for sample, group in enumerate(groups) if all(k in arrived for k in group)]
         self.sent = self.main + 16
 
 
@@ -327,9 +330,76 @@
 STEP_FIELDS = 2
 
 
+def differences(field, low, count, tiles):
+    lane = lax.broadcasted_iota(jnp.int32, (count, LANES), 1)
+    pieces = [field[t, 8 + low : 8 + low + count, :] for t in range(tiles)]
+    later = [pltpu.roll(piece, 1, 1) for piece in pieces]
+    sooner = [pltpu.roll(piece, LANES - 1, 1) for piece in pieces]
+    results = []
+    for t, here in enumerate(pieces):
+        above = jnp.where(lane == 0, later[t - 1] if t else here, later[t])
+        below = jnp.where(lane == LANES - 1, sooner[t + 1] if t + 1 < tiles else here, sooner[t])
+        sides = field[t, 7 + low : 7 + low + count, :] + field[t, 9 + low : 9 + low + count, :]
+        results.append((here, above + below + sides - 4.0 * here))
+    return results
+
+
+def early_kernel(z, place, *refs):
+    offsets = [sample * z.makers + part for sample in z.early for part in range(z.makers)]
+    blocks = dict(zip(offsets, refs))
+    results, edges, padded = refs[-3:]
+    me = place[0]
+    tiles = z.rows // LANES
+    for offset in offsets:
+        index = z.early.index(offset // z.makers)
+        for quad in range(z.quads):
+            tile = lax.rem(me ^ offset, z.makers) * z.quads + quad
+            values = blocks[offset][quad, 0 : z.main, :].astype(jnp.float32)
+            tail = blocks[offset][quad, z.main : z.sent, :].astype(jnp.float32)
+            for field in range(FIELDS):
+                target = padded.at[index, field, tile]
+                target[8 : 8 + z.span, :] = values[field * z.span : (field + 1) * z.span]
+            edges[index, tile] = tail[0:8]
+
+    def one_field(field, carry):
+        for index in range(len(z.early)):
+            for t in range(tiles):
+                padded[index, field, t, 7:8, :] = edges[index, t, pl.ds(2 * field, 1), :]
+                padded[index, field, t, 8 + z.width : 9 + z.width, :] = edges[index, t, pl.ds(2 * field + 1, 1), :]
+            for low in range(0, z.width, 8):
+                count = min(8, z.width - low)
+                found = differences(padded.at[index, field], low, count, tiles)
+                for t, pair in enumerate(found):
+                    for kind, rows in enumerate(pair):
+                        results[kind, index, field, t, low : low + count, :] = rows
+        return carry
+
+    lax.fori_loop(0, FIELDS, one_field, 0)
+
+
+def early_differences(z, place, blocks, last):
+    tiles = z.rows // LANES
+    vmem, anywhere = pl.BlockSpec(memory_space=pltpu.VMEM), pl.BlockSpec(memory_space=pl.ANY)
+    shape = (2, len(z.early), FIELDS, tiles, z.span, LANES)
+    return pl.pallas_call(
+        functools.partial(early_kernel, z),
+        out_shape=[jax.ShapeDtypeStruct(last.shape, last.dtype), jax.ShapeDtypeStruct(shape, jnp.float32)],
+        in_specs=[pl.BlockSpec(memory_space=pltpu.SMEM)] + [vmem] * len(blocks) + [anywhere],
+        out_specs=[anywhere, vmem],
+        scratch_shapes=[
+            pltpu.VMEM((len(z.early), tiles, 8, LANES), jnp.float32),
+            pltpu.VMEM((len(z.early), FIELDS, tiles, z.span + 16, LANES), jnp.float32),
+        ],
+        input_output_aliases={1 + len(blocks): 0},
+        compiler_params=pltpu.CompilerParams(vmem_limit_bytes=VMEM),
+        cost_estimate=pl.CostEstimate(flops=5_000_000, bytes_accessed=4_000_000, transcendentals=0),
+        name="early_differences",
+    )(place, *blocks, last)
+
+
 def score_kernel(z, place, *refs):
     blocks = dict(zip(z.offsets, refs))
-    analysis, crps, spread, strength, edges, padded = refs[z.regions :]
+    early, analysis, crps, spread, strength, edges, padded = refs[z.regions :]
     me = place[0]
     step = pl.program_id(0)
     rows = z.rows
@@ -357,6 +427,8 @@
 
     top = pl.multiple_of(step * STEP_FIELDS * z.span, 16)
     for offset in range(z.regions):
+        if offset // z.makers in z.early:
+            continue
         for quad in range(z.quads):
             values = blocks[offset][quad, pl.ds(top, STEP_FIELDS * z.span), :].astype(jnp.float32)
             for f in range(STEP_FIELDS):
@@ -365,6 +437,8 @@
                 ]
     tiles = rows // LANES
     for sample in range(SAMPLES):
+        if sample in z.early:
+            continue
         for f in range(STEP_FIELDS):
             low = 2 * (step * STEP_FIELDS + f)
             for t in range(tiles):
@@ -372,18 +446,15 @@
                 padded[sample, f, t, 8 + z.width : 9 + z.width, :] = edges[sample, t, pl.ds(low + 1, 1), :]
     for f, low in ((f, low) for f in range(STEP_FIELDS) for low in range(0, z.width, 16)):
         high = min(low + 16, z.width)
-        lane = lax.broadcasted_iota(jnp.int32, (high - low, LANES), 1)
         smoothed = [[] for _ in range(tiles)]
         for sample in range(SAMPLES):
-            field = padded.at[sample, f]
-            pieces = [field[t, 8 + low : 8 + high, :] for t in range(tiles)]
-            later = [pltpu.roll(piece, 1, 1) for piece in pieces]
-            sooner = [pltpu.roll(piece, LANES - 1, 1) for piece in pieces]
-            for t, here in enumerate(pieces):
-                above = jnp.where(lane == 0, later[t - 1] if t else here, later[t])
-                below = jnp.where(lane == LANES - 1, sooner[t + 1] if t + 1 < tiles else here, sooner[t])
-                sides = field[t, 7 + low : 7 + high, :] + field[t, 9 + low : 9 + high, :]
-                smooth = here + strength[t, low:high, :] * (above + below + sides - 4.0 * here)
+            if sample in z.early:
+                own = (z.early.index(sample), step * STEP_FIELDS + f)
+                found = [[early[kind, *own, t, low:high, :] for kind in range(2)] for t in range(tiles)]
+            else:
+                found = differences(padded.at[sample, f], low, high - low, tiles)
+            for t, (here, difference) in enumerate(found):
+                smooth = here + strength[t, low:high, :] * difference
                 smoothed[t].append(smooth.astype(jnp.bfloat16))
         for t, members in enumerate(smoothed):
             lanes = slice(LANES * t, LANES * (t + 1))
@@ -406,7 +477,7 @@
             spread[1, f, low:high, lanes] = ((average - target) ** 2).astype(jnp.bfloat16)
 
 
-def score(z, place, blocks, analysis):
+def score(z, place, blocks, early, analysis):
     width, rows = z.width, z.rows
     return pl.pallas_call(
         functools.partial(score_kernel, z),
@@ -416,7 +487,7 @@
         ],
         grid=(FIELDS // STEP_FIELDS,),
         in_specs=[pl.BlockSpec(memory_space=pltpu.SMEM)]
-        + [pl.BlockSpec(memory_space=pltpu.VMEM)] * z.regions
+        + [pl.BlockSpec(memory_space=pltpu.VMEM)] * (z.regions + 1)
         + [pl.BlockSpec((STEP_FIELDS, width, rows), lambda i: (i, 0, 0))],
         out_specs=[
             pl.BlockSpec((STEP_FIELDS, width, rows), lambda i: (i, 0, 0)),
@@ -429,7 +500,7 @@
         ],
         compiler_params=pltpu.CompilerParams(vmem_limit_bytes=VMEM),
         name="score",
-    )(place, *blocks, analysis)
+    )(place, *blocks, early, analysis)
 
 
 def shards(patch_tiles, slot_lists, blend_table, smoothing, analysis):
@@ -446,11 +517,16 @@
     shares = own_share(z, place, lists[0], tiles, blend_table)
     shares = [*shares, strength_blocks(z, smoothing, shares[-1])]
     blocks = join(z, place, lists, received, shares)
-    moved = [blocks[0]] + [
-        lax.ppermute(block, "region", [(i, i ^ offset) for i in range(z.regions)])
-        for block, offset in zip(blocks[1:], z.offsets[1:])
+    def swapped(block, offset):
+        return lax.ppermute(block, "region", [(i, i ^ offset) for i in range(z.regions)])
+
+    moved = [blocks[0]] + [swapped(block, offset) for block, offset in zip(blocks[1:-1], z.offsets[1:-1])]
+    needed = [
+        moved[z.offsets.index(sample * z.makers + part)] for sample in z.early for part in range(z.makers)
     ]
-    outs = score(z, place, moved, jnp.swapaxes(analysis, 1, 2))
+    last, early = early_differences(z, place, needed, blocks[-1])
+    moved.append(swapped(last, z.offsets[-1]))
+    outs = score(z, place, moved, early, jnp.swapaxes(analysis, 1, 2))
     return tuple(jnp.swapaxes(item, -1, -2) for item in outs)
 
 

time: 65.3 us -> 64.2 us (0.983)
  waiting for transfers between devices: 21.3 us -> 16.5 us
  starting transfers between devices: 28.4 us -> 31.9 us
    ppermute x15, waiting for transfers between devices: 19.9 us -> 14.8 us  [swapped(): lax.ppermute(block, 'region', [(i, i ^ offset) for i in range(z.regions)])]
    ppermute x15, starting transfers between devices: 27.8 us -> 31.3 us  [swapped(): lax.ppermute(block, 'region', [(i, i ^ offset) for i in range(z.regions)])]
    pallas_call x0 -> x1, Pallas kernels: none -> 1.68 us  [early_differences(): pl.pallas_call(functools.partial(early_kernel, z), out_shape=[jax.ShapeDt...]
    pallas_call x1, Pallas kernels: 5.09 us -> 3.73 us  [score(): pl.pallas_call(functools.partial(score_kernel, z), out_shape=[jax.ShapeDt...]
  transfers between devices with their start and end apart: 17 -> 17, of which waited for: 10 -> 10; matrix products, arithmetic and copies ran while one was open for 0% -> 0% of each run, Pallas kernels for 6% -> 9%
where the time goes in v11:
time: 64.2 us; the launch traced here: 63.7 us
  starting transfers between devices  31.9 us (50%)
  waiting for transfers between devices  16.5 us (26%)
  Pallas kernels  14 us (22%)
  local copies, waits for them, and re-layouts  0.7 us (1%)
  between operations  0.7 us (1%)
    ppermute x15, starting transfers between devices, swapped(): lax.ppermute(block, 'region', [(i, i ^ offset) for i in range(z.regions)])  31.3 us
    ppermute x15, waiting for transfers between devices, swapped(): lax.ppermute(block, 'region', [(i, i ^ offset) for i in range(z.regions)])  14.8 us
    pallas_call x1, Pallas kernels, join(): pl.pallas_call(functools.partial(join_kernel, z), out_shape=[jax.ShapeDty...  4.71 us
    pallas_call x1, Pallas kernels, score(): pl.pallas_call(functools.partial(score_kernel, z), out_shape=[jax.ShapeDt...  3.73 us
    pallas_call x1, Pallas kernels, own_share(): pl.pallas_call(functools.partial(own_kernel, z), out_shape=[*[jax.ShapeDt...  3.61 us
    pallas_call x1, Pallas kernels, early_differences(): pl.pallas_call(functools.partial(early_kernel, z), out_shape=[jax.ShapeDt...  1.68 us
  transfers between devices with their start and end apart: 17, of which 10 were waited for; matrix products, arithmetic and copies ran while one was open for 0% of the time, Pallas kernels for 9%

profile of v11, /device:TPU:1, one launch (start us, length us, event | category | flops | bytes accessed | tf_op | source)
XLA Modules:
  0.0 63.7 jit_solution(15796609176698558781)
XLA Ops:
  1.2 0.7 %copy-done.2 = s32[16,2,3]{0,1,2:T(2,128)S(1)} copy-done((s32[16,2,3]{0,1,2:T(2,128)S(1)}, s32[16,2,3]{0,1,2:T(2,128)}, u32[]{:S(2)}) %copy-start.2) | copy-done | bytes 408
  1.9 3.6 %own_share.1 = (f32[8,2,7,16,128]{4,3,2,1,0:T(8,128)S(1)}, f32[8,2,7,16,128]{4,3,2,1,0:T(8,128)S(1)}, f32[8,2,7,16,128]{4,3,2,1,0:T(8,128)S(1)}, f32[8,2,7,16,12...) custom-call(s32[1]{0:T(128)} %bitcast.place.refs_0_, s32[3,2,16]{2,1,0:T(2,128)S(1)} %bitcast.12, ...), custom_call_target="tpu_custom_call" | custom-call | flops 5000000 | bytes 8000000 | tf_op jit(solution)/shard_map/own_share/pallas_call | solution.py:191
  5.8 0.5 collective-permute-done.refs_2_
  6.3 1.2 %collective-permute-done.1.refs_3_ = bf16[16,2,448,128]{3,2,1,0:T(8,128)(2,1)} collective-permute-done((bf16[16,2,448,128]{3,2,1,0:T(8,128)(2,1)}, bf16[16,2,448,128]{3,2,1,0:T(8,128)(2,1)}, u32[]{:S(2)}, u32[]{:S(2)}) %collective-permute-start.1) | collective-permute-done | bytes 3670048 | tf_op jit(solution)/shard_map/ppermute | solution.py:515
  7.5 4.7 %join.1 = (bf16[2,240,128]{2,1,0:T(8,128)(2,1)S(1)}, bf16[2,240,128]{2,1,0:T(8,128)(2,1)S(1)}, bf16[2,240,128]{2,1,0:T(8,128)(2,1)S(1)}, bf16[2,240,128]{2,1,0:T...) custom-call(s32[1]{0:T(128)} %bitcast.place.refs_0_, ...), custom_call_target="tpu_custom_call" | custom-call | flops 5000000 | bytes 8000000 | tf_op jit(solution)/shard_map/join/pallas_call | solution.py:304
  12.2 4.5 %collective-permute-start.2 = (bf16[2,240,128]{2,1,0:T(8,128)(2,1)S(1)}, bf16[2,240,128]{2,1,0:T(8,128)(2,1)S(1)}, u32[]{:S(2)}, u32[]{:S(2)}) collective-permute-start(bf16[2,240,128]{2,1,0:T(8,128)(2,1)S(1)} %get-tuple-element.35), channel_id=1, source_target_pairs={{0,12},{1,13},{2,14},{3,15},{4,8},{5,9},{6,10},{7,11},{8,4},{9,5},... | collective-permute-start | bytes 368648 | tf_op jit(solution)/shard_map/ppermute | solution.py:521
  17.1 2.5 %collective-permute-start.5 = (bf16[2,240,128]{2,1,0:T(8,128)(2,1)S(1)}, bf16[2,240,128]{2,1,0:T(8,128)(2,1)S(1)}, u32[]{:S(2)}, u32[]{:S(2)}) collective-permute-start(bf16[2,240,128]{2,1,0:T(8,128)(2,1)S(1)} %get-tuple-element.38), channel_id=1, source_target_pairs={{0,5},{1,4},{2,7},{3,6},{4,1},{5,0},{6,3},{7,2},{8,13},{9,12},{10,... | collective-permute-start | bytes 368648 | tf_op jit(solution)/shard_map/ppermute | solution.py:521
  19.6 2.4 %collective-permute-start.6 = (bf16[2,240,128]{2,1,0:T(8,128)(2,1)S(1)}, bf16[2,240,128]{2,1,0:T(8,128)(2,1)S(1)}, u32[]{:S(2)}, u32[]{:S(2)}) collective-permute-start(bf16[2,240,128]{2,1,0:T(8,128)(2,1)S(1)} %get-tuple-element.39), channel_id=1, source_target_pairs={{0,13},{1,12},{2,15},{3,14},{4,9},{5,8},{6,11},{7,10},{8,5},{9,4},... | collective-permute-start | bytes 368648 | tf_op jit(solution)/shard_map/ppermute | solution.py:521
  22.1 1.1 %collective-permute-done.3.refs_2_ = bf16[2,240,128]{2,1,0:T(8,128)(2,1)S(1)} collective-permute-done((bf16[2,240,128]{2,1,0:T(8,128)(2,1)S(1)}, bf16[2,240,128]{2,1,0:T(8,128)(2,1)S(1)}, u32[]{:S(2)}, u32[]{:S(2)}) %collective-permute-start.3) | collective-permute-done | bytes 122912 | tf_op jit(solution)/shard_map/ppermute | solution.py:521
  23.2 4.0 %collective-permute-start.8 = (bf16[2,240,128]{2,1,0:T(8,128)(2,1)S(1)}, bf16[2,240,128]{2,1,0:T(8,128)(2,1)S(1)}, u32[]{:S(2)}, u32[]{:S(2)}) collective-permute-start(bf16[2,240,128]{2,1,0:T(8,128)(2,1)S(1)} %get-tuple-element.41), channel_id=1, source_target_pairs={{0,9},{1,8},{2,11},{3,10},{4,13},{5,12},{6,15},{7,14},{8,1},{9,0},... | collective-permute-start | bytes 368648 | tf_op jit(solution)/shard_map/ppermute | solution.py:521
  27.2 1.6 %collective-permute-start.9 = (bf16[2,240,128]{2,1,0:T(8,128)(2,1)S(1)}, bf16[2,240,128]{2,1,0:T(8,128)(2,1)S(1)}, u32[]{:S(2)}, u32[]{:S(2)}) collective-permute-start(bf16[2,240,128]{2,1,0:T(8,128)(2,1)S(1)} %get-tuple-element.42), channel_id=1, source_target_pairs={{0,7},{1,6},{2,5},{3,4},{4,3},{5,2},{6,1},{7,0},{8,15},{9,14},{10,... | collective-permute-start | bytes 368648 | tf_op jit(solution)/shard_map/ppermute | solution.py:521
  28.8 3.1 %collective-permute-done.5.refs_3_.refs_4_ = bf16[2,240,128]{2,1,0:T(8,128)(2,1)S(1)} collective-permute-done((bf16[2,240,128]{2,1,0:T(8,128)(2,1)S(1)}, bf16[2,240,128]{2,1,0:T(8,128)(2,1)S(1)}, u32[]{:S(2)}, u32[]{:S(2)}) %collective-permute-start.5) | collective-permute-done | bytes 122912 | tf_op jit(solution)/shard_map/ppermute | solution.py:521
  32.0 4.5 %collective-permute-start.10 = (bf16[2,240,128]{2,1,0:T(8,128)(2,1)S(1)}, bf16[2,240,128]{2,1,0:T(8,128)(2,1)S(1)}, u32[]{:S(2)}, u32[]{:S(2)}) collective-permute-start(bf16[2,240,128]{2,1,0:T(8,128)(2,1)S(1)} %get-tuple-element.43), channel_id=1, source_target_pairs={{0,14},{1,15},{2,12},{3,13},{4,10},{5,11},{6,8},{7,9},{8,6},{9,7},... | collective-permute-start | bytes 368648 | tf_op jit(solution)/shard_map/ppermute | solution.py:521
  36.6 1.3 %collective-permute-start.12 = (bf16[2,240,128]{2,1,0:T(8,128)(2,1)S(1)}, bf16[2,240,128]{2,1,0:T(8,128)(2,1)S(1)}, u32[]{:S(2)}, u32[]{:S(2)}) collective-permute-start(bf16[2,240,128]{2,1,0:T(8,128)(2,1)S(1)} %get-tuple-element.45), channel_id=1, source_target_pairs={{0,10},{1,11},{2,8},{3,9},{4,14},{5,15},{6,12},{7,13},{8,2},{9,3},... | collective-permute-start | bytes 368648 | tf_op jit(solution)/shard_map/ppermute | solution.py:521
  37.9 0.5 collective-permute-done.8.refs_7_
  38.4 1.8 %collective-permute-start.13 = (bf16[2,240,128]{2,1,0:T(8,128)(2,1)S(1)}, bf16[2,240,128]{2,1,0:T(8,128)(2,1)S(1)}, u32[]{:S(2)}, u32[]{:S(2)}) collective-permute-start(bf16[2,240,128]{2,1,0:T(8,128)(2,1)S(1)} %get-tuple-element.46), channel_id=1, source_target_pairs={{0,2},{1,3},{2,0},{3,1},{4,6},{5,7},{6,4},{7,5},{8,10},{9,11},{10,... | collective-permute-start | bytes 368648 | tf_op jit(solution)/shard_map/ppermute | solution.py:521
  40.3 1.2 %collective-permute-done.9.refs_5_.refs_8_ = bf16[2,240,128]{2,1,0:T(8,128)(2,1)S(1)} collective-permute-done((bf16[2,240,128]{2,1,0:T(8,128)(2,1)S(1)}, bf16[2,240,128]{2,1,0:T(8,128)(2,1)S(1)}, u32[]{:S(2)}, u32[]{:S(2)}) %collective-permute-start.9) | collective-permute-done | bytes 122912 | tf_op jit(solution)/shard_map/ppermute | solution.py:521
  41.7 1.3 %collective-permute-start.15 = (bf16[2,240,128]{2,1,0:T(8,128)(2,1)S(1)}, bf16[2,240,128]{2,1,0:T(8,128)(2,1)S(1)}, u32[]{:S(2)}, u32[]{:S(2)}) collective-permute-start(bf16[2,240,128]{2,1,0:T(8,128)(2,1)S(1)} %get-tuple-element.48), channel_id=1, source_target_pairs={{0,3},{1,2},{2,1},{3,0},{4,7},{5,6},{6,5},{7,4},{8,11},{9,10},{10,... | collective-permute-start | bytes 368648 | tf_op jit(solution)/shard_map/ppermute | solution.py:521
  43.0 1.7 %early_differences.1 = (bf16[2,240,128]{2,1,0:T(8,128)(2,1)S(1)}, f32[2,5,4,4,56,128]{5,4,3,2,1,0:T(8,128)S(1)}) custom-call(s32[1]{0:T(128)} %bitcast.place.refs_0_, bf16[2,240,128]{2,1,0:T(8,128)(2,1)S(1)} %get-tuple-element.34.refs_0_, bf16[2,240,128]{2,1,0:T(8,128)(2,1)S(1)} %collective-permute-done.11.refs_1_.refs_10_, ...), custom_call_target="tpu_custom_call", output_to_operand_aliasing={{0}: (11, {})} | custom-call | flops 5000000 | bytes 4000000 | tf_op jit(solution)/shard_map/early_differences/pallas_call | solution.py:384
  44.7 6.5 %collective-permute-start.16 = (bf16[2,240,128]{2,1,0:T(8,128)(2,1)S(1)}, bf16[2,240,128]{2,1,0:T(8,128)(2,1)S(1)}, u32[]{:S(2)}, u32[]{:S(2)}) collective-permute-start(bf16[2,240,128]{2,1,0:T(8,128)(2,1)S(1)} %get-tuple-element.50), channel_id=1, source_target_pairs={{0,11},{1,10},{2,9},{3,8},{4,15},{5,14},{6,13},{7,12},{8,3},{9,2},... | collective-permute-start | bytes 368648 | tf_op jit(solution)/shard_map/ppermute | solution.py:521
  51.2 0.9 %collective-permute-done.12.refs_11_ = bf16[2,240,128]{2,1,0:T(8,128)(2,1)S(1)} collective-permute-done((bf16[2,240,128]{2,1,0:T(8,128)(2,1)S(1)}, bf16[2,240,128]{2,1,0:T(8,128)(2,1)S(1)}, u32[]{:S(2)}, u32[]{:S(2)}) %collective-permute-start.12) | collective-permute-done | bytes 122912 | tf_op jit(solution)/shard_map/ppermute | solution.py:521
  52.1 1.1 %collective-permute-done.15.refs_14_ = bf16[2,240,128]{2,1,0:T(8,128)(2,1)S(1)} collective-permute-done((bf16[2,240,128]{2,1,0:T(8,128)(2,1)S(1)}, bf16[2,240,128]{2,1,0:T(8,128)(2,1)S(1)}, u32[]{:S(2)}, u32[]{:S(2)}) %collective-permute-start.15) | collective-permute-done | bytes 122912 | tf_op jit(solution)/shard_map/ppermute | solution.py:521
  53.2 6.8 %collective-permute-done.16.refs_15_ = bf16[2,240,128]{2,1,0:T(8,128)(2,1)S(1)} collective-permute-done((bf16[2,240,128]{2,1,0:T(8,128)(2,1)S(1)}, bf16[2,240,128]{2,1,0:T(8,128)(2,1)S(1)}, u32[]{:S(2)}, u32[]{:S(2)}) %collective-permute-start.16) | collective-permute-done | bytes 122912 | tf_op jit(solution)/shard_map/ppermute | solution.py:521
  60.0 3.7 %score.1 = (bf16[4,56,512]{2,1,0:T(8,128)(2,1)}, bf16[2,4,56,512]{3,2,1,0:T(8,128)(2,1)}) custom-call(s32[1]{0:T(128)} %bitcast.place.refs_0_, bf16[2,240,128]{2,1,0:T(8,128)(2,1)S(1)} %get-tuple-element.34.refs_0_, bf16[2,240,128]{2,1,0:T(8,128)(2,1)S(1)} %collective-permute-done.2.refs_8_.refs_1_, bf16[2,240,128]{2,1,0:T(8,128)(2,1)S(1)} %collective-permute-done.3.refs_2_, ...), custom_call_target="tpu_custom_call" | custom-call | tf_op jit(solution)/shard_map/score/pallas_call | solution.py:482
  (23 shorter events, 1.7 us)
Async XLA Ops:
  0.6 4.9 %copy-start.1 = (f32[32,896]{1,0:T(8,128)S(1)}, f32[32,896]{1,0:T(8,128)}, u32[]{:S(2)}) copy-start(f32[32,896]{1,0:T(8,128)} %smoothing.1) | copy-start | bytes 344068
  0.6 6.8 %collective-permute-start.1 = (bf16[16,2,448,128]{3,2,1,0:T(8,128)(2,1)}, bf16[16,2,448,128]{3,2,1,0:T(8,128)(2,1)}, u32[]{:S(2)}, u32[]{:S(2)}) collective-permute-start(bf16[16,2,448,128]{3,2,1,0:T(8,128)(2,1)} %bitcast.14), channel_id=1, source_target_pairs={{0,1},{1,0},{2,3},{3,2},{4,5},{5,4},{6,7},{7,6},{8,9},{9,8},{10,11... | collective-permute-start | bytes 11010056 | tf_op jit(solution)/shard_map/ppermute | solution.py:515
  0.8 5.5 %collective-permute-start = (s32[3,2,16]{2,1,0:T(2,128)}, s32[3,2,16]{2,1,0:T(2,128)S(1)}, u32[]{:S(2)}, u32[]{:S(2)}) collective-permute-start(s32[3,2,16]{2,1,0:T(2,128)} %bitcast.11), channel_id=1, source_target_pairs={{0,1},{1,0},{2,3},{3,2},{4,5},{5,4},{6,7},{7,6},{8,9},{9,8},{10,11... | collective-permute-start | bytes 1160 | tf_op jit(solution)/shard_map/ppermute | solution.py:516
  1.2 0.7 %copy-start.2 = (s32[16,2,3]{0,1,2:T(2,128)S(1)}, s32[16,2,3]{0,1,2:T(2,128)}, u32[]{:S(2)}) copy-start(s32[16,2,3]{0,1,2:T(2,128)} %param.6) | copy-start | bytes 1156
  1.9 5.6 %copy-start.3 = (s32[16,2,3]{0,1,2:T(2,128)S(1)}, s32[16,2,3]{0,1,2:T(2,128)}, u32[]{:S(2)}) copy-start(s32[16,2,3]{0,1,2:T(2,128)} %param.6) | copy-start | bytes 1156
  7.5 52.5 %copy-start = (bf16[4,512,56]{1,2,0:T(8,128)(2,1)S(1)}, bf16[4,512,56]{1,2,0:T(8,128)(2,1)}, u32[]{:S(2)}) copy-start(bf16[4,512,56]{1,2,0:T(8,128)(2,1)} %param.9) | copy-start | bytes 688132
  12.2 9.8 %collective-permute-start.2 = (bf16[2,240,128]{2,1,0:T(8,128)(2,1)S(1)}, bf16[2,240,128]{2,1,0:T(8,128)(2,1)S(1)}, u32[]{:S(2)}, u32[]{:S(2)}) collective-permute-start(bf16[2,240,128]{2,1,0:T(8,128)(2,1)S(1)} %get-tuple-element.35), channel_id=1, source_target_pairs={{0,12},{1,13},{2,14},{3,15},{4,8},{5,9},{6,10},{7,11},{8,4},{9,5},... | collective-permute-start | bytes 368648 | tf_op jit(solution)/shard_map/ppermute | solution.py:521
  16.7 6.5 %collective-permute-start.3 = (bf16[2,240,128]{2,1,0:T(8,128)(2,1)S(1)}, bf16[2,240,128]{2,1,0:T(8,128)(2,1)S(1)}, u32[]{:S(2)}, u32[]{:S(2)}) collective-permute-start(bf16[2,240,128]{2,1,0:T(8,128)(2,1)S(1)} %get-tuple-element.36), channel_id=1, source_target_pairs={{0,4},{1,5},{2,6},{3,7},{4,0},{5,1},{6,2},{7,3},{8,12},{9,13},{10,... | collective-permute-start | bytes 368648 | tf_op jit(solution)/shard_map/ppermute | solution.py:521
  16.7 10.5 %collective-permute-start.4 = (bf16[2,240,128]{2,1,0:T(8,128)(2,1)S(1)}, bf16[2,240,128]{2,1,0:T(8,128)(2,1)S(1)}, u32[]{:S(2)}, u32[]{:S(2)}) collective-permute-start(bf16[2,240,128]{2,1,0:T(8,128)(2,1)S(1)} %get-tuple-element.37), channel_id=1, source_target_pairs={{0,8},{1,9},{2,10},{3,11},{4,12},{5,13},{6,14},{7,15},{8,0},{9,1},... | collective-permute-start | bytes 368648 | tf_op jit(solution)/shard_map/ppermute | solution.py:521
  17.1 14.8 %collective-permute-start.5 = (bf16[2,240,128]{2,1,0:T(8,128)(2,1)S(1)}, bf16[2,240,128]{2,1,0:T(8,128)(2,1)S(1)}, u32[]{:S(2)}, u32[]{:S(2)}) collective-permute-start(bf16[2,240,128]{2,1,0:T(8,128)(2,1)S(1)} %get-tuple-element.38), channel_id=1, source_target_pairs={{0,5},{1,4},{2,7},{3,6},{4,1},{5,0},{6,3},{7,2},{8,13},{9,12},{10,... | collective-permute-start | bytes 368648 | tf_op jit(solution)/shard_map/ppermute | solution.py:521
  19.6 12.4 %collective-permute-start.6 = (bf16[2,240,128]{2,1,0:T(8,128)(2,1)S(1)}, bf16[2,240,128]{2,1,0:T(8,128)(2,1)S(1)}, u32[]{:S(2)}, u32[]{:S(2)}) collective-permute-start(bf16[2,240,128]{2,1,0:T(8,128)(2,1)S(1)} %get-tuple-element.39), channel_id=1, source_target_pairs={{0,13},{1,12},{2,15},{3,14},{4,9},{5,8},{6,11},{7,10},{8,5},{9,4},... | collective-permute-start | bytes 368648 | tf_op jit(solution)/shard_map/ppermute | solution.py:521
  22.0 14.6 %collective-permute-start.7 = (bf16[2,240,128]{2,1,0:T(8,128)(2,1)S(1)}, bf16[2,240,128]{2,1,0:T(8,128)(2,1)S(1)}, u32[]{:S(2)}, u32[]{:S(2)}) collective-permute-start(bf16[2,240,128]{2,1,0:T(8,128)(2,1)S(1)} %get-tuple-element.40), channel_id=1, source_target_pairs={{0,6},{1,7},{2,4},{3,5},{4,2},{5,3},{6,0},{7,1},{8,14},{9,15},{10,... | collective-permute-start | bytes 368648 | tf_op jit(solution)/shard_map/ppermute | solution.py:521
  23.2 15.2 %collective-permute-start.8 = (bf16[2,240,128]{2,1,0:T(8,128)(2,1)S(1)}, bf16[2,240,128]{2,1,0:T(8,128)(2,1)S(1)}, u32[]{:S(2)}, u32[]{:S(2)}) collective-permute-start(bf16[2,240,128]{2,1,0:T(8,128)(2,1)S(1)} %get-tuple-element.41), channel_id=1, source_target_pairs={{0,9},{1,8},{2,11},{3,10},{4,13},{5,12},{6,15},{7,14},{8,1},{9,0},... | collective-permute-start | bytes 368648 | tf_op jit(solution)/shard_map/ppermute | solution.py:521
  27.2 14.3 %collective-permute-start.9 = (bf16[2,240,128]{2,1,0:T(8,128)(2,1)S(1)}, bf16[2,240,128]{2,1,0:T(8,128)(2,1)S(1)}, u32[]{:S(2)}, u32[]{:S(2)}) collective-permute-start(bf16[2,240,128]{2,1,0:T(8,128)(2,1)S(1)} %get-tuple-element.42), channel_id=1, source_target_pairs={{0,7},{1,6},{2,5},{3,4},{4,3},{5,2},{6,1},{7,0},{8,15},{9,14},{10,... | collective-permute-start | bytes 368648 | tf_op jit(solution)/shard_map/ppermute | solution.py:521
  31.9 9.8 %collective-permute-start.11 = (bf16[2,240,128]{2,1,0:T(8,128)(2,1)S(1)}, bf16[2,240,128]{2,1,0:T(8,128)(2,1)S(1)}, u32[]{:S(2)}, u32[]{:S(2)}) collective-permute-start(bf16[2,240,128]{2,1,0:T(8,128)(2,1)S(1)} %get-tuple-element.44), channel_id=1, source_target_pairs={{0,1},{1,0},{2,3},{3,2},{4,5},{5,4},{6,7},{7,6},{8,9},{9,8},{10,11... | collective-permute-start | bytes 368648 | tf_op jit(solution)/shard_map/ppermute | solution.py:521
  32.0 12.7 %collective-permute-start.10 = (bf16[2,240,128]{2,1,0:T(8,128)(2,1)S(1)}, bf16[2,240,128]{2,1,0:T(8,128)(2,1)S(1)}, u32[]{:S(2)}, u32[]{:S(2)}) collective-permute-start(bf16[2,240,128]{2,1,0:T(8,128)(2,1)S(1)} %get-tuple-element.43), channel_id=1, source_target_pairs={{0,14},{1,15},{2,12},{3,13},{4,10},{5,11},{6,8},{7,9},{8,6},{9,7},... | collective-permute-start | bytes 368648 | tf_op jit(solution)/shard_map/ppermute | solution.py:521
  36.6 15.6 %collective-permute-start.12 = (bf16[2,240,128]{2,1,0:T(8,128)(2,1)S(1)}, bf16[2,240,128]{2,1,0:T(8,128)(2,1)S(1)}, u32[]{:S(2)}, u32[]{:S(2)}) collective-permute-start(bf16[2,240,128]{2,1,0:T(8,128)(2,1)S(1)} %get-tuple-element.45), channel_id=1, source_target_pairs={{0,10},{1,11},{2,8},{3,9},{4,14},{5,15},{6,12},{7,13},{8,2},{9,3},... | collective-permute-start | bytes 368648 | tf_op jit(solution)/shard_map/ppermute | solution.py:521
  38.4 13.7 %collective-permute-start.13 = (bf16[2,240,128]{2,1,0:T(8,128)(2,1)S(1)}, bf16[2,240,128]{2,1,0:T(8,128)(2,1)S(1)}, u32[]{:S(2)}, u32[]{:S(2)}) collective-permute-start(bf16[2,240,128]{2,1,0:T(8,128)(2,1)S(1)} %get-tuple-element.46), channel_id=1, source_target_pairs={{0,2},{1,3},{2,0},{3,1},{4,6},{5,7},{6,4},{7,5},{8,10},{9,11},{10,... | collective-permute-start | bytes 368648 | tf_op jit(solution)/shard_map/ppermute | solution.py:521
  41.4 10.7 %collective-permute-start.14 = (bf16[2,240,128]{2,1,0:T(8,128)(2,1)S(1)}, bf16[2,240,128]{2,1,0:T(8,128)(2,1)S(1)}, u32[]{:S(2)}, u32[]{:S(2)}) collective-permute-start(bf16[2,240,128]{2,1,0:T(8,128)(2,1)S(1)} %get-tuple-element.47), channel_id=1, source_target_pairs={{0,15},{1,14},{2,13},{3,12},{4,11},{5,10},{6,9},{7,8},{8,7},{9,6},... | collective-permute-start | bytes 368648 | tf_op jit(solution)/shard_map/ppermute | solution.py:521
  41.7 11.5 %collective-permute-start.15 = (bf16[2,240,128]{2,1,0:T(8,128)(2,1)S(1)}, bf16[2,240,128]{2,1,0:T(8,128)(2,1)S(1)}, u32[]{:S(2)}, u32[]{:S(2)}) collective-permute-start(bf16[2,240,128]{2,1,0:T(8,128)(2,1)S(1)} %get-tuple-element.48), channel_id=1, source_target_pairs={{0,3},{1,2},{2,1},{3,0},{4,7},{5,6},{6,5},{7,4},{8,11},{9,10},{10,... | collective-permute-start | bytes 368648 | tf_op jit(solution)/shard_map/ppermute | solution.py:521
  44.7 15.3 %collective-permute-start.16 = (bf16[2,240,128]{2,1,0:T(8,128)(2,1)S(1)}, bf16[2,240,128]{2,1,0:T(8,128)(2,1)S(1)}, u32[]{:S(2)}, u32[]{:S(2)}) collective-permute-start(bf16[2,240,128]{2,1,0:T(8,128)(2,1)S(1)} %get-tuple-element.50), channel_id=1, source_target_pairs={{0,11},{1,10},{2,9},{3,8},{4,15},{5,14},{6,13},{7,12},{8,3},{9,2},... | collective-permute-start | bytes 368648 | tf_op jit(solution)/shard_map/ppermute | solution.py:521

commit v12 on v11

--- a/solution.py
+++ b/solution.py
@@ -20,6 +20,7 @@
 QUAD = LANES // ROWS
 MID = 0.11
 VMEM = 40 * 1024 * 1024
+PACK_VMEM = 52 * 1024 * 1024
 MOST_VMEM = 48 * 1024 * 1024
 
 
@@ -48,6 +49,11 @@
         arrived = self.offsets[: regions - 5]
         groups = [range(sample * self.makers, (sample + 1) * self.makers) for sample in range(SAMPLES)]
         self.early = [sample for sample, group in enumerate(groups) if all(k in arrived for k in group)]
+        self.later = [
+            sample
+            for sample, group in enumerate(groups)
+            if sample not in self.early and self.offsets[-1] not in group
+        ]
         self.sent = self.main + 16
 
 
@@ -129,6 +135,33 @@
     return i * others + maker if side else QUAD * others + maker * CAP + slot
 
 
+def pack_kernel(z, place, tiles, *refs):
+    packed, sems = refs[:-1], refs[-1]
+    part = lax.rem(place[0], z.makers)
+    copies = []
+    for k, target in enumerate(packed):
+        first = lax.rem(part + k + 1, z.makers) * z.block
+        for j in range(z.block):
+            copies.append(pltpu.make_async_copy(tiles.at[first + j], target.at[j], sems.at[k, j]))
+    for copy in copies:
+        copy.start()
+    for copy in copies:
+        copy.wait()
+
+
+def pack(z, place, tiles):
+    shape = jax.ShapeDtypeStruct((z.block, *tiles.shape[1:]), tiles.dtype)
+    return pl.pallas_call(
+        functools.partial(pack_kernel, z),
+        out_shape=[shape] * (z.makers - 1),
+        in_specs=[pl.BlockSpec(memory_space=pltpu.SMEM), pl.BlockSpec(memory_space=pltpu.HBM)],
+        out_specs=[pl.BlockSpec(memory_space=pltpu.VMEM)] * (z.makers - 1),
+        scratch_shapes=[pltpu.SemaphoreType.DMA((z.makers - 1, z.block))],
+        compiler_params=pltpu.CompilerParams(vmem_limit_bytes=PACK_VMEM),
+        name="pack",
+    )(place, tiles)
+
+
 def own_kernel(z, place, lists, tiles, table_hbm, *refs):
     half, (total, weights, landed, staged, sums, table, sems) = refs[:FIELDS], refs[FIELDS:]
     first = lax.rem(place[0], z.makers) * z.block
@@ -257,7 +290,7 @@
                 return lambda t: staged_tile(staged_of(maker, slot), field, t) * weight(t), column
 
             for maker, slot in sources:
-                stage(staged_of(maker, slot), received[maker - 1][first + j, slot])
+                stage(staged_of(maker, slot), received[maker - 1][j, slot])
             others = place_all(side, sums.at[FIELDS], [weight_item(*source) for source in sources])
             inverse = [[1.0 / (total[j, parity, t] + others[parity][t]) for t in range(TILES)] for parity in range(2)]
             for field in range(FIELDS):
@@ -344,14 +377,14 @@
     return results
 
 
-def early_kernel(z, place, *refs):
-    offsets = [sample * z.makers + part for sample in z.early for part in range(z.makers)]
+def early_kernel(z, samples, place, *refs):
+    offsets = [sample * z.makers + part for sample in samples for part in range(z.makers)]
     blocks = dict(zip(offsets, refs))
     results, edges, padded = refs[-3:]
     me = place[0]
     tiles = z.rows // LANES
     for offset in offsets:
-        index = z.early.index(offset // z.makers)
+        index = samples.index(offset // z.makers)
         for quad in range(z.quads):
             tile = lax.rem(me ^ offset, z.makers) * z.quads + quad
             values = blocks[offset][quad, 0 : z.main, :].astype(jnp.float32)
@@ -362,7 +395,7 @@
             edges[index, tile] = tail[0:8]
 
     def one_field(field, carry):
-        for index in range(len(z.early)):
+        for index in range(len(samples)):
             for t in range(tiles):
                 padded[index, field, t, 7:8, :] = edges[index, t, pl.ds(2 * field, 1), :]
                 padded[index, field, t, 8 + z.width : 9 + z.width, :] = edges[index, t, pl.ds(2 * field + 1, 1), :]
@@ -377,29 +410,30 @@
     lax.fori_loop(0, FIELDS, one_field, 0)
 
 
-def early_differences(z, place, blocks, last):
+def early_differences(z, samples, place, blocks, last=()):
     tiles = z.rows // LANES
     vmem, anywhere = pl.BlockSpec(memory_space=pltpu.VMEM), pl.BlockSpec(memory_space=pl.ANY)
-    shape = (2, len(z.early), FIELDS, tiles, z.span, LANES)
+    shape = (2, len(samples), FIELDS, tiles, z.span, LANES)
     return pl.pallas_call(
-        functools.partial(early_kernel, z),
-        out_shape=[jax.ShapeDtypeStruct(last.shape, last.dtype), jax.ShapeDtypeStruct(shape, jnp.float32)],
-        in_specs=[pl.BlockSpec(memory_space=pltpu.SMEM)] + [vmem] * len(blocks) + [anywhere],
-        out_specs=[anywhere, vmem],
+        functools.partial(early_kernel, z, samples),
+        out_shape=[jax.ShapeDtypeStruct(item.shape, item.dtype) for item in last]
+        + [jax.ShapeDtypeStruct(shape, jnp.float32)],
+        in_specs=[pl.BlockSpec(memory_space=pltpu.SMEM)] + [vmem] * len(blocks) + [anywhere] * len(last),
+        out_specs=[anywhere] * len(last) + [vmem],
         scratch_shapes=[
-            pltpu.VMEM((len(z.early), tiles, 8, LANES), jnp.float32),
-            pltpu.VMEM((len(z.early), FIELDS, tiles, z.span + 16, LANES), jnp.float32),
-        ],
-        input_output_aliases={1 + len(blocks): 0},
+            pltpu.VMEM((len(samples), tiles, 8, LANES), jnp.float32),
+            pltpu.VMEM((len(samples), FIELDS, tiles, z.span + 16, LANES), jnp.float32),
+        ],
+        input_output_aliases={1 + len(blocks) + i: i for i in range(len(last))},
         compiler_params=pltpu.CompilerParams(vmem_limit_bytes=VMEM),
         cost_estimate=pl.CostEstimate(flops=5_000_000, bytes_accessed=4_000_000, transcendentals=0),
         name="early_differences",
-    )(place, *blocks, last)
+    )(place, *blocks, *last)
 
 
 def score_kernel(z, place, *refs):
     blocks = dict(zip(z.offsets, refs))
-    early, analysis, crps, spread, strength, edges, padded = refs[z.regions :]
+    early, later, analysis, crps, spread, strength, edges, padded = refs[z.regions :]
     me = place[0]
     step = pl.program_id(0)
     rows = z.rows
@@ -427,7 +461,7 @@
 
     top = pl.multiple_of(step * STEP_FIELDS * z.span, 16)
     for offset in range(z.regions):
-        if offset // z.makers in z.early:
+        if offset // z.makers in z.early + z.later:
             continue
         for quad in range(z.quads):
             values = blocks[offset][quad, pl.ds(top, STEP_FIELDS * z.span), :].astype(jnp.float32)
@@ -437,7 +471,7 @@
                 ]
     tiles = rows // LANES
     for sample in range(SAMPLES):
-        if sample in z.early:
+        if sample in z.early + z.later:
             continue
         for f in range(STEP_FIELDS):
             low = 2 * (step * STEP_FIELDS + f)
@@ -448,9 +482,10 @@
         high = min(low + 16, z.width)
         smoothed = [[] for _ in range(tiles)]
         for sample in range(SAMPLES):
-            if sample in z.early:
-                own = (z.early.index(sample), step * STEP_FIELDS + f)
-                found = [[early[kind, *own, t, low:high, :] for kind in range(2)] for t in range(tiles)]
+            if sample in z.early + z.later:
+                samples, ready = (z.early, early) if sample in z.early else (z.later, later)
+                own = (samples.index(sample), step * STEP_FIELDS + f)
+                found = [[ready[kind, *own, t, low:high, :] for kind in range(2)] for t in range(tiles)]
             else:
                 found = differences(padded.at[sample, f], low, high - low, tiles)
             for t, (here, difference) in enumerate(found):
@@ -477,7 +512,7 @@
             spread[1, f, low:high, lanes] = ((average - target) ** 2).astype(jnp.bfloat16)
 
 
-def score(z, place, blocks, early, analysis):
+def score(z, place, blocks, early, later, analysis):
     width, rows = z.width, z.rows
     return pl.pallas_call(
         functools.partial(score_kernel, z),
@@ -487,7 +522,7 @@
         ],
         grid=(FIELDS // STEP_FIELDS,),
         in_specs=[pl.BlockSpec(memory_space=pltpu.SMEM)]
-        + [pl.BlockSpec(memory_space=pltpu.VMEM)] * (z.regions + 1)
+        + [pl.BlockSpec(memory_space=pltpu.VMEM)] * (z.regions + 2)
         + [pl.BlockSpec((STEP_FIELDS, width, rows), lambda i: (i, 0, 0))],
         out_specs=[
             pl.BlockSpec((STEP_FIELDS, width, rows), lambda i: (i, 0, 0)),
@@ -500,7 +535,7 @@
         ],
         compiler_params=pltpu.CompilerParams(vmem_limit_bytes=VMEM),
         name="score",
-    )(place, *blocks, early, analysis)
+    )(place, *blocks, early, later, analysis)
 
 
 def shards(patch_tiles, slot_lists, blend_table, smoothing, analysis):
@@ -512,7 +547,7 @@
     tiles = patch_tiles.reshape(z.regions, CAP, FIELDS, PAIRS * TILES, LANES)
     tiles = jnp.swapaxes(tiles, 2, 3).reshape(z.regions, CAP, LINES, LANES)
     lists = jnp.transpose(slot_lists, (2, 1, 0))
-    received = [lax.ppermute(tiles, "region", turn) for turn in turns]
+    received = [lax.ppermute(item, "region", turn) for item, turn in zip(pack(z, place, tiles), turns)]
     lists = [lists] + [lax.ppermute(lists, "region", turn) for turn in turns]
     shares = own_share(z, place, lists[0], tiles, blend_table)
     shares = [*shares, strength_blocks(z, smoothing, shares[-1])]
@@ -521,12 +556,13 @@
         return lax.ppermute(block, "region", [(i, i ^ offset) for i in range(z.regions)])
 
     moved = [blocks[0]] + [swapped(block, offset) for block, offset in zip(blocks[1:-1], z.offsets[1:-1])]
-    needed = [
-        moved[z.offsets.index(sample * z.makers + part)] for sample in z.early for part in range(z.makers)
-    ]
-    last, early = early_differences(z, place, needed, blocks[-1])
+    def blocks_of(samples):
+        return [moved[z.offsets.index(sample * z.makers + part)] for sample in samples for part in range(z.makers)]
+
+    last, early = early_differences(z, z.early, place, blocks_of(z.early), [blocks[-1]])
+    (later,) = early_differences(z, z.later, place, blocks_of(z.later))
     moved.append(swapped(last, z.offsets[-1]))
-    outs = score(z, place, moved, early, jnp.swapaxes(analysis, 1, 2))
+    outs = score(z, place, moved, early, later, jnp.swapaxes(analysis, 1, 2))
     return tuple(jnp.swapaxes(item, -1, -2) for item in outs)
 
 

time: 64.2 us -> 61.9 us (0.964)
  waiting for transfers between devices: 16.5 us -> 13.8 us
  Pallas kernels: 14 us -> 15.3 us
  local copies, waits for them, and re-layouts: 0.7 us -> 0.01 us
    pallas_call x1 -> x3, Pallas kernels: 1.68 us -> 4.14 us  [the longest x2 2.5 us: early_differences(): pl.pallas_call(functools.partial(early_kernel, z, samples), out_shape=[ja...]
    ppermute x1, waiting for transfers between devices: 1.16 us -> 0.01 us  [shards(): lax.ppermute(item, 'region', turn)]
    pallas_call x1, Pallas kernels: 4.71 us -> 3.59 us  [join(): pl.pallas_call(functools.partial(join_kernel, z), out_shape=[jax.ShapeDty...]
    ppermute x15, waiting for transfers between devices: 14.8 us -> 13.8 us  [swapped(): lax.ppermute(block, 'region', [(i, i ^ offset) for i in range(z.regions)])]
    unnamed x8 -> x6, local copies, waits for them, and re-layouts: 0.7 us -> 0.01 us
  transfers between devices with their start and end apart: 17 -> 17, of which waited for: 10 -> 7; matrix products, arithmetic and copies ran while one was open for 0% -> 0% of each run, Pallas kernels for 9% -> 11%
where the time goes in v12:
time: 61.9 us; the launch traced here: 61.7 us
  starting transfers between devices  31.9 us (52%)
  Pallas kernels  15.3 us (25%)
  waiting for transfers between devices  13.8 us (22%)
  between operations  0.74 us (1%)
    ppermute x15, starting transfers between devices, swapped(): lax.ppermute(block, 'region', [(i, i ^ offset) for i in range(z.regions)])  31.3 us
    ppermute x15, waiting for transfers between devices, swapped(): lax.ppermute(block, 'region', [(i, i ^ offset) for i in range(z.regions)])  13.8 us
    pallas_call x1, Pallas kernels, own_share(): pl.pallas_call(functools.partial(own_kernel, z), out_shape=[*[jax.ShapeDt...  3.92 us
    pallas_call x1, Pallas kernels, join(): pl.pallas_call(functools.partial(join_kernel, z), out_shape=[jax.ShapeDty...  3.59 us
    pallas_call x1, Pallas kernels, score(): pl.pallas_call(functools.partial(score_kernel, z), out_shape=[jax.ShapeDt...  3.35 us
    pallas_call x2, Pallas kernels, early_differences(): pl.pallas_call(functools.partial(early_kernel, z, samples), out_shape=[ja...  2.5 us
    pallas_call x1, Pallas kernels, pack(): pl.pallas_call(functools.partial(pack_kernel, z), out_shape=[shape] * (z....  1.63 us
  transfers between devices with their start and end apart: 17, of which 7 were waited for; matrix products, arithmetic and copies ran while one was open for 0% of the time, Pallas kernels for 11%

profile of v12, /device:TPU:1, one launch (start us, length us, event | category | flops | bytes accessed | tf_op | source)
XLA Modules:
  0.0 61.7 jit_solution(1118642392760177453)
XLA Ops:
  0.6 1.6 %pack.1 = bf16[8,2,448,128]{3,2,1,0:T(8,128)(2,1)S(1)} custom-call(s32[1]{0:T(128)} %bitcast.place.refs_0_, bf16[16,2,448,128]{3,2,1,0:T(8,128)(2,1)} %bitcast.14), custom_call_target="tpu_custom_call" | custom-call | tf_op jit(solution)/shard_map/pack/pallas_call | solution.py:154
  2.4 0.5 collective-permute-start
  2.9 3.9 %own_share.1 = (f32[8,2,7,16,128]{4,3,2,1,0:T(8,128)S(1)}, f32[8,2,7,16,128]{4,3,2,1,0:T(8,128)S(1)}, f32[8,2,7,16,128]{4,3,2,1,0:T(8,128)S(1)}, f32[8,2,7,16,12...) custom-call(s32[1]{0:T(128)} %bitcast.place.refs_0_, s32[3,2,16]{2,1,0:T(2,128)S(1)} %bitcast.12, ...), custom_call_target="tpu_custom_call" | custom-call | flops 5000000 | bytes 8000000 | tf_op jit(solution)/shard_map/own_share/pallas_call | solution.py:224
  7.1 3.6 %join.1 = (bf16[2,240,128]{2,1,0:T(8,128)(2,1)S(1)}, bf16[2,240,128]{2,1,0:T(8,128)(2,1)S(1)}, bf16[2,240,128]{2,1,0:T(8,128)(2,1)S(1)}, bf16[2,240,128]{2,1,0:T...) custom-call(s32[1]{0:T(128)} %bitcast.place.refs_0_, ...), custom_call_target="tpu_custom_call" | custom-call | flops 5000000 | bytes 8000000 | tf_op jit(solution)/shard_map/join/pallas_call | solution.py:337
  10.7 4.5 %collective-permute-start.2 = (bf16[2,240,128]{2,1,0:T(8,128)(2,1)S(1)}, bf16[2,240,128]{2,1,0:T(8,128)(2,1)S(1)}, u32[]{:S(2)}, u32[]{:S(2)}) collective-permute-start(bf16[2,240,128]{2,1,0:T(8,128)(2,1)S(1)} %get-tuple-element.35), channel_id=1, source_target_pairs={{0,12},{1,13},{2,14},{3,15},{4,8},{5,9},{6,10},{7,11},{8,4},{9,5},... | collective-permute-start | bytes 368648 | tf_op jit(solution)/shard_map/ppermute | solution.py:556
  15.6 1.9 %collective-permute-start.5 = (bf16[2,240,128]{2,1,0:T(8,128)(2,1)S(1)}, bf16[2,240,128]{2,1,0:T(8,128)(2,1)S(1)}, u32[]{:S(2)}, u32[]{:S(2)}) collective-permute-start(bf16[2,240,128]{2,1,0:T(8,128)(2,1)S(1)} %get-tuple-element.38), channel_id=1, source_target_pairs={{0,5},{1,4},{2,7},{3,6},{4,1},{5,0},{6,3},{7,2},{8,13},{9,12},{10,... | collective-permute-start | bytes 368648 | tf_op jit(solution)/shard_map/ppermute | solution.py:556
  17.5 2.4 %collective-permute-start.6 = (bf16[2,240,128]{2,1,0:T(8,128)(2,1)S(1)}, bf16[2,240,128]{2,1,0:T(8,128)(2,1)S(1)}, u32[]{:S(2)}, u32[]{:S(2)}) collective-permute-start(bf16[2,240,128]{2,1,0:T(8,128)(2,1)S(1)} %get-tuple-element.39), channel_id=1, source_target_pairs={{0,13},{1,12},{2,15},{3,14},{4,9},{5,8},{6,11},{7,10},{8,5},{9,4},... | collective-permute-start | bytes 368648 | tf_op jit(solution)/shard_map/ppermute | solution.py:556
  19.9 1.4 %collective-permute-start.7 = (bf16[2,240,128]{2,1,0:T(8,128)(2,1)S(1)}, bf16[2,240,128]{2,1,0:T(8,128)(2,1)S(1)}, u32[]{:S(2)}, u32[]{:S(2)}) collective-permute-start(bf16[2,240,128]{2,1,0:T(8,128)(2,1)S(1)} %get-tuple-element.40), channel_id=1, source_target_pairs={{0,6},{1,7},{2,4},{3,5},{4,2},{5,3},{6,0},{7,1},{8,14},{9,15},{10,... | collective-permute-start | bytes 368648 | tf_op jit(solution)/shard_map/ppermute | solution.py:556
  21.3 1.4 %collective-permute-done.3.refs_2_ = bf16[2,240,128]{2,1,0:T(8,128)(2,1)S(1)} collective-permute-done((bf16[2,240,128]{2,1,0:T(8,128)(2,1)S(1)}, bf16[2,240,128]{2,1,0:T(8,128)(2,1)S(1)}, u32[]{:S(2)}, u32[]{:S(2)}) %collective-permute-start.3) | collective-permute-done | bytes 122912 | tf_op jit(solution)/shard_map/ppermute | solution.py:556
  22.6 2.4 %collective-permute-start.8 = (bf16[2,240,128]{2,1,0:T(8,128)(2,1)S(1)}, bf16[2,240,128]{2,1,0:T(8,128)(2,1)S(1)}, u32[]{:S(2)}, u32[]{:S(2)}) collective-permute-start(bf16[2,240,128]{2,1,0:T(8,128)(2,1)S(1)} %get-tuple-element.41), channel_id=1, source_target_pairs={{0,9},{1,8},{2,11},{3,10},{4,13},{5,12},{6,15},{7,14},{8,1},{9,0},... | collective-permute-start | bytes 368648 | tf_op jit(solution)/shard_map/ppermute | solution.py:556
  25.3 1.9 %collective-permute-start.9 = (bf16[2,240,128]{2,1,0:T(8,128)(2,1)S(1)}, bf16[2,240,128]{2,1,0:T(8,128)(2,1)S(1)}, u32[]{:S(2)}, u32[]{:S(2)}) collective-permute-start(bf16[2,240,128]{2,1,0:T(8,128)(2,1)S(1)} %get-tuple-element.42), channel_id=1, source_target_pairs={{0,7},{1,6},{2,5},{3,4},{4,3},{5,2},{6,1},{7,0},{8,15},{9,14},{10,... | collective-permute-start | bytes 368648 | tf_op jit(solution)/shard_map/ppermute | solution.py:556
  27.2 2.0 %collective-permute-done.5.refs_3_.refs_4_ = bf16[2,240,128]{2,1,0:T(8,128)(2,1)S(1)} collective-permute-done((bf16[2,240,128]{2,1,0:T(8,128)(2,1)S(1)}, bf16[2,240,128]{2,1,0:T(8,128)(2,1)S(1)}, u32[]{:S(2)}, u32[]{:S(2)}) %collective-permute-start.5) | collective-permute-done | bytes 122912 | tf_op jit(solution)/shard_map/ppermute | solution.py:556
  29.2 0.7 %collective-permute-done.6.refs_9_.refs_5_ = bf16[2,240,128]{2,1,0:T(8,128)(2,1)S(1)} collective-permute-done((bf16[2,240,128]{2,1,0:T(8,128)(2,1)S(1)}, bf16[2,240,128]{2,1,0:T(8,128)(2,1)S(1)}, u32[]{:S(2)}, u32[]{:S(2)}) %collective-permute-start.6) | collective-permute-done | bytes 122912 | tf_op jit(solution)/shard_map/ppermute | solution.py:556
  30.0 4.5 %collective-permute-start.10 = (bf16[2,240,128]{2,1,0:T(8,128)(2,1)S(1)}, bf16[2,240,128]{2,1,0:T(8,128)(2,1)S(1)}, u32[]{:S(2)}, u32[]{:S(2)}) collective-permute-start(bf16[2,240,128]{2,1,0:T(8,128)(2,1)S(1)} %get-tuple-element.43), channel_id=1, source_target_pairs={{0,14},{1,15},{2,12},{3,13},{4,10},{5,11},{6,8},{7,9},{8,6},{9,7},... | collective-permute-start | bytes 368648 | tf_op jit(solution)/shard_map/ppermute | solution.py:556
  34.9 1.9 %collective-permute-done.8.refs_7_ = bf16[2,240,128]{2,1,0:T(8,128)(2,1)S(1)} collective-permute-done((bf16[2,240,128]{2,1,0:T(8,128)(2,1)S(1)}, bf16[2,240,128]{2,1,0:T(8,128)(2,1)S(1)}, u32[]{:S(2)}, u32[]{:S(2)}) %collective-permute-start.8) | collective-permute-done | bytes 122912 | tf_op jit(solution)/shard_map/ppermute | solution.py:556
  36.8 2.2 %collective-permute-start.13 = (bf16[2,240,128]{2,1,0:T(8,128)(2,1)S(1)}, bf16[2,240,128]{2,1,0:T(8,128)(2,1)S(1)}, u32[]{:S(2)}, u32[]{:S(2)}) collective-permute-start(bf16[2,240,128]{2,1,0:T(8,128)(2,1)S(1)} %get-tuple-element.46), channel_id=1, source_target_pairs={{0,2},{1,3},{2,0},{3,1},{4,6},{5,7},{6,4},{7,5},{8,10},{9,11},{10,... | collective-permute-start | bytes 368648 | tf_op jit(solution)/shard_map/ppermute | solution.py:556
  39.0 0.7 %collective-permute-start.14 = (bf16[2,240,128]{2,1,0:T(8,128)(2,1)S(1)}, bf16[2,240,128]{2,1,0:T(8,128)(2,1)S(1)}, u32[]{:S(2)}, u32[]{:S(2)}) collective-permute-start(bf16[2,240,128]{2,1,0:T(8,128)(2,1)S(1)} %get-tuple-element.47), channel_id=1, source_target_pairs={{0,15},{1,14},{2,13},{3,12},{4,11},{5,10},{6,9},{7,8},{8,7},{9,6},... | collective-permute-start | bytes 368648 | tf_op jit(solution)/shard_map/ppermute | solution.py:556
  39.7 2.0 %collective-permute-start.15 = (bf16[2,240,128]{2,1,0:T(8,128)(2,1)S(1)}, bf16[2,240,128]{2,1,0:T(8,128)(2,1)S(1)}, u32[]{:S(2)}, u32[]{:S(2)}) collective-permute-start(bf16[2,240,128]{2,1,0:T(8,128)(2,1)S(1)} %get-tuple-element.48), channel_id=1, source_target_pairs={{0,3},{1,2},{2,1},{3,0},{4,7},{5,6},{6,5},{7,4},{8,11},{9,10},{10,... | collective-permute-start | bytes 368648 | tf_op jit(solution)/shard_map/ppermute | solution.py:556
  41.7 1.7 %early_differences.2 = (bf16[2,240,128]{2,1,0:T(8,128)(2,1)S(1)}, f32[2,5,4,4,56,128]{5,4,3,2,1,0:T(8,128)S(1)}) custom-call(s32[1]{0:T(128)} %bitcast.place.refs_0_, bf16[2,240,128]{2,1,0:T(8,128)(2,1)S(1)} %get-tuple-element.34.refs_0_, bf16[2,240,128]{2,1,0:T(8,128)(2,1)S(1)} %collective-permute-done.11.refs_1_.refs_10_, ...), custom_call_target="tpu_custom_call", output_to_operand_aliasing={{0}: (11, {})} | custom-call | flops 5000000 | bytes 4000000 | tf_op jit(solution)/shard_map/early_differences/pallas_call | solution.py:417
  43.4 6.7 %collective-permute-start.16 = (bf16[2,240,128]{2,1,0:T(8,128)(2,1)S(1)}, bf16[2,240,128]{2,1,0:T(8,128)(2,1)S(1)}, u32[]{:S(2)}, u32[]{:S(2)}) collective-permute-start(bf16[2,240,128]{2,1,0:T(8,128)(2,1)S(1)} %get-tuple-element.50), channel_id=1, source_target_pairs={{0,11},{1,10},{2,9},{3,8},{4,15},{5,14},{6,13},{7,12},{8,3},{9,2},... | collective-permute-start | bytes 368648 | tf_op jit(solution)/shard_map/ppermute | solution.py:556
  50.1 1.7 %collective-permute-done.15.refs_1_.refs_14_ = bf16[2,240,128]{2,1,0:T(8,128)(2,1)S(1)} collective-permute-done((bf16[2,240,128]{2,1,0:T(8,128)(2,1)S(1)}, bf16[2,240,128]{2,1,0:T(8,128)(2,1)S(1)}, u32[]{:S(2)}, u32[]{:S(2)}) %collective-permute-start.15) | collective-permute-done | bytes 122912 | tf_op jit(solution)/shard_map/ppermute | solution.py:556
  51.8 0.8 %early_differences.3.refs_17_ = f32[2,2,4,4,56,128]{5,4,3,2,1,0:T(8,128)S(1)} custom-call(s32[1]{0:T(128)} %bitcast.place.refs_0_, bf16[2,240,128]{2,1,0:T(8,128)(2,1)S(1)} %collective-permute-done.13.refs_0_.refs_12_, bf16[2,240,128]{2,1,0:T(8,128)(2,1)S(1)} %collective-permute-done.15.refs_1_.refs_14_, ...), custom_call_target="tpu_custom_call" | custom-call | flops 5000000 | bytes 4000000 | tf_op jit(solution)/shard_map/early_differences/pallas_call | solution.py:417
  52.6 5.8 %collective-permute-done.16.refs_15_ = bf16[2,240,128]{2,1,0:T(8,128)(2,1)S(1)} collective-permute-done((bf16[2,240,128]{2,1,0:T(8,128)(2,1)S(1)}, bf16[2,240,128]{2,1,0:T(8,128)(2,1)S(1)}, u32[]{:S(2)}, u32[]{:S(2)}) %collective-permute-start.16) | collective-permute-done | bytes 122912 | tf_op jit(solution)/shard_map/ppermute | solution.py:556
  58.4 3.3 %score.1 = (bf16[4,56,512]{2,1,0:T(8,128)(2,1)}, bf16[2,4,56,512]{3,2,1,0:T(8,128)(2,1)}) custom-call(s32[1]{0:T(128)} %bitcast.place.refs_0_, bf16[2,240,128]{2,1,0:T(8,128)(2,1)S(1)} %get-tuple-element.34.refs_0_, bf16[2,240,128]{2,1,0:T(8,128)(2,1)S(1)} %collective-permute-done.2.refs_8_.refs_1_, bf16[2,240,128]{2,1,0:T(8,128)(2,1)S(1)} %collective-permute-done.3.refs_2_, ...), custom_call_target="tpu_custom_call" | custom-call | tf_op jit(solution)/shard_map/score/pallas_call | solution.py:517
  (23 shorter events, 1.5 us)
Async XLA Ops:
  0.6 1.8 %copy-start.2 = (s32[16,2,3]{0,1,2:T(2,128)S(1)}, s32[16,2,3]{0,1,2:T(2,128)}, u32[]{:S(2)}) copy-start(s32[16,2,3]{0,1,2:T(2,128)} %param.6) | copy-start | bytes 1156
  2.3 4.8 %collective-permute-start.1 = (bf16[8,2,448,128]{3,2,1,0:T(8,128)(2,1)S(1)}, bf16[8,2,448,128]{3,2,1,0:T(8,128)(2,1)S(1)}, u32[]{:S(2)}, u32[]{:S(2)}) collective-permute-start(bf16[8,2,448,128]{3,2,1,0:T(8,128)(2,1)S(1)} %pack.1), channel_id=1, source_target_pairs={{0,1},{1,0},{2,3},{3,2},{4,5},{5,4},{6,7},{7,6},{8,9},{9,8},{10,11... | collective-permute-start | bytes 5505032 | tf_op jit(solution)/shard_map/ppermute | solution.py:550
  2.4 4.4 %copy-start.1 = (f32[32,896]{1,0:T(8,128)S(1)}, f32[32,896]{1,0:T(8,128)}, u32[]{:S(2)}) copy-start(f32[32,896]{1,0:T(8,128)} %smoothing.1) | copy-start | bytes 344068
  2.4 4.7 %collective-permute-start = (s32[3,2,16]{2,1,0:T(2,128)S(1)}, s32[3,2,16]{2,1,0:T(2,128)S(1)}, u32[]{:S(2)}, u32[]{:S(2)}) collective-permute-start(s32[3,2,16]{2,1,0:T(2,128)S(1)} %bitcast.11), channel_id=1, source_target_pairs={{0,1},{1,0},{2,3},{3,2},{4,5},{5,4},{6,7},{7,6},{8,9},{9,8},{10,11... | collective-permute-start | bytes 1160 | tf_op jit(solution)/shard_map/ppermute | solution.py:551
  10.7 9.2 %collective-permute-start.2 = (bf16[2,240,128]{2,1,0:T(8,128)(2,1)S(1)}, bf16[2,240,128]{2,1,0:T(8,128)(2,1)S(1)}, u32[]{:S(2)}, u32[]{:S(2)}) collective-permute-start(bf16[2,240,128]{2,1,0:T(8,128)(2,1)S(1)} %get-tuple-element.35), channel_id=1, source_target_pairs={{0,12},{1,13},{2,14},{3,15},{4,8},{5,9},{6,10},{7,11},{8,4},{9,5},... | collective-permute-start | bytes 368648 | tf_op jit(solution)/shard_map/ppermute | solution.py:556
  15.2 7.4 %collective-permute-start.3 = (bf16[2,240,128]{2,1,0:T(8,128)(2,1)S(1)}, bf16[2,240,128]{2,1,0:T(8,128)(2,1)S(1)}, u32[]{:S(2)}, u32[]{:S(2)}) collective-permute-start(bf16[2,240,128]{2,1,0:T(8,128)(2,1)S(1)} %get-tuple-element.36), channel_id=1, source_target_pairs={{0,4},{1,5},{2,6},{3,7},{4,0},{5,1},{6,2},{7,3},{8,12},{9,13},{10,... | collective-permute-start | bytes 368648 | tf_op jit(solution)/shard_map/ppermute | solution.py:556
  15.2 10.1 %collective-permute-start.4 = (bf16[2,240,128]{2,1,0:T(8,128)(2,1)S(1)}, bf16[2,240,128]{2,1,0:T(8,128)(2,1)S(1)}, u32[]{:S(2)}, u32[]{:S(2)}) collective-permute-start(bf16[2,240,128]{2,1,0:T(8,128)(2,1)S(1)} %get-tuple-element.37), channel_id=1, source_target_pairs={{0,8},{1,9},{2,10},{3,11},{4,12},{5,13},{6,14},{7,15},{8,0},{9,1},... | collective-permute-start | bytes 368648 | tf_op jit(solution)/shard_map/ppermute | solution.py:556
  15.6 13.7 %collective-permute-start.5 = (bf16[2,240,128]{2,1,0:T(8,128)(2,1)S(1)}, bf16[2,240,128]{2,1,0:T(8,128)(2,1)S(1)}, u32[]{:S(2)}, u32[]{:S(2)}) collective-permute-start(bf16[2,240,128]{2,1,0:T(8,128)(2,1)S(1)} %get-tuple-element.38), channel_id=1, source_target_pairs={{0,5},{1,4},{2,7},{3,6},{4,1},{5,0},{6,3},{7,2},{8,13},{9,12},{10,... | collective-permute-start | bytes 368648 | tf_op jit(solution)/shard_map/ppermute | solution.py:556
  17.5 12.5 %collective-permute-start.6 = (bf16[2,240,128]{2,1,0:T(8,128)(2,1)S(1)}, bf16[2,240,128]{2,1,0:T(8,128)(2,1)S(1)}, u32[]{:S(2)}, u32[]{:S(2)}) collective-permute-start(bf16[2,240,128]{2,1,0:T(8,128)(2,1)S(1)} %get-tuple-element.39), channel_id=1, source_target_pairs={{0,13},{1,12},{2,15},{3,14},{4,9},{5,8},{6,11},{7,10},{8,5},{9,4},... | collective-permute-start | bytes 368648 | tf_op jit(solution)/shard_map/ppermute | solution.py:556
  19.9 14.6 %collective-permute-start.7 = (bf16[2,240,128]{2,1,0:T(8,128)(2,1)S(1)}, bf16[2,240,128]{2,1,0:T(8,128)(2,1)S(1)}, u32[]{:S(2)}, u32[]{:S(2)}) collective-permute-start(bf16[2,240,128]{2,1,0:T(8,128)(2,1)S(1)} %get-tuple-element.40), channel_id=1, source_target_pairs={{0,6},{1,7},{2,4},{3,5},{4,2},{5,3},{6,0},{7,1},{8,14},{9,15},{10,... | collective-permute-start | bytes 368648 | tf_op jit(solution)/shard_map/ppermute | solution.py:556
  22.6 14.2 %collective-permute-start.8 = (bf16[2,240,128]{2,1,0:T(8,128)(2,1)S(1)}, bf16[2,240,128]{2,1,0:T(8,128)(2,1)S(1)}, u32[]{:S(2)}, u32[]{:S(2)}) collective-permute-start(bf16[2,240,128]{2,1,0:T(8,128)(2,1)S(1)} %get-tuple-element.41), channel_id=1, source_target_pairs={{0,9},{1,8},{2,11},{3,10},{4,13},{5,12},{6,15},{7,14},{8,1},{9,0},... | collective-permute-start | bytes 368648 | tf_op jit(solution)/shard_map/ppermute | solution.py:556
  25.3 13.7 %collective-permute-start.9 = (bf16[2,240,128]{2,1,0:T(8,128)(2,1)S(1)}, bf16[2,240,128]{2,1,0:T(8,128)(2,1)S(1)}, u32[]{:S(2)}, u32[]{:S(2)}) collective-permute-start(bf16[2,240,128]{2,1,0:T(8,128)(2,1)S(1)} %get-tuple-element.42), channel_id=1, source_target_pairs={{0,7},{1,6},{2,5},{3,4},{4,3},{5,2},{6,1},{7,0},{8,15},{9,14},{10,... | collective-permute-start | bytes 368648 | tf_op jit(solution)/shard_map/ppermute | solution.py:556
  29.2 10.5 %collective-permute-start.11 = (bf16[2,240,128]{2,1,0:T(8,128)(2,1)S(1)}, bf16[2,240,128]{2,1,0:T(8,128)(2,1)S(1)}, u32[]{:S(2)}, u32[]{:S(2)}) collective-permute-start(bf16[2,240,128]{2,1,0:T(8,128)(2,1)S(1)} %get-tuple-element.44), channel_id=1, source_target_pairs={{0,1},{1,0},{2,3},{3,2},{4,5},{5,4},{6,7},{7,6},{8,9},{9,8},{10,11... | collective-permute-start | bytes 368648 | tf_op jit(solution)/shard_map/ppermute | solution.py:556
  30.0 13.4 %collective-permute-start.10 = (bf16[2,240,128]{2,1,0:T(8,128)(2,1)S(1)}, bf16[2,240,128]{2,1,0:T(8,128)(2,1)S(1)}, u32[]{:S(2)}, u32[]{:S(2)}) collective-permute-start(bf16[2,240,128]{2,1,0:T(8,128)(2,1)S(1)} %get-tuple-element.43), channel_id=1, source_target_pairs={{0,14},{1,15},{2,12},{3,13},{4,10},{5,11},{6,8},{7,9},{8,6},{9,7},... | collective-permute-start | bytes 368648 | tf_op jit(solution)/shard_map/ppermute | solution.py:556
  34.5 18.1 %collective-permute-start.12 = (bf16[2,240,128]{2,1,0:T(8,128)(2,1)S(1)}, bf16[2,240,128]{2,1,0:T(8,128)(2,1)S(1)}, u32[]{:S(2)}, u32[]{:S(2)}) collective-permute-start(bf16[2,240,128]{2,1,0:T(8,128)(2,1)S(1)} %get-tuple-element.45), channel_id=1, source_target_pairs={{0,10},{1,11},{2,8},{3,9},{4,14},{5,15},{6,12},{7,13},{8,2},{9,3},... | collective-permute-start | bytes 368648 | tf_op jit(solution)/shard_map/ppermute | solution.py:556
  36.8 13.3 %collective-permute-start.13 = (bf16[2,240,128]{2,1,0:T(8,128)(2,1)S(1)}, bf16[2,240,128]{2,1,0:T(8,128)(2,1)S(1)}, u32[]{:S(2)}, u32[]{:S(2)}) collective-permute-start(bf16[2,240,128]{2,1,0:T(8,128)(2,1)S(1)} %get-tuple-element.46), channel_id=1, source_target_pairs={{0,2},{1,3},{2,0},{3,1},{4,6},{5,7},{6,4},{7,5},{8,10},{9,11},{10,... | collective-permute-start | bytes 368648 | tf_op jit(solution)/shard_map/ppermute | solution.py:556
  39.0 11.1 %collective-permute-start.14 = (bf16[2,240,128]{2,1,0:T(8,128)(2,1)S(1)}, bf16[2,240,128]{2,1,0:T(8,128)(2,1)S(1)}, u32[]{:S(2)}, u32[]{:S(2)}) collective-permute-start(bf16[2,240,128]{2,1,0:T(8,128)(2,1)S(1)} %get-tuple-element.47), channel_id=1, source_target_pairs={{0,15},{1,14},{2,13},{3,12},{4,11},{5,10},{6,9},{7,8},{8,7},{9,6},... | collective-permute-start | bytes 368648 | tf_op jit(solution)/shard_map/ppermute | solution.py:556
  39.7 12.1 %collective-permute-start.15 = (bf16[2,240,128]{2,1,0:T(8,128)(2,1)S(1)}, bf16[2,240,128]{2,1,0:T(8,128)(2,1)S(1)}, u32[]{:S(2)}, u32[]{:S(2)}) collective-permute-start(bf16[2,240,128]{2,1,0:T(8,128)(2,1)S(1)} %get-tuple-element.48), channel_id=1, source_target_pairs={{0,3},{1,2},{2,1},{3,0},{4,7},{5,6},{6,5},{7,4},{8,11},{9,10},{10,... | collective-permute-start | bytes 368648 | tf_op jit(solution)/shard_map/ppermute | solution.py:556
  41.7 16.7 %copy-start = (bf16[4,512,56]{1,2,0:T(8,128)(2,1)S(1)}, bf16[4,512,56]{1,2,0:T(8,128)(2,1)}, u32[]{:S(2)}) copy-start(bf16[4,512,56]{1,2,0:T(8,128)(2,1)} %param.9) | copy-start | bytes 688132
  43.4 15.0 %collective-permute-start.16 = (bf16[2,240,128]{2,1,0:T(8,128)(2,1)S(1)}, bf16[2,240,128]{2,1,0:T(8,128)(2,1)S(1)}, u32[]{:S(2)}, u32[]{:S(2)}) collective-permute-start(bf16[2,240,128]{2,1,0:T(8,128)(2,1)S(1)} %get-tuple-element.50), channel_id=1, source_target_pairs={{0,11},{1,10},{2,9},{3,8},{4,15},{5,14},{6,13},{7,12},{8,3},{9,2},... | collective-permute-start | bytes 368648 | tf_op jit(solution)/shard_map/ppermute | solution.py:556

commit v13 on v12

--- a/solution.py
+++ b/solution.py
@@ -163,16 +163,21 @@
 
 
 def own_kernel(z, place, lists, tiles, table_hbm, *refs):
-    half, (total, weights, landed, staged, sums, table, sems) = refs[:FIELDS], refs[FIELDS:]
+    half, (total, weights, landed, staged, sums, table, sems, table_sem) = refs[:FIELDS], refs[FIELDS:]
     first = lax.rem(place[0], z.makers) * z.block
 
-    def fetch(j):
-        return pltpu.make_async_copy(tiles.at[first + j], landed.at[j], sems.at[j])
-
-    fetch_table = pltpu.make_async_copy(table_hbm, table, sems.at[z.block])
+    def fetch(j, slot):
+        return pltpu.make_async_copy(tiles.at[first + j, slot], landed.at[j, slot], sems.at[j, slot])
+
+    def heavy(j):
+        return lists[0, 1, first + j] >= 0
+
+    fetch_table = pltpu.make_async_copy(table_hbm, table, table_sem.at[0])
     fetch_table.start()
     for j in range(z.block):
-        fetch(j).start()
+        fetch(j, 0).start()
+    for j in range(z.block):
+        pl.when(heavy(j))(fetch(j, 1).start)
     fetch_table.wait()
     kinds = table.shape[0]
     for k in range(PAIRS):
@@ -186,10 +191,12 @@
 
     def group(quad, carry):
         for i in range(QUAD):
-            fetch(quad * QUAD + i).wait()
+            fetch(quad * QUAD + i, 0).wait()
 
         def body(i, side, slots):
             j = quad * QUAD + i
+            if len(slots) > 1:
+                fetch(j, 1).wait()
 
             def weight_item(slot):
                 column, kind = (lists[entry, slot, first + j] for entry in (1, 2))
@@ -210,7 +217,7 @@
                     for t in range(TILES):
                         target[j, parity, t] = pieces[parity][t]
 
-        each_region(z, lambda i: lists[0, 1, first + quad * QUAD + i] >= 0, body)
+        each_region(z, lambda i: heavy(quad * QUAD + i), body)
         return carry
 
     lax.fori_loop(0, z.quads, group, 0)
@@ -234,7 +241,8 @@
             pltpu.VMEM((QUAD + CAP, LINES, LANES), jnp.float32),
             pltpu.VMEM((FIELDS + 1, 2, SLOTS, PAIRS, LANES), jnp.float32),
             pltpu.VMEM(table.shape, jnp.float32),
-            pltpu.SemaphoreType.DMA((z.block + 1,)),
+            pltpu.SemaphoreType.DMA((z.block, CAP)),
+            pltpu.SemaphoreType.DMA((1,)),
         ],
         compiler_params=pltpu.CompilerParams(vmem_limit_bytes=MOST_VMEM),
         cost_estimate=pl.CostEstimate(flops=5_000_000, bytes_accessed=8_000_000, transcendentals=0),

time: 61.9 us -> 62.5 us (level)
  transfers between devices with their start and end apart: 17 -> 17, of which waited for: 7 -> 7; matrix products, arithmetic and copies ran while one was open for 0% -> 0% of each run, Pallas kernels for 11% -> 12%
where the time goes in v13:
time: 62.5 us; the launch traced here: 62.3 us
  starting transfers between devices  32.1 us (51%)
  Pallas kernels  15.8 us (25%)
  waiting for transfers between devices  13.6 us (22%)
  between operations  0.74 us (1%)
    ppermute x15, starting transfers between devices, swapped(): lax.ppermute(block, 'region', [(i, i ^ offset) for i in range(z.regions)])  31.5 us
    ppermute x15, waiting for transfers between devices, swapped(): lax.ppermute(block, 'region', [(i, i ^ offset) for i in range(z.regions)])  13.6 us
    pallas_call x1, Pallas kernels, own_share(): pl.pallas_call(functools.partial(own_kernel, z), out_shape=[*[jax.ShapeDt...  4.45 us
    pallas_call x1, Pallas kernels, join(): pl.pallas_call(functools.partial(join_kernel, z), out_shape=[jax.ShapeDty...  3.58 us
    pallas_call x1, Pallas kernels, score(): pl.pallas_call(functools.partial(score_kernel, z), out_shape=[jax.ShapeDt...  3.35 us
    pallas_call x2, Pallas kernels, early_differences(): pl.pallas_call(functools.partial(early_kernel, z, samples), out_shape=[ja...  2.5 us
    pallas_call x1, Pallas kernels, pack(): pl.pallas_call(functools.partial(pack_kernel, z), out_shape=[shape] * (z....  1.63 us
  transfers between devices with their start and end apart: 17, of which 7 were waited for; matrix products, arithmetic and copies ran while one was open for 0% of the time, Pallas kernels for 12%

profile of v13, /device:TPU:1, one launch (start us, length us, event | category | flops | bytes accessed | tf_op | source)
XLA Modules:
  0.0 62.3 jit_solution(2233566315789341917)
XLA Ops:
  0.6 1.6 %pack.1 = bf16[8,2,448,128]{3,2,1,0:T(8,128)(2,1)S(1)} custom-call(s32[1]{0:T(128)} %bitcast.place.refs_0_, bf16[16,2,448,128]{3,2,1,0:T(8,128)(2,1)} %bitcast.14), custom_call_target="tpu_custom_call" | custom-call | tf_op jit(solution)/shard_map/pack/pallas_call | solution.py:154
  2.9 4.4 %own_share.1 = (f32[8,2,7,16,128]{4,3,2,1,0:T(8,128)S(1)}, f32[8,2,7,16,128]{4,3,2,1,0:T(8,128)S(1)}, f32[8,2,7,16,128]{4,3,2,1,0:T(8,128)S(1)}, f32[8,2,7,16,12...) custom-call(s32[1]{0:T(128)} %bitcast.place.refs_0_, s32[3,2,16]{2,1,0:T(2,128)S(1)} %bitcast.12, ...), custom_call_target="tpu_custom_call" | custom-call | flops 5000000 | bytes 8000000 | tf_op jit(solution)/shard_map/own_share/pallas_call | solution.py:231
  7.6 3.6 %join.1 = (bf16[2,240,128]{2,1,0:T(8,128)(2,1)S(1)}, bf16[2,240,128]{2,1,0:T(8,128)(2,1)S(1)}, bf16[2,240,128]{2,1,0:T(8,128)(2,1)S(1)}, bf16[2,240,128]{2,1,0:T...) custom-call(s32[1]{0:T(128)} %bitcast.place.refs_0_, ...), custom_call_target="tpu_custom_call" | custom-call | flops 5000000 | bytes 8000000 | tf_op jit(solution)/shard_map/join/pallas_call | solution.py:345
  11.2 4.5 %collective-permute-start.2 = (bf16[2,240,128]{2,1,0:T(8,128)(2,1)S(1)}, bf16[2,240,128]{2,1,0:T(8,128)(2,1)S(1)}, u32[]{:S(2)}, u32[]{:S(2)}) collective-permute-start(bf16[2,240,128]{2,1,0:T(8,128)(2,1)S(1)} %get-tuple-element.35), channel_id=1, source_target_pairs={{0,12},{1,13},{2,14},{3,15},{4,8},{5,9},{6,10},{7,11},{8,4},{9,5},... | collective-permute-start | bytes 368648 | tf_op jit(solution)/shard_map/ppermute | solution.py:564
  16.1 2.0 %collective-permute-start.5 = (bf16[2,240,128]{2,1,0:T(8,128)(2,1)S(1)}, bf16[2,240,128]{2,1,0:T(8,128)(2,1)S(1)}, u32[]{:S(2)}, u32[]{:S(2)}) collective-permute-start(bf16[2,240,128]{2,1,0:T(8,128)(2,1)S(1)} %get-tuple-element.38), channel_id=1, source_target_pairs={{0,5},{1,4},{2,7},{3,6},{4,1},{5,0},{6,3},{7,2},{8,13},{9,12},{10,... | collective-permute-start | bytes 368648 | tf_op jit(solution)/shard_map/ppermute | solution.py:564
  18.0 2.4 %collective-permute-start.6 = (bf16[2,240,128]{2,1,0:T(8,128)(2,1)S(1)}, bf16[2,240,128]{2,1,0:T(8,128)(2,1)S(1)}, u32[]{:S(2)}, u32[]{:S(2)}) collective-permute-start(bf16[2,240,128]{2,1,0:T(8,128)(2,1)S(1)} %get-tuple-element.39), channel_id=1, source_target_pairs={{0,13},{1,12},{2,15},{3,14},{4,9},{5,8},{6,11},{7,10},{8,5},{9,4},... | collective-permute-start | bytes 368648 | tf_op jit(solution)/shard_map/ppermute | solution.py:564
  20.4 1.4 %collective-permute-start.7 = (bf16[2,240,128]{2,1,0:T(8,128)(2,1)S(1)}, bf16[2,240,128]{2,1,0:T(8,128)(2,1)S(1)}, u32[]{:S(2)}, u32[]{:S(2)}) collective-permute-start(bf16[2,240,128]{2,1,0:T(8,128)(2,1)S(1)} %get-tuple-element.40), channel_id=1, source_target_pairs={{0,6},{1,7},{2,4},{3,5},{4,2},{5,3},{6,0},{7,1},{8,14},{9,15},{10,... | collective-permute-start | bytes 368648 | tf_op jit(solution)/shard_map/ppermute | solution.py:564
  21.8 1.4 %collective-permute-done.3.refs_2_ = bf16[2,240,128]{2,1,0:T(8,128)(2,1)S(1)} collective-permute-done((bf16[2,240,128]{2,1,0:T(8,128)(2,1)S(1)}, bf16[2,240,128]{2,1,0:T(8,128)(2,1)S(1)}, u32[]{:S(2)}, u32[]{:S(2)}) %collective-permute-start.3) | collective-permute-done | bytes 122912 | tf_op jit(solution)/shard_map/ppermute | solution.py:564
  23.1 2.4 %collective-permute-start.8 = (bf16[2,240,128]{2,1,0:T(8,128)(2,1)S(1)}, bf16[2,240,128]{2,1,0:T(8,128)(2,1)S(1)}, u32[]{:S(2)}, u32[]{:S(2)}) collective-permute-start(bf16[2,240,128]{2,1,0:T(8,128)(2,1)S(1)} %get-tuple-element.41), channel_id=1, source_target_pairs={{0,9},{1,8},{2,11},{3,10},{4,13},{5,12},{6,15},{7,14},{8,1},{9,0},... | collective-permute-start | bytes 368648 | tf_op jit(solution)/shard_map/ppermute | solution.py:564
  25.8 1.9 %collective-permute-start.9 = (bf16[2,240,128]{2,1,0:T(8,128)(2,1)S(1)}, bf16[2,240,128]{2,1,0:T(8,128)(2,1)S(1)}, u32[]{:S(2)}, u32[]{:S(2)}) collective-permute-start(bf16[2,240,128]{2,1,0:T(8,128)(2,1)S(1)} %get-tuple-element.42), channel_id=1, source_target_pairs={{0,7},{1,6},{2,5},{3,4},{4,3},{5,2},{6,1},{7,0},{8,15},{9,14},{10,... | collective-permute-start | bytes 368648 | tf_op jit(solution)/shard_map/ppermute | solution.py:564
  27.7 2.0 %collective-permute-done.5.refs_3_.refs_4_ = bf16[2,240,128]{2,1,0:T(8,128)(2,1)S(1)} collective-permute-done((bf16[2,240,128]{2,1,0:T(8,128)(2,1)S(1)}, bf16[2,240,128]{2,1,0:T(8,128)(2,1)S(1)}, u32[]{:S(2)}, u32[]{:S(2)}) %collective-permute-start.5) | collective-permute-done | bytes 122912 | tf_op jit(solution)/shard_map/ppermute | solution.py:564
  29.7 0.8 %collective-permute-done.6.refs_9_.refs_5_ = bf16[2,240,128]{2,1,0:T(8,128)(2,1)S(1)} collective-permute-done((bf16[2,240,128]{2,1,0:T(8,128)(2,1)S(1)}, bf16[2,240,128]{2,1,0:T(8,128)(2,1)S(1)}, u32[]{:S(2)}, u32[]{:S(2)}) %collective-permute-start.6) | collective-permute-done | bytes 122912 | tf_op jit(solution)/shard_map/ppermute | solution.py:564
  30.5 4.5 %collective-permute-start.10 = (bf16[2,240,128]{2,1,0:T(8,128)(2,1)S(1)}, bf16[2,240,128]{2,1,0:T(8,128)(2,1)S(1)}, u32[]{:S(2)}, u32[]{:S(2)}) collective-permute-start(bf16[2,240,128]{2,1,0:T(8,128)(2,1)S(1)} %get-tuple-element.43), channel_id=1, source_target_pairs={{0,14},{1,15},{2,12},{3,13},{4,10},{5,11},{6,8},{7,9},{8,6},{9,7},... | collective-permute-start | bytes 368648 | tf_op jit(solution)/shard_map/ppermute | solution.py:564
  35.0 0.6 collective-permute-start.12
  35.5 1.7 %collective-permute-done.8.refs_7_ = bf16[2,240,128]{2,1,0:T(8,128)(2,1)S(1)} collective-permute-done((bf16[2,240,128]{2,1,0:T(8,128)(2,1)S(1)}, bf16[2,240,128]{2,1,0:T(8,128)(2,1)S(1)}, u32[]{:S(2)}, u32[]{:S(2)}) %collective-permute-start.8) | collective-permute-done | bytes 122912 | tf_op jit(solution)/shard_map/ppermute | solution.py:564
  37.3 2.3 %collective-permute-start.13 = (bf16[2,240,128]{2,1,0:T(8,128)(2,1)S(1)}, bf16[2,240,128]{2,1,0:T(8,128)(2,1)S(1)}, u32[]{:S(2)}, u32[]{:S(2)}) collective-permute-start(bf16[2,240,128]{2,1,0:T(8,128)(2,1)S(1)} %get-tuple-element.46), channel_id=1, source_target_pairs={{0,2},{1,3},{2,0},{3,1},{4,6},{5,7},{6,4},{7,5},{8,10},{9,11},{10,... | collective-permute-start | bytes 368648 | tf_op jit(solution)/shard_map/ppermute | solution.py:564
  39.6 0.6 collective-permute-start.14
  40.1 2.2 %collective-permute-start.15 = (bf16[2,240,128]{2,1,0:T(8,128)(2,1)S(1)}, bf16[2,240,128]{2,1,0:T(8,128)(2,1)S(1)}, u32[]{:S(2)}, u32[]{:S(2)}) collective-permute-start(bf16[2,240,128]{2,1,0:T(8,128)(2,1)S(1)} %get-tuple-element.48), channel_id=1, source_target_pairs={{0,3},{1,2},{2,1},{3,0},{4,7},{5,6},{6,5},{7,4},{8,11},{9,10},{10,... | collective-permute-start | bytes 368648 | tf_op jit(solution)/shard_map/ppermute | solution.py:564
  42.3 1.7 %early_differences.2 = (bf16[2,240,128]{2,1,0:T(8,128)(2,1)S(1)}, f32[2,5,4,4,56,128]{5,4,3,2,1,0:T(8,128)S(1)}) custom-call(s32[1]{0:T(128)} %bitcast.place.refs_0_, bf16[2,240,128]{2,1,0:T(8,128)(2,1)S(1)} %get-tuple-element.34.refs_0_, bf16[2,240,128]{2,1,0:T(8,128)(2,1)S(1)} %collective-permute-done.11.refs_1_.refs_10_, ...), custom_call_target="tpu_custom_call", output_to_operand_aliasing={{0}: (11, {})} | custom-call | flops 5000000 | bytes 4000000 | tf_op jit(solution)/shard_map/early_differences/pallas_call | solution.py:425
  44.0 6.6 %collective-permute-start.16 = (bf16[2,240,128]{2,1,0:T(8,128)(2,1)S(1)}, bf16[2,240,128]{2,1,0:T(8,128)(2,1)S(1)}, u32[]{:S(2)}, u32[]{:S(2)}) collective-permute-start(bf16[2,240,128]{2,1,0:T(8,128)(2,1)S(1)} %get-tuple-element.50), channel_id=1, source_target_pairs={{0,11},{1,10},{2,9},{3,8},{4,15},{5,14},{6,13},{7,12},{8,3},{9,2},... | collective-permute-start | bytes 368648 | tf_op jit(solution)/shard_map/ppermute | solution.py:564
  50.6 1.6 %collective-permute-done.15.refs_1_.refs_14_ = bf16[2,240,128]{2,1,0:T(8,128)(2,1)S(1)} collective-permute-done((bf16[2,240,128]{2,1,0:T(8,128)(2,1)S(1)}, bf16[2,240,128]{2,1,0:T(8,128)(2,1)S(1)}, u32[]{:S(2)}, u32[]{:S(2)}) %collective-permute-start.15) | collective-permute-done | bytes 122912 | tf_op jit(solution)/shard_map/ppermute | solution.py:564
  52.2 0.8 %early_differences.3.refs_17_ = f32[2,2,4,4,56,128]{5,4,3,2,1,0:T(8,128)S(1)} custom-call(s32[1]{0:T(128)} %bitcast.place.refs_0_, bf16[2,240,128]{2,1,0:T(8,128)(2,1)S(1)} %collective-permute-done.13.refs_0_.refs_12_, bf16[2,240,128]{2,1,0:T(8,128)(2,1)S(1)} %collective-permute-done.15.refs_1_.refs_14_, ...), custom_call_target="tpu_custom_call" | custom-call | flops 5000000 | bytes 4000000 | tf_op jit(solution)/shard_map/early_differences/pallas_call | solution.py:425
  53.0 5.9 %collective-permute-done.16.refs_15_ = bf16[2,240,128]{2,1,0:T(8,128)(2,1)S(1)} collective-permute-done((bf16[2,240,128]{2,1,0:T(8,128)(2,1)S(1)}, bf16[2,240,128]{2,1,0:T(8,128)(2,1)S(1)}, u32[]{:S(2)}, u32[]{:S(2)}) %collective-permute-start.16) | collective-permute-done | bytes 122912 | tf_op jit(solution)/shard_map/ppermute | solution.py:564
  58.9 3.3 %score.1 = (bf16[4,56,512]{2,1,0:T(8,128)(2,1)}, bf16[2,4,56,512]{3,2,1,0:T(8,128)(2,1)}) custom-call(s32[1]{0:T(128)} %bitcast.place.refs_0_, bf16[2,240,128]{2,1,0:T(8,128)(2,1)S(1)} %get-tuple-element.34.refs_0_, bf16[2,240,128]{2,1,0:T(8,128)(2,1)S(1)} %collective-permute-done.2.refs_8_.refs_1_, bf16[2,240,128]{2,1,0:T(8,128)(2,1)S(1)} %collective-permute-done.3.refs_2_, ...), custom_call_target="tpu_custom_call" | custom-call | tf_op jit(solution)/shard_map/score/pallas_call | solution.py:525
  (23 shorter events, 1.5 us)
Async XLA Ops:
  0.6 1.8 %copy-start.2 = (s32[16,2,3]{0,1,2:T(2,128)S(1)}, s32[16,2,3]{0,1,2:T(2,128)}, u32[]{:S(2)}) copy-start(s32[16,2,3]{0,1,2:T(2,128)} %param.6) | copy-start | bytes 1156
  2.3 5.4 %collective-permute-start.1 = (bf16[8,2,448,128]{3,2,1,0:T(8,128)(2,1)S(1)}, bf16[8,2,448,128]{3,2,1,0:T(8,128)(2,1)S(1)}, u32[]{:S(2)}, u32[]{:S(2)}) collective-permute-start(bf16[8,2,448,128]{3,2,1,0:T(8,128)(2,1)S(1)} %pack.1), channel_id=1, source_target_pairs={{0,1},{1,0},{2,3},{3,2},{4,5},{5,4},{6,7},{7,6},{8,9},{9,8},{10,11... | collective-permute-start | bytes 5505032 | tf_op jit(solution)/shard_map/ppermute | solution.py:558
  2.4 4.9 %copy-start.1 = (f32[32,896]{1,0:T(8,128)S(1)}, f32[32,896]{1,0:T(8,128)}, u32[]{:S(2)}) copy-start(f32[32,896]{1,0:T(8,128)} %smoothing.1) | copy-start | bytes 344068
  2.4 5.2 %collective-permute-start = (s32[3,2,16]{2,1,0:T(2,128)S(1)}, s32[3,2,16]{2,1,0:T(2,128)S(1)}, u32[]{:S(2)}, u32[]{:S(2)}) collective-permute-start(s32[3,2,16]{2,1,0:T(2,128)S(1)} %bitcast.11), channel_id=1, source_target_pairs={{0,1},{1,0},{2,3},{3,2},{4,5},{5,4},{6,7},{7,6},{8,9},{9,8},{10,11... | collective-permute-start | bytes 1160 | tf_op jit(solution)/shard_map/ppermute | solution.py:559
  11.2 9.2 %collective-permute-start.2 = (bf16[2,240,128]{2,1,0:T(8,128)(2,1)S(1)}, bf16[2,240,128]{2,1,0:T(8,128)(2,1)S(1)}, u32[]{:S(2)}, u32[]{:S(2)}) collective-permute-start(bf16[2,240,128]{2,1,0:T(8,128)(2,1)S(1)} %get-tuple-element.35), channel_id=1, source_target_pairs={{0,12},{1,13},{2,14},{3,15},{4,8},{5,9},{6,10},{7,11},{8,4},{9,5},... | collective-permute-start | bytes 368648 | tf_op jit(solution)/shard_map/ppermute | solution.py:564
  15.7 7.4 %collective-permute-start.3 = (bf16[2,240,128]{2,1,0:T(8,128)(2,1)S(1)}, bf16[2,240,128]{2,1,0:T(8,128)(2,1)S(1)}, u32[]{:S(2)}, u32[]{:S(2)}) collective-permute-start(bf16[2,240,128]{2,1,0:T(8,128)(2,1)S(1)} %get-tuple-element.36), channel_id=1, source_target_pairs={{0,4},{1,5},{2,6},{3,7},{4,0},{5,1},{6,2},{7,3},{8,12},{9,13},{10,... | collective-permute-start | bytes 368648 | tf_op jit(solution)/shard_map/ppermute | solution.py:564
  15.7 10.1 %collective-permute-start.4 = (bf16[2,240,128]{2,1,0:T(8,128)(2,1)S(1)}, bf16[2,240,128]{2,1,0:T(8,128)(2,1)S(1)}, u32[]{:S(2)}, u32[]{:S(2)}) collective-permute-start(bf16[2,240,128]{2,1,0:T(8,128)(2,1)S(1)} %get-tuple-element.37), channel_id=1, source_target_pairs={{0,8},{1,9},{2,10},{3,11},{4,12},{5,13},{6,14},{7,15},{8,0},{9,1},... | collective-permute-start | bytes 368648 | tf_op jit(solution)/shard_map/ppermute | solution.py:564
  16.1 13.6 %collective-permute-start.5 = (bf16[2,240,128]{2,1,0:T(8,128)(2,1)S(1)}, bf16[2,240,128]{2,1,0:T(8,128)(2,1)S(1)}, u32[]{:S(2)}, u32[]{:S(2)}) collective-permute-start(bf16[2,240,128]{2,1,0:T(8,128)(2,1)S(1)} %get-tuple-element.38), channel_id=1, source_target_pairs={{0,5},{1,4},{2,7},{3,6},{4,1},{5,0},{6,3},{7,2},{8,13},{9,12},{10,... | collective-permute-start | bytes 368648 | tf_op jit(solution)/shard_map/ppermute | solution.py:564
  18.0 12.5 %collective-permute-start.6 = (bf16[2,240,128]{2,1,0:T(8,128)(2,1)S(1)}, bf16[2,240,128]{2,1,0:T(8,128)(2,1)S(1)}, u32[]{:S(2)}, u32[]{:S(2)}) collective-permute-start(bf16[2,240,128]{2,1,0:T(8,128)(2,1)S(1)} %get-tuple-element.39), channel_id=1, source_target_pairs={{0,13},{1,12},{2,15},{3,14},{4,9},{5,8},{6,11},{7,10},{8,5},{9,4},... | collective-permute-start | bytes 368648 | tf_op jit(solution)/shard_map/ppermute | solution.py:564
  20.4 14.5 %collective-permute-start.7 = (bf16[2,240,128]{2,1,0:T(8,128)(2,1)S(1)}, bf16[2,240,128]{2,1,0:T(8,128)(2,1)S(1)}, u32[]{:S(2)}, u32[]{:S(2)}) collective-permute-start(bf16[2,240,128]{2,1,0:T(8,128)(2,1)S(1)} %get-tuple-element.40), channel_id=1, source_target_pairs={{0,6},{1,7},{2,4},{3,5},{4,2},{5,3},{6,0},{7,1},{8,14},{9,15},{10,... | collective-permute-start | bytes 368648 | tf_op jit(solution)/shard_map/ppermute | solution.py:564
  23.1 14.1 %collective-permute-start.8 = (bf16[2,240,128]{2,1,0:T(8,128)(2,1)S(1)}, bf16[2,240,128]{2,1,0:T(8,128)(2,1)S(1)}, u32[]{:S(2)}, u32[]{:S(2)}) collective-permute-start(bf16[2,240,128]{2,1,0:T(8,128)(2,1)S(1)} %get-tuple-element.41), channel_id=1, source_target_pairs={{0,9},{1,8},{2,11},{3,10},{4,13},{5,12},{6,15},{7,14},{8,1},{9,0},... | collective-permute-start | bytes 368648 | tf_op jit(solution)/shard_map/ppermute | solution.py:564
  25.8 13.8 %collective-permute-start.9 = (bf16[2,240,128]{2,1,0:T(8,128)(2,1)S(1)}, bf16[2,240,128]{2,1,0:T(8,128)(2,1)S(1)}, u32[]{:S(2)}, u32[]{:S(2)}) collective-permute-start(bf16[2,240,128]{2,1,0:T(8,128)(2,1)S(1)} %get-tuple-element.42), channel_id=1, source_target_pairs={{0,7},{1,6},{2,5},{3,4},{4,3},{5,2},{6,1},{7,0},{8,15},{9,14},{10,... | collective-permute-start | bytes 368648 | tf_op jit(solution)/shard_map/ppermute | solution.py:564
  29.7 10.4 %collective-permute-start.11 = (bf16[2,240,128]{2,1,0:T(8,128)(2,1)S(1)}, bf16[2,240,128]{2,1,0:T(8,128)(2,1)S(1)}, u32[]{:S(2)}, u32[]{:S(2)}) collective-permute-start(bf16[2,240,128]{2,1,0:T(8,128)(2,1)S(1)} %get-tuple-element.44), channel_id=1, source_target_pairs={{0,1},{1,0},{2,3},{3,2},{4,5},{5,4},{6,7},{7,6},{8,9},{9,8},{10,11... | collective-permute-start | bytes 368648 | tf_op jit(solution)/shard_map/ppermute | solution.py:564
  30.5 13.5 %collective-permute-start.10 = (bf16[2,240,128]{2,1,0:T(8,128)(2,1)S(1)}, bf16[2,240,128]{2,1,0:T(8,128)(2,1)S(1)}, u32[]{:S(2)}, u32[]{:S(2)}) collective-permute-start(bf16[2,240,128]{2,1,0:T(8,128)(2,1)S(1)} %get-tuple-element.43), channel_id=1, source_target_pairs={{0,14},{1,15},{2,12},{3,13},{4,10},{5,11},{6,8},{7,9},{8,6},{9,7},... | collective-permute-start | bytes 368648 | tf_op jit(solution)/shard_map/ppermute | solution.py:564
  35.0 18.1 %collective-permute-start.12 = (bf16[2,240,128]{2,1,0:T(8,128)(2,1)S(1)}, bf16[2,240,128]{2,1,0:T(8,128)(2,1)S(1)}, u32[]{:S(2)}, u32[]{:S(2)}) collective-permute-start(bf16[2,240,128]{2,1,0:T(8,128)(2,1)S(1)} %get-tuple-element.45), channel_id=1, source_target_pairs={{0,10},{1,11},{2,8},{3,9},{4,14},{5,15},{6,12},{7,13},{8,2},{9,3},... | collective-permute-start | bytes 368648 | tf_op jit(solution)/shard_map/ppermute | solution.py:564
  37.3 13.3 %collective-permute-start.13 = (bf16[2,240,128]{2,1,0:T(8,128)(2,1)S(1)}, bf16[2,240,128]{2,1,0:T(8,128)(2,1)S(1)}, u32[]{:S(2)}, u32[]{:S(2)}) collective-permute-start(bf16[2,240,128]{2,1,0:T(8,128)(2,1)S(1)} %get-tuple-element.46), channel_id=1, source_target_pairs={{0,2},{1,3},{2,0},{3,1},{4,6},{5,7},{6,4},{7,5},{8,10},{9,11},{10,... | collective-permute-start | bytes 368648 | tf_op jit(solution)/shard_map/ppermute | solution.py:564
  39.6 11.0 %collective-permute-start.14 = (bf16[2,240,128]{2,1,0:T(8,128)(2,1)S(1)}, bf16[2,240,128]{2,1,0:T(8,128)(2,1)S(1)}, u32[]{:S(2)}, u32[]{:S(2)}) collective-permute-start(bf16[2,240,128]{2,1,0:T(8,128)(2,1)S(1)} %get-tuple-element.47), channel_id=1, source_target_pairs={{0,15},{1,14},{2,13},{3,12},{4,11},{5,10},{6,9},{7,8},{8,7},{9,6},... | collective-permute-start | bytes 368648 | tf_op jit(solution)/shard_map/ppermute | solution.py:564
  40.1 12.0 %collective-permute-start.15 = (bf16[2,240,128]{2,1,0:T(8,128)(2,1)S(1)}, bf16[2,240,128]{2,1,0:T(8,128)(2,1)S(1)}, u32[]{:S(2)}, u32[]{:S(2)}) collective-permute-start(bf16[2,240,128]{2,1,0:T(8,128)(2,1)S(1)} %get-tuple-element.48), channel_id=1, source_target_pairs={{0,3},{1,2},{2,1},{3,0},{4,7},{5,6},{6,5},{7,4},{8,11},{9,10},{10,... | collective-permute-start | bytes 368648 | tf_op jit(solution)/shard_map/ppermute | solution.py:564
  42.3 16.6 %copy-start = (bf16[4,512,56]{1,2,0:T(8,128)(2,1)S(1)}, bf16[4,512,56]{1,2,0:T(8,128)(2,1)}, u32[]{:S(2)}) copy-start(bf16[4,512,56]{1,2,0:T(8,128)(2,1)} %param.9) | copy-start | bytes 688132
  44.0 14.9 %collective-permute-start.16 = (bf16[2,240,128]{2,1,0:T(8,128)(2,1)S(1)}, bf16[2,240,128]{2,1,0:T(8,128)(2,1)S(1)}, u32[]{:S(2)}, u32[]{:S(2)}) collective-permute-start(bf16[2,240,128]{2,1,0:T(8,128)(2,1)S(1)} %get-tuple-element.50), channel_id=1, source_target_pairs={{0,11},{1,10},{2,9},{3,8},{4,15},{5,14},{6,13},{7,12},{8,3},{9,2},... | collective-permute-start | bytes 368648 | tf_op jit(solution)/shard_map/ppermute | solution.py:564

commit v14 on v12

--- a/solution.py
+++ b/solution.py
@@ -14,6 +14,7 @@
 ROWS = 32
 COLS = 896
 PAIRS = ROWS // 2
+PITCH = PAIRS + 1
 LINES = FIELDS * ROWS * PATCH // 128
 LANES = 128
 TILES = COLS // LANES
@@ -21,7 +22,7 @@
 MID = 0.11
 VMEM = 40 * 1024 * 1024
 PACK_VMEM = 52 * 1024 * 1024
-MOST_VMEM = 48 * 1024 * 1024
+MOST_VMEM = 47 * 1024 * 1024
 
 
 def round_up(value, step):
@@ -66,7 +67,7 @@
 
 
 def weight_tile(weights, kind, t):
-    return weights[t, pl.ds(pl.multiple_of(kind * PAIRS, PAIRS), PAIRS), :]
+    return weights[t, pl.ds(kind * PITCH, PAIRS), :]
 
 
 SLOTS = TILES + 2
@@ -180,7 +181,7 @@
             at = COLS * k + LANES * t
             for low in range(0, kinds, 8):
                 count = min(8, kinds - low)
-                weights[t, pl.ds(PAIRS * low + k, count, stride=PAIRS), :] = table[
+                weights[t, pl.ds(PITCH * low + k, count, stride=PITCH), :] = table[
                     low : low + count, at : at + LANES
                 ]
 
@@ -225,7 +226,7 @@
         functools.partial(own_kernel, z),
         out_shape=[
             *[jax.ShapeDtypeStruct((z.block, 2, TILES, PAIRS, LANES), jnp.float32)] * (FIELDS + 1),
-            jax.ShapeDtypeStruct((TILES, kinds * PAIRS, LANES), jnp.float32),
+            jax.ShapeDtypeStruct((TILES, kinds * PITCH, LANES), jnp.float32),
         ],
         in_specs=[smem, smem, hbm, hbm],
         out_specs=[vmem] * (FIELDS + 2),

time: 61.9 us -> 61.9 us (level)
  no operation moved by 1% of the time
where the time goes in v14:
time: 61.9 us; the launch traced here: 61.7 us
  starting transfers between devices  32.1 us (52%)
  Pallas kernels  15.3 us (25%)
  waiting for transfers between devices  13.6 us (22%)
  between operations  0.75 us (1%)
    ppermute x15, starting transfers between devices, swapped(): lax.ppermute(block, 'region', [(i, i ^ offset) for i in range(z.regions)])  31.5 us
    ppermute x15, waiting for transfers between devices, swapped(): lax.ppermute(block, 'region', [(i, i ^ offset) for i in range(z.regions)])  13.6 us
    pallas_call x1, Pallas kernels, own_share(): pl.pallas_call(functools.partial(own_kernel, z), out_shape=[*[jax.ShapeDt...  3.83 us
    pallas_call x1, Pallas kernels, join(): pl.pallas_call(functools.partial(join_kernel, z), out_shape=[jax.ShapeDty...  3.6 us
    pallas_call x1, Pallas kernels, score(): pl.pallas_call(functools.partial(score_kernel, z), out_shape=[jax.ShapeDt...  3.35 us
    pallas_call x2, Pallas kernels, early_differences(): pl.pallas_call(functools.partial(early_kernel, z, samples), out_shape=[ja...  2.5 us
    pallas_call x1, Pallas kernels, pack(): pl.pallas_call(functools.partial(pack_kernel, z), out_shape=[shape] * (z....  1.7 us
  transfers between devices with their start and end apart: 17, of which 7 were waited for; matrix products, arithmetic and copies ran while one was open for 0% of the time, Pallas kernels for 11%

profile of v14, /device:TPU:1, one launch (start us, length us, event | category | flops | bytes accessed | tf_op | source)
XLA Modules:
  0.0 61.7 jit_solution(1816503410820336205)
XLA Ops:
  0.7 1.7 %pack.1 = bf16[8,2,448,128]{3,2,1,0:T(8,128)(2,1)S(1)} custom-call(s32[1]{0:T(128)} %bitcast.place.refs_0_, bf16[16,2,448,128]{3,2,1,0:T(8,128)(2,1)} %bitcast.14), custom_call_target="tpu_custom_call" | custom-call | tf_op jit(solution)/shard_map/pack/pallas_call | solution.py:155
  2.9 3.8 %own_share.1 = (f32[8,2,7,16,128]{4,3,2,1,0:T(8,128)S(1)}, f32[8,2,7,16,128]{4,3,2,1,0:T(8,128)S(1)}, f32[8,2,7,16,128]{4,3,2,1,0:T(8,128)S(1)}, f32[8,2,7,16,12...) custom-call(s32[1]{0:T(128)} %bitcast.place.refs_0_, s32[3,2,16]{2,1,0:T(2,128)S(1)} %bitcast.12, ...), custom_call_target="tpu_custom_call" | custom-call | flops 5000000 | bytes 8000000 | tf_op jit(solution)/shard_map/own_share/pallas_call | solution.py:225
  7.1 3.6 %join.1 = (bf16[2,240,128]{2,1,0:T(8,128)(2,1)S(1)}, bf16[2,240,128]{2,1,0:T(8,128)(2,1)S(1)}, bf16[2,240,128]{2,1,0:T(8,128)(2,1)S(1)}, bf16[2,240,128]{2,1,0:T...) custom-call(s32[1]{0:T(128)} %bitcast.place.refs_0_, ...), custom_call_target="tpu_custom_call" | custom-call | flops 5000000 | bytes 8000000 | tf_op jit(solution)/shard_map/join/pallas_call | solution.py:338
  10.7 4.5 %collective-permute-start.2 = (bf16[2,240,128]{2,1,0:T(8,128)(2,1)S(1)}, bf16[2,240,128]{2,1,0:T(8,128)(2,1)S(1)}, u32[]{:S(2)}, u32[]{:S(2)}) collective-permute-start(bf16[2,240,128]{2,1,0:T(8,128)(2,1)S(1)} %get-tuple-element.35), channel_id=1, source_target_pairs={{0,12},{1,13},{2,14},{3,15},{4,8},{5,9},{6,10},{7,11},{8,4},{9,5},... | collective-permute-start | bytes 368648 | tf_op jit(solution)/shard_map/ppermute | solution.py:557
  15.6 2.0 %collective-permute-start.5 = (bf16[2,240,128]{2,1,0:T(8,128)(2,1)S(1)}, bf16[2,240,128]{2,1,0:T(8,128)(2,1)S(1)}, u32[]{:S(2)}, u32[]{:S(2)}) collective-permute-start(bf16[2,240,128]{2,1,0:T(8,128)(2,1)S(1)} %get-tuple-element.38), channel_id=1, source_target_pairs={{0,5},{1,4},{2,7},{3,6},{4,1},{5,0},{6,3},{7,2},{8,13},{9,12},{10,... | collective-permute-start | bytes 368648 | tf_op jit(solution)/shard_map/ppermute | solution.py:557
  17.5 2.4 %collective-permute-start.6 = (bf16[2,240,128]{2,1,0:T(8,128)(2,1)S(1)}, bf16[2,240,128]{2,1,0:T(8,128)(2,1)S(1)}, u32[]{:S(2)}, u32[]{:S(2)}) collective-permute-start(bf16[2,240,128]{2,1,0:T(8,128)(2,1)S(1)} %get-tuple-element.39), channel_id=1, source_target_pairs={{0,13},{1,12},{2,15},{3,14},{4,9},{5,8},{6,11},{7,10},{8,5},{9,4},... | collective-permute-start | bytes 368648 | tf_op jit(solution)/shard_map/ppermute | solution.py:557
  19.9 1.4 %collective-permute-start.7 = (bf16[2,240,128]{2,1,0:T(8,128)(2,1)S(1)}, bf16[2,240,128]{2,1,0:T(8,128)(2,1)S(1)}, u32[]{:S(2)}, u32[]{:S(2)}) collective-permute-start(bf16[2,240,128]{2,1,0:T(8,128)(2,1)S(1)} %get-tuple-element.40), channel_id=1, source_target_pairs={{0,6},{1,7},{2,4},{3,5},{4,2},{5,3},{6,0},{7,1},{8,14},{9,15},{10,... | collective-permute-start | bytes 368648 | tf_op jit(solution)/shard_map/ppermute | solution.py:557
  21.2 1.4 %collective-permute-done.3.refs_2_ = bf16[2,240,128]{2,1,0:T(8,128)(2,1)S(1)} collective-permute-done((bf16[2,240,128]{2,1,0:T(8,128)(2,1)S(1)}, bf16[2,240,128]{2,1,0:T(8,128)(2,1)S(1)}, u32[]{:S(2)}, u32[]{:S(2)}) %collective-permute-start.3) | collective-permute-done | bytes 122912 | tf_op jit(solution)/shard_map/ppermute | solution.py:557
  22.6 2.4 %collective-permute-start.8 = (bf16[2,240,128]{2,1,0:T(8,128)(2,1)S(1)}, bf16[2,240,128]{2,1,0:T(8,128)(2,1)S(1)}, u32[]{:S(2)}, u32[]{:S(2)}) collective-permute-start(bf16[2,240,128]{2,1,0:T(8,128)(2,1)S(1)} %get-tuple-element.41), channel_id=1, source_target_pairs={{0,9},{1,8},{2,11},{3,10},{4,13},{5,12},{6,15},{7,14},{8,1},{9,0},... | collective-permute-start | bytes 368648 | tf_op jit(solution)/shard_map/ppermute | solution.py:557
  25.3 1.9 %collective-permute-start.9 = (bf16[2,240,128]{2,1,0:T(8,128)(2,1)S(1)}, bf16[2,240,128]{2,1,0:T(8,128)(2,1)S(1)}, u32[]{:S(2)}, u32[]{:S(2)}) collective-permute-start(bf16[2,240,128]{2,1,0:T(8,128)(2,1)S(1)} %get-tuple-element.42), channel_id=1, source_target_pairs={{0,7},{1,6},{2,5},{3,4},{4,3},{5,2},{6,1},{7,0},{8,15},{9,14},{10,... | collective-permute-start | bytes 368648 | tf_op jit(solution)/shard_map/ppermute | solution.py:557
  27.2 2.0 %collective-permute-done.5.refs_3_.refs_4_ = bf16[2,240,128]{2,1,0:T(8,128)(2,1)S(1)} collective-permute-done((bf16[2,240,128]{2,1,0:T(8,128)(2,1)S(1)}, bf16[2,240,128]{2,1,0:T(8,128)(2,1)S(1)}, u32[]{:S(2)}, u32[]{:S(2)}) %collective-permute-start.5) | collective-permute-done | bytes 122912 | tf_op jit(solution)/shard_map/ppermute | solution.py:557
  29.2 0.8 %collective-permute-done.6.refs_9_.refs_5_ = bf16[2,240,128]{2,1,0:T(8,128)(2,1)S(1)} collective-permute-done((bf16[2,240,128]{2,1,0:T(8,128)(2,1)S(1)}, bf16[2,240,128]{2,1,0:T(8,128)(2,1)S(1)}, u32[]{:S(2)}, u32[]{:S(2)}) %collective-permute-start.6) | collective-permute-done | bytes 122912 | tf_op jit(solution)/shard_map/ppermute | solution.py:557
  30.0 4.5 %collective-permute-start.10 = (bf16[2,240,128]{2,1,0:T(8,128)(2,1)S(1)}, bf16[2,240,128]{2,1,0:T(8,128)(2,1)S(1)}, u32[]{:S(2)}, u32[]{:S(2)}) collective-permute-start(bf16[2,240,128]{2,1,0:T(8,128)(2,1)S(1)} %get-tuple-element.43), channel_id=1, source_target_pairs={{0,14},{1,15},{2,12},{3,13},{4,10},{5,11},{6,8},{7,9},{8,6},{9,7},... | collective-permute-start | bytes 368648 | tf_op jit(solution)/shard_map/ppermute | solution.py:557
  34.4 0.6 collective-permute-start.12
  35.0 1.7 %collective-permute-done.8.refs_7_ = bf16[2,240,128]{2,1,0:T(8,128)(2,1)S(1)} collective-permute-done((bf16[2,240,128]{2,1,0:T(8,128)(2,1)S(1)}, bf16[2,240,128]{2,1,0:T(8,128)(2,1)S(1)}, u32[]{:S(2)}, u32[]{:S(2)}) %collective-permute-start.8) | collective-permute-done | bytes 122912 | tf_op jit(solution)/shard_map/ppermute | solution.py:557
  36.7 2.3 %collective-permute-start.13 = (bf16[2,240,128]{2,1,0:T(8,128)(2,1)S(1)}, bf16[2,240,128]{2,1,0:T(8,128)(2,1)S(1)}, u32[]{:S(2)}, u32[]{:S(2)}) collective-permute-start(bf16[2,240,128]{2,1,0:T(8,128)(2,1)S(1)} %get-tuple-element.46), channel_id=1, source_target_pairs={{0,2},{1,3},{2,0},{3,1},{4,6},{5,7},{6,4},{7,5},{8,10},{9,11},{10,... | collective-permute-start | bytes 368648 | tf_op jit(solution)/shard_map/ppermute | solution.py:557
  39.1 0.6 collective-permute-start.14
  39.6 2.2 %collective-permute-start.15 = (bf16[2,240,128]{2,1,0:T(8,128)(2,1)S(1)}, bf16[2,240,128]{2,1,0:T(8,128)(2,1)S(1)}, u32[]{:S(2)}, u32[]{:S(2)}) collective-permute-start(bf16[2,240,128]{2,1,0:T(8,128)(2,1)S(1)} %get-tuple-element.48), channel_id=1, source_target_pairs={{0,3},{1,2},{2,1},{3,0},{4,7},{5,6},{6,5},{7,4},{8,11},{9,10},{10,... | collective-permute-start | bytes 368648 | tf_op jit(solution)/shard_map/ppermute | solution.py:557
  41.8 1.7 %early_differences.2 = (bf16[2,240,128]{2,1,0:T(8,128)(2,1)S(1)}, f32[2,5,4,4,56,128]{5,4,3,2,1,0:T(8,128)S(1)}) custom-call(s32[1]{0:T(128)} %bitcast.place.refs_0_, bf16[2,240,128]{2,1,0:T(8,128)(2,1)S(1)} %get-tuple-element.34.refs_0_, bf16[2,240,128]{2,1,0:T(8,128)(2,1)S(1)} %collective-permute-done.11.refs_1_.refs_10_, ...), custom_call_target="tpu_custom_call", output_to_operand_aliasing={{0}: (11, {})} | custom-call | flops 5000000 | bytes 4000000 | tf_op jit(solution)/shard_map/early_differences/pallas_call | solution.py:418
  43.5 6.6 %collective-permute-start.16 = (bf16[2,240,128]{2,1,0:T(8,128)(2,1)S(1)}, bf16[2,240,128]{2,1,0:T(8,128)(2,1)S(1)}, u32[]{:S(2)}, u32[]{:S(2)}) collective-permute-start(bf16[2,240,128]{2,1,0:T(8,128)(2,1)S(1)} %get-tuple-element.50), channel_id=1, source_target_pairs={{0,11},{1,10},{2,9},{3,8},{4,15},{5,14},{6,13},{7,12},{8,3},{9,2},... | collective-permute-start | bytes 368648 | tf_op jit(solution)/shard_map/ppermute | solution.py:557
  50.1 1.6 %collective-permute-done.15.refs_1_.refs_14_ = bf16[2,240,128]{2,1,0:T(8,128)(2,1)S(1)} collective-permute-done((bf16[2,240,128]{2,1,0:T(8,128)(2,1)S(1)}, bf16[2,240,128]{2,1,0:T(8,128)(2,1)S(1)}, u32[]{:S(2)}, u32[]{:S(2)}) %collective-permute-start.15) | collective-permute-done | bytes 122912 | tf_op jit(solution)/shard_map/ppermute | solution.py:557
  51.7 0.8 %early_differences.3.refs_17_ = f32[2,2,4,4,56,128]{5,4,3,2,1,0:T(8,128)S(1)} custom-call(s32[1]{0:T(128)} %bitcast.place.refs_0_, bf16[2,240,128]{2,1,0:T(8,128)(2,1)S(1)} %collective-permute-done.13.refs_0_.refs_12_, bf16[2,240,128]{2,1,0:T(8,128)(2,1)S(1)} %collective-permute-done.15.refs_1_.refs_14_, ...), custom_call_target="tpu_custom_call" | custom-call | flops 5000000 | bytes 4000000 | tf_op jit(solution)/shard_map/early_differences/pallas_call | solution.py:418
  52.5 5.9 %collective-permute-done.16.refs_15_ = bf16[2,240,128]{2,1,0:T(8,128)(2,1)S(1)} collective-permute-done((bf16[2,240,128]{2,1,0:T(8,128)(2,1)S(1)}, bf16[2,240,128]{2,1,0:T(8,128)(2,1)S(1)}, u32[]{:S(2)}, u32[]{:S(2)}) %collective-permute-start.16) | collective-permute-done | bytes 122912 | tf_op jit(solution)/shard_map/ppermute | solution.py:557
  58.4 3.3 %score.1 = (bf16[4,56,512]{2,1,0:T(8,128)(2,1)}, bf16[2,4,56,512]{3,2,1,0:T(8,128)(2,1)}) custom-call(s32[1]{0:T(128)} %bitcast.place.refs_0_, bf16[2,240,128]{2,1,0:T(8,128)(2,1)S(1)} %get-tuple-element.34.refs_0_, bf16[2,240,128]{2,1,0:T(8,128)(2,1)S(1)} %collective-permute-done.2.refs_8_.refs_1_, bf16[2,240,128]{2,1,0:T(8,128)(2,1)S(1)} %collective-permute-done.3.refs_2_, ...), custom_call_target="tpu_custom_call" | custom-call | tf_op jit(solution)/shard_map/score/pallas_call | solution.py:518
  (25 shorter events, 1.5 us)
Async XLA Ops:
  0.6 1.9 %copy-start.3 = (s32[16,2,3]{0,1,2:T(2,128)S(1)}, s32[16,2,3]{0,1,2:T(2,128)}, u32[]{:S(2)}) copy-start(s32[16,2,3]{0,1,2:T(2,128)} %param.6) | copy-start | bytes 1156
  0.6 2.3 %copy-start = (f32[14,14336]{1,0:T(8,128)S(1)}, f32[14,14336]{1,0:T(8,128)}, u32[]{:S(2)}) copy-start(f32[14,14336]{1,0:T(8,128)} %table_hbm.1) | copy-start | bytes 2408452
  2.4 4.7 %collective-permute-start.1 = (bf16[8,2,448,128]{3,2,1,0:T(8,128)(2,1)S(1)}, bf16[8,2,448,128]{3,2,1,0:T(8,128)(2,1)S(1)}, u32[]{:S(2)}, u32[]{:S(2)}) collective-permute-start(bf16[8,2,448,128]{3,2,1,0:T(8,128)(2,1)S(1)} %pack.1), channel_id=1, source_target_pairs={{0,1},{1,0},{2,3},{3,2},{4,5},{5,4},{6,7},{7,6},{8,9},{9,8},{10,11... | collective-permute-start | bytes 5505032 | tf_op jit(solution)/shard_map/ppermute | solution.py:551
  2.5 4.3 %copy-start.2 = (f32[32,896]{1,0:T(8,128)S(1)}, f32[32,896]{1,0:T(8,128)}, u32[]{:S(2)}) copy-start(f32[32,896]{1,0:T(8,128)} %smoothing.1) | copy-start | bytes 344068
  2.5 4.6 %collective-permute-start = (s32[3,2,16]{2,1,0:T(2,128)S(1)}, s32[3,2,16]{2,1,0:T(2,128)S(1)}, u32[]{:S(2)}, u32[]{:S(2)}) collective-permute-start(s32[3,2,16]{2,1,0:T(2,128)S(1)} %bitcast.11), channel_id=1, source_target_pairs={{0,1},{1,0},{2,3},{3,2},{4,5},{5,4},{6,7},{7,6},{8,9},{9,8},{10,11... | collective-permute-start | bytes 1160 | tf_op jit(solution)/shard_map/ppermute | solution.py:552
  10.7 9.2 %collective-permute-start.2 = (bf16[2,240,128]{2,1,0:T(8,128)(2,1)S(1)}, bf16[2,240,128]{2,1,0:T(8,128)(2,1)S(1)}, u32[]{:S(2)}, u32[]{:S(2)}) collective-permute-start(bf16[2,240,128]{2,1,0:T(8,128)(2,1)S(1)} %get-tuple-element.35), channel_id=1, source_target_pairs={{0,12},{1,13},{2,14},{3,15},{4,8},{5,9},{6,10},{7,11},{8,4},{9,5},... | collective-permute-start | bytes 368648 | tf_op jit(solution)/shard_map/ppermute | solution.py:557
  15.2 7.4 %collective-permute-start.3 = (bf16[2,240,128]{2,1,0:T(8,128)(2,1)S(1)}, bf16[2,240,128]{2,1,0:T(8,128)(2,1)S(1)}, u32[]{:S(2)}, u32[]{:S(2)}) collective-permute-start(bf16[2,240,128]{2,1,0:T(8,128)(2,1)S(1)} %get-tuple-element.36), channel_id=1, source_target_pairs={{0,4},{1,5},{2,6},{3,7},{4,0},{5,1},{6,2},{7,3},{8,12},{9,13},{10,... | collective-permute-start | bytes 368648 | tf_op jit(solution)/shard_map/ppermute | solution.py:557
  15.2 10.1 %collective-permute-start.4 = (bf16[2,240,128]{2,1,0:T(8,128)(2,1)S(1)}, bf16[2,240,128]{2,1,0:T(8,128)(2,1)S(1)}, u32[]{:S(2)}, u32[]{:S(2)}) collective-permute-start(bf16[2,240,128]{2,1,0:T(8,128)(2,1)S(1)} %get-tuple-element.37), channel_id=1, source_target_pairs={{0,8},{1,9},{2,10},{3,11},{4,12},{5,13},{6,14},{7,15},{8,0},{9,1},... | collective-permute-start | bytes 368648 | tf_op jit(solution)/shard_map/ppermute | solution.py:557
  15.6 13.6 %collective-permute-start.5 = (bf16[2,240,128]{2,1,0:T(8,128)(2,1)S(1)}, bf16[2,240,128]{2,1,0:T(8,128)(2,1)S(1)}, u32[]{:S(2)}, u32[]{:S(2)}) collective-permute-start(bf16[2,240,128]{2,1,0:T(8,128)(2,1)S(1)} %get-tuple-element.38), channel_id=1, source_target_pairs={{0,5},{1,4},{2,7},{3,6},{4,1},{5,0},{6,3},{7,2},{8,13},{9,12},{10,... | collective-permute-start | bytes 368648 | tf_op jit(solution)/shard_map/ppermute | solution.py:557
  17.5 12.5 %collective-permute-start.6 = (bf16[2,240,128]{2,1,0:T(8,128)(2,1)S(1)}, bf16[2,240,128]{2,1,0:T(8,128)(2,1)S(1)}, u32[]{:S(2)}, u32[]{:S(2)}) collective-permute-start(bf16[2,240,128]{2,1,0:T(8,128)(2,1)S(1)} %get-tuple-element.39), channel_id=1, source_target_pairs={{0,13},{1,12},{2,15},{3,14},{4,9},{5,8},{6,11},{7,10},{8,5},{9,4},... | collective-permute-start | bytes 368648 | tf_op jit(solution)/shard_map/ppermute | solution.py:557
  19.9 14.5 %collective-permute-start.7 = (bf16[2,240,128]{2,1,0:T(8,128)(2,1)S(1)}, bf16[2,240,128]{2,1,0:T(8,128)(2,1)S(1)}, u32[]{:S(2)}, u32[]{:S(2)}) collective-permute-start(bf16[2,240,128]{2,1,0:T(8,128)(2,1)S(1)} %get-tuple-element.40), channel_id=1, source_target_pairs={{0,6},{1,7},{2,4},{3,5},{4,2},{5,3},{6,0},{7,1},{8,14},{9,15},{10,... | collective-permute-start | bytes 368648 | tf_op jit(solution)/shard_map/ppermute | solution.py:557
  22.6 14.1 %collective-permute-start.8 = (bf16[2,240,128]{2,1,0:T(8,128)(2,1)S(1)}, bf16[2,240,128]{2,1,0:T(8,128)(2,1)S(1)}, u32[]{:S(2)}, u32[]{:S(2)}) collective-permute-start(bf16[2,240,128]{2,1,0:T(8,128)(2,1)S(1)} %get-tuple-element.41), channel_id=1, source_target_pairs={{0,9},{1,8},{2,11},{3,10},{4,13},{5,12},{6,15},{7,14},{8,1},{9,0},... | collective-permute-start | bytes 368648 | tf_op jit(solution)/shard_map/ppermute | solution.py:557
  25.3 13.8 %collective-permute-start.9 = (bf16[2,240,128]{2,1,0:T(8,128)(2,1)S(1)}, bf16[2,240,128]{2,1,0:T(8,128)(2,1)S(1)}, u32[]{:S(2)}, u32[]{:S(2)}) collective-permute-start(bf16[2,240,128]{2,1,0:T(8,128)(2,1)S(1)} %get-tuple-element.42), channel_id=1, source_target_pairs={{0,7},{1,6},{2,5},{3,4},{4,3},{5,2},{6,1},{7,0},{8,15},{9,14},{10,... | collective-permute-start | bytes 368648 | tf_op jit(solution)/shard_map/ppermute | solution.py:557
  29.2 10.4 %collective-permute-start.11 = (bf16[2,240,128]{2,1,0:T(8,128)(2,1)S(1)}, bf16[2,240,128]{2,1,0:T(8,128)(2,1)S(1)}, u32[]{:S(2)}, u32[]{:S(2)}) collective-permute-start(bf16[2,240,128]{2,1,0:T(8,128)(2,1)S(1)} %get-tuple-element.44), channel_id=1, source_target_pairs={{0,1},{1,0},{2,3},{3,2},{4,5},{5,4},{6,7},{7,6},{8,9},{9,8},{10,11... | collective-permute-start | bytes 368648 | tf_op jit(solution)/shard_map/ppermute | solution.py:557
  30.0 13.5 %collective-permute-start.10 = (bf16[2,240,128]{2,1,0:T(8,128)(2,1)S(1)}, bf16[2,240,128]{2,1,0:T(8,128)(2,1)S(1)}, u32[]{:S(2)}, u32[]{:S(2)}) collective-permute-start(bf16[2,240,128]{2,1,0:T(8,128)(2,1)S(1)} %get-tuple-element.43), channel_id=1, source_target_pairs={{0,14},{1,15},{2,12},{3,13},{4,10},{5,11},{6,8},{7,9},{8,6},{9,7},... | collective-permute-start | bytes 368648 | tf_op jit(solution)/shard_map/ppermute | solution.py:557
  34.4 18.1 %collective-permute-start.12 = (bf16[2,240,128]{2,1,0:T(8,128)(2,1)S(1)}, bf16[2,240,128]{2,1,0:T(8,128)(2,1)S(1)}, u32[]{:S(2)}, u32[]{:S(2)}) collective-permute-start(bf16[2,240,128]{2,1,0:T(8,128)(2,1)S(1)} %get-tuple-element.45), channel_id=1, source_target_pairs={{0,10},{1,11},{2,8},{3,9},{4,14},{5,15},{6,12},{7,13},{8,2},{9,3},... | collective-permute-start | bytes 368648 | tf_op jit(solution)/shard_map/ppermute | solution.py:557
  36.7 13.3 %collective-permute-start.13 = (bf16[2,240,128]{2,1,0:T(8,128)(2,1)S(1)}, bf16[2,240,128]{2,1,0:T(8,128)(2,1)S(1)}, u32[]{:S(2)}, u32[]{:S(2)}) collective-permute-start(bf16[2,240,128]{2,1,0:T(8,128)(2,1)S(1)} %get-tuple-element.46), channel_id=1, source_target_pairs={{0,2},{1,3},{2,0},{3,1},{4,6},{5,7},{6,4},{7,5},{8,10},{9,11},{10,... | collective-permute-start | bytes 368648 | tf_op jit(solution)/shard_map/ppermute | solution.py:557
  39.1 11.0 %collective-permute-start.14 = (bf16[2,240,128]{2,1,0:T(8,128)(2,1)S(1)}, bf16[2,240,128]{2,1,0:T(8,128)(2,1)S(1)}, u32[]{:S(2)}, u32[]{:S(2)}) collective-permute-start(bf16[2,240,128]{2,1,0:T(8,128)(2,1)S(1)} %get-tuple-element.47), channel_id=1, source_target_pairs={{0,15},{1,14},{2,13},{3,12},{4,11},{5,10},{6,9},{7,8},{8,7},{9,6},... | collective-permute-start | bytes 368648 | tf_op jit(solution)/shard_map/ppermute | solution.py:557
  39.6 12.0 %collective-permute-start.15 = (bf16[2,240,128]{2,1,0:T(8,128)(2,1)S(1)}, bf16[2,240,128]{2,1,0:T(8,128)(2,1)S(1)}, u32[]{:S(2)}, u32[]{:S(2)}) collective-permute-start(bf16[2,240,128]{2,1,0:T(8,128)(2,1)S(1)} %get-tuple-element.48), channel_id=1, source_target_pairs={{0,3},{1,2},{2,1},{3,0},{4,7},{5,6},{6,5},{7,4},{8,11},{9,10},{10,... | collective-permute-start | bytes 368648 | tf_op jit(solution)/shard_map/ppermute | solution.py:557
  41.8 16.6 %copy-start.1 = (bf16[4,512,56]{1,2,0:T(8,128)(2,1)S(1)}, bf16[4,512,56]{1,2,0:T(8,128)(2,1)}, u32[]{:S(2)}) copy-start(bf16[4,512,56]{1,2,0:T(8,128)(2,1)} %param.9) | copy-start | bytes 688132
  43.5 14.9 %collective-permute-start.16 = (bf16[2,240,128]{2,1,0:T(8,128)(2,1)S(1)}, bf16[2,240,128]{2,1,0:T(8,128)(2,1)S(1)}, u32[]{:S(2)}, u32[]{:S(2)}) collective-permute-start(bf16[2,240,128]{2,1,0:T(8,128)(2,1)S(1)} %get-tuple-element.50), channel_id=1, source_target_pairs={{0,11},{1,10},{2,9},{3,8},{4,15},{5,14},{6,13},{7,12},{8,3},{9,2},... | collective-permute-start | bytes 368648 | tf_op jit(solution)/shard_map/ppermute | solution.py:557

commit v15 on v12

--- a/solution.py
+++ b/solution.py
@@ -31,8 +31,8 @@
 def swap_order(regions):
     half, quarter = regions // 2, regions // 4
     far = [offset for i in range(quarter) for offset in (half + quarter + i, half + i)]
-    near = list(range(quarter, half)) + list(range(1, quarter))
-    return [0] + [item for pair in zip(far, near + [None]) for item in pair if item is not None]
+    near = list(range(1, half))
+    return [0] + [item for pair in zip(near + [None], far) for item in pair if item is not None]
 
 
 class Sizes:

time: 61.9 us -> 63.2 us (1.021)
  starting transfers between devices: 31.9 us -> 34.9 us
  waiting for transfers between devices: 13.8 us -> 11.4 us
    ppermute x15, starting transfers between devices: 31.3 us -> 34.3 us  [swapped(): lax.ppermute(block, 'region', [(i, i ^ offset) for i in range(z.regions)])]
    ppermute x15, waiting for transfers between devices: 13.8 us -> 11.4 us  [swapped(): lax.ppermute(block, 'region', [(i, i ^ offset) for i in range(z.regions)])]
  transfers between devices with their start and end apart: 17 -> 17, of which waited for: 7 -> 3; matrix products, arithmetic and copies ran while one was open for 0% -> 0% of each run, Pallas kernels for 11% -> 11%
where the time goes in v15:
time: 63.2 us; the launch traced here: 62.9 us
  starting transfers between devices  34.9 us (55%)
  Pallas kernels  15.9 us (25%)
  waiting for transfers between devices  11.4 us (18%)
  between operations  0.75 us (1%)
    ppermute x15, starting transfers between devices, swapped(): lax.ppermute(block, 'region', [(i, i ^ offset) for i in range(z.regions)])  34.3 us
    ppermute x15, waiting for transfers between devices, swapped(): lax.ppermute(block, 'region', [(i, i ^ offset) for i in range(z.regions)])  11.4 us
    pallas_call x1, Pallas kernels, own_share(): pl.pallas_call(functools.partial(own_kernel, z), out_shape=[*[jax.ShapeDt...  4.21 us
    pallas_call x1, Pallas kernels, join(): pl.pallas_call(functools.partial(join_kernel, z), out_shape=[jax.ShapeDty...  3.9 us
    pallas_call x1, Pallas kernels, score(): pl.pallas_call(functools.partial(score_kernel, z), out_shape=[jax.ShapeDt...  3.35 us
    pallas_call x2, Pallas kernels, early_differences(): pl.pallas_call(functools.partial(early_kernel, z, samples), out_shape=[ja...  2.5 us
    pallas_call x1, Pallas kernels, pack(): pl.pallas_call(functools.partial(pack_kernel, z), out_shape=[shape] * (z....  1.63 us
  transfers between devices with their start and end apart: 17, of which 3 were waited for; matrix products, arithmetic and copies ran while one was open for 0% of the time, Pallas kernels for 11%

profile of v15, /device:TPU:1, one launch (start us, length us, event | category | flops | bytes accessed | tf_op | source)
XLA Modules:
  0.0 62.9 jit_solution(2899407387186587189)
XLA Ops:
  0.6 1.6 %pack.1 = bf16[8,2,448,128]{3,2,1,0:T(8,128)(2,1)S(1)} custom-call(s32[1]{0:T(128)} %bitcast.place.refs_0_, bf16[16,2,448,128]{3,2,1,0:T(8,128)(2,1)} %bitcast.14), custom_call_target="tpu_custom_call" | custom-call | tf_op jit(solution)/shard_map/pack/pallas_call | solution.py:154
  2.3 0.1 collective-permute-start.1
  2.4 0.5 collective-permute-start
  2.9 4.2 %own_share.1 = (f32[8,2,7,16,128]{4,3,2,1,0:T(8,128)S(1)}, f32[8,2,7,16,128]{4,3,2,1,0:T(8,128)S(1)}, f32[8,2,7,16,128]{4,3,2,1,0:T(8,128)S(1)}, f32[8,2,7,16,12...) custom-call(s32[1]{0:T(128)} %bitcast.place.refs_0_, s32[3,2,16]{2,1,0:T(2,128)S(1)} %bitcast.12, ...), custom_call_target="tpu_custom_call" | custom-call | flops 5000000 | bytes 8000000 | tf_op jit(solution)/shard_map/own_share/pallas_call | solution.py:224
  7.1 0.3 strength_blocks.1.refs_10_
  7.4 3.9 %join.1 = (bf16[2,240,128]{2,1,0:T(8,128)(2,1)S(1)}, bf16[2,240,128]{2,1,0:T(8,128)(2,1)S(1)}, bf16[2,240,128]{2,1,0:T(8,128)(2,1)S(1)}, bf16[2,240,128]{2,1,0:T...) custom-call(s32[1]{0:T(128)} %bitcast.place.refs_0_, ...), custom_call_target="tpu_custom_call" | custom-call | flops 5000000 | bytes 8000000 | tf_op jit(solution)/shard_map/join/pallas_call | solution.py:337
  11.4 4.5 %collective-permute-start.3 = (bf16[2,240,128]{2,1,0:T(8,128)(2,1)S(1)}, bf16[2,240,128]{2,1,0:T(8,128)(2,1)S(1)}, u32[]{:S(2)}, u32[]{:S(2)}) collective-permute-start(bf16[2,240,128]{2,1,0:T(8,128)(2,1)S(1)} %get-tuple-element.36), channel_id=1, source_target_pairs={{0,12},{1,13},{2,14},{3,15},{4,8},{5,9},{6,10},{7,11},{8,4},{9,5},... | collective-permute-start | bytes 368648 | tf_op jit(solution)/shard_map/ppermute | solution.py:556
  15.9 1.2 %collective-permute-start.4 = (bf16[2,240,128]{2,1,0:T(8,128)(2,1)S(1)}, bf16[2,240,128]{2,1,0:T(8,128)(2,1)S(1)}, u32[]{:S(2)}, u32[]{:S(2)}) collective-permute-start(bf16[2,240,128]{2,1,0:T(8,128)(2,1)S(1)} %get-tuple-element.37), channel_id=1, source_target_pairs={{0,2},{1,3},{2,0},{3,1},{4,6},{5,7},{6,4},{7,5},{8,10},{9,11},{10,... | collective-permute-start | bytes 368648 | tf_op jit(solution)/shard_map/ppermute | solution.py:556
  17.1 1.1 %collective-permute-start.6 = (bf16[2,240,128]{2,1,0:T(8,128)(2,1)S(1)}, bf16[2,240,128]{2,1,0:T(8,128)(2,1)S(1)}, u32[]{:S(2)}, u32[]{:S(2)}) collective-permute-start(bf16[2,240,128]{2,1,0:T(8,128)(2,1)S(1)} %get-tuple-element.39), channel_id=1, source_target_pairs={{0,3},{1,2},{2,1},{3,0},{4,7},{5,6},{6,5},{7,4},{8,11},{9,10},{10,... | collective-permute-start | bytes 368648 | tf_op jit(solution)/shard_map/ppermute | solution.py:556
  18.2 1.4 %collective-permute-start.7 = (bf16[2,240,128]{2,1,0:T(8,128)(2,1)S(1)}, bf16[2,240,128]{2,1,0:T(8,128)(2,1)S(1)}, u32[]{:S(2)}, u32[]{:S(2)}) collective-permute-start(bf16[2,240,128]{2,1,0:T(8,128)(2,1)S(1)} %get-tuple-element.40), channel_id=1, source_target_pairs={{0,13},{1,12},{2,15},{3,14},{4,9},{5,8},{6,11},{7,10},{8,5},{9,4},... | collective-permute-start | bytes 368648 | tf_op jit(solution)/shard_map/ppermute | solution.py:556
  19.6 6.6 %collective-permute-start.8 = (bf16[2,240,128]{2,1,0:T(8,128)(2,1)S(1)}, bf16[2,240,128]{2,1,0:T(8,128)(2,1)S(1)}, u32[]{:S(2)}, u32[]{:S(2)}) collective-permute-start(bf16[2,240,128]{2,1,0:T(8,128)(2,1)S(1)} %get-tuple-element.41), channel_id=1, source_target_pairs={{0,4},{1,5},{2,6},{3,7},{4,0},{5,1},{6,2},{7,3},{8,12},{9,13},{10,... | collective-permute-start | bytes 368648 | tf_op jit(solution)/shard_map/ppermute | solution.py:556
  26.2 2.7 %collective-permute-start.9 = (bf16[2,240,128]{2,1,0:T(8,128)(2,1)S(1)}, bf16[2,240,128]{2,1,0:T(8,128)(2,1)S(1)}, u32[]{:S(2)}, u32[]{:S(2)}) collective-permute-start(bf16[2,240,128]{2,1,0:T(8,128)(2,1)S(1)} %get-tuple-element.42), channel_id=1, source_target_pairs={{0,9},{1,8},{2,11},{3,10},{4,13},{5,12},{6,15},{7,14},{8,1},{9,0},... | collective-permute-start | bytes 368648 | tf_op jit(solution)/shard_map/ppermute | solution.py:556
  29.0 0.7 %collective-permute-start.10 = (bf16[2,240,128]{2,1,0:T(8,128)(2,1)S(1)}, bf16[2,240,128]{2,1,0:T(8,128)(2,1)S(1)}, u32[]{:S(2)}, u32[]{:S(2)}) collective-permute-start(bf16[2,240,128]{2,1,0:T(8,128)(2,1)S(1)} %get-tuple-element.43), channel_id=1, source_target_pairs={{0,5},{1,4},{2,7},{3,6},{4,1},{5,0},{6,3},{7,2},{8,13},{9,12},{10,... | collective-permute-start | bytes 368648 | tf_op jit(solution)/shard_map/ppermute | solution.py:556
  29.7 2.3 %collective-permute-start.11 = (bf16[2,240,128]{2,1,0:T(8,128)(2,1)S(1)}, bf16[2,240,128]{2,1,0:T(8,128)(2,1)S(1)}, u32[]{:S(2)}, u32[]{:S(2)}) collective-permute-start(bf16[2,240,128]{2,1,0:T(8,128)(2,1)S(1)} %get-tuple-element.44), channel_id=1, source_target_pairs={{0,14},{1,15},{2,12},{3,13},{4,10},{5,11},{6,8},{7,9},{8,6},{9,7},... | collective-permute-start | bytes 368648 | tf_op jit(solution)/shard_map/ppermute | solution.py:556
  32.0 2.8 %collective-permute-start.12 = (bf16[2,240,128]{2,1,0:T(8,128)(2,1)S(1)}, bf16[2,240,128]{2,1,0:T(8,128)(2,1)S(1)}, u32[]{:S(2)}, u32[]{:S(2)}) collective-permute-start(bf16[2,240,128]{2,1,0:T(8,128)(2,1)S(1)} %get-tuple-element.45), channel_id=1, source_target_pairs={{0,6},{1,7},{2,4},{3,5},{4,2},{5,3},{6,0},{7,1},{8,14},{9,15},{10,... | collective-permute-start | bytes 368648 | tf_op jit(solution)/shard_map/ppermute | solution.py:556
  34.8 0.6 collective-permute-start.13
  35.4 3.4 %collective-permute-done.9.refs_7_.refs_8_ = bf16[2,240,128]{2,1,0:T(8,128)(2,1)S(1)} collective-permute-done((bf16[2,240,128]{2,1,0:T(8,128)(2,1)S(1)}, bf16[2,240,128]{2,1,0:T(8,128)(2,1)S(1)}, u32[]{:S(2)}, u32[]{:S(2)}) %collective-permute-start.9) | collective-permute-done | bytes 122912 | tf_op jit(solution)/shard_map/ppermute | solution.py:556
  38.8 2.3 %collective-permute-start.15 = (bf16[2,240,128]{2,1,0:T(8,128)(2,1)S(1)}, bf16[2,240,128]{2,1,0:T(8,128)(2,1)S(1)}, u32[]{:S(2)}, u32[]{:S(2)}) collective-permute-start(bf16[2,240,128]{2,1,0:T(8,128)(2,1)S(1)} %get-tuple-element.48), channel_id=1, source_target_pairs={{0,15},{1,14},{2,13},{3,12},{4,11},{5,10},{6,9},{7,8},{8,7},{9,6},... | collective-permute-start | bytes 368648 | tf_op jit(solution)/shard_map/ppermute | solution.py:556
  41.1 1.7 %early_differences.2 = (bf16[2,240,128]{2,1,0:T(8,128)(2,1)S(1)}, f32[2,5,4,4,56,128]{5,4,3,2,1,0:T(8,128)S(1)}) custom-call(s32[1]{0:T(128)} %bitcast.place.refs_0_, bf16[2,240,128]{2,1,0:T(8,128)(2,1)S(1)} %get-tuple-element.34.refs_0_, bf16[2,240,128]{2,1,0:T(8,128)(2,1)S(1)} %collective-permute-done.2.refs_1_, ...), custom_call_target="tpu_custom_call", output_to_operand_aliasing={{0}: (11, {})} | custom-call | flops 5000000 | bytes 4000000 | tf_op jit(solution)/shard_map/early_differences/pallas_call | solution.py:417
  42.8 7.9 %collective-permute-start.16 = (bf16[2,240,128]{2,1,0:T(8,128)(2,1)S(1)}, bf16[2,240,128]{2,1,0:T(8,128)(2,1)S(1)}, u32[]{:S(2)}, u32[]{:S(2)}) collective-permute-start(bf16[2,240,128]{2,1,0:T(8,128)(2,1)S(1)} %get-tuple-element.50), channel_id=1, source_target_pairs={{0,11},{1,10},{2,9},{3,8},{4,15},{5,14},{6,13},{7,12},{8,3},{9,2},... | collective-permute-start | bytes 368648 | tf_op jit(solution)/shard_map/ppermute | solution.py:556
  50.7 3.6 %collective-permute-done.15.refs_3_.refs_14_ = bf16[2,240,128]{2,1,0:T(8,128)(2,1)S(1)} collective-permute-done((bf16[2,240,128]{2,1,0:T(8,128)(2,1)S(1)}, bf16[2,240,128]{2,1,0:T(8,128)(2,1)S(1)}, u32[]{:S(2)}, u32[]{:S(2)}) %collective-permute-start.15) | collective-permute-done | bytes 122912 | tf_op jit(solution)/shard_map/ppermute | solution.py:556
  54.4 0.8 %early_differences.3.refs_17_ = f32[2,2,4,4,56,128]{5,4,3,2,1,0:T(8,128)S(1)} custom-call(s32[1]{0:T(128)} %bitcast.place.refs_0_, bf16[2,240,128]{2,1,0:T(8,128)(2,1)S(1)} %collective-permute-done.12.refs_0_.refs_11_, bf16[2,240,128]{2,1,0:T(8,128)(2,1)S(1)} %collective-permute-done.14.refs_1_.refs_13_, ...), custom_call_target="tpu_custom_call" | custom-call | flops 5000000 | bytes 4000000 | tf_op jit(solution)/shard_map/early_differences/pallas_call | solution.py:417
  55.2 4.4 %collective-permute-done.16.refs_15_ = bf16[2,240,128]{2,1,0:T(8,128)(2,1)S(1)} collective-permute-done((bf16[2,240,128]{2,1,0:T(8,128)(2,1)S(1)}, bf16[2,240,128]{2,1,0:T(8,128)(2,1)S(1)}, u32[]{:S(2)}, u32[]{:S(2)}) %collective-permute-start.16) | collective-permute-done | bytes 122912 | tf_op jit(solution)/shard_map/ppermute | solution.py:556
  59.6 3.3 %score.1 = (bf16[4,56,512]{2,1,0:T(8,128)(2,1)}, bf16[2,4,56,512]{3,2,1,0:T(8,128)(2,1)}) custom-call(s32[1]{0:T(128)} %bitcast.place.refs_0_, bf16[2,240,128]{2,1,0:T(8,128)(2,1)S(1)} %get-tuple-element.34.refs_0_, bf16[2,240,128]{2,1,0:T(8,128)(2,1)S(1)} %collective-permute-done.2.refs_1_, bf16[2,240,128]{2,1,0:T(8,128)(2,1)S(1)} %collective-permute-done.3.refs_8_.refs_2_, ...), custom_call_target="tpu_custom_call" | custom-call | tf_op jit(solution)/shard_map/score/pallas_call | solution.py:517
  (23 shorter events, 0.1 us)
Async XLA Ops:
  0.6 1.8 %copy-start.2 = (s32[16,2,3]{0,1,2:T(2,128)S(1)}, s32[16,2,3]{0,1,2:T(2,128)}, u32[]{:S(2)}) copy-start(s32[16,2,3]{0,1,2:T(2,128)} %param.6) | copy-start | bytes 1156
  2.3 5.1 %collective-permute-start.1 = (bf16[8,2,448,128]{3,2,1,0:T(8,128)(2,1)S(1)}, bf16[8,2,448,128]{3,2,1,0:T(8,128)(2,1)S(1)}, u32[]{:S(2)}, u32[]{:S(2)}) collective-permute-start(bf16[8,2,448,128]{3,2,1,0:T(8,128)(2,1)S(1)} %pack.1), channel_id=1, source_target_pairs={{0,1},{1,0},{2,3},{3,2},{4,5},{5,4},{6,7},{7,6},{8,9},{9,8},{10,11... | collective-permute-start | bytes 5505032 | tf_op jit(solution)/shard_map/ppermute | solution.py:550
  2.4 4.7 %copy-start.1 = (f32[32,896]{1,0:T(8,128)S(1)}, f32[32,896]{1,0:T(8,128)}, u32[]{:S(2)}) copy-start(f32[32,896]{1,0:T(8,128)} %smoothing.1) | copy-start | bytes 344068
  2.4 5.0 %collective-permute-start = (s32[3,2,16]{2,1,0:T(2,128)S(1)}, s32[3,2,16]{2,1,0:T(2,128)S(1)}, u32[]{:S(2)}, u32[]{:S(2)}) collective-permute-start(s32[3,2,16]{2,1,0:T(2,128)S(1)} %bitcast.11), channel_id=1, source_target_pairs={{0,1},{1,0},{2,3},{3,2},{4,5},{5,4},{6,7},{7,6},{8,9},{9,8},{10,11... | collective-permute-start | bytes 1160 | tf_op jit(solution)/shard_map/ppermute | solution.py:551
  11.3 6.9 %collective-permute-start.2 = (bf16[2,240,128]{2,1,0:T(8,128)(2,1)S(1)}, bf16[2,240,128]{2,1,0:T(8,128)(2,1)S(1)}, u32[]{:S(2)}, u32[]{:S(2)}) collective-permute-start(bf16[2,240,128]{2,1,0:T(8,128)(2,1)S(1)} %get-tuple-element.35), channel_id=1, source_target_pairs={{0,1},{1,0},{2,3},{3,2},{4,5},{5,4},{6,7},{7,6},{8,9},{9,8},{10,11... | collective-permute-start | bytes 368648 | tf_op jit(solution)/shard_map/ppermute | solution.py:556
  11.4 8.2 %collective-permute-start.3 = (bf16[2,240,128]{2,1,0:T(8,128)(2,1)S(1)}, bf16[2,240,128]{2,1,0:T(8,128)(2,1)S(1)}, u32[]{:S(2)}, u32[]{:S(2)}) collective-permute-start(bf16[2,240,128]{2,1,0:T(8,128)(2,1)S(1)} %get-tuple-element.36), channel_id=1, source_target_pairs={{0,12},{1,13},{2,14},{3,15},{4,8},{5,9},{6,10},{7,11},{8,4},{9,5},... | collective-permute-start | bytes 368648 | tf_op jit(solution)/shard_map/ppermute | solution.py:556
  15.9 10.4 %collective-permute-start.4 = (bf16[2,240,128]{2,1,0:T(8,128)(2,1)S(1)}, bf16[2,240,128]{2,1,0:T(8,128)(2,1)S(1)}, u32[]{:S(2)}, u32[]{:S(2)}) collective-permute-start(bf16[2,240,128]{2,1,0:T(8,128)(2,1)S(1)} %get-tuple-element.37), channel_id=1, source_target_pairs={{0,2},{1,3},{2,0},{3,1},{4,6},{5,7},{6,4},{7,5},{8,10},{9,11},{10,... | collective-permute-start | bytes 368648 | tf_op jit(solution)/shard_map/ppermute | solution.py:556
  17.1 11.9 %collective-permute-start.5 = (bf16[2,240,128]{2,1,0:T(8,128)(2,1)S(1)}, bf16[2,240,128]{2,1,0:T(8,128)(2,1)S(1)}, u32[]{:S(2)}, u32[]{:S(2)}) collective-permute-start(bf16[2,240,128]{2,1,0:T(8,128)(2,1)S(1)} %get-tuple-element.38), channel_id=1, source_target_pairs={{0,8},{1,9},{2,10},{3,11},{4,12},{5,13},{6,14},{7,15},{8,0},{9,1},... | collective-permute-start | bytes 368648 | tf_op jit(solution)/shard_map/ppermute | solution.py:556
  17.1 12.6 %collective-permute-start.6 = (bf16[2,240,128]{2,1,0:T(8,128)(2,1)S(1)}, bf16[2,240,128]{2,1,0:T(8,128)(2,1)S(1)}, u32[]{:S(2)}, u32[]{:S(2)}) collective-permute-start(bf16[2,240,128]{2,1,0:T(8,128)(2,1)S(1)} %get-tuple-element.39), channel_id=1, source_target_pairs={{0,3},{1,2},{2,1},{3,0},{4,7},{5,6},{6,5},{7,4},{8,11},{9,10},{10,... | collective-permute-start | bytes 368648 | tf_op jit(solution)/shard_map/ppermute | solution.py:556
  18.2 13.8 %collective-permute-start.7 = (bf16[2,240,128]{2,1,0:T(8,128)(2,1)S(1)}, bf16[2,240,128]{2,1,0:T(8,128)(2,1)S(1)}, u32[]{:S(2)}, u32[]{:S(2)}) collective-permute-start(bf16[2,240,128]{2,1,0:T(8,128)(2,1)S(1)} %get-tuple-element.40), channel_id=1, source_target_pairs={{0,13},{1,12},{2,15},{3,14},{4,9},{5,8},{6,11},{7,10},{8,5},{9,4},... | collective-permute-start | bytes 368648 | tf_op jit(solution)/shard_map/ppermute | solution.py:556
  19.6 15.1 %collective-permute-start.8 = (bf16[2,240,128]{2,1,0:T(8,128)(2,1)S(1)}, bf16[2,240,128]{2,1,0:T(8,128)(2,1)S(1)}, u32[]{:S(2)}, u32[]{:S(2)}) collective-permute-start(bf16[2,240,128]{2,1,0:T(8,128)(2,1)S(1)} %get-tuple-element.41), channel_id=1, source_target_pairs={{0,4},{1,5},{2,6},{3,7},{4,0},{5,1},{6,2},{7,3},{8,12},{9,13},{10,... | collective-permute-start | bytes 368648 | tf_op jit(solution)/shard_map/ppermute | solution.py:556
  26.2 12.5 %collective-permute-start.9 = (bf16[2,240,128]{2,1,0:T(8,128)(2,1)S(1)}, bf16[2,240,128]{2,1,0:T(8,128)(2,1)S(1)}, u32[]{:S(2)}, u32[]{:S(2)}) collective-permute-start(bf16[2,240,128]{2,1,0:T(8,128)(2,1)S(1)} %get-tuple-element.42), channel_id=1, source_target_pairs={{0,9},{1,8},{2,11},{3,10},{4,13},{5,12},{6,15},{7,14},{8,1},{9,0},... | collective-permute-start | bytes 368648 | tf_op jit(solution)/shard_map/ppermute | solution.py:556
  29.0 9.8 %collective-permute-start.10 = (bf16[2,240,128]{2,1,0:T(8,128)(2,1)S(1)}, bf16[2,240,128]{2,1,0:T(8,128)(2,1)S(1)}, u32[]{:S(2)}, u32[]{:S(2)}) collective-permute-start(bf16[2,240,128]{2,1,0:T(8,128)(2,1)S(1)} %get-tuple-element.43), channel_id=1, source_target_pairs={{0,5},{1,4},{2,7},{3,6},{4,1},{5,0},{6,3},{7,2},{8,13},{9,12},{10,... | collective-permute-start | bytes 368648 | tf_op jit(solution)/shard_map/ppermute | solution.py:556
  29.7 13.1 %collective-permute-start.11 = (bf16[2,240,128]{2,1,0:T(8,128)(2,1)S(1)}, bf16[2,240,128]{2,1,0:T(8,128)(2,1)S(1)}, u32[]{:S(2)}, u32[]{:S(2)}) collective-permute-start(bf16[2,240,128]{2,1,0:T(8,128)(2,1)S(1)} %get-tuple-element.44), channel_id=1, source_target_pairs={{0,14},{1,15},{2,12},{3,13},{4,10},{5,11},{6,8},{7,9},{8,6},{9,7},... | collective-permute-start | bytes 368648 | tf_op jit(solution)/shard_map/ppermute | solution.py:556
  32.0 18.7 %collective-permute-start.12 = (bf16[2,240,128]{2,1,0:T(8,128)(2,1)S(1)}, bf16[2,240,128]{2,1,0:T(8,128)(2,1)S(1)}, u32[]{:S(2)}, u32[]{:S(2)}) collective-permute-start(bf16[2,240,128]{2,1,0:T(8,128)(2,1)S(1)} %get-tuple-element.45), channel_id=1, source_target_pairs={{0,6},{1,7},{2,4},{3,5},{4,2},{5,3},{6,0},{7,1},{8,14},{9,15},{10,... | collective-permute-start | bytes 368648 | tf_op jit(solution)/shard_map/ppermute | solution.py:556
  34.8 20.4 %collective-permute-start.13 = (bf16[2,240,128]{2,1,0:T(8,128)(2,1)S(1)}, bf16[2,240,128]{2,1,0:T(8,128)(2,1)S(1)}, u32[]{:S(2)}, u32[]{:S(2)}) collective-permute-start(bf16[2,240,128]{2,1,0:T(8,128)(2,1)S(1)} %get-tuple-element.46), channel_id=1, source_target_pairs={{0,10},{1,11},{2,8},{3,9},{4,14},{5,15},{6,12},{7,13},{8,2},{9,3},... | collective-permute-start | bytes 368648 | tf_op jit(solution)/shard_map/ppermute | solution.py:556
  38.8 12.0 %collective-permute-start.14 = (bf16[2,240,128]{2,1,0:T(8,128)(2,1)S(1)}, bf16[2,240,128]{2,1,0:T(8,128)(2,1)S(1)}, u32[]{:S(2)}, u32[]{:S(2)}) collective-permute-start(bf16[2,240,128]{2,1,0:T(8,128)(2,1)S(1)} %get-tuple-element.47), channel_id=1, source_target_pairs={{0,7},{1,6},{2,5},{3,4},{4,3},{5,2},{6,1},{7,0},{8,15},{9,14},{10,... | collective-permute-start | bytes 368648 | tf_op jit(solution)/shard_map/ppermute | solution.py:556
  38.8 15.6 %collective-permute-start.15 = (bf16[2,240,128]{2,1,0:T(8,128)(2,1)S(1)}, bf16[2,240,128]{2,1,0:T(8,128)(2,1)S(1)}, u32[]{:S(2)}, u32[]{:S(2)}) collective-permute-start(bf16[2,240,128]{2,1,0:T(8,128)(2,1)S(1)} %get-tuple-element.48), channel_id=1, source_target_pairs={{0,15},{1,14},{2,13},{3,12},{4,11},{5,10},{6,9},{7,8},{8,7},{9,6},... | collective-permute-start | bytes 368648 | tf_op jit(solution)/shard_map/ppermute | solution.py:556
  41.1 18.5 %copy-start = (bf16[4,512,56]{1,2,0:T(8,128)(2,1)S(1)}, bf16[4,512,56]{1,2,0:T(8,128)(2,1)}, u32[]{:S(2)}) copy-start(bf16[4,512,56]{1,2,0:T(8,128)(2,1)} %param.9) | copy-start | bytes 688132
  42.8 16.8 %collective-permute-start.16 = (bf16[2,240,128]{2,1,0:T(8,128)(2,1)S(1)}, bf16[2,240,128]{2,1,0:T(8,128)(2,1)S(1)}, u32[]{:S(2)}, u32[]{:S(2)}) collective-permute-start(bf16[2,240,128]{2,1,0:T(8,128)(2,1)S(1)} %get-tuple-element.50), channel_id=1, source_target_pairs={{0,11},{1,10},{2,9},{3,8},{4,15},{5,14},{6,13},{7,12},{8,3},{9,2},... | collective-permute-start | bytes 368648 | tf_op jit(solution)/shard_map/ppermute | solution.py:556
